TPU v7x, 32 devices: a whole 2x2x4 slice. The times are simulated.
32 devices in a mesh: layer: 8 (over y, x, core), feat: 4 (over z).
Axes of the slice: x: 2, y: 2, z: 4, core: 2. Of those that a mesh axis runs over, the one named last changes fastest.
Arguments:
- tokens_in: bfloat16 [512, 4096], P('feat', 'layer'), may hold values from -6 to 6
- targets: bfloat16 [512, 4096], P('feat', 'layer'), may hold values from -6 to 6
- enc_weight: bfloat16 [2048, 32768], P(None, ('layer', 'feat')), may hold values from -0.125 to 0.125
- enc_bias: float32 [32768], P(('layer', 'feat')), may hold values from -1 to 0.5
- dec_weight: bfloat16 [2, 32768, 2048], P(None, ('layer', 'feat')), may hold values from -0.046875 to 0.046875
Outputs:
- recon_error: float32 [512, 4096], P('feat', 'layer')
- mean_square: float32 [], replicated
- enc_grad: bfloat16 [2048, 32768], P(None, ('layer', 'feat'))
- bias_grad: float32 [32768], P(('layer', 'feat'))
- dec_grad: bfloat16 [2, 32768, 2048], P(None, ('layer', 'feat'))
All inputs are finite; a program needn't handle non-finite values.
Results may differ from a plain program's by a relative error of at most 0.02.
Values may be sent and summed in bfloat16 or wider, within the bound.
No kernel may reach another device: no remote copies, remote signals or barrier semaphores. Data moves between devices by JAX's collectives and lax.ppermute only.
A program may use at most 128 MiB of HBM per device.

v0:
```python
import jax
import jax.numpy as jnp
from jax import lax
from jax.experimental import pallas as pl
from jax.experimental.pallas import tpu as pltpu
from jax.sharding import PartitionSpec as P

loss_scale = 64.0
tile = 256
in_vmem = pl.BlockSpec(memory_space=pltpu.VMEM)
in_smem = pl.BlockSpec(memory_space=pltpu.SMEM)
in_hbm = pl.BlockSpec(memory_space=pltpu.HBM)


def over_feat(value, mask):
    pairs = [(source, source ^ mask) for source in range(lax.axis_size("feat"))]
    return lax.ppermute(value, "feat", pairs)


def over_members(value, bit_level):
    mask = 2**bit_level
    pairs = [(source, source ^ mask) for source in range(lax.axis_size("layer"))]
    return lax.ppermute(value, "layer", pairs)


def to_layer(value, offset, sub_count):
    count = lax.axis_size("layer")
    shift = offset * sub_count
    pairs = [(p, p + shift) for p in range(count - shift)]
    return lax.ppermute(value, "layer", pairs)


def from_layer(value, offset, sub_count):
    count = lax.axis_size("layer")
    pairs = [(p, (p - offset * sub_count) % count) for p in range(count)]
    return lax.ppermute(value, "layer", pairs)


def after(value, *others):
    return lax.optimization_barrier((value, *others))[0]


def all_over_feat(value):
    blocks = [value, over_feat(value, 1)]
    for s in range(2, lax.axis_size("feat")):
        blocks.append(over_feat(after(value, blocks[1]) if s > 2 else value, s))
    return blocks


def params(flops, bytes_accessed, scratch_mib):
    return dict(
        compiler_params=pltpu.CompilerParams(vmem_limit_bytes=scratch_mib * 1024 * 1024),
        cost_estimate=pl.CostEstimate(
            flops=flops, bytes_accessed=bytes_accessed, transcendentals=0
        ),
    )


def dot(left, right, contract):
    return lax.dot_general(
        left, right, ((contract[:1], contract[1:]), ((), ())), preferred_element_type=jnp.float32
    )


def span(index, size):
    return pl.ds(pl.multiple_of(index * size, size), size)


def fetch(*arrays):
    parts = [(number, start) for number, array in enumerate(arrays) for start in range(4)]

    def kernel(*refs):
        copies = []
        for place, (number, start) in enumerate(parts):
            source, target = refs[number], refs[len(arrays) + number]
            size = source.shape[-2] // 4
            here = (slice(None),) * (len(source.shape) - 2) + (pl.ds(start * size, size),)
            copies.append(
                pltpu.make_async_copy(source.at[here], target.at[here], refs[-1].at[place])
            )
        for copy in copies:
            copy.start()
        for copy in copies:
            copy.wait()

    total = sum(2 * array.size for array in arrays)
    return pl.pallas_call(
        kernel,
        in_specs=[in_hbm] * len(arrays),
        out_specs=[in_vmem] * len(arrays),
        out_shape=[jax.ShapeDtypeStruct(array.shape, array.dtype) for array in arrays],
        scratch_shapes=[pltpu.SemaphoreType.DMA((len(parts),))],
        name="fetch",
        **params(0, total, 14),
    )(*arrays)


def encode(indices, pieces, weights, partial, bias):
    feat_count, rows, cols = pieces[0].shape
    tok = feat_count * rows
    width = weights.shape[1]
    extra = [value for value in (partial, bias) if value is not None]

    def kernel(index_ref, *refs):
        piece_refs, weight_ref = refs[: len(pieces)], refs[len(pieces)]
        extra_refs, out_ref = refs[len(pieces) + 1 : -1], refs[-1]
        left = jnp.concatenate([ref[...].reshape(tok, cols) for ref in piece_refs], 1)
        for start in range(0, width, tile):
            here = slice(start, start + tile)
            right = jnp.concatenate(
                [weight_ref[span(index_ref[i], cols), here] for i in range(len(pieces))], 0
            )
            total = dot(left, right, (1, 0))
            if partial is not None:
                total += extra_refs[0][:, here]
            if bias is None:
                out_ref[:, here] = total
            else:
                pre_act = total + extra_refs[-1][:, here]
                out_ref[0, :, here] = jnp.maximum(pre_act, 0.0).astype(jnp.bfloat16)
                out_ref[1, :, here] = jnp.where(pre_act > 0.0, 1.0, 0.0).astype(jnp.bfloat16)

    if bias is None:
        out_shape = jax.ShapeDtypeStruct((tok, width), jnp.float32)
    else:
        out_shape = jax.ShapeDtypeStruct((2, tok, width), jnp.bfloat16)
    return pl.pallas_call(
        kernel,
        in_specs=[in_smem] + [in_vmem] * (len(pieces) + 1 + len(extra)),
        out_specs=in_vmem,
        out_shape=out_shape,
        name="encode",
        **params(
            2 * len(pieces) * tok * cols * width, 2 * len(pieces) * cols * (tok + width), 4
        ),
    )(indices, *pieces, weights, *extra)


def decode(indices, features, weights, offset, groups, rows, cols):
    _, tok, width = features.shape
    count = indices.shape[0]

    def kernel(index_ref, feat_ref, weight_ref, *out_refs):
        left = feat_ref[0]
        for piece in range(count):
            for start in range(0, cols, tile):
                columns = pl.ds(pl.multiple_of(index_ref[piece] * cols + start, tile), tile)
                product = dot(left, weight_ref[offset, :, columns], (1, 0)).astype(jnp.bfloat16)
                for group, out_ref in zip(groups, out_refs):
                    for place, block in enumerate(group):
                        out_ref[piece, place, :, start : start + tile] = product[
                            block * rows : (block + 1) * rows
                        ]

    return pl.pallas_call(
        kernel,
        in_specs=[in_smem, in_vmem, in_vmem],
        out_specs=[in_vmem] * len(groups),
        out_shape=[
            jax.ShapeDtypeStruct((count, len(group), rows, cols), jnp.bfloat16) for group in groups
        ],
        name="decode",
        **params(2 * count * tok * cols * width, 2 * count * cols * width, 4),
    )(indices, features, weights)


def turned(value):
    count, tok, width = value.shape

    def kernel(in_ref, out_ref):
        for piece in range(count):
            for start in range(0, width, tile):
                out_ref[piece, start : start + tile, :] = in_ref[
                    piece, :, start : start + tile
                ].T

    return pl.pallas_call(
        kernel,
        in_specs=[in_vmem],
        out_specs=in_vmem,
        out_shape=jax.ShapeDtypeStruct((count, width, tok), value.dtype),
        name="turned",
        **params(0, 4 * count * tok * width, 4),
    )(value)


def tree_sum(values):
    while len(values) > 1:
        values = [values[i] + values[i + 1] for i in range(0, len(values), 2)]
    return values[0]


def backward_piece(info, offset, grads, turned_features, dec_weight, feature_grad, dec_grad):
    layers, width, depth = dec_weight.shape
    tok = turned_features.shape[1]
    cols = grads[0].shape[2]
    first = feature_grad is None
    extra = [] if first else [feature_grad, dec_grad]

    def kernel(info_ref, *refs):
        grad_refs = refs[: len(grads)]
        feat_ref, weight_ref = refs[len(grads) : len(grads) + 2]
        out_ref, dec_ref, square_ref, held, sems = refs[-5:]
        columns = span(info_ref[0], cols)
        starts = range(0, width, tile)
        copies = [
            pltpu.make_async_copy(
                held.at[slice(start, start + tile)],
                dec_ref.at[offset, slice(start, start + tile), columns],
                sems.at[place],
            )
            for place, start in enumerate(starts)
        ]
        blocks = [ref[i] for ref in grad_refs for i in range(ref.shape[0])]
        sums = []
        for block in blocks:
            total = jnp.zeros((8, 128), jnp.float32)
            for row in range(0, block.shape[0], 8):
                for col in range(0, cols, 128):
                    part = block[row : row + 8, col : col + 128].astype(jnp.float32)
                    total += part * part
            sums.append(total)
        square_ref[...] = tree_sum(sums)

        def products():
            grad = jnp.concatenate(blocks, 0)
            for copy, start in zip(copies, starts):
                here = slice(start, start + tile)
                held[here] = dot(feat_ref[here], grad, (1, 0)).astype(jnp.bfloat16)
                copy.start()
            for start in starts:
                here = slice(start, start + tile)
                product = dot(grad, weight_ref[offset, here, columns], (1, 1))
                if not first:
                    product += refs[len(grads) + 2][:, here]
                out_ref[:, here] = product

        def nothing():
            held[...] = jnp.zeros_like(held)
            for copy in copies:
                copy.start()
            out_ref[...] = refs[len(grads) + 2][...]

        if offset == 0:
            products()
        else:
            pl.when(info_ref[1] > 0)(products)
            pl.when(info_ref[1] == 0)(nothing)
        for copy in copies:
            copy.wait()

    return pl.pallas_call(
        kernel,
        in_specs=[in_smem]
        + [in_vmem] * (len(grads) + 2)
        + ([] if first else [in_vmem, in_hbm]),
        out_specs=[in_vmem, in_hbm, in_vmem],
        out_shape=[
            jax.ShapeDtypeStruct((tok, width), jnp.float32),
            jax.ShapeDtypeStruct((layers, width, depth), jnp.bfloat16),
            jax.ShapeDtypeStruct((8, 128), jnp.float32),
        ],
        scratch_shapes=[
            pltpu.VMEM((width, cols), jnp.bfloat16),
            pltpu.SemaphoreType.DMA((width // tile,)),
        ],
        input_output_aliases={} if first else {len(grads) + 3: 0, len(grads) + 4: 1},
        name="backward_piece",
        **params(tok * cols, tok * cols, 6),
    )(info, *grads, turned_features, dec_weight, *extra)


def encoder_grad(indices, turned_tokens, features, feature_grad, squares, scale):
    count, cols, tok = turned_tokens[0].shape
    width = features.shape[2]
    pieces = len(turned_tokens) * count

    def kernel(index_ref, *refs):
        token_refs = refs[: len(turned_tokens)]
        mask_ref, grad_ref = refs[len(turned_tokens) : len(turned_tokens) + 2]
        square_refs = refs[len(turned_tokens) + 2 : -6]
        enc_ref, bias_ref, mean_ref, preact, held, sems = refs[-6:]
        mean_ref[...] = scale * jnp.sum(
            tree_sum([ref[...] for ref in square_refs]), (0, 1), keepdims=True
        )
        for start in range(0, width, tile):
            here = slice(start, start + tile)
            kept = jnp.where(mask_ref[1, :, here] > 0.0, grad_ref[:, here], 0.0).astype(jnp.bfloat16)
            preact[:, here] = kept
            bias_ref[:, here] = jnp.sum(kept.astype(jnp.float32), 0, keepdims=True)
        copies = []
        for piece in range(pieces):
            held[piece] = dot(
                token_refs[piece // count][piece % count], preact[...], (1, 0)
            ).astype(jnp.bfloat16)
            copy = pltpu.make_async_copy(
                held.at[piece], enc_ref.at[span(index_ref[piece], cols)], sems.at[piece]
            )
            copy.start()
            copies.append(copy)
        for copy in copies:
            copy.wait()

    return pl.pallas_call(
        kernel,
        in_specs=[in_smem] + [in_vmem] * (len(turned_tokens) + 2 + len(squares)),
        out_specs=[in_hbm, in_vmem, in_vmem],
        out_shape=[
            jax.ShapeDtypeStruct((pieces * cols, width), jnp.bfloat16),
            jax.ShapeDtypeStruct((1, width), jnp.float32),
            jax.ShapeDtypeStruct((1, 1), jnp.float32),
        ],
        scratch_shapes=[
            pltpu.VMEM((tok, width), jnp.bfloat16),
            pltpu.VMEM((pieces, cols, width), jnp.bfloat16),
            pltpu.SemaphoreType.DMA((pieces,)),
        ],
        name="encoder_grad",
        **params(
            2 * pieces * tok * cols * width, 2 * pieces * cols * (tok + width) + 6 * tok * width, 10
        ),
    )(indices, *turned_tokens, features, feature_grad, *squares)


def add_pair(left, right):
    return (left.astype(jnp.float32) + right.astype(jnp.float32)).astype(jnp.bfloat16)


def on_device(tokens_in, targets, enc_weight, enc_bias, dec_weight):
    layers, width, depth = dec_weight.shape
    feat_count = lax.axis_size("feat")
    sub_count = lax.axis_size("layer") // layers
    member = lax.axis_index("layer") % sub_count
    rows, cols = tokens_in.shape
    tok = feat_count * rows
    bit_count = sub_count.bit_length() - 1
    near = member ^ (2 * jnp.arange(sub_count // 2, dtype=jnp.int32))
    far = near ^ 1
    groups = [list(range(feat_count // 2)), list(range(feat_count // 2, feat_count))]

    enc_weight = pltpu.with_memory_space_constraint(enc_weight, pltpu.HBM)
    dec_weight = pltpu.with_memory_space_constraint(dec_weight, pltpu.HBM)

    held = {0: all_over_feat(tokens_in)}
    for bit_level in range(bit_count - 1, 0, -1):
        for rel in list(held):
            held[rel ^ 2**bit_level] = [None] * feat_count
    for s in range(feat_count):
        known = [0]
        for bit_level in range(bit_count - 1, 0, -1):
            for rel in known:
                held[rel ^ 2**bit_level][s] = over_members(held[rel][s], bit_level)
            known += [rel ^ 2**bit_level for rel in known]
    order = [rel for pair in sorted(held) for rel in (pair, pair ^ 1)]
    enc_held, dec_held = fetch(enc_weight, after(dec_weight, held[0][1]))
    early = [held[rel][s] for rel in order[2::2] for s in range(2)]
    tokens = {0: after(jnp.stack(held[0], 0), enc_held, *early)}
    tokens[1] = over_members(tokens[0], 0)
    index = {rel: (member ^ rel).reshape(1) for rel in order}
    partial = encode(
        jnp.concatenate([index[0], index[1]]), [tokens[0], tokens[1]], enc_held, None, None
    )
    for rel in order[2::2]:
        tokens[rel] = jnp.stack([after(block, partial) for block in held[rel]], 0)
        tokens[rel ^ 1] = over_members(tokens[rel], 0)
    for rel in order[2:-1]:
        partial = encode(index[rel], [tokens[rel]], enc_held, partial, None)
    features = encode(index[order[-1]], [tokens[order[-1]]], enc_held, partial, enc_bias[None])

    current, source = {}, features
    for k in reversed(range(layers)):
        sent = decode(far, source, dec_held, k, groups, rows, cols)
        kept = decode(near, source, dec_held, k, groups, rows, cols)
        for place in reversed(range(len(groups))):
            current[place, k] = add_pair(kept[place], over_members(sent[place], 0))
        source = after(features, current[len(groups) - 1, k])
    turns = sorted(current, reverse=True)
    joined = {}
    for bit_level in range(1, bit_count):
        halves = {}
        for turn, value in current.items():
            split = value.reshape((value.shape[0] // 2, 2) + value.shape[1:])
            halves[turn] = (split[:, 0], split[:, 1])
        if bit_level == bit_count - 1:
            for k in range(1, layers):
                joined[k], sent = halves.pop((0, k))
                sent = to_layer(sent, k, sub_count)
                halves[0, 0] = (halves[0, 0][0], add_pair(halves[0, 0][1], sent))
        turns = [turn for turn in turns if turn in halves]
        received, operands = [], []
        for turn in turns:
            operand = halves[turn][1]
            if len(received) > 1:
                operand = after(operand, received[-2], operands[-1])
            operands.append(operand)
            received.append(over_members(operand, bit_level))
        for place, turn in enumerate(turns):
            arrived = after(received[place], *operands[place + 1 :][:1])
            if bit_level < bit_count - 1:
                current[turn] = add_pair(halves[turn][0], arrived)
            else:
                current[turn] = (halves[turn][0], arrived)
    blocks, operands = [None] * feat_count, []
    for place in reversed(range(len(groups))):
        total = sum(part.astype(jnp.float32) for part in current[place, 0])
        for k in range(1, layers):
            if place > 0:
                moved = to_layer(add_pair(*current[place, k]), k, sub_count)
            else:
                moved = to_layer(after(joined[k], *operands), k, sub_count)
            total = total + moved.astype(jnp.float32)
        for spot, block in enumerate(groups[place]):
            if block == 0:
                rebuilt = total[0, spot]
            else:
                operands.append(total[0, spot].astype(jnp.bfloat16))
                blocks[block] = over_feat(operands[-1], block)
    for block in reversed(blocks[1:]):
        rebuilt = rebuilt + block.astype(jnp.float32)
    turned_features = turned(source[:1])[0]
    turned_tokens = [
        turned(after(tokens[rel], turned_features).reshape(1, tok, cols)) for rel in order
    ]
    (dec_held,) = fetch(after(dec_weight, turned_features))
    recon_error = rebuilt - after(targets, dec_held, *turned_tokens).astype(jnp.float32)
    scaled = (loss_scale / tok * recon_error).astype(jnp.bfloat16)

    layer = lax.axis_index("layer") // sub_count
    there = [(layer + k < layers).astype(jnp.int32) for k in range(layers)]
    blocks = all_over_feat(scaled)
    stages = [[0]]
    for level in range(bit_count - 1, 0, -1):
        known = [rel for stage in stages for rel in stage]
        stages.append([rel ^ 2**level for rel in known])
    spans = [[s] for s in range(min(2, feat_count))]
    spans += [list(range(2, feat_count))] if feat_count > 2 else []
    groups_of = {(0, k): [None] * len(spans) for k in range(layers)}
    early, last = [], len(spans) - 1
    for place, group in enumerate(spans):
        stacked = jnp.stack([after(blocks[s], *early) for s in group], 0)
        groups_of[0, 0][place] = stacked
        for k in range(1, layers):
            groups_of[0, k][place] = from_layer(stacked, k, sub_count)
        known = [0]
        for level in range(bit_count - 1, 0, -1):
            for rel in known:
                other = rel ^ 2**level
                for k in range(layers):
                    if k == 0 or place < last:
                        part = over_members(groups_of[rel, k][place], level)
                    else:
                        part = from_layer(groups_of[other, 0][place], k, sub_count)
                    groups_of.setdefault((other, k), [None] * len(spans))[place] = part
            known += [rel ^ 2**level for rel in known]
        if place == last - 1:
            early = [part for parts in groups_of.values() for part in parts if part is not None]
            early.pop()

    feature_grad, dec_grad, squares = None, None, {}
    for number, stage in enumerate(stages):
        for k in range(layers):
            if k > 0 and number + 1 < len(stages):
                guard = [part for rel in stages[number + 1] for part in groups_of[rel, k - 1]]
                feature_grad = after(feature_grad, *guard)
            for rel in stage:
                parts = groups_of[rel, k]
                if feature_grad is not None:
                    parts = [after(part, feature_grad) for part in parts]
                groups_of[rel ^ 1, k] = [over_members(part, 0) for part in parts]
                for half in (rel, rel ^ 1):
                    if k == 0 and number > 0:
                        coming = groups_of[rel, layers - 1][-(half % 2)]
                        feature_grad = after(feature_grad, coming)
                    feature_grad, dec_grad, squares[k, half] = backward_piece(
                        jnp.stack([member ^ half, there[k]]),
                        k,
                        groups_of[half, k],
                        turned_features,
                        dec_held,
                        feature_grad,
                        dec_grad,
                    )
    scale = (tok / loss_scale) ** 2 / (layers * tok * depth)
    enc_grad, bias_grad, mean_square = encoder_grad(
        jnp.stack([member ^ rel for rel in order]),
        turned_tokens,
        features,
        feature_grad,
        [squares[key] for key in sorted(squares)],
        scale,
    )
    return (recon_error, mean_square[0, 0], enc_grad, bias_grad[0], dec_grad)


def solution(mesh):
    placed = (
        P("feat", "layer"),
        P("feat", "layer"),
        P(None, ("layer", "feat")),
        P(("layer", "feat")),
        P(None, ("layer", "feat"), None),
    )
    return jax.shard_map(
        on_device,
        mesh=mesh,
        in_specs=placed,
        out_specs=(
            P("feat", "layer"),
            P(),
            P(None, ("layer", "feat")),
            P(("layer", "feat")),
            P(None, ("layer", "feat"), None),
        ),
        check_vma=False,
    )
```

profile of v0, /device:TPU:0, one launch (start us, length us, event | category | flops | bytes accessed | tf_op | source)
XLA Modules:
  0.0 143.1 jit_solution(14633439962961466150)
XLA Ops:
  0.6 3.1 %collective-permute-start.1 = (bf16[128,512]{1,0:T(8,128)(2,1)}, bf16[128,512]{1,0:T(8,128)(2,1)S(1)}, u32[]{:S(2)}, u32[]{:S(2)}) collective-permute-start(bf16[128,512]{1,0:T(8,128)(2,1)} %param.5), channel_id=1, source_target_pairs={{0,1},{1,0},{2,3},{3,2},{4,5},{5,4},{6,7},{7,6},{8,9},{9,8},{10,11... | collective-permute-start | bytes 393224 | tf_op jit(solution)/shard_map/ppermute | solution.py:17
  3.7 2.6 %collective-permute-start.2 = (bf16[128,512]{1,0:T(8,128)(2,1)}, bf16[128,512]{1,0:T(8,128)(2,1)S(1)}, u32[]{:S(2)}, u32[]{:S(2)}) collective-permute-start(bf16[128,512]{1,0:T(8,128)(2,1)} %param.5), channel_id=1, source_target_pairs={{0,2},{1,3},{2,0},{3,1},{4,6},{5,7},{6,4},{7,5},{8,10},{9,11},{10,... | collective-permute-start | bytes 393224 | tf_op jit(solution)/shard_map/ppermute | solution.py:17
  6.3 2.9 %collective-permute-done.1 = bf16[128,512]{1,0:T(8,128)(2,1)S(1)} collective-permute-done((bf16[128,512]{1,0:T(8,128)(2,1)}, bf16[128,512]{1,0:T(8,128)(2,1)S(1)}, u32[]{:S(2)}, u32[]{:S(2)}) %collective-permute-start.1) | collective-permute-done | bytes 131104 | tf_op jit(solution)/shard_map/ppermute | solution.py:17
  9.2 3.5 %collective-permute-start.3 = (bf16[128,512]{1,0:T(8,128)(2,1)}, bf16[128,512]{1,0:T(8,128)(2,1)}, u32[]{:S(2)}, u32[]{:S(2)}) collective-permute-start(bf16[128,512]{1,0:T(8,128)(2,1)} %param.5), channel_id=1, source_target_pairs={{0,3},{1,2},{2,1},{3,0},{4,7},{5,6},{6,5},{7,4},{8,11},{9,10},{10,... | collective-permute-start | bytes 393224 | tf_op jit(solution)/shard_map/ppermute | solution.py:17
  12.8 1.5 %collective-permute-start = (bf16[128,512]{1,0:T(8,128)(2,1)}, bf16[128,512]{1,0:T(8,128)(2,1)S(1)}, u32[]{:S(2)}, u32[]{:S(2)}) collective-permute-start(bf16[128,512]{1,0:T(8,128)(2,1)} %param.5), channel_id=1, source_target_pairs={{0,8},{4,12},{8,0},{12,4},{16,24},{20,28},{24,16},{28,20},{1,9},{5... | collective-permute-start | bytes 393224 | tf_op jit(solution)/shard_map/ppermute | solution.py:23
  14.3 0.5 collective-permute-start.4
  14.8 4.7 %fetch.2 = (bf16[2048,1024]{1,0:T(8,128)(2,1)S(1)}, bf16[2,1024,2048]{2,1,0:T(8,128)(2,1)S(1)}) custom-call(bf16[2048,1024]{1,0:T(8,128)(2,1)} %refs_0_.1, bf16[2,1024,2048]{2,1,0:T(8,128)(2,1)} %refs_0_.2), custom_call_target="tpu_custom_call" | custom-call | bytes 12582912 | tf_op jit(solution)/shard_map/fetch/pallas_call | solution.py:87
  19.6 3.4 %copy-done.3 = bf16[2,1024,2048]{2,1,0:T(8,128)(2,1)} copy-done((bf16[2,1024,2048]{2,1,0:T(8,128)(2,1)}, bf16[2,1024,2048]{2,1,0:T(8,128)(2,1)S(1)}, u32[]{:S(2)}) %copy-start.3) | copy-done | bytes 8388632
  23.0 2.0 %copy-done.6 = bf16[2048,1024]{1,0:T(8,128)(2,1)} copy-done((bf16[2048,1024]{1,0:T(8,128)(2,1)}, bf16[2048,1024]{1,0:T(8,128)(2,1)S(1)}, u32[]{:S(2)}) %copy-start.6) | copy-done | bytes 4194328
  25.0 1.0 pad_maximum_fusion.refs_0_
  26.1 1.6 %collective-permute-start.6 = (bf16[128,512]{1,0:T(8,128)(2,1)S(1)}, bf16[128,512]{1,0:T(8,128)(2,1)S(1)}, u32[]{:S(2)}, u32[]{:S(2)}) collective-permute-start(bf16[128,512]{1,0:T(8,128)(2,1)S(1)} %collective-permute-done.2), channel_id=1, source_target_pairs={{0,8},{4,12},{8,0},{12,4},{16,24},{20,28},{24,16},{28,20},{1,9},{5... | collective-permute-start | bytes 393224 | tf_op jit(solution)/shard_map/ppermute | solution.py:23
  27.6 0.5 collective-permute-start.7
  28.2 2.2 %copy-done.7 = bf16[2048,1024]{1,0:T(8,128)(2,1)S(1)} copy-done((bf16[2048,1024]{1,0:T(8,128)(2,1)S(1)}, bf16[2048,1024]{1,0:T(8,128)(2,1)}, u32[]{:S(2)}) %copy-start.7) | copy-done | bytes 4194328
  30.4 1.8 %encode.3.refs_2_ = f32[512,1024]{1,0:T(8,128)S(1)} custom-call(s32[2]{0:T(128)S(1)} %pad_add_fusion.index_ref, bf16[4,128,512]{2,1,0:T(8,128)(2,1)S(1)} %pad_maximum_fusion.refs_0_, bf16[4,128,512]{2,1,0:T(8,128)(2,1)S(1)} %collective-permute-done.5.refs_1_, bf16[2048,1024]{1,0:T(8,128)(2,1)S(1)} %copy-done.7), custom_call_target="tpu_custom_call" | custom-call | flops 1073741824 | bytes 3145728 | tf_op jit(solution)/shard_map/encode/pallas_call | solution.py:127
  32.2 2.5 %collective-permute-done.7 = bf16[128,512]{1,0:T(8,128)(2,1)S(1)} collective-permute-done((bf16[128,512]{1,0:T(8,128)(2,1)}, bf16[128,512]{1,0:T(8,128)(2,1)S(1)}, u32[]{:S(2)}, u32[]{:S(2)}) %collective-permute-start.7) | collective-permute-done | bytes 131104 | tf_op jit(solution)/shard_map/ppermute | solution.py:23
  35.0 2.3 %copy-done.8 = bf16[2048,1024]{1,0:T(8,128)(2,1)S(1)} copy-done((bf16[2048,1024]{1,0:T(8,128)(2,1)S(1)}, bf16[2048,1024]{1,0:T(8,128)(2,1)}, u32[]{:S(2)}) %copy-start.8) | copy-done | bytes 4194328
  37.3 0.7 encode.4.refs_2_
  38.0 0.9 encode.5.feat_ref.refs_4_
  38.9 0.7 slice-done.2
  39.7 2.2 %slice-done.3 = s8[4194304]{0:T(1024)(128)(4,1)S(1)} async-done(((s8[8388608]{0:T(1024)(128)(4,1)}), s8[4194304]{0:T(1024)(128)(4,1)S(1)}, s32[]{:S(2)}) %slice-start.3) | async-done | bytes 4194328
  41.8 1.8 %decode.5 = (bf16[2,2,128,512]{3,2,1,0:T(8,128)(2,1)S(1)}, bf16[2,2,128,512]{3,2,1,0:T(8,128)(2,1)S(1)}) custom-call(s32[2]{0:T(128)S(1)} %get-tuple-element.154.index_ref, bf16[2,512,1024]{2,1,0:T(8,128)(2,1)S(1)} %encode.5.feat_ref.refs_4_, bf16[2,1024,2048]{2,1,0:T(8,128)(2,1)S(1)} %bitcast.80), custom_call_target="tpu_custom_call" | custom-call | flops 1073741824 | bytes 2097152 | tf_op jit(solution)/shard_map/decode/pallas_call | solution.py:155
  44.2 1.8 %decode.4 = (bf16[2,2,128,512]{3,2,1,0:T(8,128)(2,1)S(1)}, bf16[2,2,128,512]{3,2,1,0:T(8,128)(2,1)S(1)}) custom-call(s32[2]{0:T(128)S(1)} %get-tuple-element.153.index_ref, bf16[2,512,1024]{2,1,0:T(8,128)(2,1)S(1)} %encode.5.feat_ref.refs_4_, bf16[2,1024,2048]{2,1,0:T(8,128)(2,1)S(1)} %bitcast.80), custom_call_target="tpu_custom_call" | custom-call | flops 1073741824 | bytes 2097152 | tf_op jit(solution)/shard_map/decode/pallas_call | solution.py:155
  46.2 1.8 %decode.7 = (bf16[2,2,128,512]{3,2,1,0:T(8,128)(2,1)S(1)}, bf16[2,2,128,512]{3,2,1,0:T(8,128)(2,1)S(1)}) custom-call(s32[2]{0:T(128)S(1)} %get-tuple-element.154.index_ref, bf16[2,512,1024]{2,1,0:T(8,128)(2,1)S(1)} %encode.5.feat_ref.refs_4_, bf16[2,1024,2048]{2,1,0:T(8,128)(2,1)S(1)} %bitcast.80), custom_call_target="tpu_custom_call" | custom-call | flops 1073741824 | bytes 2097152 | tf_op jit(solution)/shard_map/decode/pallas_call | solution.py:155
  48.8 3.5 %collective-permute-start.12 = (bf16[1,2,128,512]{3,2,1,0:T(8,128)(2,1)S(1)}, bf16[1,2,128,512]{3,2,1,0:T(8,128)(2,1)S(1)}, u32[]{:S(2)}, u32[]{:S(2)}) collective-permute-start(bf16[1,2,128,512]{3,2,1,0:T(8,128)(2,1)S(1)} %get-tuple-element.149), channel_id=1, source_target_pairs={{0,16},{4,20},{8,24},{12,28},{1,17},{5,21},{9,25},{13,29},{2,18},{... | collective-permute-start | bytes 786440 | tf_op jit(solution)/shard_map/ppermute | solution.py:30
  52.3 1.6 %collective-permute-start.13 = (bf16[1,2,128,512]{3,2,1,0:T(8,128)(2,1)S(1)}, bf16[1,2,128,512]{3,2,1,0:T(8,128)(2,1)S(1)}, u32[]{:S(2)}, u32[]{:S(2)}) collective-permute-start(bf16[1,2,128,512]{3,2,1,0:T(8,128)(2,1)S(1)} %slice_bitcast_fusion.5), channel_id=1, source_target_pairs={{0,8},{4,12},{8,0},{12,4},{16,24},{20,28},{24,16},{28,20},{1,9},{5... | collective-permute-start | bytes 786440 | tf_op jit(solution)/shard_map/ppermute | solution.py:23
  53.8 1.8 %decode.6 = (bf16[2,2,128,512]{3,2,1,0:T(8,128)(2,1)S(1)}, bf16[2,2,128,512]{3,2,1,0:T(8,128)(2,1)S(1)}) custom-call(s32[2]{0:T(128)S(1)} %get-tuple-element.153.index_ref, bf16[2,512,1024]{2,1,0:T(8,128)(2,1)S(1)} %encode.5.feat_ref.refs_4_, bf16[2,1024,2048]{2,1,0:T(8,128)(2,1)S(1)} %bitcast.80), custom_call_target="tpu_custom_call" | custom-call | flops 1073741824 | bytes 2097152 | tf_op jit(solution)/shard_map/decode/pallas_call | solution.py:155
  55.8 0.6 collective-permute-start.16
  56.4 5.1 %collective-permute-done.13 = bf16[1,2,128,512]{3,2,1,0:T(8,128)(2,1)S(1)} collective-permute-done((bf16[1,2,128,512]{3,2,1,0:T(8,128)(2,1)S(1)}, bf16[1,2,128,512]{3,2,1,0:T(8,128)(2,1)S(1)}, u32[]{:S(2)}, u32[]{:S(2)}) %collective-permute-start.13) | collective-permute-done | bytes 262176 | tf_op jit(solution)/shard_map/ppermute | solution.py:23
  61.6 1.3 collective-permute-start.17
  63.2 1.6 %collective-permute-start.15 = (bf16[1,2,128,512]{3,2,1,0:T(8,128)(2,1)S(1)}, bf16[1,2,128,512]{3,2,1,0:T(8,128)(2,1)S(1)}, u32[]{:S(2)}, u32[]{:S(2)}) collective-permute-start(bf16[1,2,128,512]{3,2,1,0:T(8,128)(2,1)S(1)} %fusion.5), channel_id=1, source_target_pairs={{0,8},{4,12},{8,0},{12,4},{16,24},{20,28},{24,16},{28,20},{1,9},{5... | collective-permute-start | bytes 786440 | tf_op jit(solution)/shard_map/ppermute | solution.py:23
  64.7 2.4 %collective-permute-done.16 = bf16[1,2,128,512]{3,2,1,0:T(8,128)(2,1)S(1)} collective-permute-done((bf16[1,2,128,512]{3,2,1,0:T(8,128)(2,1)S(1)}, bf16[1,2,128,512]{3,2,1,0:T(8,128)(2,1)S(1)}, u32[]{:S(2)}, u32[]{:S(2)}) %collective-permute-start.16) | collective-permute-done | bytes 262176 | tf_op jit(solution)/shard_map/ppermute | solution.py:23
  67.7 4.7 %collective-permute-start.18 = (bf16[1,2,128,512]{3,2,1,0:T(8,128)(2,1)S(1)}, bf16[1,2,128,512]{3,2,1,0:T(8,128)(2,1)S(1)}, u32[]{:S(2)}, u32[]{:S(2)}) collective-permute-start(bf16[1,2,128,512]{3,2,1,0:T(8,128)(2,1)S(1)} %get-tuple-element.97), channel_id=1, source_target_pairs={{0,16},{4,20},{8,24},{12,28},{1,17},{5,21},{9,25},{13,29},{2,18},{... | collective-permute-start | bytes 786440 | tf_op jit(solution)/shard_map/ppermute | solution.py:30
  72.4 0.7 collective-permute-start.19
  73.1 3.0 %collective-permute-done.18 = bf16[1,2,128,512]{3,2,1,0:T(8,128)(2,1)S(1)} collective-permute-done((bf16[1,2,128,512]{3,2,1,0:T(8,128)(2,1)S(1)}, bf16[1,2,128,512]{3,2,1,0:T(8,128)(2,1)S(1)}, u32[]{:S(2)}, u32[]{:S(2)}) %collective-permute-start.18) | collective-permute-done | bytes 262176 | tf_op jit(solution)/shard_map/ppermute | solution.py:30
  76.2 0.9 collective-permute-start.21
  78.1 0.8 copy-done.21
  79.1 0.8 copy-done.23
  79.9 3.5 %fetch.3.refs_4_ = bf16[2,1024,2048]{2,1,0:T(8,128)(2,1)S(1)} custom-call(bf16[2,1024,2048]{2,1,0:T(8,128)(2,1)} %refs_0_.2), custom_call_target="tpu_custom_call" | custom-call | bytes 8388608 | tf_op jit(solution)/shard_map/fetch/pallas_call | solution.py:87
  83.4 3.3 %copy-done = bf16[2,1024,2048]{2,1,0:T(8,128)(2,1)} copy-done((bf16[2,1024,2048]{2,1,0:T(8,128)(2,1)}, bf16[2,1024,2048]{2,1,0:T(8,128)(2,1)S(1)}, u32[]{:S(2)}) %copy-start) | copy-done | bytes 8388632
  86.8 0.8 multiply_convert_fusion
  87.6 1.2 collective-permute-start.26
  88.8 2.5 %collective-permute-start.22 = (bf16[1,128,512]{2,1,0:T(8,128)(2,1)S(1)}, bf16[1,128,512]{2,1,0:T(8,128)(2,1)}, u32[]{:S(2)}, u32[]{:S(2)}) collective-permute-start(bf16[1,128,512]{2,1,0:T(8,128)(2,1)S(1)} %bitcast.93), channel_id=1, source_target_pairs={{0,16},{4,20},{8,24},{12,28},{16,0},{20,4},{24,8},{28,12},{1,17},{... | collective-permute-start | bytes 393224 | tf_op jit(solution)/shard_map/ppermute | solution.py:36
  91.3 1.5 %collective-permute-start.24 = (bf16[1,128,512]{2,1,0:T(8,128)(2,1)S(1)}, bf16[1,128,512]{2,1,0:T(8,128)(2,1)S(1)}, u32[]{:S(2)}, u32[]{:S(2)}) collective-permute-start(bf16[1,128,512]{2,1,0:T(8,128)(2,1)S(1)} %bitcast.94), channel_id=1, source_target_pairs={{0,8},{4,12},{8,0},{12,4},{16,24},{20,28},{24,16},{28,20},{1,9},{5... | collective-permute-start | bytes 393224 | tf_op jit(solution)/shard_map/ppermute | solution.py:23
  93.1 2.6 %collective-permute-start.29 = (bf16[1,128,512]{2,1,0:T(8,128)(2,1)}, bf16[1,128,512]{2,1,0:T(8,128)(2,1)S(1)}, u32[]{:S(2)}, u32[]{:S(2)}) collective-permute-start(bf16[1,128,512]{2,1,0:T(8,128)(2,1)} %bitcast.37.refs_1_), channel_id=1, source_target_pairs={{0,16},{4,20},{8,24},{12,28},{16,0},{20,4},{24,8},{28,12},{1,17},{... | collective-permute-start | bytes 393224 | tf_op jit(solution)/shard_map/ppermute | solution.py:36
  95.7 1.3 collective-permute-start.30
  97.0 0.8 collective-permute-start.23
  98.0 2.7 %collective-permute-done.28 = bf16[128,512]{1,0:T(8,128)(2,1)S(1)} collective-permute-done((bf16[128,512]{1,0:T(8,128)(2,1)S(1)}, bf16[128,512]{1,0:T(8,128)(2,1)S(1)}, u32[]{:S(2)}, u32[]{:S(2)}) %collective-permute-start.28) | collective-permute-done | bytes 131104 | tf_op jit(solution)/shard_map/ppermute | solution.py:17
  100.7 1.6 %collective-permute-done.23.refs_0_ = bf16[1,128,512]{2,1,0:T(8,128)(2,1)S(1)} collective-permute-done((bf16[1,128,512]{2,1,0:T(8,128)(2,1)}, bf16[1,128,512]{2,1,0:T(8,128)(2,1)S(1)}, u32[]{:S(2)}, u32[]{:S(2)}) %collective-permute-start.23) | collective-permute-done | bytes 131104 | tf_op jit(solution)/shard_map/ppermute | solution.py:23
  102.3 2.2 %collective-permute-done.31 = bf16[128,512]{1,0:T(8,128)(2,1)S(1)} collective-permute-done((bf16[128,512]{1,0:T(8,128)(2,1)S(1)}, bf16[128,512]{1,0:T(8,128)(2,1)S(1)}, u32[]{:S(2)}, u32[]{:S(2)}) %collective-permute-start.31) | collective-permute-done | bytes 131104 | tf_op jit(solution)/shard_map/ppermute | solution.py:17
  104.6 1.4 collective-permute-start.33
  106.5 0.5 collective-permute-start.27
  107.2 3.4 %copy-done.1 = bf16[2,1024,2048]{2,1,0:T(8,128)(2,1)S(1)} copy-done((bf16[2,1024,2048]{2,1,0:T(8,128)(2,1)S(1)}, bf16[2,1024,2048]{2,1,0:T(8,128)(2,1)}, u32[]{:S(2)}) %copy-start.1) | copy-done | bytes 8388632
  110.6 2.4 %backward_piece.8 = (f32[512,1024]{1,0:T(8,128)S(1)}, bf16[2,1024,2048]{2,1,0:T(8,128)(2,1)}, f32[8,128]{1,0:T(8,128)S(1)}) custom-call(s32[2]{0:T(128)S(1)} %pad_add_fusion.9.info_ref, bf16[1,128,512]{2,1,0:T(8,128)(2,1)S(1)} %bitcast.96, bf16[1,128,512]{2,1,0:T(8,128)(2,1)} %bitcast.37.refs_1_, bf16[2,128,512]{2,1,0:T(8,128)(2,1)S(1)} %pad_maximum_fusion.2.refs_2_, ...), custom_call_target="tpu_custom_call" | custom-call | flops 262144 | bytes 262144 | tf_op jit(solution)/shard_map/backward_piece/pallas_call | solution.py:252
  113.0 2.5 %backward_piece.9 = (f32[512,1024]{1,0:T(8,128)S(1)}, bf16[2,1024,2048]{2,1,0:T(8,128)(2,1)}, f32[8,128]{1,0:T(8,128)S(1)}) custom-call(s32[2]{0:T(128)S(1)} %pad_add_fusion.4.info_ref, bf16[1,128,512]{2,1,0:T(8,128)(2,1)S(1)} %collective-permute-done.25.refs_0_, ...), custom_call_target="tpu_custom_call", output_to_operand_aliasing={{0}: (6, {}), {1}: (7, {})} | custom-call | flops 262144 | bytes 262144 | tf_op jit(solution)/shard_map/backward_piece/pallas_call | solution.py:252
  116.4 1.6 %collective-permute-start.41 = (bf16[2,128,512]{2,1,0:T(8,128)(2,1)}, bf16[2,128,512]{2,1,0:T(8,128)(2,1)S(1)}, u32[]{:S(2)}, u32[]{:S(2)}) collective-permute-start(bf16[2,128,512]{2,1,0:T(8,128)(2,1)} %collective-permute-done.33.refs_2_), channel_id=1, source_target_pairs={{0,16},{4,20},{8,24},{12,28},{16,0},{20,4},{24,8},{28,12},{1,17},{... | collective-permute-start | bytes 786440 | tf_op jit(solution)/shard_map/ppermute | solution.py:36
  117.9 3.4 %copy-done.2 = bf16[2,1024,2048]{2,1,0:T(8,128)(2,1)S(1)} copy-done((bf16[2,1024,2048]{2,1,0:T(8,128)(2,1)S(1)}, bf16[2,1024,2048]{2,1,0:T(8,128)(2,1)}, u32[]{:S(2)}) %copy-start.2) | copy-done | bytes 8388632
  121.3 2.6 %backward_piece.10 = (f32[512,1024]{1,0:T(8,128)S(1)}, bf16[2,1024,2048]{2,1,0:T(8,128)(2,1)}, f32[8,128]{1,0:T(8,128)S(1)}) custom-call(s32[2]{0:T(128)S(1)} %pad_add_fusion.8.info_ref, bf16[1,128,512]{2,1,0:T(8,128)(2,1)} %collective-permute-done.22.refs_0_, bf16[1,128,512]{2,1,0:T(8,128)(2,1)S(1)} %copy-done.28, ...), custom_call_target="tpu_custom_call", output_to_operand_aliasing={{0}: (6, {}), {1}: (7, {})} | custom-call | flops 262144 | bytes 262144 | tf_op jit(solution)/shard_map/backward_piece/pallas_call | solution.py:252
  124.0 2.1 %backward_piece.11 = (f32[512,1024]{1,0:T(8,128)S(1)}, bf16[2,1024,2048]{2,1,0:T(8,128)(2,1)}, f32[8,128]{1,0:T(8,128)S(1)}) custom-call(s32[2]{0:T(128)S(1)} %pad_add_fusion.5.info_ref, bf16[1,128,512]{2,1,0:T(8,128)(2,1)S(1)} %collective-permute-done.34.refs_0_, ...), custom_call_target="tpu_custom_call", output_to_operand_aliasing={{0}: (6, {}), {1}: (7, {})} | custom-call | flops 262144 | bytes 262144 | tf_op jit(solution)/shard_map/backward_piece/pallas_call | solution.py:252
  126.9 0.7 collective-permute-start.43
  127.9 2.4 %backward_piece.12 = (f32[512,1024]{1,0:T(8,128)S(1)}, bf16[2,1024,2048]{2,1,0:T(8,128)(2,1)}, f32[8,128]{1,0:T(8,128)S(1)}) custom-call(s32[2]{0:T(128)S(1)} %pad_add_fusion.7.info_ref, bf16[1,128,512]{2,1,0:T(8,128)(2,1)S(1)} %copy-done.30, bf16[1,128,512]{2,1,0:T(8,128)(2,1)S(1)} %copy-done.32, ...), custom_call_target="tpu_custom_call", output_to_operand_aliasing={{0}: (6, {}), {1}: (7, {})} | custom-call | flops 262144 | bytes 262144 | tf_op jit(solution)/shard_map/backward_piece/pallas_call | solution.py:252
  130.4 2.0 %backward_piece.13 = (f32[512,1024]{1,0:T(8,128)S(1)}, bf16[2,1024,2048]{2,1,0:T(8,128)(2,1)}, f32[8,128]{1,0:T(8,128)S(1)}) custom-call(s32[2]{0:T(128)S(1)} %pad_add_fusion.2.info_ref, bf16[1,128,512]{2,1,0:T(8,128)(2,1)S(1)} %collective-permute-done.38.refs_0_, ...), custom_call_target="tpu_custom_call", output_to_operand_aliasing={{0}: (6, {}), {1}: (7, {})} | custom-call | flops 262144 | bytes 262144 | tf_op jit(solution)/shard_map/backward_piece/pallas_call | solution.py:252
  133.4 2.3 %backward_piece.14 = (f32[512,1024]{1,0:T(8,128)S(1)}, bf16[2,1024,2048]{2,1,0:T(8,128)(2,1)}, f32[8,128]{1,0:T(8,128)S(1)}) custom-call(s32[2]{0:T(128)S(1)} %pad_add_fusion.6.info_ref, bf16[1,128,512]{2,1,0:T(8,128)(2,1)S(1)} %copy-done.26, bf16[1,128,512]{2,1,0:T(8,128)(2,1)S(1)} %collective-permute-done.43.refs_1_, ...), custom_call_target="tpu_custom_call", output_to_operand_aliasing={{0}: (6, {}), {1}: (7, {})} | custom-call | flops 262144 | bytes 262144 | tf_op jit(solution)/shard_map/backward_piece/pallas_call | solution.py:252
  135.8 2.1 %backward_piece.15 = (f32[512,1024]{1,0:T(8,128)S(1)}, bf16[2,1024,2048]{2,1,0:T(8,128)(2,1)}, f32[8,128]{1,0:T(8,128)S(1)}) custom-call(s32[2]{0:T(128)S(1)} %pad_add_fusion.3.info_ref, bf16[1,128,512]{2,1,0:T(8,128)(2,1)S(1)} %collective-permute-done.42.refs_0_, ...), custom_call_target="tpu_custom_call", output_to_operand_aliasing={{0}: (6, {}), {1}: (7, {})} | custom-call | flops 262144 | bytes 262144 | tf_op jit(solution)/shard_map/backward_piece/pallas_call | solution.py:252
  138.3 4.7 %encoder_grad.1 = (bf16[2048,1024]{1,0:T(8,128)(2,1)}, f32[1,1024]{1,0:T(1,128)}, f32[1,1]{1,0:T(1,128)}) custom-call(s32[4]{0:T(128)S(1)} %pad_add_fusion.1.index_ref, bf16[1,512,512]{2,1,0:T(8,128)(2,1)S(1)} %copy-done.24, bf16[1,512,512]{2,1,0:T(8,128)(2,1)S(1)} %copy-done.22, bf16[1,512,512]{2,1,0:T(8,128)(2,1)S(1)} %copy-done.20, ...), custom_call_target="tpu_custom_call" | custom-call | flops 2147483648 | bytes 9437184 | tf_op jit(solution)/shard_map/encoder_grad/pallas_call | solution.py:304
  (162 shorter events, 8.8 us)
Async XLA Ops:
  0.6 24.3 %copy-start.35 = (bf16[128,512]{1,0:T(8,128)(2,1)S(1)}, bf16[128,512]{1,0:T(8,128)(2,1)}, u32[]{:S(2)}) copy-start(bf16[128,512]{1,0:T(8,128)(2,1)} %param.5) | copy-start | bytes 393220
  0.6 8.6 %collective-permute-start.1 = (bf16[128,512]{1,0:T(8,128)(2,1)}, bf16[128,512]{1,0:T(8,128)(2,1)S(1)}, u32[]{:S(2)}, u32[]{:S(2)}) collective-permute-start(bf16[128,512]{1,0:T(8,128)(2,1)} %param.5), channel_id=1, source_target_pairs={{0,1},{1,0},{2,3},{3,2},{4,5},{5,4},{6,7},{7,6},{8,9},{9,8},{10,11... | collective-permute-start | bytes 393224 | tf_op jit(solution)/shard_map/ppermute | solution.py:17
  3.7 21.2 %collective-permute-start.2 = (bf16[128,512]{1,0:T(8,128)(2,1)}, bf16[128,512]{1,0:T(8,128)(2,1)S(1)}, u32[]{:S(2)}, u32[]{:S(2)}) collective-permute-start(bf16[128,512]{1,0:T(8,128)(2,1)} %param.5), channel_id=1, source_target_pairs={{0,2},{1,3},{2,0},{3,1},{4,6},{5,7},{6,4},{7,5},{8,10},{9,11},{10,... | collective-permute-start | bytes 393224 | tf_op jit(solution)/shard_map/ppermute | solution.py:17
  9.2 15.7 %collective-permute-start.3 = (bf16[128,512]{1,0:T(8,128)(2,1)}, bf16[128,512]{1,0:T(8,128)(2,1)}, u32[]{:S(2)}, u32[]{:S(2)}) collective-permute-start(bf16[128,512]{1,0:T(8,128)(2,1)} %param.5), channel_id=1, source_target_pairs={{0,3},{1,2},{2,1},{3,0},{4,7},{5,6},{6,5},{7,4},{8,11},{9,10},{10,... | collective-permute-start | bytes 393224 | tf_op jit(solution)/shard_map/ppermute | solution.py:17
  12.8 13.2 %collective-permute-start = (bf16[128,512]{1,0:T(8,128)(2,1)}, bf16[128,512]{1,0:T(8,128)(2,1)S(1)}, u32[]{:S(2)}, u32[]{:S(2)}) collective-permute-start(bf16[128,512]{1,0:T(8,128)(2,1)} %param.5), channel_id=1, source_target_pairs={{0,8},{4,12},{8,0},{12,4},{16,24},{20,28},{24,16},{28,20},{1,9},{5... | collective-permute-start | bytes 393224 | tf_op jit(solution)/shard_map/ppermute | solution.py:23
  14.3 11.7 %collective-permute-start.4 = (bf16[128,512]{1,0:T(8,128)(2,1)S(1)}, bf16[128,512]{1,0:T(8,128)(2,1)S(1)}, u32[]{:S(2)}, u32[]{:S(2)}) collective-permute-start(bf16[128,512]{1,0:T(8,128)(2,1)S(1)} %collective-permute-done.1), channel_id=1, source_target_pairs={{0,8},{4,12},{8,0},{12,4},{16,24},{20,28},{24,16},{28,20},{1,9},{5... | collective-permute-start | bytes 393224 | tf_op jit(solution)/shard_map/ppermute | solution.py:23
  19.5 3.4 %copy-start.3 = (bf16[2,1024,2048]{2,1,0:T(8,128)(2,1)}, bf16[2,1024,2048]{2,1,0:T(8,128)(2,1)S(1)}, u32[]{:S(2)}) copy-start(bf16[2,1024,2048]{2,1,0:T(8,128)(2,1)S(1)} %get-tuple-element.84.weight_ref) | copy-start | bytes 25165828
  25.9 8.8 %copy-start.11 = (bf16[4,128,512]{2,1,0:T(8,128)(2,1)}, bf16[4,128,512]{2,1,0:T(8,128)(2,1)S(1)}, u32[]{:S(2)}) copy-start(bf16[4,128,512]{2,1,0:T(8,128)(2,1)S(1)} %pad_maximum_fusion.refs_0_) | copy-start | bytes 1572868
  26.0 2.3 %collective-permute-start.5 = (bf16[4,128,512]{2,1,0:T(8,128)(2,1)S(1)}, bf16[4,128,512]{2,1,0:T(8,128)(2,1)S(1)}, u32[]{:S(2)}, u32[]{:S(2)}) collective-permute-start(bf16[4,128,512]{2,1,0:T(8,128)(2,1)S(1)} %pad_maximum_fusion.refs_0_), channel_id=1, source_target_pairs={{0,4},{4,0},{8,12},{12,8},{16,20},{20,16},{24,28},{28,24},{1,5},{5... | collective-permute-start | bytes 1572872 | tf_op jit(solution)/shard_map/ppermute | solution.py:23
  26.1 8.7 %collective-permute-start.6 = (bf16[128,512]{1,0:T(8,128)(2,1)S(1)}, bf16[128,512]{1,0:T(8,128)(2,1)S(1)}, u32[]{:S(2)}, u32[]{:S(2)}) collective-permute-start(bf16[128,512]{1,0:T(8,128)(2,1)S(1)} %collective-permute-done.2), channel_id=1, source_target_pairs={{0,8},{4,12},{8,0},{12,4},{16,24},{20,28},{24,16},{28,20},{1,9},{5... | collective-permute-start | bytes 393224 | tf_op jit(solution)/shard_map/ppermute | solution.py:23
  27.6 7.1 %collective-permute-start.7 = (bf16[128,512]{1,0:T(8,128)(2,1)}, bf16[128,512]{1,0:T(8,128)(2,1)S(1)}, u32[]{:S(2)}, u32[]{:S(2)}) collective-permute-start(bf16[128,512]{1,0:T(8,128)(2,1)} %collective-permute-done.3), channel_id=1, source_target_pairs={{0,8},{4,12},{8,0},{12,4},{16,24},{20,28},{24,16},{28,20},{1,9},{5... | collective-permute-start | bytes 393224 | tf_op jit(solution)/shard_map/ppermute | solution.py:23
  30.4 4.4 %copy-start.15 = (bf16[4,128,512]{2,1,0:T(8,128)(2,1)}, bf16[4,128,512]{2,1,0:T(8,128)(2,1)S(1)}, u32[]{:S(2)}) copy-start(bf16[4,128,512]{2,1,0:T(8,128)(2,1)S(1)} %collective-permute-done.5.refs_1_) | copy-start | bytes 1572868
  34.9 3.1 %copy-start.9 = (bf16[4,128,512]{2,1,0:T(8,128)(2,1)}, bf16[4,128,512]{2,1,0:T(8,128)(2,1)S(1)}, u32[]{:S(2)}) copy-start(bf16[4,128,512]{2,1,0:T(8,128)(2,1)S(1)} %pad_maximum_fusion.1.refs_0_) | copy-start | bytes 1572868
  34.9 3.1 %collective-permute-start.8 = (bf16[4,128,512]{2,1,0:T(8,128)(2,1)S(1)}, bf16[4,128,512]{2,1,0:T(8,128)(2,1)S(1)}, u32[]{:S(2)}, u32[]{:S(2)}) collective-permute-start(bf16[4,128,512]{2,1,0:T(8,128)(2,1)S(1)} %pad_maximum_fusion.1.refs_0_), channel_id=1, source_target_pairs={{0,4},{4,0},{8,12},{12,8},{16,20},{20,16},{24,28},{28,24},{1,5},{5... | collective-permute-start | bytes 1572872 | tf_op jit(solution)/shard_map/ppermute | solution.py:23
  38.0 3.8 %slice-start.3 = ((s8[8388608]{0:T(1024)(128)(4,1)}), s8[4194304]{0:T(1024)(128)(4,1)S(1)}, s32[]{:S(2)}) async-start(s8[8388608]{0:T(1024)(128)(4,1)} %bitcast.79), calls=%async_computation.3 | async-start | bytes 8388608
  38.9 38.2 %copy-start.4 = (bf16[2,512,1024]{2,1,0:T(8,128)(2,1)}, bf16[2,512,1024]{2,1,0:T(8,128)(2,1)S(1)}, u32[]{:S(2)}) copy-start(bf16[2,512,1024]{2,1,0:T(8,128)(2,1)S(1)} %encode.5.feat_ref.refs_4_) | copy-start | bytes 6291460
  43.6 2.4 %collective-permute-start.9 = (bf16[2,2,128,512]{3,2,1,0:T(8,128)(2,1)S(1)}, bf16[2,2,128,512]{3,2,1,0:T(8,128)(2,1)S(1)}, u32[]{:S(2)}, u32[]{:S(2)}) collective-permute-start(bf16[2,2,128,512]{3,2,1,0:T(8,128)(2,1)S(1)} %get-tuple-element.86), channel_id=1, source_target_pairs={{0,4},{4,0},{8,12},{12,8},{16,20},{20,16},{24,28},{28,24},{1,5},{5... | collective-permute-start | bytes 1572872 | tf_op jit(solution)/shard_map/ppermute | solution.py:23
  44.1 4.5 %collective-permute-start.11 = (bf16[2,2,128,512]{3,2,1,0:T(8,128)(2,1)S(1)}, bf16[2,2,128,512]{3,2,1,0:T(8,128)(2,1)S(1)}, u32[]{:S(2)}, u32[]{:S(2)}) collective-permute-start(bf16[2,2,128,512]{3,2,1,0:T(8,128)(2,1)S(1)} %get-tuple-element.91), channel_id=1, source_target_pairs={{0,4},{4,0},{8,12},{12,8},{16,20},{20,16},{24,28},{28,24},{1,5},{5... | collective-permute-start | bytes 1572872 | tf_op jit(solution)/shard_map/ppermute | solution.py:23
  48.0 14.9 %collective-permute-start.10 = (bf16[2,2,128,512]{3,2,1,0:T(8,128)(2,1)S(1)}, bf16[2,2,128,512]{3,2,1,0:T(8,128)(2,1)S(1)}, u32[]{:S(2)}, u32[]{:S(2)}) collective-permute-start(bf16[2,2,128,512]{3,2,1,0:T(8,128)(2,1)S(1)} %get-tuple-element.89), channel_id=1, source_target_pairs={{0,4},{4,0},{8,12},{12,8},{16,20},{20,16},{24,28},{28,24},{1,5},{5... | collective-permute-start | bytes 1572872 | tf_op jit(solution)/shard_map/ppermute | solution.py:23
  48.5 7.2 %collective-permute-start.14 = (bf16[2,2,128,512]{3,2,1,0:T(8,128)(2,1)S(1)}, bf16[2,2,128,512]{3,2,1,0:T(8,128)(2,1)S(1)}, u32[]{:S(2)}, u32[]{:S(2)}) collective-permute-start(bf16[2,2,128,512]{3,2,1,0:T(8,128)(2,1)S(1)} %get-tuple-element.93), channel_id=1, source_target_pairs={{0,4},{4,0},{8,12},{12,8},{16,20},{20,16},{24,28},{28,24},{1,5},{5... | collective-permute-start | bytes 1572872 | tf_op jit(solution)/shard_map/ppermute | solution.py:23
  48.8 14.3 %collective-permute-start.12 = (bf16[1,2,128,512]{3,2,1,0:T(8,128)(2,1)S(1)}, bf16[1,2,128,512]{3,2,1,0:T(8,128)(2,1)S(1)}, u32[]{:S(2)}, u32[]{:S(2)}) collective-permute-start(bf16[1,2,128,512]{3,2,1,0:T(8,128)(2,1)S(1)} %get-tuple-element.149), channel_id=1, source_target_pairs={{0,16},{4,20},{8,24},{12,28},{1,17},{5,21},{9,25},{13,29},{2,18},{... | collective-permute-start | bytes 786440 | tf_op jit(solution)/shard_map/ppermute | solution.py:30
  52.3 9.2 %collective-permute-start.13 = (bf16[1,2,128,512]{3,2,1,0:T(8,128)(2,1)S(1)}, bf16[1,2,128,512]{3,2,1,0:T(8,128)(2,1)S(1)}, u32[]{:S(2)}, u32[]{:S(2)}) collective-permute-start(bf16[1,2,128,512]{3,2,1,0:T(8,128)(2,1)S(1)} %slice_bitcast_fusion.5), channel_id=1, source_target_pairs={{0,8},{4,12},{8,0},{12,4},{16,24},{20,28},{24,16},{28,20},{1,9},{5... | collective-permute-start | bytes 786440 | tf_op jit(solution)/shard_map/ppermute | solution.py:23
  55.8 11.3 %collective-permute-start.16 = (bf16[1,2,128,512]{3,2,1,0:T(8,128)(2,1)S(1)}, bf16[1,2,128,512]{3,2,1,0:T(8,128)(2,1)S(1)}, u32[]{:S(2)}, u32[]{:S(2)}) collective-permute-start(bf16[1,2,128,512]{3,2,1,0:T(8,128)(2,1)S(1)} %slice_bitcast_fusion.4), channel_id=1, source_target_pairs={{0,8},{4,12},{8,0},{12,4},{16,24},{20,28},{24,16},{28,20},{1,9},{5... | collective-permute-start | bytes 786440 | tf_op jit(solution)/shard_map/ppermute | solution.py:23
  61.6 6.0 %collective-permute-start.17 = (bf16[1,2,128,512]{3,2,1,0:T(8,128)(2,1)S(1)}, bf16[1,2,128,512]{3,2,1,0:T(8,128)(2,1)S(1)}, u32[]{:S(2)}, u32[]{:S(2)}) collective-permute-start(bf16[1,2,128,512]{3,2,1,0:T(8,128)(2,1)S(1)} %fusion.2), channel_id=1, source_target_pairs={{0,16},{4,20},{8,24},{12,28},{1,17},{5,21},{9,25},{13,29},{2,18},{... | collective-permute-start | bytes 786440 | tf_op jit(solution)/shard_map/ppermute | solution.py:30
  63.1 14.4 %copy-start.14 = (bf16[4,128,512]{2,1,0:T(8,128)(2,1)S(1)}, bf16[4,128,512]{2,1,0:T(8,128)(2,1)}, u32[]{:S(2)}) copy-start(bf16[4,128,512]{2,1,0:T(8,128)(2,1)} %copy-done.13) | copy-start | bytes 1572868
  63.2 14.5 %copy-start.10 = (bf16[4,128,512]{2,1,0:T(8,128)(2,1)S(1)}, bf16[4,128,512]{2,1,0:T(8,128)(2,1)}, u32[]{:S(2)}) copy-start(bf16[4,128,512]{2,1,0:T(8,128)(2,1)} %copy-done.9) | copy-start | bytes 1572868
  63.2 10.0 %collective-permute-start.15 = (bf16[1,2,128,512]{3,2,1,0:T(8,128)(2,1)S(1)}, bf16[1,2,128,512]{3,2,1,0:T(8,128)(2,1)S(1)}, u32[]{:S(2)}, u32[]{:S(2)}) collective-permute-start(bf16[1,2,128,512]{3,2,1,0:T(8,128)(2,1)S(1)} %fusion.5), channel_id=1, source_target_pairs={{0,8},{4,12},{8,0},{12,4},{16,24},{20,28},{24,16},{28,20},{1,9},{5... | collective-permute-start | bytes 786440 | tf_op jit(solution)/shard_map/ppermute | solution.py:23
  67.7 10.2 %copy-start.16 = (bf16[4,128,512]{2,1,0:T(8,128)(2,1)S(1)}, bf16[4,128,512]{2,1,0:T(8,128)(2,1)}, u32[]{:S(2)}) copy-start(bf16[4,128,512]{2,1,0:T(8,128)(2,1)} %copy-done.15) | copy-start | bytes 1572868
  67.7 11.2 %copy-start.12 = (bf16[4,128,512]{2,1,0:T(8,128)(2,1)S(1)}, bf16[4,128,512]{2,1,0:T(8,128)(2,1)}, u32[]{:S(2)}) copy-start(bf16[4,128,512]{2,1,0:T(8,128)(2,1)} %copy-done.11) | copy-start | bytes 1572868
  67.7 8.4 %collective-permute-start.18 = (bf16[1,2,128,512]{3,2,1,0:T(8,128)(2,1)S(1)}, bf16[1,2,128,512]{3,2,1,0:T(8,128)(2,1)S(1)}, u32[]{:S(2)}, u32[]{:S(2)}) collective-permute-start(bf16[1,2,128,512]{3,2,1,0:T(8,128)(2,1)S(1)} %get-tuple-element.97), channel_id=1, source_target_pairs={{0,16},{4,20},{8,24},{12,28},{1,17},{5,21},{9,25},{13,29},{2,18},{... | collective-permute-start | bytes 786440 | tf_op jit(solution)/shard_map/ppermute | solution.py:30
  72.4 14.3 %collective-permute-start.19 = (bf16[128,512]{1,0:T(8,128)(2,1)S(1)}, bf16[128,512]{1,0:T(8,128)(2,1)S(1)}, u32[]{:S(2)}, u32[]{:S(2)}) collective-permute-start(bf16[128,512]{1,0:T(8,128)(2,1)S(1)} %get-tuple-element.151), channel_id=1, source_target_pairs={{0,3},{1,2},{2,1},{3,0},{4,7},{5,6},{6,5},{7,4},{8,11},{9,10},{10,... | collective-permute-start | bytes 393224 | tf_op jit(solution)/shard_map/ppermute | solution.py:17
  73.1 13.6 %collective-permute-start.20 = (bf16[128,512]{1,0:T(8,128)(2,1)S(1)}, bf16[128,512]{1,0:T(8,128)(2,1)S(1)}, u32[]{:S(2)}, u32[]{:S(2)}) collective-permute-start(bf16[128,512]{1,0:T(8,128)(2,1)S(1)} %get-tuple-element.152), channel_id=1, source_target_pairs={{0,2},{1,3},{2,0},{3,1},{4,6},{5,7},{6,4},{7,5},{8,10},{9,11},{10,... | collective-permute-start | bytes 393224 | tf_op jit(solution)/shard_map/ppermute | solution.py:17
  76.2 10.5 %collective-permute-start.21 = (bf16[128,512]{1,0:T(8,128)(2,1)S(1)}, bf16[128,512]{1,0:T(8,128)(2,1)S(1)}, u32[]{:S(2)}, u32[]{:S(2)}) collective-permute-start(bf16[128,512]{1,0:T(8,128)(2,1)S(1)} %fusion.11), channel_id=1, source_target_pairs={{0,1},{1,0},{2,3},{3,2},{4,5},{5,4},{6,7},{7,6},{8,9},{9,8},{10,11... | collective-permute-start | bytes 393224 | tf_op jit(solution)/shard_map/ppermute | solution.py:17
  79.9 6.9 %copy-start.34 = (bf16[128,512]{1,0:T(8,128)(2,1)S(1)}, bf16[128,512]{1,0:T(8,128)(2,1)}, u32[]{:S(2)}) copy-start(bf16[128,512]{1,0:T(8,128)(2,1)} %param.6) | copy-start | bytes 393220
  83.4 3.3 %copy-start = (bf16[2,1024,2048]{2,1,0:T(8,128)(2,1)}, bf16[2,1024,2048]{2,1,0:T(8,128)(2,1)S(1)}, u32[]{:S(2)}) copy-start(bf16[2,1024,2048]{2,1,0:T(8,128)(2,1)S(1)} %fetch.3.refs_4_) | copy-start | bytes 25165828
  87.6 5.6 %collective-permute-start.26 = (bf16[128,512]{1,0:T(8,128)(2,1)S(1)}, bf16[128,512]{1,0:T(8,128)(2,1)}, u32[]{:S(2)}, u32[]{:S(2)}) collective-permute-start(bf16[128,512]{1,0:T(8,128)(2,1)S(1)} %get-tuple-element.106), channel_id=1, source_target_pairs={{0,1},{1,0},{2,3},{3,2},{4,5},{5,4},{6,7},{7,6},{8,9},{9,8},{10,11... | collective-permute-start | bytes 393224 | tf_op jit(solution)/shard_map/ppermute | solution.py:17
  88.8 8.2 %collective-permute-start.22 = (bf16[1,128,512]{2,1,0:T(8,128)(2,1)S(1)}, bf16[1,128,512]{2,1,0:T(8,128)(2,1)}, u32[]{:S(2)}, u32[]{:S(2)}) collective-permute-start(bf16[1,128,512]{2,1,0:T(8,128)(2,1)S(1)} %bitcast.93), channel_id=1, source_target_pairs={{0,16},{4,20},{8,24},{12,28},{16,0},{20,4},{24,8},{28,12},{1,17},{... | collective-permute-start | bytes 393224 | tf_op jit(solution)/shard_map/ppermute | solution.py:36
  91.3 6.5 %collective-permute-start.24 = (bf16[1,128,512]{2,1,0:T(8,128)(2,1)S(1)}, bf16[1,128,512]{2,1,0:T(8,128)(2,1)S(1)}, u32[]{:S(2)}, u32[]{:S(2)}) collective-permute-start(bf16[1,128,512]{2,1,0:T(8,128)(2,1)S(1)} %bitcast.94), channel_id=1, source_target_pairs={{0,8},{4,12},{8,0},{12,4},{16,24},{20,28},{24,16},{28,20},{1,9},{5... | collective-permute-start | bytes 393224 | tf_op jit(solution)/shard_map/ppermute | solution.py:23
  92.8 7.9 %collective-permute-start.28 = (bf16[128,512]{1,0:T(8,128)(2,1)S(1)}, bf16[128,512]{1,0:T(8,128)(2,1)S(1)}, u32[]{:S(2)}, u32[]{:S(2)}) collective-permute-start(bf16[128,512]{1,0:T(8,128)(2,1)S(1)} %get-tuple-element.106), channel_id=1, source_target_pairs={{0,2},{1,3},{2,0},{3,1},{4,6},{5,7},{6,4},{7,5},{8,10},{9,11},{10,... | collective-permute-start | bytes 393224 | tf_op jit(solution)/shard_map/ppermute | solution.py:17
  93.1 9.2 %collective-permute-start.29 = (bf16[1,128,512]{2,1,0:T(8,128)(2,1)}, bf16[1,128,512]{2,1,0:T(8,128)(2,1)S(1)}, u32[]{:S(2)}, u32[]{:S(2)}) collective-permute-start(bf16[1,128,512]{2,1,0:T(8,128)(2,1)} %bitcast.37.refs_1_), channel_id=1, source_target_pairs={{0,16},{4,20},{8,24},{12,28},{16,0},{20,4},{24,8},{28,12},{1,17},{... | collective-permute-start | bytes 393224 | tf_op jit(solution)/shard_map/ppermute | solution.py:36
  95.7 6.6 %collective-permute-start.30 = (bf16[1,128,512]{2,1,0:T(8,128)(2,1)}, bf16[1,128,512]{2,1,0:T(8,128)(2,1)S(1)}, u32[]{:S(2)}, u32[]{:S(2)}) collective-permute-start(bf16[1,128,512]{2,1,0:T(8,128)(2,1)} %bitcast.37.refs_1_), channel_id=1, source_target_pairs={{0,8},{4,12},{8,0},{12,4},{16,24},{20,28},{24,16},{28,20},{1,9},{5... | collective-permute-start | bytes 393224 | tf_op jit(solution)/shard_map/ppermute | solution.py:23
  97.0 5.3 %collective-permute-start.23 = (bf16[1,128,512]{2,1,0:T(8,128)(2,1)}, bf16[1,128,512]{2,1,0:T(8,128)(2,1)S(1)}, u32[]{:S(2)}, u32[]{:S(2)}) collective-permute-start(bf16[1,128,512]{2,1,0:T(8,128)(2,1)} %collective-permute-done.22.refs_0_), channel_id=1, source_target_pairs={{0,8},{4,12},{8,0},{12,4},{16,24},{20,28},{24,16},{28,20},{1,9},{5... | collective-permute-start | bytes 393224 | tf_op jit(solution)/shard_map/ppermute | solution.py:23
  97.7 6.8 %copy-start.29 = (bf16[1,128,512]{2,1,0:T(8,128)(2,1)}, bf16[1,128,512]{2,1,0:T(8,128)(2,1)S(1)}, u32[]{:S(2)}) copy-start(bf16[1,128,512]{2,1,0:T(8,128)(2,1)S(1)} %collective-permute-done.24.refs_0_) | copy-start | bytes 393220
  97.7 6.8 %collective-permute-start.31 = (bf16[128,512]{1,0:T(8,128)(2,1)S(1)}, bf16[128,512]{1,0:T(8,128)(2,1)S(1)}, u32[]{:S(2)}, u32[]{:S(2)}) collective-permute-start(bf16[128,512]{1,0:T(8,128)(2,1)S(1)} %get-tuple-element.106), channel_id=1, source_target_pairs={{0,3},{1,2},{2,1},{3,0},{4,7},{5,6},{6,5},{7,4},{8,11},{9,10},{10,... | collective-permute-start | bytes 393224 | tf_op jit(solution)/shard_map/ppermute | solution.py:17
  104.6 8.4 %collective-permute-start.32 = (bf16[2,128,512]{2,1,0:T(8,128)(2,1)S(1)}, bf16[2,128,512]{2,1,0:T(8,128)(2,1)}, u32[]{:S(2)}, u32[]{:S(2)}) collective-permute-start(bf16[2,128,512]{2,1,0:T(8,128)(2,1)S(1)} %pad_maximum_fusion.2.refs_2_), channel_id=1, source_target_pairs={{0,4},{4,0},{8,12},{12,8},{16,20},{20,16},{24,28},{28,24},{1,5},{5... | collective-permute-start | bytes 786440 | tf_op jit(solution)/shard_map/ppermute | solution.py:23
  104.6 10.9 %collective-permute-start.33 = (bf16[2,128,512]{2,1,0:T(8,128)(2,1)S(1)}, bf16[2,128,512]{2,1,0:T(8,128)(2,1)}, u32[]{:S(2)}, u32[]{:S(2)}) collective-permute-start(bf16[2,128,512]{2,1,0:T(8,128)(2,1)S(1)} %pad_maximum_fusion.2.refs_2_), channel_id=1, source_target_pairs={{0,8},{4,12},{8,0},{12,4},{16,24},{20,28},{24,16},{28,20},{1,9},{5... | collective-permute-start | bytes 786440 | tf_op jit(solution)/shard_map/ppermute | solution.py:23
  106.1 9.5 %collective-permute-start.36 = (bf16[2,128,512]{2,1,0:T(8,128)(2,1)S(1)}, bf16[2,128,512]{2,1,0:T(8,128)(2,1)}, u32[]{:S(2)}, u32[]{:S(2)}) collective-permute-start(bf16[2,128,512]{2,1,0:T(8,128)(2,1)S(1)} %pad_maximum_fusion.2.refs_2_), channel_id=1, source_target_pairs={{0,16},{4,20},{8,24},{12,28},{16,0},{20,4},{24,8},{28,12},{1,17},{... | collective-permute-start | bytes 786440 | tf_op jit(solution)/shard_map/ppermute | solution.py:36
  106.5 6.4 %collective-permute-start.25 = (bf16[1,128,512]{2,1,0:T(8,128)(2,1)S(1)}, bf16[1,128,512]{2,1,0:T(8,128)(2,1)S(1)}, u32[]{:S(2)}, u32[]{:S(2)}) collective-permute-start(bf16[1,128,512]{2,1,0:T(8,128)(2,1)S(1)} %bitcast.95), channel_id=1, source_target_pairs={{0,4},{4,0},{8,12},{12,8},{16,20},{20,16},{24,28},{28,24},{1,5},{5... | collective-permute-start | bytes 393224 | tf_op jit(solution)/shard_map/ppermute | solution.py:23
  106.5 6.5 %collective-permute-start.27 = (bf16[1,128,512]{2,1,0:T(8,128)(2,1)}, bf16[1,128,512]{2,1,0:T(8,128)(2,1)S(1)}, u32[]{:S(2)}, u32[]{:S(2)}) collective-permute-start(bf16[1,128,512]{2,1,0:T(8,128)(2,1)} %bitcast.37.refs_1_), channel_id=1, source_target_pairs={{0,4},{4,0},{8,12},{12,8},{16,20},{20,16},{24,28},{28,24},{1,5},{5... | collective-permute-start | bytes 393224 | tf_op jit(solution)/shard_map/ppermute | solution.py:23
  107.2 3.4 %copy-start.1 = (bf16[2,1024,2048]{2,1,0:T(8,128)(2,1)S(1)}, bf16[2,1024,2048]{2,1,0:T(8,128)(2,1)}, u32[]{:S(2)}) copy-start(bf16[2,1024,2048]{2,1,0:T(8,128)(2,1)} %copy-done) | copy-start | bytes 25165828
  115.5 8.4 %collective-permute-start.37 = (bf16[2,128,512]{2,1,0:T(8,128)(2,1)}, bf16[2,128,512]{2,1,0:T(8,128)(2,1)S(1)}, u32[]{:S(2)}, u32[]{:S(2)}) collective-permute-start(bf16[2,128,512]{2,1,0:T(8,128)(2,1)} %collective-permute-done.36.refs_2_), channel_id=1, source_target_pairs={{0,4},{4,0},{8,12},{12,8},{16,20},{20,16},{24,28},{28,24},{1,5},{5... | collective-permute-start | bytes 786440 | tf_op jit(solution)/shard_map/ppermute | solution.py:23
  115.6 8.3 %collective-permute-start.35 = (bf16[1,128,512]{2,1,0:T(8,128)(2,1)S(1)}, bf16[1,128,512]{2,1,0:T(8,128)(2,1)S(1)}, u32[]{:S(2)}, u32[]{:S(2)}) collective-permute-start(bf16[1,128,512]{2,1,0:T(8,128)(2,1)S(1)} %copy-done.28), channel_id=1, source_target_pairs={{0,4},{4,0},{8,12},{12,8},{16,20},{20,16},{24,28},{28,24},{1,5},{5... | collective-permute-start | bytes 393224 | tf_op jit(solution)/shard_map/ppermute | solution.py:23
  116.1 7.8 %collective-permute-start.34 = (bf16[1,128,512]{2,1,0:T(8,128)(2,1)}, bf16[1,128,512]{2,1,0:T(8,128)(2,1)S(1)}, u32[]{:S(2)}, u32[]{:S(2)}) collective-permute-start(bf16[1,128,512]{2,1,0:T(8,128)(2,1)} %collective-permute-done.22.refs_0_), channel_id=1, source_target_pairs={{0,4},{4,0},{8,12},{12,8},{16,20},{20,16},{24,28},{28,24},{1,5},{5... | collective-permute-start | bytes 393224 | tf_op jit(solution)/shard_map/ppermute | solution.py:23
  116.4 14.0 %collective-permute-start.41 = (bf16[2,128,512]{2,1,0:T(8,128)(2,1)}, bf16[2,128,512]{2,1,0:T(8,128)(2,1)S(1)}, u32[]{:S(2)}, u32[]{:S(2)}) collective-permute-start(bf16[2,128,512]{2,1,0:T(8,128)(2,1)} %collective-permute-done.33.refs_2_), channel_id=1, source_target_pairs={{0,16},{4,20},{8,24},{12,28},{16,0},{20,4},{24,8},{28,12},{1,17},{... | collective-permute-start | bytes 786440 | tf_op jit(solution)/shard_map/ppermute | solution.py:36
  117.9 3.4 %copy-start.2 = (bf16[2,1024,2048]{2,1,0:T(8,128)(2,1)S(1)}, bf16[2,1024,2048]{2,1,0:T(8,128)(2,1)}, u32[]{:S(2)}) copy-start(bf16[2,1024,2048]{2,1,0:T(8,128)(2,1)} %copy-done) | copy-start | bytes 25165828
  123.9 3.7 %slice-start = ((s8[8388608]{0:T(1024)(128)(4,1)}), s8[4194304]{0:T(1024)(128)(4,1)S(1)}, s32[]{:S(2)}) async-start(s8[8388608]{0:T(1024)(128)(4,1)} %bitcast.77), calls=%async_computation | async-start | bytes 8388608
  124.0 3.9 %slice-start.1 = ((s8[8388608]{0:T(1024)(128)(4,1)}), s8[4194304]{0:T(1024)(128)(4,1)S(1)}, s32[]{:S(2)}) async-start(s8[8388608]{0:T(1024)(128)(4,1)} %bitcast.77), calls=%async_computation.1 | async-start | bytes 8388608
  126.1 4.3 %collective-permute-start.40 = (bf16[2,128,512]{2,1,0:T(8,128)(2,1)}, bf16[2,128,512]{2,1,0:T(8,128)(2,1)S(1)}, u32[]{:S(2)}, u32[]{:S(2)}) collective-permute-start(bf16[2,128,512]{2,1,0:T(8,128)(2,1)} %collective-permute-done.33.refs_2_), channel_id=1, source_target_pairs={{0,4},{4,0},{8,12},{12,8},{16,20},{20,16},{24,28},{28,24},{1,5},{5... | collective-permute-start | bytes 786440 | tf_op jit(solution)/shard_map/ppermute | solution.py:23
  126.3 4.0 %collective-permute-start.39 = (bf16[1,128,512]{2,1,0:T(8,128)(2,1)S(1)}, bf16[1,128,512]{2,1,0:T(8,128)(2,1)S(1)}, u32[]{:S(2)}, u32[]{:S(2)}) collective-permute-start(bf16[1,128,512]{2,1,0:T(8,128)(2,1)S(1)} %copy-done.32), channel_id=1, source_target_pairs={{0,4},{4,0},{8,12},{12,8},{16,20},{20,16},{24,28},{28,24},{1,5},{5... | collective-permute-start | bytes 393224 | tf_op jit(solution)/shard_map/ppermute | solution.py:23
  126.7 3.7 %collective-permute-start.38 = (bf16[1,128,512]{2,1,0:T(8,128)(2,1)S(1)}, bf16[1,128,512]{2,1,0:T(8,128)(2,1)S(1)}, u32[]{:S(2)}, u32[]{:S(2)}) collective-permute-start(bf16[1,128,512]{2,1,0:T(8,128)(2,1)S(1)} %copy-done.30), channel_id=1, source_target_pairs={{0,4},{4,0},{8,12},{12,8},{16,20},{20,16},{24,28},{28,24},{1,5},{5... | collective-permute-start | bytes 393224 | tf_op jit(solution)/shard_map/ppermute | solution.py:23
  126.9 5.8 %collective-permute-start.43 = (bf16[1,128,512]{2,1,0:T(8,128)(2,1)S(1)}, bf16[1,128,512]{2,1,0:T(8,128)(2,1)S(1)}, u32[]{:S(2)}, u32[]{:S(2)}) collective-permute-start(bf16[1,128,512]{2,1,0:T(8,128)(2,1)S(1)} %copy-done.28), channel_id=1, source_target_pairs={{0,8},{4,12},{8,0},{12,4},{16,24},{20,28},{24,16},{28,20},{1,9},{5... | collective-permute-start | bytes 393224 | tf_op jit(solution)/shard_map/ppermute | solution.py:23
  132.4 3.3 %collective-permute-start.45 = (bf16[2,128,512]{2,1,0:T(8,128)(2,1)S(1)}, bf16[2,128,512]{2,1,0:T(8,128)(2,1)S(1)}, u32[]{:S(2)}, u32[]{:S(2)}) collective-permute-start(bf16[2,128,512]{2,1,0:T(8,128)(2,1)S(1)} %collective-permute-done.41.refs_2_), channel_id=1, source_target_pairs={{0,4},{4,0},{8,12},{12,8},{16,20},{20,16},{24,28},{28,24},{1,5},{5... | collective-permute-start | bytes 786440 | tf_op jit(solution)/shard_map/ppermute | solution.py:23
  132.7 3.0 %collective-permute-start.44 = (bf16[1,128,512]{2,1,0:T(8,128)(2,1)S(1)}, bf16[1,128,512]{2,1,0:T(8,128)(2,1)S(1)}, u32[]{:S(2)}, u32[]{:S(2)}) collective-permute-start(bf16[1,128,512]{2,1,0:T(8,128)(2,1)S(1)} %collective-permute-done.43.refs_1_), channel_id=1, source_target_pairs={{0,4},{4,0},{8,12},{12,8},{16,20},{20,16},{24,28},{28,24},{1,5},{5... | collective-permute-start | bytes 393224 | tf_op jit(solution)/shard_map/ppermute | solution.py:23
  133.1 2.7 %collective-permute-start.42 = (bf16[1,128,512]{2,1,0:T(8,128)(2,1)S(1)}, bf16[1,128,512]{2,1,0:T(8,128)(2,1)S(1)}, u32[]{:S(2)}, u32[]{:S(2)}) collective-permute-start(bf16[1,128,512]{2,1,0:T(8,128)(2,1)S(1)} %copy-done.26), channel_id=1, source_target_pairs={{0,4},{4,0},{8,12},{12,8},{16,20},{20,16},{24,28},{28,24},{1,5},{5... | collective-permute-start | bytes 393224 | tf_op jit(solution)/shard_map/ppermute | solution.py:23
  (22 other events, 42.6 us)
where the time goes:
time: 144 us; the launch traced here: 143 us
  starting transfers between devices  46.3 us (32%)
  Pallas kernels  43.1 us (30%)
  local copies, waits for them, and re-layouts  25.2 us (18%)
  waiting for transfers between devices  23.3 us (16%)
  other arithmetic  3.53 us (2%)
  between operations  1.73 us (1%)
    unnamed x80, local copies, waits for them, and re-layouts  25.1 us
    pallas_call x8, Pallas kernels, backward_piece(): pl.pallas_call(kernel, in_specs=[in_smem] + [in_vmem] * (len(grads) + 2)...  18.5 us
    ppermute x30, starting transfers between devices, over_members(): return lax.ppermute(value, 'layer', pairs)  17.4 us
    ppermute x9, starting transfers between devices, over_feat(): return lax.ppermute(value, 'feat', pairs)  12.2 us
    ppermute x30, waiting for transfers between devices, over_members(): return lax.ppermute(value, 'layer', pairs)  11.7 us
    ppermute x3, starting transfers between devices, to_layer(): return lax.ppermute(value, 'layer', pairs)  9.5 us
    pallas_call x2, Pallas kernels, fetch(): pl.pallas_call(kernel, in_specs=[in_hbm] * len(arrays), out_specs=[in_vme...  8.27 us
    ppermute x9, waiting for transfers between devices, over_feat(): return lax.ppermute(value, 'feat', pairs)  8.15 us
  transfers between devices with their start and end apart: 46, of which 10 were waited for; matrix products, arithmetic and copies ran while one was open for 2% of the time, Pallas kernels for 23%

commit v1 on v0

--- a/solution.py
+++ b/solution.py
@@ -23,11 +23,11 @@
     return lax.ppermute(value, "layer", pairs)
 
 
-def to_layer(value, offset, sub_count):
+def to_layer(value, offset, sub_count, real):
     count = lax.axis_size("layer")
-    shift = offset * sub_count
-    pairs = [(p, p + shift) for p in range(count - shift)]
-    return lax.ppermute(value, "layer", pairs)
+    pairs = [(p, (p + offset * sub_count) % count) for p in range(count)]
+    moved = lax.ppermute(value, "layer", pairs)
+    return jnp.where(real[offset], moved, jnp.zeros_like(moved))
 
 
 def from_layer(value, offset, sub_count):
@@ -43,7 +43,7 @@
 def all_over_feat(value):
     blocks = [value, over_feat(value, 1)]
     for s in range(2, lax.axis_size("feat")):
-        blocks.append(over_feat(after(value, blocks[1]) if s > 2 else value, s))
+        blocks.append(over_feat(value, s))
     return blocks
 
 
@@ -95,20 +95,20 @@
     )(*arrays)
 
 
-def encode(indices, pieces, weights, partial, bias):
+def encode(info, rels, pieces, weights, partial, bias):
     feat_count, rows, cols = pieces[0].shape
     tok = feat_count * rows
     width = weights.shape[1]
     extra = [value for value in (partial, bias) if value is not None]
 
-    def kernel(index_ref, *refs):
+    def kernel(info_ref, *refs):
         piece_refs, weight_ref = refs[: len(pieces)], refs[len(pieces)]
         extra_refs, out_ref = refs[len(pieces) + 1 : -1], refs[-1]
         left = jnp.concatenate([ref[...].reshape(tok, cols) for ref in piece_refs], 1)
         for start in range(0, width, tile):
             here = slice(start, start + tile)
             right = jnp.concatenate(
-                [weight_ref[span(index_ref[i], cols), here] for i in range(len(pieces))], 0
+                [weight_ref[span(info_ref[0] ^ rel, cols), here] for rel in rels], 0
             )
             total = dot(left, right, (1, 0))
             if partial is not None:
@@ -133,39 +133,48 @@
         **params(
             2 * len(pieces) * tok * cols * width, 2 * len(pieces) * cols * (tok + width), 4
         ),
-    )(indices, *pieces, weights, *extra)
-
-
-def decode(indices, features, weights, offset, groups, rows, cols):
+    )(info, *pieces, weights, *extra)
+
+
+def decode(info, features, weights, offset, groups, rows, cols):
     _, tok, width = features.shape
-    count = indices.shape[0]
-
-    def kernel(index_ref, feat_ref, weight_ref, *out_refs):
+    count = weights.shape[2] // cols // 2
+
+    def kernel(info_ref, feat_ref, weight_ref, *out_refs):
         left = feat_ref[0]
-        for piece in range(count):
+        even = info_ref[0] % 2 == 0
+        for pair in range(count):
+            piece = pair ^ (info_ref[0] // 2)
             for start in range(0, cols, tile):
-                columns = pl.ds(pl.multiple_of(index_ref[piece] * cols + start, tile), tile)
-                product = dot(left, weight_ref[offset, :, columns], (1, 0)).astype(jnp.bfloat16)
-                for group, out_ref in zip(groups, out_refs):
-                    for place, block in enumerate(group):
-                        out_ref[piece, place, :, start : start + tile] = product[
-                            block * rows : (block + 1) * rows
-                        ]
-
-    return pl.pallas_call(
+                low, high = (
+                    dot(left, weight_ref[offset, :, base + start : base + start + tile], (1, 0)).astype(
+                        jnp.bfloat16
+                    )
+                    for base in (2 * pair * cols, (2 * pair + 1) * cols)
+                )
+                sides = (jnp.where(even, high, low), jnp.where(even, low, high))
+                for side, product in enumerate(sides):
+                    for number, group in enumerate(groups):
+                        for place, block in enumerate(group):
+                            out_refs[side * len(groups) + number][
+                                piece, place, :, start : start + tile
+                            ] = product[block * rows : (block + 1) * rows]
+    out_shape = [
+        jax.ShapeDtypeStruct((count, len(group), rows, cols), jnp.bfloat16) for group in groups
+    ] * 2
+    result = pl.pallas_call(
         kernel,
         in_specs=[in_smem, in_vmem, in_vmem],
-        out_specs=[in_vmem] * len(groups),
-        out_shape=[
-            jax.ShapeDtypeStruct((count, len(group), rows, cols), jnp.bfloat16) for group in groups
-        ],
+        out_specs=[in_vmem] * len(out_shape),
+        out_shape=out_shape,
         name="decode",
-        **params(2 * count * tok * cols * width, 2 * count * cols * width, 4),
-    )(indices, features, weights)
-
-
-def turned(value):
-    count, tok, width = value.shape
+        **params(4 * count * tok * cols * width, 4 * count * cols * width, 4),
+    )(info, features, weights)
+    return result[: len(groups)], result[len(groups) :]
+
+
+def turned(value, count):
+    _, tok, width = value.shape
 
     def kernel(in_ref, out_ref):
         for piece in range(count):
@@ -190,18 +199,19 @@
     return values[0]
 
 
-def backward_piece(info, offset, grads, turned_features, dec_weight, feature_grad, dec_grad):
+def backward_pair(info, rel, offset, own, other, turned_features, dec_weight, feature_grad, dec_grad):
     layers, width, depth = dec_weight.shape
     tok = turned_features.shape[1]
-    cols = grads[0].shape[2]
+    cols = own[0].shape[2]
     first = feature_grad is None
     extra = [] if first else [feature_grad, dec_grad]
+    inputs = [*own, *other]
 
     def kernel(info_ref, *refs):
-        grad_refs = refs[: len(grads)]
-        feat_ref, weight_ref = refs[len(grads) : len(grads) + 2]
+        grad_refs = refs[: len(inputs)]
+        feat_ref, weight_ref = refs[len(inputs) : len(inputs) + 2]
         out_ref, dec_ref, square_ref, held, sems = refs[-5:]
-        columns = span(info_ref[0], cols)
+        columns = span((info_ref[0] ^ rel) // 2, 2 * cols)
         starts = range(0, width, tile)
         copies = [
             pltpu.make_async_copy(
@@ -211,19 +221,26 @@
             )
             for place, start in enumerate(starts)
         ]
-        blocks = [ref[i] for ref in grad_refs for i in range(ref.shape[0])]
-        sums = []
-        for block in blocks:
-            total = jnp.zeros((8, 128), jnp.float32)
-            for row in range(0, block.shape[0], 8):
-                for col in range(0, cols, 128):
-                    part = block[row : row + 8, col : col + 128].astype(jnp.float32)
-                    total += part * part
-            sums.append(total)
+        sides, sums = [], []
+        for side in (grad_refs[: len(own)], grad_refs[len(own) :]):
+            blocks = [ref[i] for ref in side for i in range(ref.shape[0])]
+            totals = []
+            for block in blocks:
+                total = jnp.zeros((8, 128), jnp.float32)
+                for row in range(0, block.shape[0], 8):
+                    for col in range(0, cols, 128):
+                        part = block[row : row + 8, col : col + 128].astype(jnp.float32)
+                        total += part * part
+                totals.append(total)
+            sums.append(tree_sum(totals))
+            sides.append(jnp.concatenate(blocks, 0))
         square_ref[...] = tree_sum(sums)
 
         def products():
-            grad = jnp.concatenate(blocks, 0)
+            second = info_ref[0] % 2 > 0
+            grad = jnp.concatenate(
+                [jnp.where(second, sides[1], sides[0]), jnp.where(second, sides[0], sides[1])], 1
+            )
             for copy, start in zip(copies, starts):
                 here = slice(start, start + tile)
                 held[here] = dot(feat_ref[here], grad, (1, 0)).astype(jnp.bfloat16)
@@ -232,27 +249,27 @@
                 here = slice(start, start + tile)
                 product = dot(grad, weight_ref[offset, here, columns], (1, 1))
                 if not first:
-                    product += refs[len(grads) + 2][:, here]
+                    product += refs[len(inputs) + 2][:, here]
                 out_ref[:, here] = product
 
         def nothing():
             held[...] = jnp.zeros_like(held)
             for copy in copies:
                 copy.start()
-            out_ref[...] = refs[len(grads) + 2][...]
+            out_ref[...] = refs[len(inputs) + 2][...]
 
         if offset == 0:
             products()
         else:
-            pl.when(info_ref[1] > 0)(products)
-            pl.when(info_ref[1] == 0)(nothing)
+            pl.when(info_ref[1] >= offset)(products)
+            pl.when(info_ref[1] < offset)(nothing)
         for copy in copies:
             copy.wait()
 
     return pl.pallas_call(
         kernel,
         in_specs=[in_smem]
-        + [in_vmem] * (len(grads) + 2)
+        + [in_vmem] * (len(inputs) + 2)
         + ([] if first else [in_vmem, in_hbm]),
         out_specs=[in_vmem, in_hbm, in_vmem],
         out_shape=[
@@ -261,21 +278,21 @@
             jax.ShapeDtypeStruct((8, 128), jnp.float32),
         ],
         scratch_shapes=[
-            pltpu.VMEM((width, cols), jnp.bfloat16),
+            pltpu.VMEM((width, 2 * cols), jnp.bfloat16),
             pltpu.SemaphoreType.DMA((width // tile,)),
         ],
-        input_output_aliases={} if first else {len(grads) + 3: 0, len(grads) + 4: 1},
-        name="backward_piece",
-        **params(tok * cols, tok * cols, 6),
-    )(info, *grads, turned_features, dec_weight, *extra)
-
-
-def encoder_grad(indices, turned_tokens, features, feature_grad, squares, scale):
+        input_output_aliases={} if first else {len(inputs) + 3: 0, len(inputs) + 4: 1},
+        name="backward_pair",
+        **params(tok * cols, tok * cols, 8),
+    )(info, *inputs, turned_features, dec_weight, *extra)
+
+
+def encoder_grad(info, rels, turned_tokens, features, feature_grad, squares, scale):
     count, cols, tok = turned_tokens[0].shape
     width = features.shape[2]
     pieces = len(turned_tokens) * count
 
-    def kernel(index_ref, *refs):
+    def kernel(info_ref, *refs):
         token_refs = refs[: len(turned_tokens)]
         mask_ref, grad_ref = refs[len(turned_tokens) : len(turned_tokens) + 2]
         square_refs = refs[len(turned_tokens) + 2 : -6]
@@ -294,7 +311,7 @@
                 token_refs[piece // count][piece % count], preact[...], (1, 0)
             ).astype(jnp.bfloat16)
             copy = pltpu.make_async_copy(
-                held.at[piece], enc_ref.at[span(index_ref[piece], cols)], sems.at[piece]
+                held.at[piece], enc_ref.at[span(info_ref[0] ^ rels[piece], cols)], sems.at[piece]
             )
             copy.start()
             copies.append(copy)
@@ -319,7 +336,7 @@
         **params(
             2 * pieces * tok * cols * width, 2 * pieces * cols * (tok + width) + 6 * tok * width, 10
         ),
-    )(indices, *turned_tokens, features, feature_grad, *squares)
+    )(info, *turned_tokens, features, feature_grad, *squares)
 
 
 def add_pair(left, right):
@@ -330,14 +347,17 @@
     layers, width, depth = dec_weight.shape
     feat_count = lax.axis_size("feat")
     sub_count = lax.axis_size("layer") // layers
-    member = lax.axis_index("layer") % sub_count
+    position = lax.axis_index("layer")
+    layer = position // sub_count
     rows, cols = tokens_in.shape
     tok = feat_count * rows
     bit_count = sub_count.bit_length() - 1
-    near = member ^ (2 * jnp.arange(sub_count // 2, dtype=jnp.int32))
-    far = near ^ 1
-    groups = [list(range(feat_count // 2)), list(range(feat_count // 2, feat_count))]
-
+    groups = [list(range(feat_count // 2))]
+    groups += [[s] for s in range(feat_count // 2, feat_count)]
+
+    info = jnp.stack([position % sub_count, layers - 1 - layer]).astype(jnp.int32)
+    real = [layer >= k for k in range(layers)]
+    tokens_in, info, *real = lax.optimization_barrier((tokens_in, info, *real))
     enc_weight = pltpu.with_memory_space_constraint(enc_weight, pltpu.HBM)
     dec_weight = pltpu.with_memory_space_constraint(dec_weight, pltpu.HBM)
 
@@ -356,21 +376,17 @@
     early = [held[rel][s] for rel in order[2::2] for s in range(2)]
     tokens = {0: after(jnp.stack(held[0], 0), enc_held, *early)}
     tokens[1] = over_members(tokens[0], 0)
-    index = {rel: (member ^ rel).reshape(1) for rel in order}
-    partial = encode(
-        jnp.concatenate([index[0], index[1]]), [tokens[0], tokens[1]], enc_held, None, None
-    )
+    partial = encode(info, [0, 1], [tokens[0], tokens[1]], enc_held, None, None)
     for rel in order[2::2]:
         tokens[rel] = jnp.stack([after(block, partial) for block in held[rel]], 0)
         tokens[rel ^ 1] = over_members(tokens[rel], 0)
     for rel in order[2:-1]:
-        partial = encode(index[rel], [tokens[rel]], enc_held, partial, None)
-    features = encode(index[order[-1]], [tokens[order[-1]]], enc_held, partial, enc_bias[None])
+        partial = encode(info, [rel], [tokens[rel]], enc_held, partial, None)
+    features = encode(info, order[-1:], [tokens[order[-1]]], enc_held, partial, enc_bias[None])
 
     current, source = {}, features
     for k in reversed(range(layers)):
-        sent = decode(far, source, dec_held, k, groups, rows, cols)
-        kept = decode(near, source, dec_held, k, groups, rows, cols)
+        sent, kept = decode(info, source, dec_held, k, groups, rows, cols)
         for place in reversed(range(len(groups))):
             current[place, k] = add_pair(kept[place], over_members(sent[place], 0))
         source = after(features, current[len(groups) - 1, k])
@@ -384,7 +400,7 @@
         if bit_level == bit_count - 1:
             for k in range(1, layers):
                 joined[k], sent = halves.pop((0, k))
-                sent = to_layer(sent, k, sub_count)
+                sent = to_layer(after(sent, halves[len(groups) - 1, 0][1]), k, sub_count, real)
                 halves[0, 0] = (halves[0, 0][0], add_pair(halves[0, 0][1], sent))
         turns = [turn for turn in turns if turn in halves]
         received, operands = [], []
@@ -405,9 +421,9 @@
         total = sum(part.astype(jnp.float32) for part in current[place, 0])
         for k in range(1, layers):
             if place > 0:
-                moved = to_layer(add_pair(*current[place, k]), k, sub_count)
+                moved = to_layer(add_pair(*current[place, k]), k, sub_count, real)
             else:
-                moved = to_layer(after(joined[k], *operands), k, sub_count)
+                moved = to_layer(after(joined[k], *operands), k, sub_count, real)
             total = total + moved.astype(jnp.float32)
         for spot, block in enumerate(groups[place]):
             if block == 0:
@@ -417,16 +433,13 @@
                 blocks[block] = over_feat(operands[-1], block)
     for block in reversed(blocks[1:]):
         rebuilt = rebuilt + block.astype(jnp.float32)
-    turned_features = turned(source[:1])[0]
+    turned_features = turned(source, 1)[0]
     turned_tokens = [
-        turned(after(tokens[rel], turned_features).reshape(1, tok, cols)) for rel in order
+        turned(after(tokens[rel], turned_features).reshape(1, tok, cols), 1) for rel in order
     ]
-    (dec_held,) = fetch(after(dec_weight, turned_features))
-    recon_error = rebuilt - after(targets, dec_held, *turned_tokens).astype(jnp.float32)
+    recon_error = rebuilt - after(targets, turned_features, *turned_tokens).astype(jnp.float32)
     scaled = (loss_scale / tok * recon_error).astype(jnp.bfloat16)
 
-    layer = lax.axis_index("layer") // sub_count
-    there = [(layer + k < layers).astype(jnp.int32) for k in range(layers)]
     blocks = all_over_feat(scaled)
     stages = [[0]]
     for level in range(bit_count - 1, 0, -1):
@@ -437,7 +450,7 @@
     groups_of = {(0, k): [None] * len(spans) for k in range(layers)}
     early, last = [], len(spans) - 1
     for place, group in enumerate(spans):
-        stacked = jnp.stack([after(blocks[s], *early) for s in group], 0)
+        stacked = jnp.stack([blocks[s] for s in group], 0)
         groups_of[0, 0][place] = stacked
         for k in range(1, layers):
             groups_of[0, k][place] = from_layer(stacked, k, sub_count)
@@ -459,30 +472,32 @@
     feature_grad, dec_grad, squares = None, None, {}
     for number, stage in enumerate(stages):
         for k in range(layers):
-            if k > 0 and number + 1 < len(stages):
-                guard = [part for rel in stages[number + 1] for part in groups_of[rel, k - 1]]
-                feature_grad = after(feature_grad, *guard)
             for rel in stage:
                 parts = groups_of[rel, k]
-                if feature_grad is not None:
+                if feature_grad is None:
+                    parts = [after(parts[0], *early)] + parts[1:]
+                else:
                     parts = [after(part, feature_grad) for part in parts]
-                groups_of[rel ^ 1, k] = [over_members(part, 0) for part in parts]
-                for half in (rel, rel ^ 1):
-                    if k == 0 and number > 0:
-                        coming = groups_of[rel, layers - 1][-(half % 2)]
-                        feature_grad = after(feature_grad, coming)
-                    feature_grad, dec_grad, squares[k, half] = backward_piece(
-                        jnp.stack([member ^ half, there[k]]),
-                        k,
-                        groups_of[half, k],
-                        turned_features,
-                        dec_held,
-                        feature_grad,
-                        dec_grad,
-                    )
+                if k == 0 and number > 0:
+                    feature_grad = after(feature_grad, groups_of[rel, layers - 1][-1])
+                elif k > 0 and number + 1 < len(stages):
+                    coming = [groups_of[other, k - 1][-1] for other in stages[number + 1]]
+                    feature_grad = after(feature_grad, *coming)
+                feature_grad, dec_grad, squares[k, rel] = backward_pair(
+                    info,
+                    rel,
+                    k,
+                    parts,
+                    [over_members(part, 0) for part in parts],
+                    turned_features,
+                    dec_held,
+                    feature_grad,
+                    dec_grad,
+                )
     scale = (tok / loss_scale) ** 2 / (layers * tok * depth)
     enc_grad, bias_grad, mean_square = encoder_grad(
-        jnp.stack([member ^ rel for rel in order]),
+        info,
+        order,
         turned_tokens,
         features,
         feature_grad,

time: 144 us -> 116 us (0.81)
  local copies, waits for them, and re-layouts: 25.2 us -> 0.11 us
  waiting for transfers between devices: 23.3 us -> 34.3 us
  Pallas kernels: 43.1 us -> 34.4 us
  starting transfers between devices: 46.3 us -> 44.2 us
  other arithmetic: 3.53 us -> 1.97 us
    unnamed x80 -> x6, local copies, waits for them, and re-layouts: 25.1 us -> 0.02 us
    ppermute x9, waiting for transfers between devices: 8.15 us -> 14.3 us  [over_feat(): return lax.ppermute(value, 'feat', pairs)]
    pallas_call x8 -> x4, Pallas kernels: 18.5 us -> 13.6 us  [backward_pair(): pl.pallas_call(kernel, in_specs=[in_smem] + [in_vmem] * (len(inputs) + 2)...]
    ppermute x4, waiting for transfers between devices: 0.01 us -> 4.15 us  [from_layer(): return lax.ppermute(value, 'layer', pairs)]
    ppermute x30 -> x34, starting transfers between devices: 17.4 us -> 21.5 us  [over_members(): return lax.ppermute(value, 'layer', pairs)]
    pallas_call x2 -> x1, Pallas kernels: 8.27 us -> 4.74 us  [fetch(): pl.pallas_call(kernel, in_specs=[in_hbm] * len(arrays), out_specs=[in_vme...]
    ppermute x3 -> x4, starting transfers between devices: 9.5 us -> 6.28 us  [to_layer(): moved = lax.ppermute(value, 'layer', pairs)]
    ppermute x4, starting transfers between devices: 7.08 us -> 4.62 us  [from_layer(): return lax.ppermute(value, 'layer', pairs)]
  transfers between devices with their start and end apart: 46 -> 51, of which waited for: 10 -> 20; matrix products, arithmetic and copies ran while one was open for 2% -> 1% of each run, Pallas kernels for 23% -> 19%
where the time goes in v1:
time: 116 us
  starting transfers between devices  44.2 us (38%)
  Pallas kernels  34.4 us (30%)
  waiting for transfers between devices  34.3 us (30%)
  other arithmetic  1.97 us (2%)
  between operations  1.22 us (1%)
    ppermute x34, starting transfers between devices, over_members(): return lax.ppermute(value, 'layer', pairs)  21.5 us
    ppermute x9, waiting for transfers between devices, over_feat(): return lax.ppermute(value, 'feat', pairs)  14.3 us
    pallas_call x4, Pallas kernels, backward_pair(): pl.pallas_call(kernel, in_specs=[in_smem] + [in_vmem] * (len(inputs) + 2)...  13.6 us
    ppermute x34, waiting for transfers between devices, over_members(): return lax.ppermute(value, 'layer', pairs)  12.5 us
    ppermute x9, starting transfers between devices, over_feat(): return lax.ppermute(value, 'feat', pairs)  11.8 us
    ppermute x4, starting transfers between devices, to_layer(): moved = lax.ppermute(value, 'layer', pairs)  6.28 us
    pallas_call x2, Pallas kernels, decode(): pl.pallas_call(kernel, in_specs=[in_smem, in_vmem, in_vmem], out_specs=[i...  5.79 us
    pallas_call x1, Pallas kernels, fetch(): pl.pallas_call(kernel, in_specs=[in_hbm] * len(arrays), out_specs=[in_vme...  4.74 us
  transfers between devices with their start and end apart: 51, of which 20 were waited for; matrix products, arithmetic and copies ran while one was open for 1% of the time, Pallas kernels for 19%

profile of v1, /device:TPU:0, one launch (start us, length us, event | category | flops | bytes accessed | tf_op | source)
XLA Modules:
  0.0 116.2 jit_solution(16205271543085642786)
XLA Ops:
  0.7 3.0 %collective-permute-start.1 = (bf16[128,512]{1,0:T(8,128)(2,1)}, bf16[128,512]{1,0:T(8,128)(2,1)S(1)}, u32[]{:S(2)}, u32[]{:S(2)}) collective-permute-start(bf16[128,512]{1,0:T(8,128)(2,1)} %param.5), channel_id=1, source_target_pairs={{0,1},{1,0},{2,3},{3,2},{4,5},{5,4},{6,7},{7,6},{8,9},{9,8},{10,11... | collective-permute-start | bytes 393224 | tf_op jit(solution)/shard_map/ppermute | solution.py:17
  3.8 2.5 %collective-permute-start.3 = (bf16[128,512]{1,0:T(8,128)(2,1)}, bf16[128,512]{1,0:T(8,128)(2,1)S(1)}, u32[]{:S(2)}, u32[]{:S(2)}) collective-permute-start(bf16[128,512]{1,0:T(8,128)(2,1)} %param.5), channel_id=1, source_target_pairs={{0,3},{1,2},{2,1},{3,0},{4,7},{5,6},{6,5},{7,4},{8,11},{9,10},{10,... | collective-permute-start | bytes 393224 | tf_op jit(solution)/shard_map/ppermute | solution.py:17
  6.4 1.5 %collective-permute-start = (bf16[128,512]{1,0:T(8,128)(2,1)}, bf16[128,512]{1,0:T(8,128)(2,1)S(1)}, u32[]{:S(2)}, u32[]{:S(2)}) collective-permute-start(bf16[128,512]{1,0:T(8,128)(2,1)} %param.5), channel_id=1, source_target_pairs={{0,8},{4,12},{8,0},{12,4},{16,24},{20,28},{24,16},{28,20},{1,9},{5... | collective-permute-start | bytes 393224 | tf_op jit(solution)/shard_map/ppermute | solution.py:23
  7.9 1.3 %collective-permute-start.4 = (bf16[128,512]{1,0:T(8,128)(2,1)S(1)}, bf16[128,512]{1,0:T(8,128)(2,1)S(1)}, u32[]{:S(2)}, u32[]{:S(2)}) collective-permute-start(bf16[128,512]{1,0:T(8,128)(2,1)S(1)} %collective-permute-done.1), channel_id=1, source_target_pairs={{0,8},{4,12},{8,0},{12,4},{16,24},{20,28},{24,16},{28,20},{1,9},{5... | collective-permute-start | bytes 393224 | tf_op jit(solution)/shard_map/ppermute | solution.py:23
  9.1 4.7 %fetch.1 = (bf16[2048,1024]{1,0:T(8,128)(2,1)S(1)}, bf16[2,1024,2048]{2,1,0:T(8,128)(2,1)S(1)}) custom-call(bf16[2048,1024]{1,0:T(8,128)(2,1)} %refs_0_.1, bf16[2,1024,2048]{2,1,0:T(8,128)(2,1)} %refs_1_), custom_call_target="tpu_custom_call" | custom-call | bytes 12582912 | tf_op jit(solution)/shard_map/fetch/pallas_call | solution.py:87
  13.9 4.3 %collective-permute-done.2 = bf16[128,512]{1,0:T(8,128)(2,1)S(1)} collective-permute-done((bf16[128,512]{1,0:T(8,128)(2,1)}, bf16[128,512]{1,0:T(8,128)(2,1)S(1)}, u32[]{:S(2)}, u32[]{:S(2)}) %collective-permute-start.2) | collective-permute-done | bytes 131104 | tf_op jit(solution)/shard_map/ppermute | solution.py:17
  18.4 1.6 %collective-permute-start.7 = (bf16[128,512]{1,0:T(8,128)(2,1)S(1)}, bf16[128,512]{1,0:T(8,128)(2,1)S(1)}, u32[]{:S(2)}, u32[]{:S(2)}) collective-permute-start(bf16[128,512]{1,0:T(8,128)(2,1)S(1)} %collective-permute-done.3), channel_id=1, source_target_pairs={{0,8},{4,12},{8,0},{12,4},{16,24},{20,28},{24,16},{28,20},{1,9},{5... | collective-permute-start | bytes 393224 | tf_op jit(solution)/shard_map/ppermute | solution.py:23
  20.0 0.5 collective-permute-start.6
  20.5 1.8 %encode.3.refs_2_ = f32[512,1024]{1,0:T(8,128)S(1)} custom-call(s32[2]{0:T(128)S(1)} %pad_add_fusion.info_ref, bf16[4,128,512]{2,1,0:T(8,128)(2,1)S(1)} %pad_maximum_fusion.refs_0_, bf16[4,128,512]{2,1,0:T(8,128)(2,1)S(1)} %collective-permute-done.5.refs_1_, bf16[2048,1024]{1,0:T(8,128)(2,1)S(1)} %get-tuple-element.74.refs_2_.refs_1_), custom_call_target="tpu_custom_call" | custom-call | flops 1073741824 | bytes 3145728 | tf_op jit(solution)/shard_map/encode/pallas_call | solution.py:127
  22.3 2.5 %collective-permute-done.7 = bf16[128,512]{1,0:T(8,128)(2,1)S(1)} collective-permute-done((bf16[128,512]{1,0:T(8,128)(2,1)S(1)}, bf16[128,512]{1,0:T(8,128)(2,1)S(1)}, u32[]{:S(2)}, u32[]{:S(2)}) %collective-permute-start.7) | collective-permute-done | bytes 131104 | tf_op jit(solution)/shard_map/ppermute | solution.py:23
  24.8 2.4 %collective-permute-done.6 = bf16[128,512]{1,0:T(8,128)(2,1)S(1)} collective-permute-done((bf16[128,512]{1,0:T(8,128)(2,1)S(1)}, bf16[128,512]{1,0:T(8,128)(2,1)S(1)}, u32[]{:S(2)}, u32[]{:S(2)}) %collective-permute-start.6) | collective-permute-done | bytes 131104 | tf_op jit(solution)/shard_map/ppermute | solution.py:23
  27.3 1.3 %encode.4.refs_2_ = f32[512,1024]{1,0:T(8,128)S(1)} custom-call(s32[2]{0:T(128)S(1)} %pad_add_fusion.info_ref, bf16[4,128,512]{2,1,0:T(8,128)(2,1)S(1)} %pad_maximum_fusion.1.refs_0_, bf16[2048,1024]{1,0:T(8,128)(2,1)S(1)} %get-tuple-element.74.refs_2_.refs_1_, f32[512,1024]{1,0:T(8,128)S(1)} %encode.3.refs_2_), custom_call_target="tpu_custom_call" | custom-call | flops 536870912 | bytes 1572864 | tf_op jit(solution)/shard_map/encode/pallas_call | solution.py:127
  28.6 0.6 collective-permute-done.8.refs_0_
  29.2 1.4 %encode.5.feat_ref.in_ref.refs_4_ = bf16[2,512,1024]{2,1,0:T(8,128)(2,1)S(1)} custom-call(s32[2]{0:T(128)S(1)} %pad_add_fusion.info_ref, bf16[4,128,512]{2,1,0:T(8,128)(2,1)S(1)} %collective-permute-done.8.refs_0_, bf16[2048,1024]{1,0:T(8,128)(2,1)S(1)} %get-tuple-element.74.refs_2_.refs_1_, f32[512,1024]{1,0:T(8,128)S(1)} %encode.4.refs_2_, ...), custom_call_target="tpu_custom_call" | custom-call | flops 536870912 | bytes 1572864 | tf_op jit(solution)/shard_map/encode/pallas_call | solution.py:127
  30.6 2.9 %decode.2 = (bf16[2,2,128,512]{3,2,1,0:T(8,128)(2,1)S(1)}, bf16[2,1,128,512]{3,2,1,0:T(8,128)(2,1)S(1)}, bf16[2,1,128,512]{3,2,1,0:T(8,128)(2,1)S(1)}, bf16[2,2,...) custom-call(s32[2]{0:T(128)S(1)} %pad_add_fusion.info_ref, ...), custom_call_target="tpu_custom_call" | custom-call | flops 2147483648 | bytes 4194304 | tf_op jit(solution)/shard_map/decode/pallas_call | solution.py:165
  33.7 0.4 collective-permute-start.11
  34.3 0.9 collective-permute-done.9
  35.2 2.9 %decode.3 = (bf16[2,2,128,512]{3,2,1,0:T(8,128)(2,1)S(1)}, bf16[2,1,128,512]{3,2,1,0:T(8,128)(2,1)S(1)}, bf16[2,1,128,512]{3,2,1,0:T(8,128)(2,1)S(1)}, bf16[2,2,...) custom-call(s32[2]{0:T(128)S(1)} %pad_add_fusion.info_ref, ...), custom_call_target="tpu_custom_call" | custom-call | flops 2147483648 | bytes 4194304 | tf_op jit(solution)/shard_map/decode/pallas_call | solution.py:165
  38.3 0.4 collective-permute-start.10
  38.7 1.6 %collective-permute-start.15 = (bf16[1,1,128,512]{3,2,1,0:T(8,128)(2,1)S(1)}, bf16[1,1,128,512]{3,2,1,0:T(8,128)(2,1)S(1)}, u32[]{:S(2)}, u32[]{:S(2)}) collective-permute-start(bf16[1,1,128,512]{3,2,1,0:T(8,128)(2,1)S(1)} %slice_bitcast_fusion.10), channel_id=1, source_target_pairs={{0,8},{4,12},{8,0},{12,4},{16,24},{20,28},{24,16},{28,20},{1,9},{5... | collective-permute-start | bytes 393224 | tf_op jit(solution)/shard_map/ppermute | solution.py:23
  40.7 0.7 collective-permute-start.18
  41.4 1.5 %collective-permute-start.13 = (bf16[1,2,128,512]{3,2,1,0:T(8,128)(2,1)S(1)}, bf16[1,2,128,512]{3,2,1,0:T(8,128)(2,1)S(1)}, u32[]{:S(2)}, u32[]{:S(2)}) collective-permute-start(bf16[1,2,128,512]{3,2,1,0:T(8,128)(2,1)S(1)} %get-tuple-element.91), channel_id=1, source_target_pairs={{0,16},{4,20},{8,24},{12,28},{16,0},{20,4},{24,8},{28,12},{1,17},{... | collective-permute-start | bytes 786440 | tf_op jit(solution)/shard_map/ppermute | solution.py:29
  42.9 1.8 %collective-permute-done.15 = bf16[1,1,128,512]{3,2,1,0:T(8,128)(2,1)S(1)} collective-permute-done((bf16[1,1,128,512]{3,2,1,0:T(8,128)(2,1)S(1)}, bf16[1,1,128,512]{3,2,1,0:T(8,128)(2,1)S(1)}, u32[]{:S(2)}, u32[]{:S(2)}) %collective-permute-start.15) | collective-permute-done | bytes 131104 | tf_op jit(solution)/shard_map/ppermute | solution.py:23
  44.7 1.9 %collective-permute-start.16 = (bf16[1,1,128,512]{3,2,1,0:T(8,128)(2,1)S(1)}, bf16[1,1,128,512]{3,2,1,0:T(8,128)(2,1)S(1)}, u32[]{:S(2)}, u32[]{:S(2)}) collective-permute-start(bf16[1,1,128,512]{3,2,1,0:T(8,128)(2,1)S(1)} %slice_bitcast_fusion.11), channel_id=1, source_target_pairs={{0,8},{4,12},{8,0},{12,4},{16,24},{20,28},{24,16},{28,20},{1,9},{5... | collective-permute-start | bytes 393224 | tf_op jit(solution)/shard_map/ppermute | solution.py:23
  46.7 1.6 %collective-permute-start.20 = (bf16[1,1,128,512]{3,2,1,0:T(8,128)(2,1)S(1)}, bf16[1,1,128,512]{3,2,1,0:T(8,128)(2,1)S(1)}, u32[]{:S(2)}, u32[]{:S(2)}) collective-permute-start(bf16[1,1,128,512]{3,2,1,0:T(8,128)(2,1)S(1)} %fusion.13), channel_id=1, source_target_pairs={{0,16},{4,20},{8,24},{12,28},{16,0},{20,4},{24,8},{28,12},{1,17},{... | collective-permute-start | bytes 393224 | tf_op jit(solution)/shard_map/ppermute | solution.py:29
  48.3 1.1 collective-permute-start.21
  49.4 1.0 collective-permute-done.16
  50.5 1.6 %collective-permute-start.22 = (bf16[1,1,128,512]{3,2,1,0:T(8,128)(2,1)S(1)}, bf16[1,1,128,512]{3,2,1,0:T(8,128)(2,1)S(1)}, u32[]{:S(2)}, u32[]{:S(2)}) collective-permute-start(bf16[1,1,128,512]{3,2,1,0:T(8,128)(2,1)S(1)} %fusion.10), channel_id=1, source_target_pairs={{0,16},{4,20},{8,24},{12,28},{16,0},{20,4},{24,8},{28,12},{1,17},{... | collective-permute-start | bytes 393224 | tf_op jit(solution)/shard_map/ppermute | solution.py:29
  52.0 1.3 %collective-permute-done.20 = bf16[1,1,128,512]{3,2,1,0:T(8,128)(2,1)S(1)} collective-permute-done((bf16[1,1,128,512]{3,2,1,0:T(8,128)(2,1)S(1)}, bf16[1,1,128,512]{3,2,1,0:T(8,128)(2,1)S(1)}, u32[]{:S(2)}, u32[]{:S(2)}) %collective-permute-start.20) | collective-permute-done | bytes 131104 | tf_op jit(solution)/shard_map/ppermute | solution.py:29
  53.6 1.4 %collective-permute-start.19 = (bf16[1,2,128,512]{3,2,1,0:T(8,128)(2,1)S(1)}, bf16[1,2,128,512]{3,2,1,0:T(8,128)(2,1)S(1)}, u32[]{:S(2)}, u32[]{:S(2)}) collective-permute-start(bf16[1,2,128,512]{3,2,1,0:T(8,128)(2,1)S(1)} %fusion.2), channel_id=1, source_target_pairs={{0,8},{4,12},{8,0},{12,4},{16,24},{20,28},{24,16},{28,20},{1,9},{5... | collective-permute-start | bytes 786440 | tf_op jit(solution)/shard_map/ppermute | solution.py:23
  55.1 0.4 collective-permute-done.22
  55.6 1.6 %collective-permute-start.23 = (bf16[1,2,128,512]{3,2,1,0:T(8,128)(2,1)S(1)}, bf16[1,2,128,512]{3,2,1,0:T(8,128)(2,1)S(1)}, u32[]{:S(2)}, u32[]{:S(2)}) collective-permute-start(bf16[1,2,128,512]{3,2,1,0:T(8,128)(2,1)S(1)} %get-tuple-element.103), channel_id=1, source_target_pairs={{0,16},{4,20},{8,24},{12,28},{16,0},{20,4},{24,8},{28,12},{1,17},{... | collective-permute-start | bytes 786440 | tf_op jit(solution)/shard_map/ppermute | solution.py:29
  57.2 2.6 %collective-permute-start.24 = (bf16[128,512]{1,0:T(8,128)(2,1)S(1)}, bf16[128,512]{1,0:T(8,128)(2,1)S(1)}, u32[]{:S(2)}, u32[]{:S(2)}) collective-permute-start(bf16[128,512]{1,0:T(8,128)(2,1)S(1)} %fusion.16), channel_id=1, source_target_pairs={{0,3},{1,2},{2,1},{3,0},{4,7},{5,6},{6,5},{7,4},{8,11},{9,10},{10,... | collective-permute-start | bytes 393224 | tf_op jit(solution)/shard_map/ppermute | solution.py:17
  59.8 0.7 collective-permute-done.19
  60.4 1.7 %collective-permute-done.23 = bf16[1,2,128,512]{3,2,1,0:T(8,128)(2,1)S(1)} collective-permute-done((bf16[1,2,128,512]{3,2,1,0:T(8,128)(2,1)S(1)}, bf16[1,2,128,512]{3,2,1,0:T(8,128)(2,1)S(1)}, u32[]{:S(2)}, u32[]{:S(2)}) %collective-permute-start.23) | collective-permute-done | bytes 262176 | tf_op jit(solution)/shard_map/ppermute | solution.py:29
  63.4 1.4 %collective-permute-done.24 = bf16[128,512]{1,0:T(8,128)(2,1)S(1)} collective-permute-done((bf16[128,512]{1,0:T(8,128)(2,1)S(1)}, bf16[128,512]{1,0:T(8,128)(2,1)S(1)}, u32[]{:S(2)}, u32[]{:S(2)}) %collective-permute-start.24) | collective-permute-done | bytes 131104 | tf_op jit(solution)/shard_map/ppermute | solution.py:17
  64.8 4.5 %collective-permute-done.25 = bf16[128,512]{1,0:T(8,128)(2,1)S(1)} collective-permute-done((bf16[128,512]{1,0:T(8,128)(2,1)S(1)}, bf16[128,512]{1,0:T(8,128)(2,1)S(1)}, u32[]{:S(2)}, u32[]{:S(2)}) %collective-permute-start.25) | collective-permute-done | bytes 131104 | tf_op jit(solution)/shard_map/ppermute | solution.py:17
  69.4 0.8 multiply_convert_fusion
  70.2 1.4 %collective-permute-start.27 = (bf16[1,128,512]{2,1,0:T(8,128)(2,1)S(1)}, bf16[1,128,512]{2,1,0:T(8,128)(2,1)S(1)}, u32[]{:S(2)}, u32[]{:S(2)}) collective-permute-start(bf16[1,128,512]{2,1,0:T(8,128)(2,1)S(1)} %bitcast.111), channel_id=1, source_target_pairs={{0,16},{4,20},{8,24},{12,28},{16,0},{20,4},{24,8},{28,12},{1,17},{... | collective-permute-start | bytes 393224 | tf_op jit(solution)/shard_map/ppermute | solution.py:36
  71.6 2.5 %collective-permute-start.34 = (bf16[128,512]{1,0:T(8,128)(2,1)S(1)}, bf16[128,512]{1,0:T(8,128)(2,1)S(1)}, u32[]{:S(2)}, u32[]{:S(2)}) collective-permute-start(bf16[128,512]{1,0:T(8,128)(2,1)S(1)} %get-tuple-element.137), channel_id=1, source_target_pairs={{0,3},{1,2},{2,1},{3,0},{4,7},{5,6},{6,5},{7,4},{8,11},{9,10},{10,... | collective-permute-start | bytes 393224 | tf_op jit(solution)/shard_map/ppermute | solution.py:17
  74.1 0.9 collective-permute-start.33
  75.1 1.7 %collective-permute-start.29 = (bf16[1,128,512]{2,1,0:T(8,128)(2,1)S(1)}, bf16[1,128,512]{2,1,0:T(8,128)(2,1)S(1)}, u32[]{:S(2)}, u32[]{:S(2)}) collective-permute-start(bf16[1,128,512]{2,1,0:T(8,128)(2,1)S(1)} %bitcast.112), channel_id=1, source_target_pairs={{0,8},{4,12},{8,0},{12,4},{16,24},{20,28},{24,16},{28,20},{1,9},{5... | collective-permute-start | bytes 393224 | tf_op jit(solution)/shard_map/ppermute | solution.py:23
  76.8 0.3 collective-permute-done.30
  77.1 1.1 collective-permute-start.31
  78.3 1.0 collective-permute-start.32
  79.3 1.3 %collective-permute-start.28 = (bf16[1,128,512]{2,1,0:T(8,128)(2,1)S(1)}, bf16[1,128,512]{2,1,0:T(8,128)(2,1)S(1)}, u32[]{:S(2)}, u32[]{:S(2)}) collective-permute-start(bf16[1,128,512]{2,1,0:T(8,128)(2,1)S(1)} %collective-permute-done.27.refs_0_), channel_id=1, source_target_pairs={{0,8},{4,12},{8,0},{12,4},{16,24},{20,28},{24,16},{28,20},{1,9},{5... | collective-permute-start | bytes 393224 | tf_op jit(solution)/shard_map/ppermute | solution.py:23
  80.6 3.6 %collective-permute-done.33 = bf16[128,512]{1,0:T(8,128)(2,1)S(1)} collective-permute-done((bf16[128,512]{1,0:T(8,128)(2,1)S(1)}, bf16[128,512]{1,0:T(8,128)(2,1)S(1)}, u32[]{:S(2)}, u32[]{:S(2)}) %collective-permute-start.33) | collective-permute-done | bytes 131104 | tf_op jit(solution)/shard_map/ppermute | solution.py:17
  84.3 1.6 %collective-permute-start.38 = (bf16[2,128,512]{2,1,0:T(8,128)(2,1)S(1)}, bf16[2,128,512]{2,1,0:T(8,128)(2,1)S(1)}, u32[]{:S(2)}, u32[]{:S(2)}) collective-permute-start(bf16[2,128,512]{2,1,0:T(8,128)(2,1)S(1)} %pad_maximum_fusion.2.refs_2_), channel_id=1, source_target_pairs={{0,16},{4,20},{8,24},{12,28},{16,0},{20,4},{24,8},{28,12},{1,17},{... | collective-permute-start | bytes 786440 | tf_op jit(solution)/shard_map/ppermute | solution.py:36
  86.1 0.4 collective-permute-start.35
  86.4 1.1 collective-permute-start.42
  87.5 3.3 %backward_pair.4 = (f32[512,1024]{1,0:T(8,128)S(1)}, bf16[2,1024,2048]{2,1,0:T(8,128)(2,1)}, f32[8,128]{1,0:T(8,128)S(1)}) custom-call(s32[2]{0:T(128)S(1)} %pad_add_fusion.info_ref, bf16[1,128,512]{2,1,0:T(8,128)(2,1)S(1)} %bitcast.114, bf16[1,128,512]{2,1,0:T(8,128)(2,1)S(1)} %bitcast.118, bf16[2,128,512]{2,1,0:T(8,128)(2,1)S(1)} %pad_maximum_fusion.2.refs_2_, ...), custom_call_target="tpu_custom_call" | custom-call | flops 262144 | bytes 262144 | tf_op jit(solution)/shard_map/backward_pair/pallas_call | solution.py:269
  90.9 2.2 %collective-permute-done.38.refs_2_ = bf16[2,128,512]{2,1,0:T(8,128)(2,1)S(1)} collective-permute-done((bf16[2,128,512]{2,1,0:T(8,128)(2,1)S(1)}, bf16[2,128,512]{2,1,0:T(8,128)(2,1)S(1)}, u32[]{:S(2)}, u32[]{:S(2)}) %collective-permute-start.38) | collective-permute-done | bytes 262176 | tf_op jit(solution)/shard_map/ppermute | solution.py:36
  93.0 0.5 collective-permute-start.39
  93.5 1.2 %collective-permute-done.42.refs_2_ = bf16[2,128,512]{2,1,0:T(8,128)(2,1)S(1)} collective-permute-done((bf16[2,128,512]{2,1,0:T(8,128)(2,1)S(1)}, bf16[2,128,512]{2,1,0:T(8,128)(2,1)S(1)}, u32[]{:S(2)}, u32[]{:S(2)}) %collective-permute-start.42) | collective-permute-done | bytes 262176 | tf_op jit(solution)/shard_map/ppermute | solution.py:23
  94.8 0.5 collective-permute-start.46
  95.3 3.3 %backward_pair.5 = (f32[512,1024]{1,0:T(8,128)S(1)}, bf16[2,1024,2048]{2,1,0:T(8,128)(2,1)}, f32[8,128]{1,0:T(8,128)S(1)}) custom-call(s32[2]{0:T(128)S(1)} %pad_add_fusion.info_ref, bf16[1,128,512]{2,1,0:T(8,128)(2,1)S(1)} %collective-permute-done.27.refs_0_, ...), custom_call_target="tpu_custom_call", output_to_operand_aliasing={{0}: (9, {}), {1}: (10, {})} | custom-call | flops 262144 | bytes 262144 | tf_op jit(solution)/shard_map/backward_pair/pallas_call | solution.py:269
  98.7 0.5 collective-permute-start.43
  99.3 1.1 collective-permute-start.47
  100.3 2.0 %collective-permute-done.46.refs_2_ = bf16[2,128,512]{2,1,0:T(8,128)(2,1)S(1)} collective-permute-done((bf16[2,128,512]{2,1,0:T(8,128)(2,1)S(1)}, bf16[2,128,512]{2,1,0:T(8,128)(2,1)S(1)}, u32[]{:S(2)}, u32[]{:S(2)}) %collective-permute-start.46) | collective-permute-done | bytes 262176 | tf_op jit(solution)/shard_map/ppermute | solution.py:36
  102.3 3.8 %backward_pair.6 = (f32[512,1024]{1,0:T(8,128)S(1)}, bf16[2,1024,2048]{2,1,0:T(8,128)(2,1)}, f32[8,128]{1,0:T(8,128)S(1)}) custom-call(s32[2]{0:T(128)S(1)} %pad_add_fusion.info_ref, bf16[1,128,512]{2,1,0:T(8,128)(2,1)S(1)} %collective-permute-done.29.refs_0_, ...), custom_call_target="tpu_custom_call", output_to_operand_aliasing={{0}: (9, {}), {1}: (10, {})} | custom-call | flops 262144 | bytes 262144 | tf_op jit(solution)/shard_map/backward_pair/pallas_call | solution.py:269
  106.2 0.5 collective-permute-start.48
  106.8 1.1 collective-permute-done.48.refs_3_
  108.1 3.3 %backward_pair.7 = (f32[512,1024]{1,0:T(8,128)S(1)}, bf16[2,1024,2048]{2,1,0:T(8,128)(2,1)}, f32[8,128]{1,0:T(8,128)S(1)}) custom-call(s32[2]{0:T(128)S(1)} %pad_add_fusion.info_ref, bf16[1,128,512]{2,1,0:T(8,128)(2,1)S(1)} %collective-permute-done.28.refs_0_, ...), custom_call_target="tpu_custom_call", output_to_operand_aliasing={{0}: (9, {}), {1}: (10, {})} | custom-call | flops 262144 | bytes 262144 | tf_op jit(solution)/shard_map/backward_pair/pallas_call | solution.py:269
  111.4 4.7 %encoder_grad.1 = (bf16[2048,1024]{1,0:T(8,128)(2,1)}, f32[1,1024]{1,0:T(1,128)}, f32[1,1]{1,0:T(1,128)}) custom-call(s32[2]{0:T(128)S(1)} %pad_add_fusion.info_ref, bf16[1,512,512]{2,1,0:T(8,128)(2,1)S(1)} %turned.6.refs_0_, bf16[1,512,512]{2,1,0:T(8,128)(2,1)S(1)} %turned.7.refs_1_, bf16[1,512,512]{2,1,0:T(8,128)(2,1)S(1)} %turned.8.refs_2_, ...), custom_call_target="tpu_custom_call" | custom-call | flops 2147483648 | bytes 9437184 | tf_op jit(solution)/shard_map/encoder_grad/pallas_call | solution.py:321
  (83 shorter events, 4.1 us)
Async XLA Ops:
  0.7 17.5 %copy-start.2 = (bf16[128,512]{1,0:T(8,128)(2,1)S(1)}, bf16[128,512]{1,0:T(8,128)(2,1)}, u32[]{:S(2)}) copy-start(bf16[128,512]{1,0:T(8,128)(2,1)} %param.5) | copy-start | bytes 393220
  0.7 7.1 %collective-permute-start.1 = (bf16[128,512]{1,0:T(8,128)(2,1)}, bf16[128,512]{1,0:T(8,128)(2,1)S(1)}, u32[]{:S(2)}, u32[]{:S(2)}) collective-permute-start(bf16[128,512]{1,0:T(8,128)(2,1)} %param.5), channel_id=1, source_target_pairs={{0,1},{1,0},{2,3},{3,2},{4,5},{5,4},{6,7},{7,6},{8,9},{9,8},{10,11... | collective-permute-start | bytes 393224 | tf_op jit(solution)/shard_map/ppermute | solution.py:17
  3.8 10.1 %collective-permute-start.3 = (bf16[128,512]{1,0:T(8,128)(2,1)}, bf16[128,512]{1,0:T(8,128)(2,1)S(1)}, u32[]{:S(2)}, u32[]{:S(2)}) collective-permute-start(bf16[128,512]{1,0:T(8,128)(2,1)} %param.5), channel_id=1, source_target_pairs={{0,3},{1,2},{2,1},{3,0},{4,7},{5,6},{6,5},{7,4},{8,11},{9,10},{10,... | collective-permute-start | bytes 393224 | tf_op jit(solution)/shard_map/ppermute | solution.py:17
  6.2 12.0 %collective-permute-start.2 = (bf16[128,512]{1,0:T(8,128)(2,1)}, bf16[128,512]{1,0:T(8,128)(2,1)S(1)}, u32[]{:S(2)}, u32[]{:S(2)}) collective-permute-start(bf16[128,512]{1,0:T(8,128)(2,1)} %param.5), channel_id=1, source_target_pairs={{0,2},{1,3},{2,0},{3,1},{4,6},{5,7},{6,4},{7,5},{8,10},{9,11},{10,... | collective-permute-start | bytes 393224 | tf_op jit(solution)/shard_map/ppermute | solution.py:17
  6.4 12.0 %collective-permute-start = (bf16[128,512]{1,0:T(8,128)(2,1)}, bf16[128,512]{1,0:T(8,128)(2,1)S(1)}, u32[]{:S(2)}, u32[]{:S(2)}) collective-permute-start(bf16[128,512]{1,0:T(8,128)(2,1)} %param.5), channel_id=1, source_target_pairs={{0,8},{4,12},{8,0},{12,4},{16,24},{20,28},{24,16},{28,20},{1,9},{5... | collective-permute-start | bytes 393224 | tf_op jit(solution)/shard_map/ppermute | solution.py:23
  7.9 10.5 %collective-permute-start.4 = (bf16[128,512]{1,0:T(8,128)(2,1)S(1)}, bf16[128,512]{1,0:T(8,128)(2,1)S(1)}, u32[]{:S(2)}, u32[]{:S(2)}) collective-permute-start(bf16[128,512]{1,0:T(8,128)(2,1)S(1)} %collective-permute-done.1), channel_id=1, source_target_pairs={{0,8},{4,12},{8,0},{12,4},{16,24},{20,28},{24,16},{28,20},{1,9},{5... | collective-permute-start | bytes 393224 | tf_op jit(solution)/shard_map/ppermute | solution.py:23
  18.3 2.2 %collective-permute-start.5 = (bf16[4,128,512]{2,1,0:T(8,128)(2,1)S(1)}, bf16[4,128,512]{2,1,0:T(8,128)(2,1)S(1)}, u32[]{:S(2)}, u32[]{:S(2)}) collective-permute-start(bf16[4,128,512]{2,1,0:T(8,128)(2,1)S(1)} %pad_maximum_fusion.refs_0_), channel_id=1, source_target_pairs={{0,4},{4,0},{8,12},{12,8},{16,20},{20,16},{24,28},{28,24},{1,5},{5... | collective-permute-start | bytes 1572872 | tf_op jit(solution)/shard_map/ppermute | solution.py:23
  18.4 6.4 %collective-permute-start.7 = (bf16[128,512]{1,0:T(8,128)(2,1)S(1)}, bf16[128,512]{1,0:T(8,128)(2,1)S(1)}, u32[]{:S(2)}, u32[]{:S(2)}) collective-permute-start(bf16[128,512]{1,0:T(8,128)(2,1)S(1)} %collective-permute-done.3), channel_id=1, source_target_pairs={{0,8},{4,12},{8,0},{12,4},{16,24},{20,28},{24,16},{28,20},{1,9},{5... | collective-permute-start | bytes 393224 | tf_op jit(solution)/shard_map/ppermute | solution.py:23
  20.0 7.2 %collective-permute-start.6 = (bf16[128,512]{1,0:T(8,128)(2,1)S(1)}, bf16[128,512]{1,0:T(8,128)(2,1)S(1)}, u32[]{:S(2)}, u32[]{:S(2)}) collective-permute-start(bf16[128,512]{1,0:T(8,128)(2,1)S(1)} %collective-permute-done.2), channel_id=1, source_target_pairs={{0,8},{4,12},{8,0},{12,4},{16,24},{20,28},{24,16},{28,20},{1,9},{5... | collective-permute-start | bytes 393224 | tf_op jit(solution)/shard_map/ppermute | solution.py:23
  27.2 2.0 %copy-start = (f32[1024]{0:T(1024)S(1)}, f32[1024]{0:T(1024)}, u32[]{:S(2)}) copy-start(f32[1024]{0:T(1024)} %param.8) | copy-start | bytes 12292
  27.2 2.0 %collective-permute-start.8 = (bf16[4,128,512]{2,1,0:T(8,128)(2,1)S(1)}, bf16[4,128,512]{2,1,0:T(8,128)(2,1)S(1)}, u32[]{:S(2)}, u32[]{:S(2)}) collective-permute-start(bf16[4,128,512]{2,1,0:T(8,128)(2,1)S(1)} %pad_maximum_fusion.1.refs_0_), channel_id=1, source_target_pairs={{0,4},{4,0},{8,12},{12,8},{16,20},{20,16},{24,28},{28,24},{1,5},{5... | collective-permute-start | bytes 1572872 | tf_op jit(solution)/shard_map/ppermute | solution.py:23
  33.5 1.6 %collective-permute-start.9 = (bf16[2,1,128,512]{3,2,0,1:T(8,128)(2,1)S(1)}, bf16[2,1,128,512]{3,2,0,1:T(8,128)(2,1)S(1)}, u32[]{:S(2)}, u32[]{:S(2)}) collective-permute-start(bf16[2,1,128,512]{3,2,0,1:T(8,128)(2,1)S(1)} %bitcast.123), channel_id=1, source_target_pairs={{0,4},{4,0},{8,12},{12,8},{16,20},{20,16},{24,28},{28,24},{1,5},{5... | collective-permute-start | bytes 786440 | tf_op jit(solution)/shard_map/ppermute | solution.py:23
  33.7 6.6 %collective-permute-start.11 = (bf16[2,2,128,512]{3,2,1,0:T(8,128)(2,1)S(1)}, bf16[2,2,128,512]{3,2,1,0:T(8,128)(2,1)S(1)}, u32[]{:S(2)}, u32[]{:S(2)}) collective-permute-start(bf16[2,2,128,512]{3,2,1,0:T(8,128)(2,1)S(1)} %get-tuple-element.88), channel_id=1, source_target_pairs={{0,4},{4,0},{8,12},{12,8},{16,20},{20,16},{24,28},{28,24},{1,5},{5... | collective-permute-start | bytes 1572872 | tf_op jit(solution)/shard_map/ppermute | solution.py:23
  34.1 6.1 %collective-permute-start.14 = (bf16[2,1,128,512]{3,2,0,1:T(8,128)(2,1)S(1)}, bf16[2,1,128,512]{3,2,0,1:T(8,128)(2,1)S(1)}, u32[]{:S(2)}, u32[]{:S(2)}) collective-permute-start(bf16[2,1,128,512]{3,2,0,1:T(8,128)(2,1)S(1)} %bitcast.121), channel_id=1, source_target_pairs={{0,4},{4,0},{8,12},{12,8},{16,20},{20,16},{24,28},{28,24},{1,5},{5... | collective-permute-start | bytes 786440 | tf_op jit(solution)/shard_map/ppermute | solution.py:23
  38.1 2.4 %collective-permute-start.12 = (bf16[2,1,128,512]{3,2,0,1:T(8,128)(2,1)S(1)}, bf16[2,1,128,512]{3,2,0,1:T(8,128)(2,1)S(1)}, u32[]{:S(2)}, u32[]{:S(2)}) collective-permute-start(bf16[2,1,128,512]{3,2,0,1:T(8,128)(2,1)S(1)} %bitcast.122), channel_id=1, source_target_pairs={{0,4},{4,0},{8,12},{12,8},{16,20},{20,16},{24,28},{28,24},{1,5},{5... | collective-permute-start | bytes 786440 | tf_op jit(solution)/shard_map/ppermute | solution.py:23
  38.3 15.1 %collective-permute-start.10 = (bf16[2,2,128,512]{3,2,1,0:T(8,128)(2,1)S(1)}, bf16[2,2,128,512]{3,2,1,0:T(8,128)(2,1)S(1)}, u32[]{:S(2)}, u32[]{:S(2)}) collective-permute-start(bf16[2,2,128,512]{3,2,1,0:T(8,128)(2,1)S(1)} %get-tuple-element.85), channel_id=1, source_target_pairs={{0,4},{4,0},{8,12},{12,8},{16,20},{20,16},{24,28},{28,24},{1,5},{5... | collective-permute-start | bytes 1572872 | tf_op jit(solution)/shard_map/ppermute | solution.py:23
  38.7 6.0 %collective-permute-start.15 = (bf16[1,1,128,512]{3,2,1,0:T(8,128)(2,1)S(1)}, bf16[1,1,128,512]{3,2,1,0:T(8,128)(2,1)S(1)}, u32[]{:S(2)}, u32[]{:S(2)}) collective-permute-start(bf16[1,1,128,512]{3,2,1,0:T(8,128)(2,1)S(1)} %slice_bitcast_fusion.10), channel_id=1, source_target_pairs={{0,8},{4,12},{8,0},{12,4},{16,24},{20,28},{24,16},{28,20},{1,9},{5... | collective-permute-start | bytes 393224 | tf_op jit(solution)/shard_map/ppermute | solution.py:23
  40.3 6.4 %collective-permute-start.17 = (bf16[2,1,128,512]{3,2,0,1:T(8,128)(2,1)S(1)}, bf16[2,1,128,512]{3,2,0,1:T(8,128)(2,1)S(1)}, u32[]{:S(2)}, u32[]{:S(2)}) collective-permute-start(bf16[2,1,128,512]{3,2,0,1:T(8,128)(2,1)S(1)} %bitcast.120), channel_id=1, source_target_pairs={{0,4},{4,0},{8,12},{12,8},{16,20},{20,16},{24,28},{28,24},{1,5},{5... | collective-permute-start | bytes 786440 | tf_op jit(solution)/shard_map/ppermute | solution.py:23
  40.7 7.7 %collective-permute-start.18 = (bf16[1,1,128,512]{3,2,1,0:T(8,128)(2,1)S(1)}, bf16[1,1,128,512]{3,2,1,0:T(8,128)(2,1)S(1)}, u32[]{:S(2)}, u32[]{:S(2)}) collective-permute-start(bf16[1,1,128,512]{3,2,1,0:T(8,128)(2,1)S(1)} %slice_bitcast_fusion.12), channel_id=1, source_target_pairs={{0,8},{4,12},{8,0},{12,4},{16,24},{20,28},{24,16},{28,20},{1,9},{5... | collective-permute-start | bytes 393224 | tf_op jit(solution)/shard_map/ppermute | solution.py:23
  41.4 12.2 %collective-permute-start.13 = (bf16[1,2,128,512]{3,2,1,0:T(8,128)(2,1)S(1)}, bf16[1,2,128,512]{3,2,1,0:T(8,128)(2,1)S(1)}, u32[]{:S(2)}, u32[]{:S(2)}) collective-permute-start(bf16[1,2,128,512]{3,2,1,0:T(8,128)(2,1)S(1)} %get-tuple-element.91), channel_id=1, source_target_pairs={{0,16},{4,20},{8,24},{12,28},{16,0},{20,4},{24,8},{28,12},{1,17},{... | collective-permute-start | bytes 786440 | tf_op jit(solution)/shard_map/ppermute | solution.py:29
  44.7 5.7 %collective-permute-start.16 = (bf16[1,1,128,512]{3,2,1,0:T(8,128)(2,1)S(1)}, bf16[1,1,128,512]{3,2,1,0:T(8,128)(2,1)S(1)}, u32[]{:S(2)}, u32[]{:S(2)}) collective-permute-start(bf16[1,1,128,512]{3,2,1,0:T(8,128)(2,1)S(1)} %slice_bitcast_fusion.11), channel_id=1, source_target_pairs={{0,8},{4,12},{8,0},{12,4},{16,24},{20,28},{24,16},{28,20},{1,9},{5... | collective-permute-start | bytes 393224 | tf_op jit(solution)/shard_map/ppermute | solution.py:23
  46.7 6.6 %collective-permute-start.20 = (bf16[1,1,128,512]{3,2,1,0:T(8,128)(2,1)S(1)}, bf16[1,1,128,512]{3,2,1,0:T(8,128)(2,1)S(1)}, u32[]{:S(2)}, u32[]{:S(2)}) collective-permute-start(bf16[1,1,128,512]{3,2,1,0:T(8,128)(2,1)S(1)} %fusion.13), channel_id=1, source_target_pairs={{0,16},{4,20},{8,24},{12,28},{16,0},{20,4},{24,8},{28,12},{1,17},{... | collective-permute-start | bytes 393224 | tf_op jit(solution)/shard_map/ppermute | solution.py:29
  48.3 6.8 %collective-permute-start.21 = (bf16[1,1,128,512]{3,2,1,0:T(8,128)(2,1)S(1)}, bf16[1,1,128,512]{3,2,1,0:T(8,128)(2,1)S(1)}, u32[]{:S(2)}, u32[]{:S(2)}) collective-permute-start(bf16[1,1,128,512]{3,2,1,0:T(8,128)(2,1)S(1)} %slice_bitcast_fusion.9), channel_id=1, source_target_pairs={{0,8},{4,12},{8,0},{12,4},{16,24},{20,28},{24,16},{28,20},{1,9},{5... | collective-permute-start | bytes 393224 | tf_op jit(solution)/shard_map/ppermute | solution.py:23
  50.5 5.0 %collective-permute-start.22 = (bf16[1,1,128,512]{3,2,1,0:T(8,128)(2,1)S(1)}, bf16[1,1,128,512]{3,2,1,0:T(8,128)(2,1)S(1)}, u32[]{:S(2)}, u32[]{:S(2)}) collective-permute-start(bf16[1,1,128,512]{3,2,1,0:T(8,128)(2,1)S(1)} %fusion.10), channel_id=1, source_target_pairs={{0,16},{4,20},{8,24},{12,28},{16,0},{20,4},{24,8},{28,12},{1,17},{... | collective-permute-start | bytes 393224 | tf_op jit(solution)/shard_map/ppermute | solution.py:29
  53.6 6.8 %collective-permute-start.19 = (bf16[1,2,128,512]{3,2,1,0:T(8,128)(2,1)S(1)}, bf16[1,2,128,512]{3,2,1,0:T(8,128)(2,1)S(1)}, u32[]{:S(2)}, u32[]{:S(2)}) collective-permute-start(bf16[1,2,128,512]{3,2,1,0:T(8,128)(2,1)S(1)} %fusion.2), channel_id=1, source_target_pairs={{0,8},{4,12},{8,0},{12,4},{16,24},{20,28},{24,16},{28,20},{1,9},{5... | collective-permute-start | bytes 786440 | tf_op jit(solution)/shard_map/ppermute | solution.py:23
  55.6 13.8 %copy-start.1 = (bf16[128,512]{1,0:T(8,128)(2,1)S(1)}, bf16[128,512]{1,0:T(8,128)(2,1)}, u32[]{:S(2)}) copy-start(bf16[128,512]{1,0:T(8,128)(2,1)} %param.6) | copy-start | bytes 393220
  55.6 6.5 %collective-permute-start.23 = (bf16[1,2,128,512]{3,2,1,0:T(8,128)(2,1)S(1)}, bf16[1,2,128,512]{3,2,1,0:T(8,128)(2,1)S(1)}, u32[]{:S(2)}, u32[]{:S(2)}) collective-permute-start(bf16[1,2,128,512]{3,2,1,0:T(8,128)(2,1)S(1)} %get-tuple-element.103), channel_id=1, source_target_pairs={{0,16},{4,20},{8,24},{12,28},{16,0},{20,4},{24,8},{28,12},{1,17},{... | collective-permute-start | bytes 786440 | tf_op jit(solution)/shard_map/ppermute | solution.py:29
  57.2 7.7 %collective-permute-start.24 = (bf16[128,512]{1,0:T(8,128)(2,1)S(1)}, bf16[128,512]{1,0:T(8,128)(2,1)S(1)}, u32[]{:S(2)}, u32[]{:S(2)}) collective-permute-start(bf16[128,512]{1,0:T(8,128)(2,1)S(1)} %fusion.16), channel_id=1, source_target_pairs={{0,3},{1,2},{2,1},{3,0},{4,7},{5,6},{6,5},{7,4},{8,11},{9,10},{10,... | collective-permute-start | bytes 393224 | tf_op jit(solution)/shard_map/ppermute | solution.py:17
  59.8 9.6 %collective-permute-start.25 = (bf16[128,512]{1,0:T(8,128)(2,1)S(1)}, bf16[128,512]{1,0:T(8,128)(2,1)S(1)}, u32[]{:S(2)}, u32[]{:S(2)}) collective-permute-start(bf16[128,512]{1,0:T(8,128)(2,1)S(1)} %fusion.17), channel_id=1, source_target_pairs={{0,2},{1,3},{2,0},{3,1},{4,6},{5,7},{6,4},{7,5},{8,10},{9,11},{10,... | collective-permute-start | bytes 393224 | tf_op jit(solution)/shard_map/ppermute | solution.py:17
  62.2 7.1 %collective-permute-start.26 = (bf16[128,512]{1,0:T(8,128)(2,1)S(1)}, bf16[128,512]{1,0:T(8,128)(2,1)S(1)}, u32[]{:S(2)}, u32[]{:S(2)}) collective-permute-start(bf16[128,512]{1,0:T(8,128)(2,1)S(1)} %fusion.18), channel_id=1, source_target_pairs={{0,1},{1,0},{2,3},{3,2},{4,5},{5,4},{6,7},{7,6},{8,9},{9,8},{10,11... | collective-permute-start | bytes 393224 | tf_op jit(solution)/shard_map/ppermute | solution.py:17
  70.2 7.0 %collective-permute-start.30 = (bf16[128,512]{1,0:T(8,128)(2,1)S(1)}, bf16[128,512]{1,0:T(8,128)(2,1)S(1)}, u32[]{:S(2)}, u32[]{:S(2)}) collective-permute-start(bf16[128,512]{1,0:T(8,128)(2,1)S(1)} %get-tuple-element.137), channel_id=1, source_target_pairs={{0,1},{1,0},{2,3},{3,2},{4,5},{5,4},{6,7},{7,6},{8,9},{9,8},{10,11... | collective-permute-start | bytes 393224 | tf_op jit(solution)/shard_map/ppermute | solution.py:17
  70.2 8.1 %collective-permute-start.27 = (bf16[1,128,512]{2,1,0:T(8,128)(2,1)S(1)}, bf16[1,128,512]{2,1,0:T(8,128)(2,1)S(1)}, u32[]{:S(2)}, u32[]{:S(2)}) collective-permute-start(bf16[1,128,512]{2,1,0:T(8,128)(2,1)S(1)} %bitcast.111), channel_id=1, source_target_pairs={{0,16},{4,20},{8,24},{12,28},{16,0},{20,4},{24,8},{28,12},{1,17},{... | collective-permute-start | bytes 393224 | tf_op jit(solution)/shard_map/ppermute | solution.py:36
  71.6 7.7 %collective-permute-start.34 = (bf16[128,512]{1,0:T(8,128)(2,1)S(1)}, bf16[128,512]{1,0:T(8,128)(2,1)S(1)}, u32[]{:S(2)}, u32[]{:S(2)}) collective-permute-start(bf16[128,512]{1,0:T(8,128)(2,1)S(1)} %get-tuple-element.137), channel_id=1, source_target_pairs={{0,3},{1,2},{2,1},{3,0},{4,7},{5,6},{6,5},{7,4},{8,11},{9,10},{10,... | collective-permute-start | bytes 393224 | tf_op jit(solution)/shard_map/ppermute | solution.py:17
  74.1 10.1 %collective-permute-start.33 = (bf16[128,512]{1,0:T(8,128)(2,1)S(1)}, bf16[128,512]{1,0:T(8,128)(2,1)S(1)}, u32[]{:S(2)}, u32[]{:S(2)}) collective-permute-start(bf16[128,512]{1,0:T(8,128)(2,1)S(1)} %get-tuple-element.137), channel_id=1, source_target_pairs={{0,2},{1,3},{2,0},{3,1},{4,6},{5,7},{6,4},{7,5},{8,10},{9,11},{10,... | collective-permute-start | bytes 393224 | tf_op jit(solution)/shard_map/ppermute | solution.py:17
  75.1 9.2 %collective-permute-start.29 = (bf16[1,128,512]{2,1,0:T(8,128)(2,1)S(1)}, bf16[1,128,512]{2,1,0:T(8,128)(2,1)S(1)}, u32[]{:S(2)}, u32[]{:S(2)}) collective-permute-start(bf16[1,128,512]{2,1,0:T(8,128)(2,1)S(1)} %bitcast.112), channel_id=1, source_target_pairs={{0,8},{4,12},{8,0},{12,4},{16,24},{20,28},{24,16},{28,20},{1,9},{5... | collective-permute-start | bytes 393224 | tf_op jit(solution)/shard_map/ppermute | solution.py:23
  77.1 8.9 %collective-permute-start.31 = (bf16[1,128,512]{2,1,0:T(8,128)(2,1)S(1)}, bf16[1,128,512]{2,1,0:T(8,128)(2,1)S(1)}, u32[]{:S(2)}, u32[]{:S(2)}) collective-permute-start(bf16[1,128,512]{2,1,0:T(8,128)(2,1)S(1)} %bitcast.115), channel_id=1, source_target_pairs={{0,16},{4,20},{8,24},{12,28},{16,0},{20,4},{24,8},{28,12},{1,17},{... | collective-permute-start | bytes 393224 | tf_op jit(solution)/shard_map/ppermute | solution.py:36
  78.3 7.8 %collective-permute-start.32 = (bf16[1,128,512]{2,1,0:T(8,128)(2,1)S(1)}, bf16[1,128,512]{2,1,0:T(8,128)(2,1)S(1)}, u32[]{:S(2)}, u32[]{:S(2)}) collective-permute-start(bf16[1,128,512]{2,1,0:T(8,128)(2,1)S(1)} %bitcast.116), channel_id=1, source_target_pairs={{0,8},{4,12},{8,0},{12,4},{16,24},{20,28},{24,16},{28,20},{1,9},{5... | collective-permute-start | bytes 393224 | tf_op jit(solution)/shard_map/ppermute | solution.py:23
  79.3 6.6 %collective-permute-start.28 = (bf16[1,128,512]{2,1,0:T(8,128)(2,1)S(1)}, bf16[1,128,512]{2,1,0:T(8,128)(2,1)S(1)}, u32[]{:S(2)}, u32[]{:S(2)}) collective-permute-start(bf16[1,128,512]{2,1,0:T(8,128)(2,1)S(1)} %collective-permute-done.27.refs_0_), channel_id=1, source_target_pairs={{0,8},{4,12},{8,0},{12,4},{16,24},{20,28},{24,16},{28,20},{1,9},{5... | collective-permute-start | bytes 393224 | tf_op jit(solution)/shard_map/ppermute | solution.py:23
  84.2 3.3 %collective-permute-start.37 = (bf16[2,128,512]{2,1,0:T(8,128)(2,1)S(1)}, bf16[2,128,512]{2,1,0:T(8,128)(2,1)S(1)}, u32[]{:S(2)}, u32[]{:S(2)}) collective-permute-start(bf16[2,128,512]{2,1,0:T(8,128)(2,1)S(1)} %pad_maximum_fusion.2.refs_2_), channel_id=1, source_target_pairs={{0,4},{4,0},{8,12},{12,8},{16,20},{20,16},{24,28},{28,24},{1,5},{5... | collective-permute-start | bytes 786440 | tf_op jit(solution)/shard_map/ppermute | solution.py:23
  84.3 8.7 %collective-permute-start.38 = (bf16[2,128,512]{2,1,0:T(8,128)(2,1)S(1)}, bf16[2,128,512]{2,1,0:T(8,128)(2,1)S(1)}, u32[]{:S(2)}, u32[]{:S(2)}) collective-permute-start(bf16[2,128,512]{2,1,0:T(8,128)(2,1)S(1)} %pad_maximum_fusion.2.refs_2_), channel_id=1, source_target_pairs={{0,16},{4,20},{8,24},{12,28},{16,0},{20,4},{24,8},{28,12},{1,17},{... | collective-permute-start | bytes 786440 | tf_op jit(solution)/shard_map/ppermute | solution.py:36
  85.9 1.6 %collective-permute-start.36 = (bf16[1,128,512]{2,1,0:T(8,128)(2,1)S(1)}, bf16[1,128,512]{2,1,0:T(8,128)(2,1)S(1)}, u32[]{:S(2)}, u32[]{:S(2)}) collective-permute-start(bf16[1,128,512]{2,1,0:T(8,128)(2,1)S(1)} %bitcast.117), channel_id=1, source_target_pairs={{0,4},{4,0},{8,12},{12,8},{16,20},{20,16},{24,28},{28,24},{1,5},{5... | collective-permute-start | bytes 393224 | tf_op jit(solution)/shard_map/ppermute | solution.py:23
  86.1 1.5 %collective-permute-start.35 = (bf16[1,128,512]{2,1,0:T(8,128)(2,1)S(1)}, bf16[1,128,512]{2,1,0:T(8,128)(2,1)S(1)}, u32[]{:S(2)}, u32[]{:S(2)}) collective-permute-start(bf16[1,128,512]{2,1,0:T(8,128)(2,1)S(1)} %bitcast.113), channel_id=1, source_target_pairs={{0,4},{4,0},{8,12},{12,8},{16,20},{20,16},{24,28},{28,24},{1,5},{5... | collective-permute-start | bytes 393224 | tf_op jit(solution)/shard_map/ppermute | solution.py:23
  86.4 8.4 %collective-permute-start.42 = (bf16[2,128,512]{2,1,0:T(8,128)(2,1)S(1)}, bf16[2,128,512]{2,1,0:T(8,128)(2,1)S(1)}, u32[]{:S(2)}, u32[]{:S(2)}) collective-permute-start(bf16[2,128,512]{2,1,0:T(8,128)(2,1)S(1)} %pad_maximum_fusion.2.refs_2_), channel_id=1, source_target_pairs={{0,8},{4,12},{8,0},{12,4},{16,24},{20,28},{24,16},{28,20},{1,9},{5... | collective-permute-start | bytes 786440 | tf_op jit(solution)/shard_map/ppermute | solution.py:23
  93.0 2.3 %collective-permute-start.41 = (bf16[2,128,512]{2,1,0:T(8,128)(2,1)S(1)}, bf16[2,128,512]{2,1,0:T(8,128)(2,1)S(1)}, u32[]{:S(2)}, u32[]{:S(2)}) collective-permute-start(bf16[2,128,512]{2,1,0:T(8,128)(2,1)S(1)} %collective-permute-done.38.refs_2_), channel_id=1, source_target_pairs={{0,4},{4,0},{8,12},{12,8},{16,20},{20,16},{24,28},{28,24},{1,5},{5... | collective-permute-start | bytes 786440 | tf_op jit(solution)/shard_map/ppermute | solution.py:23
  93.0 2.3 %collective-permute-start.39 = (bf16[1,128,512]{2,1,0:T(8,128)(2,1)S(1)}, bf16[1,128,512]{2,1,0:T(8,128)(2,1)S(1)}, u32[]{:S(2)}, u32[]{:S(2)}) collective-permute-start(bf16[1,128,512]{2,1,0:T(8,128)(2,1)S(1)} %collective-permute-done.27.refs_0_), channel_id=1, source_target_pairs={{0,4},{4,0},{8,12},{12,8},{16,20},{20,16},{24,28},{28,24},{1,5},{5... | collective-permute-start | bytes 393224 | tf_op jit(solution)/shard_map/ppermute | solution.py:23
  93.5 1.8 %collective-permute-start.40 = (bf16[1,128,512]{2,1,0:T(8,128)(2,1)S(1)}, bf16[1,128,512]{2,1,0:T(8,128)(2,1)S(1)}, u32[]{:S(2)}, u32[]{:S(2)}) collective-permute-start(bf16[1,128,512]{2,1,0:T(8,128)(2,1)S(1)} %collective-permute-done.31.refs_1_), channel_id=1, source_target_pairs={{0,4},{4,0},{8,12},{12,8},{16,20},{20,16},{24,28},{28,24},{1,5},{5... | collective-permute-start | bytes 393224 | tf_op jit(solution)/shard_map/ppermute | solution.py:23
  94.8 7.5 %collective-permute-start.46 = (bf16[2,128,512]{2,1,0:T(8,128)(2,1)S(1)}, bf16[2,128,512]{2,1,0:T(8,128)(2,1)S(1)}, u32[]{:S(2)}, u32[]{:S(2)}) collective-permute-start(bf16[2,128,512]{2,1,0:T(8,128)(2,1)S(1)} %collective-permute-done.42.refs_2_), channel_id=1, source_target_pairs={{0,16},{4,20},{8,24},{12,28},{16,0},{20,4},{24,8},{28,12},{1,17},{... | collective-permute-start | bytes 786440 | tf_op jit(solution)/shard_map/ppermute | solution.py:36
  98.6 3.7 %collective-permute-start.45 = (bf16[2,128,512]{2,1,0:T(8,128)(2,1)S(1)}, bf16[2,128,512]{2,1,0:T(8,128)(2,1)S(1)}, u32[]{:S(2)}, u32[]{:S(2)}) collective-permute-start(bf16[2,128,512]{2,1,0:T(8,128)(2,1)S(1)} %collective-permute-done.42.refs_2_), channel_id=1, source_target_pairs={{0,4},{4,0},{8,12},{12,8},{16,20},{20,16},{24,28},{28,24},{1,5},{5... | collective-permute-start | bytes 786440 | tf_op jit(solution)/shard_map/ppermute | solution.py:23
  98.7 3.7 %collective-permute-start.43 = (bf16[1,128,512]{2,1,0:T(8,128)(2,1)S(1)}, bf16[1,128,512]{2,1,0:T(8,128)(2,1)S(1)}, u32[]{:S(2)}, u32[]{:S(2)}) collective-permute-start(bf16[1,128,512]{2,1,0:T(8,128)(2,1)S(1)} %collective-permute-done.29.refs_0_), channel_id=1, source_target_pairs={{0,4},{4,0},{8,12},{12,8},{16,20},{20,16},{24,28},{28,24},{1,5},{5... | collective-permute-start | bytes 393224 | tf_op jit(solution)/shard_map/ppermute | solution.py:23
  99.2 3.2 %collective-permute-start.44 = (bf16[1,128,512]{2,1,0:T(8,128)(2,1)S(1)}, bf16[1,128,512]{2,1,0:T(8,128)(2,1)S(1)}, u32[]{:S(2)}, u32[]{:S(2)}) collective-permute-start(bf16[1,128,512]{2,1,0:T(8,128)(2,1)S(1)} %collective-permute-done.32.refs_1_), channel_id=1, source_target_pairs={{0,4},{4,0},{8,12},{12,8},{16,20},{20,16},{24,28},{28,24},{1,5},{5... | collective-permute-start | bytes 393224 | tf_op jit(solution)/shard_map/ppermute | solution.py:23
  99.3 6.9 %collective-permute-start.47 = (bf16[1,128,512]{2,1,0:T(8,128)(2,1)S(1)}, bf16[1,128,512]{2,1,0:T(8,128)(2,1)S(1)}, u32[]{:S(2)}, u32[]{:S(2)}) collective-permute-start(bf16[1,128,512]{2,1,0:T(8,128)(2,1)S(1)} %collective-permute-done.31.refs_1_), channel_id=1, source_target_pairs={{0,8},{4,12},{8,0},{12,4},{16,24},{20,28},{24,16},{28,20},{1,9},{5... | collective-permute-start | bytes 393224 | tf_op jit(solution)/shard_map/ppermute | solution.py:23
  106.1 2.0 %collective-permute-start.50 = (bf16[2,128,512]{2,1,0:T(8,128)(2,1)S(1)}, bf16[2,128,512]{2,1,0:T(8,128)(2,1)S(1)}, u32[]{:S(2)}, u32[]{:S(2)}) collective-permute-start(bf16[2,128,512]{2,1,0:T(8,128)(2,1)S(1)} %collective-permute-done.46.refs_2_), channel_id=1, source_target_pairs={{0,4},{4,0},{8,12},{12,8},{16,20},{20,16},{24,28},{28,24},{1,5},{5... | collective-permute-start | bytes 786440 | tf_op jit(solution)/shard_map/ppermute | solution.py:23
  106.2 1.7 %collective-permute-start.48 = (bf16[1,128,512]{2,1,0:T(8,128)(2,1)S(1)}, bf16[1,128,512]{2,1,0:T(8,128)(2,1)S(1)}, u32[]{:S(2)}, u32[]{:S(2)}) collective-permute-start(bf16[1,128,512]{2,1,0:T(8,128)(2,1)S(1)} %collective-permute-done.28.refs_0_), channel_id=1, source_target_pairs={{0,4},{4,0},{8,12},{12,8},{16,20},{20,16},{24,28},{28,24},{1,5},{5... | collective-permute-start | bytes 393224 | tf_op jit(solution)/shard_map/ppermute | solution.py:23
  106.7 1.4 %collective-permute-start.49 = (bf16[1,128,512]{2,1,0:T(8,128)(2,1)S(1)}, bf16[1,128,512]{2,1,0:T(8,128)(2,1)S(1)}, u32[]{:S(2)}, u32[]{:S(2)}) collective-permute-start(bf16[1,128,512]{2,1,0:T(8,128)(2,1)S(1)} %collective-permute-done.47.refs_1_), channel_id=1, source_target_pairs={{0,4},{4,0},{8,12},{12,8},{16,20},{20,16},{24,28},{28,24},{1,5},{5... | collective-permute-start | bytes 393224 | tf_op jit(solution)/shard_map/ppermute | solution.py:23

commit v2 on v1

--- a/solution.py
+++ b/solution.py
@@ -41,9 +41,13 @@
 
 
 def all_over_feat(value):
-    blocks = [value, over_feat(value, 1)]
-    for s in range(2, lax.axis_size("feat")):
-        blocks.append(over_feat(value, s))
+    count = lax.axis_size("feat")
+    blocks = [value] + [None] * (count - 1)
+    mask = count // 2
+    while mask > 0:
+        for s in range(0, count, 2 * mask):
+            blocks[s ^ mask] = over_feat(blocks[s], mask)
+        mask //= 2
     return blocks
 
 
@@ -358,6 +362,7 @@
     info = jnp.stack([position % sub_count, layers - 1 - layer]).astype(jnp.int32)
     real = [layer >= k for k in range(layers)]
     tokens_in, info, *real = lax.optimization_barrier((tokens_in, info, *real))
+
     enc_weight = pltpu.with_memory_space_constraint(enc_weight, pltpu.HBM)
     dec_weight = pltpu.with_memory_space_constraint(dec_weight, pltpu.HBM)
 
@@ -372,13 +377,14 @@
                 held[rel ^ 2**bit_level][s] = over_members(held[rel][s], bit_level)
             known += [rel ^ 2**bit_level for rel in known]
     order = [rel for pair in sorted(held) for rel in (pair, pair ^ 1)]
-    enc_held, dec_held = fetch(enc_weight, after(dec_weight, held[0][1]))
-    early = [held[rel][s] for rel in order[2::2] for s in range(2)]
+    (enc_held,) = fetch(after(enc_weight, held[0][1]))
+    early = [held[rel][s] for rel in order[2::2] for s in range(feat_count - 1)]
     tokens = {0: after(jnp.stack(held[0], 0), enc_held, *early)}
     tokens[1] = over_members(tokens[0], 0)
     partial = encode(info, [0, 1], [tokens[0], tokens[1]], enc_held, None, None)
+    (dec_held,) = fetch(after(dec_weight, partial))
     for rel in order[2::2]:
-        tokens[rel] = jnp.stack([after(block, partial) for block in held[rel]], 0)
+        tokens[rel] = jnp.stack([after(block, dec_held) for block in held[rel]], 0)
         tokens[rel ^ 1] = over_members(tokens[rel], 0)
     for rel in order[2:-1]:
         partial = encode(info, [rel], [tokens[rel]], enc_held, partial, None)
@@ -389,7 +395,7 @@
         sent, kept = decode(info, source, dec_held, k, groups, rows, cols)
         for place in reversed(range(len(groups))):
             current[place, k] = add_pair(kept[place], over_members(sent[place], 0))
-        source = after(features, current[len(groups) - 1, k])
+        source = after(features, kept[-1])
     turns = sorted(current, reverse=True)
     joined = {}
     for bit_level in range(1, bit_count):
@@ -426,13 +432,16 @@
                 moved = to_layer(after(joined[k], *operands), k, sub_count, real)
             total = total + moved.astype(jnp.float32)
         for spot, block in enumerate(groups[place]):
-            if block == 0:
-                rebuilt = total[0, spot]
-            else:
-                operands.append(total[0, spot].astype(jnp.bfloat16))
-                blocks[block] = over_feat(operands[-1], block)
-    for block in reversed(blocks[1:]):
-        rebuilt = rebuilt + block.astype(jnp.float32)
+            blocks[block] = total[0, spot]
+            if place > 0:
+                operands.append(blocks[block].astype(jnp.bfloat16))
+    mask = 1
+    while mask < feat_count:
+        for s in range(0, feat_count, 2 * mask):
+            sent = blocks[s ^ mask].astype(jnp.bfloat16)
+            blocks[s] = blocks[s] + over_feat(sent, mask).astype(jnp.float32)
+        mask *= 2
+    rebuilt = blocks[0]
     turned_features = turned(source, 1)[0]
     turned_tokens = [
         turned(after(tokens[rel], turned_features).reshape(1, tok, cols), 1) for rel in order
@@ -445,8 +454,7 @@
     for level in range(bit_count - 1, 0, -1):
         known = [rel for stage in stages for rel in stage]
         stages.append([rel ^ 2**level for rel in known])
-    spans = [[s] for s in range(min(2, feat_count))]
-    spans += [list(range(2, feat_count))] if feat_count > 2 else []
+    spans = [list(range(feat_count // 2)), list(range(feat_count // 2, feat_count))]
     groups_of = {(0, k): [None] * len(spans) for k in range(layers)}
     early, last = [], len(spans) - 1
     for place, group in enumerate(spans):
@@ -470,30 +478,30 @@
             early.pop()
 
     feature_grad, dec_grad, squares = None, None, {}
-    for number, stage in enumerate(stages):
-        for k in range(layers):
-            for rel in stage:
-                parts = groups_of[rel, k]
-                if feature_grad is None:
-                    parts = [after(parts[0], *early)] + parts[1:]
+    other_rels = [rel for stage in stages[1:] for rel in stage]
+    for k in range(layers):
+        for rel in [rel for stage in stages for rel in stage]:
+            parts = groups_of[rel, k]
+            if feature_grad is None:
+                parts = [after(parts[0], *early)] + parts[1:]
+            else:
+                parts = [after(part, feature_grad) for part in parts]
+                if k == 0:
+                    coming = [groups_of[0, later][-1] for later in range(1, layers)]
                 else:
-                    parts = [after(part, feature_grad) for part in parts]
-                if k == 0 and number > 0:
-                    feature_grad = after(feature_grad, groups_of[rel, layers - 1][-1])
-                elif k > 0 and number + 1 < len(stages):
-                    coming = [groups_of[other, k - 1][-1] for other in stages[number + 1]]
-                    feature_grad = after(feature_grad, *coming)
-                feature_grad, dec_grad, squares[k, rel] = backward_pair(
-                    info,
-                    rel,
-                    k,
-                    parts,
-                    [over_members(part, 0) for part in parts],
-                    turned_features,
-                    dec_held,
-                    feature_grad,
-                    dec_grad,
-                )
+                    coming = [part for r in other_rels for part in groups_of[r, k]]
+                feature_grad = after(feature_grad, *coming)
+            feature_grad, dec_grad, squares[k, rel] = backward_pair(
+                info,
+                rel,
+                k,
+                parts,
+                [over_members(part, 0) for part in parts],
+                turned_features,
+                dec_held,
+                feature_grad,
+                dec_grad,
+            )
     scale = (tok / loss_scale) ** 2 / (layers * tok * depth)
     enc_grad, bias_grad, mean_square = encoder_grad(
         info,

time: 116 us -> 125 us (1.078)
  waiting for transfers between devices: 34.3 us -> 40.4 us
  starting transfers between devices: 44.2 us -> 46.1 us
    ppermute x34 -> x28, waiting for transfers between devices: 12.5 us -> 20.2 us  [over_members(): return lax.ppermute(value, 'layer', pairs)]
    ppermute x9, starting transfers between devices: 11.8 us -> 17.2 us  [over_feat(): return lax.ppermute(value, 'feat', pairs)]
    ppermute x34 -> x28, starting transfers between devices: 21.5 us -> 17.1 us  [over_members(): return lax.ppermute(value, 'layer', pairs)]
    ppermute x4 -> x3, waiting for transfers between devices: 4.15 us -> 0.55 us  [from_layer(): return lax.ppermute(value, 'layer', pairs)]
    ppermute x4, waiting for transfers between devices: 3.34 us -> 6.83 us  [to_layer(): moved = lax.ppermute(value, 'layer', pairs)]
    ppermute x9, waiting for transfers between devices: 14.3 us -> 12.8 us  [over_feat(): return lax.ppermute(value, 'feat', pairs)]
    ppermute x4 -> x3, starting transfers between devices: 4.62 us -> 5.91 us  [from_layer(): return lax.ppermute(value, 'layer', pairs)]
    pallas_call x1 -> x2, Pallas kernels: 4.74 us -> 5.71 us  [fetch(): pl.pallas_call(kernel, in_specs=[in_hbm] * len(arrays), out_specs=[in_vme...]
  transfers between devices with their start and end apart: 51 -> 44, of which waited for: 20 -> 22; matrix products, arithmetic and copies ran while one was open for 1% -> 1% of each run, Pallas kernels for 19% -> 16%
where the time goes in v2:
time: 125 us
  starting transfers between devices  46.1 us (37%)
  waiting for transfers between devices  40.4 us (32%)
  Pallas kernels  35.3 us (28%)
  other arithmetic  1.99 us (2%)
    ppermute x28, waiting for transfers between devices, over_members(): return lax.ppermute(value, 'layer', pairs)  20.2 us
    ppermute x9, starting transfers between devices, over_feat(): return lax.ppermute(value, 'feat', pairs)  17.2 us
    ppermute x28, starting transfers between devices, over_members(): return lax.ppermute(value, 'layer', pairs)  17.1 us
    pallas_call x4, Pallas kernels, backward_pair(): pl.pallas_call(kernel, in_specs=[in_smem] + [in_vmem] * (len(inputs) + 2)...  13.6 us
    ppermute x9, waiting for transfers between devices, over_feat(): return lax.ppermute(value, 'feat', pairs)  12.8 us
    ppermute x4, waiting for transfers between devices, to_layer(): moved = lax.ppermute(value, 'layer', pairs)  6.83 us
    ppermute x4, starting transfers between devices, to_layer(): moved = lax.ppermute(value, 'layer', pairs)  5.94 us
    ppermute x3, starting transfers between devices, from_layer(): return lax.ppermute(value, 'layer', pairs)  5.91 us
  transfers between devices with their start and end apart: 44, of which 22 were waited for; matrix products, arithmetic and copies ran while one was open for 1% of the time, Pallas kernels for 16%

profile of v2, /device:TPU:0, one launch (start us, length us, event | category | flops | bytes accessed | tf_op | source)
XLA Modules:
  0.0 125.2 jit_solution(5838416703922552293)
XLA Ops:
  0.7 4.1 %collective-permute-start.2 = (bf16[128,512]{1,0:T(8,128)(2,1)}, bf16[128,512]{1,0:T(8,128)(2,1)S(1)}, u32[]{:S(2)}, u32[]{:S(2)}) collective-permute-start(bf16[128,512]{1,0:T(8,128)(2,1)} %param.5), channel_id=1, source_target_pairs={{0,2},{1,3},{2,0},{3,1},{4,6},{5,7},{6,4},{7,5},{8,10},{9,11},{10,... | collective-permute-start | bytes 393224 | tf_op jit(solution)/shard_map/ppermute | solution.py:17
  4.8 1.6 %collective-permute-start.1 = (bf16[128,512]{1,0:T(8,128)(2,1)}, bf16[128,512]{1,0:T(8,128)(2,1)S(1)}, u32[]{:S(2)}, u32[]{:S(2)}) collective-permute-start(bf16[128,512]{1,0:T(8,128)(2,1)} %param.5), channel_id=1, source_target_pairs={{0,1},{1,0},{2,3},{3,2},{4,5},{5,4},{6,7},{7,6},{8,9},{9,8},{10,11... | collective-permute-start | bytes 393224 | tf_op jit(solution)/shard_map/ppermute | solution.py:17
  6.4 5.1 %collective-permute-done.2 = bf16[128,512]{1,0:T(8,128)(2,1)S(1)} collective-permute-done((bf16[128,512]{1,0:T(8,128)(2,1)}, bf16[128,512]{1,0:T(8,128)(2,1)S(1)}, u32[]{:S(2)}, u32[]{:S(2)}) %collective-permute-start.2) | collective-permute-done | bytes 131104 | tf_op jit(solution)/shard_map/ppermute | solution.py:17
  11.5 0.7 collective-permute-start.3
  12.1 1.5 %collective-permute-start = (bf16[128,512]{1,0:T(8,128)(2,1)}, bf16[128,512]{1,0:T(8,128)(2,1)S(1)}, u32[]{:S(2)}, u32[]{:S(2)}) collective-permute-start(bf16[128,512]{1,0:T(8,128)(2,1)} %param.5), channel_id=1, source_target_pairs={{0,8},{4,12},{8,0},{12,4},{16,24},{20,28},{24,16},{28,20},{1,9},{5... | collective-permute-start | bytes 393224 | tf_op jit(solution)/shard_map/ppermute | solution.py:23
  13.6 0.5 collective-permute-start.4
  14.2 1.5 %collective-permute-start.5 = (bf16[128,512]{1,0:T(8,128)(2,1)S(1)}, bf16[128,512]{1,0:T(8,128)(2,1)S(1)}, u32[]{:S(2)}, u32[]{:S(2)}) collective-permute-start(bf16[128,512]{1,0:T(8,128)(2,1)S(1)} %collective-permute-done.2), channel_id=1, source_target_pairs={{0,8},{4,12},{8,0},{12,4},{16,24},{20,28},{24,16},{28,20},{1,9},{5... | collective-permute-start | bytes 393224 | tf_op jit(solution)/shard_map/ppermute | solution.py:23
  15.6 2.2 %fetch.2.refs_2_.refs_1_ = bf16[2048,1024]{1,0:T(8,128)(2,1)S(1)} custom-call(bf16[2048,1024]{1,0:T(8,128)(2,1)} %refs_0_), custom_call_target="tpu_custom_call" | custom-call | bytes 4194304 | tf_op jit(solution)/shard_map/fetch/pallas_call | solution.py:91
  18.0 0.8 collective-permute-done
  18.7 2.8 %collective-permute-done.4 = bf16[128,512]{1,0:T(8,128)(2,1)S(1)} collective-permute-done((bf16[128,512]{1,0:T(8,128)(2,1)S(1)}, bf16[128,512]{1,0:T(8,128)(2,1)S(1)}, u32[]{:S(2)}, u32[]{:S(2)}) %collective-permute-start.4) | collective-permute-done | bytes 131104 | tf_op jit(solution)/shard_map/ppermute | solution.py:23
  21.5 1.5 %collective-permute-done.5 = bf16[128,512]{1,0:T(8,128)(2,1)S(1)} collective-permute-done((bf16[128,512]{1,0:T(8,128)(2,1)S(1)}, bf16[128,512]{1,0:T(8,128)(2,1)S(1)}, u32[]{:S(2)}, u32[]{:S(2)}) %collective-permute-start.5) | collective-permute-done | bytes 131104 | tf_op jit(solution)/shard_map/ppermute | solution.py:23
  23.1 1.5 %collective-permute-start.7 = (bf16[128,512]{1,0:T(8,128)(2,1)S(1)}, bf16[128,512]{1,0:T(8,128)(2,1)S(1)}, u32[]{:S(2)}, u32[]{:S(2)}) collective-permute-start(bf16[128,512]{1,0:T(8,128)(2,1)S(1)} %collective-permute-done.3), channel_id=1, source_target_pairs={{0,8},{4,12},{8,0},{12,4},{16,24},{20,28},{24,16},{28,20},{1,9},{5... | collective-permute-start | bytes 393224 | tf_op jit(solution)/shard_map/ppermute | solution.py:23
  24.6 0.4 collective-permute-done.6.refs_1_
  25.0 1.8 %encode.3.refs_2_ = f32[512,1024]{1,0:T(8,128)S(1)} custom-call(s32[2]{0:T(128)S(1)} %pad_add_fusion.info_ref, bf16[4,128,512]{2,1,0:T(8,128)(2,1)S(1)} %pad_maximum_fusion.refs_0_, bf16[4,128,512]{2,1,0:T(8,128)(2,1)S(1)} %collective-permute-done.6.refs_1_, bf16[2048,1024]{1,0:T(8,128)(2,1)S(1)} %fetch.2.refs_2_.refs_1_), custom_call_target="tpu_custom_call" | custom-call | flops 1073741824 | bytes 3145728 | tf_op jit(solution)/shard_map/encode/pallas_call | solution.py:131
  26.8 3.5 %fetch.3.weight_ref.refs_5_ = bf16[2,1024,2048]{2,1,0:T(8,128)(2,1)S(1)} custom-call(bf16[2,1024,2048]{2,1,0:T(8,128)(2,1)} %refs_0_.1), custom_call_target="tpu_custom_call" | custom-call | bytes 8388608 | tf_op jit(solution)/shard_map/fetch/pallas_call | solution.py:91
  30.6 1.3 %encode.4.refs_2_ = f32[512,1024]{1,0:T(8,128)S(1)} custom-call(s32[2]{0:T(128)S(1)} %pad_add_fusion.info_ref, bf16[4,128,512]{2,1,0:T(8,128)(2,1)S(1)} %pad_maximum_fusion.1.refs_0_, bf16[2048,1024]{1,0:T(8,128)(2,1)S(1)} %fetch.2.refs_2_.refs_1_, f32[512,1024]{1,0:T(8,128)S(1)} %encode.3.refs_2_), custom_call_target="tpu_custom_call" | custom-call | flops 536870912 | bytes 1572864 | tf_op jit(solution)/shard_map/encode/pallas_call | solution.py:131
  31.9 0.5 collective-permute-done.8.refs_0_
  32.4 1.4 %encode.5.feat_ref.in_ref.refs_4_ = bf16[2,512,1024]{2,1,0:T(8,128)(2,1)S(1)} custom-call(s32[2]{0:T(128)S(1)} %pad_add_fusion.info_ref, bf16[4,128,512]{2,1,0:T(8,128)(2,1)S(1)} %collective-permute-done.8.refs_0_, bf16[2048,1024]{1,0:T(8,128)(2,1)S(1)} %fetch.2.refs_2_.refs_1_, f32[512,1024]{1,0:T(8,128)S(1)} %encode.4.refs_2_, f32[1,1024]{1,0:T(1,128)S(1)} %bitcast.115), custom_call_target="tpu_custom_call" | custom-call | flops 536870912 | bytes 1572864 | tf_op jit(solution)/shard_map/encode/pallas_call | solution.py:131
  33.8 2.9 %decode.2 = (bf16[2,2,128,512]{3,2,1,0:T(8,128)(2,1)S(1)}, bf16[2,1,128,512]{3,2,1,0:T(8,128)(2,1)S(1)}, bf16[2,1,128,512]{3,2,1,0:T(8,128)(2,1)S(1)}, bf16[2,2,...) custom-call(s32[2]{0:T(128)S(1)} %pad_add_fusion.info_ref, ...), custom_call_target="tpu_custom_call" | custom-call | flops 2147483648 | bytes 4194304 | tf_op jit(solution)/shard_map/decode/pallas_call | solution.py:169
  36.9 0.4 collective-permute-start.10
  37.3 2.9 %decode.3 = (bf16[2,2,128,512]{3,2,1,0:T(8,128)(2,1)S(1)}, bf16[2,1,128,512]{3,2,1,0:T(8,128)(2,1)S(1)}, bf16[2,1,128,512]{3,2,1,0:T(8,128)(2,1)S(1)}, bf16[2,2,...) custom-call(s32[2]{0:T(128)S(1)} %pad_add_fusion.info_ref, ...), custom_call_target="tpu_custom_call" | custom-call | flops 2147483648 | bytes 4194304 | tf_op jit(solution)/shard_map/decode/pallas_call | solution.py:169
  40.4 0.4 collective-permute-start.13
  40.9 0.4 collective-permute-start.17
  41.4 0.4 collective-permute-done.11
  41.8 1.5 %collective-permute-start.15 = (bf16[1,1,128,512]{3,2,1,0:T(8,128)(2,1)S(1)}, bf16[1,1,128,512]{3,2,1,0:T(8,128)(2,1)S(1)}, u32[]{:S(2)}, u32[]{:S(2)}) collective-permute-start(bf16[1,1,128,512]{3,2,1,0:T(8,128)(2,1)S(1)} %slice_bitcast_fusion.10), channel_id=1, source_target_pairs={{0,8},{4,12},{8,0},{12,4},{16,24},{20,28},{24,16},{28,20},{1,9},{5... | collective-permute-start | bytes 393224 | tf_op jit(solution)/shard_map/ppermute | solution.py:23
  43.4 0.6 collective-permute-start.18
  44.2 4.0 %collective-permute-done.15 = bf16[1,1,128,512]{3,2,1,0:T(8,128)(2,1)S(1)} collective-permute-done((bf16[1,1,128,512]{3,2,1,0:T(8,128)(2,1)S(1)}, bf16[1,1,128,512]{3,2,1,0:T(8,128)(2,1)S(1)}, u32[]{:S(2)}, u32[]{:S(2)}) %collective-permute-start.15) | collective-permute-done | bytes 131104 | tf_op jit(solution)/shard_map/ppermute | solution.py:23
  48.2 1.6 %collective-permute-start.20 = (bf16[1,1,128,512]{3,2,1,0:T(8,128)(2,1)S(1)}, bf16[1,1,128,512]{3,2,1,0:T(8,128)(2,1)S(1)}, u32[]{:S(2)}, u32[]{:S(2)}) collective-permute-start(bf16[1,1,128,512]{3,2,1,0:T(8,128)(2,1)S(1)} %fusion.16), channel_id=1, source_target_pairs={{0,16},{4,20},{8,24},{12,28},{16,0},{20,4},{24,8},{28,12},{1,17},{... | collective-permute-start | bytes 393224 | tf_op jit(solution)/shard_map/ppermute | solution.py:29
  49.8 1.6 %collective-permute-start.16 = (bf16[1,1,128,512]{3,2,1,0:T(8,128)(2,1)S(1)}, bf16[1,1,128,512]{3,2,1,0:T(8,128)(2,1)S(1)}, u32[]{:S(2)}, u32[]{:S(2)}) collective-permute-start(bf16[1,1,128,512]{3,2,1,0:T(8,128)(2,1)S(1)} %slice_bitcast_fusion.11), channel_id=1, source_target_pairs={{0,8},{4,12},{8,0},{12,4},{16,24},{20,28},{24,16},{28,20},{1,9},{5... | collective-permute-start | bytes 393224 | tf_op jit(solution)/shard_map/ppermute | solution.py:23
  51.3 0.5 collective-permute-start.23
  51.9 1.3 %collective-permute-done.20 = bf16[1,1,128,512]{3,2,1,0:T(8,128)(2,1)S(1)} collective-permute-done((bf16[1,1,128,512]{3,2,1,0:T(8,128)(2,1)S(1)}, bf16[1,1,128,512]{3,2,1,0:T(8,128)(2,1)S(1)}, u32[]{:S(2)}, u32[]{:S(2)}) %collective-permute-start.20) | collective-permute-done | bytes 131104 | tf_op jit(solution)/shard_map/ppermute | solution.py:29
  53.3 0.4 collective-permute-start.25
  53.9 1.5 %collective-permute-start.12 = (bf16[1,2,128,512]{3,2,1,0:T(8,128)(2,1)S(1)}, bf16[1,2,128,512]{3,2,1,0:T(8,128)(2,1)S(1)}, u32[]{:S(2)}, u32[]{:S(2)}) collective-permute-start(bf16[1,2,128,512]{3,2,1,0:T(8,128)(2,1)S(1)} %get-tuple-element.86), channel_id=1, source_target_pairs={{0,16},{4,20},{8,24},{12,28},{16,0},{20,4},{24,8},{28,12},{1,17},{... | collective-permute-start | bytes 786440 | tf_op jit(solution)/shard_map/ppermute | solution.py:29
  55.4 1.1 collective-permute-start.24
  56.7 4.3 %collective-permute-done.12 = bf16[1,2,128,512]{3,2,1,0:T(8,128)(2,1)S(1)} collective-permute-done((bf16[1,2,128,512]{3,2,1,0:T(8,128)(2,1)S(1)}, bf16[1,2,128,512]{3,2,1,0:T(8,128)(2,1)S(1)}, u32[]{:S(2)}, u32[]{:S(2)}) %collective-permute-start.12) | collective-permute-done | bytes 262176 | tf_op jit(solution)/shard_map/ppermute | solution.py:29
  61.1 2.3 %collective-permute-start.19 = (bf16[1,2,128,512]{3,2,1,0:T(8,128)(2,1)S(1)}, bf16[1,2,128,512]{3,2,1,0:T(8,128)(2,1)S(1)}, u32[]{:S(2)}, u32[]{:S(2)}) collective-permute-start(bf16[1,2,128,512]{3,2,1,0:T(8,128)(2,1)S(1)} %fusion.2), channel_id=1, source_target_pairs={{0,8},{4,12},{8,0},{12,4},{16,24},{20,28},{24,16},{28,20},{1,9},{5... | collective-permute-start | bytes 786440 | tf_op jit(solution)/shard_map/ppermute | solution.py:23
  63.4 1.8 %collective-permute-start.21 = (bf16[1,2,128,512]{3,2,1,0:T(8,128)(2,1)S(1)}, bf16[1,2,128,512]{3,2,1,0:T(8,128)(2,1)S(1)}, u32[]{:S(2)}, u32[]{:S(2)}) collective-permute-start(bf16[1,2,128,512]{3,2,1,0:T(8,128)(2,1)S(1)} %get-tuple-element.97), channel_id=1, source_target_pairs={{0,16},{4,20},{8,24},{12,28},{16,0},{20,4},{24,8},{28,12},{1,17},{... | collective-permute-start | bytes 786440 | tf_op jit(solution)/shard_map/ppermute | solution.py:29
  65.2 3.3 %collective-permute-start.26 = (bf16[128,512]{1,0:T(8,128)(2,1)S(1)}, bf16[128,512]{1,0:T(8,128)(2,1)S(1)}, u32[]{:S(2)}, u32[]{:S(2)}) collective-permute-start(bf16[128,512]{1,0:T(8,128)(2,1)S(1)} %fusion.15), channel_id=1, source_target_pairs={{0,2},{1,3},{2,0},{3,1},{4,6},{5,7},{6,4},{7,5},{8,10},{9,11},{10,... | collective-permute-start | bytes 393224 | tf_op jit(solution)/shard_map/ppermute | solution.py:17
  68.6 1.1 collective-permute-done.21
  69.9 1.6 %collective-permute-start.22 = (bf16[128,512]{1,0:T(8,128)(2,1)S(1)}, bf16[128,512]{1,0:T(8,128)(2,1)S(1)}, u32[]{:S(2)}, u32[]{:S(2)}) collective-permute-start(bf16[128,512]{1,0:T(8,128)(2,1)S(1)} %fusion.20), channel_id=1, source_target_pairs={{0,1},{1,0},{2,3},{3,2},{4,5},{5,4},{6,7},{7,6},{8,9},{9,8},{10,11... | collective-permute-start | bytes 393224 | tf_op jit(solution)/shard_map/ppermute | solution.py:17
  71.5 0.3 turned.5
  72.6 2.9 %collective-permute-done.22 = bf16[128,512]{1,0:T(8,128)(2,1)S(1)} collective-permute-done((bf16[128,512]{1,0:T(8,128)(2,1)S(1)}, bf16[128,512]{1,0:T(8,128)(2,1)S(1)}, u32[]{:S(2)}, u32[]{:S(2)}) %collective-permute-start.22) | collective-permute-done | bytes 131104 | tf_op jit(solution)/shard_map/ppermute | solution.py:17
  75.5 0.8 multiply_convert_fusion
  76.3 1.7 %collective-permute-start.27 = (bf16[128,512]{1,0:T(8,128)(2,1)S(1)}, bf16[128,512]{1,0:T(8,128)(2,1)S(1)}, u32[]{:S(2)}, u32[]{:S(2)}) collective-permute-start(bf16[128,512]{1,0:T(8,128)(2,1)S(1)} %get-tuple-element.131), channel_id=1, source_target_pairs={{0,1},{1,0},{2,3},{3,2},{4,5},{5,4},{6,7},{7,6},{8,9},{9,8},{10,11... | collective-permute-start | bytes 393224 | tf_op jit(solution)/shard_map/ppermute | solution.py:17
  78.0 3.6 %collective-permute-start.31 = (bf16[128,512]{1,0:T(8,128)(2,1)S(1)}, bf16[128,512]{1,0:T(8,128)(2,1)S(1)}, u32[]{:S(2)}, u32[]{:S(2)}) collective-permute-start(bf16[128,512]{1,0:T(8,128)(2,1)S(1)} %get-tuple-element.131), channel_id=1, source_target_pairs={{0,2},{1,3},{2,0},{3,1},{4,6},{5,7},{6,4},{7,5},{8,10},{9,11},{10,... | collective-permute-start | bytes 393224 | tf_op jit(solution)/shard_map/ppermute | solution.py:17
  81.7 5.8 %collective-permute-start.28 = (bf16[2,128,512]{2,1,0:T(8,128)(2,1)S(1)}, bf16[2,128,512]{2,1,0:T(8,128)(2,1)S(1)}, u32[]{:S(2)}, u32[]{:S(2)}) collective-permute-start(bf16[2,128,512]{2,1,0:T(8,128)(2,1)S(1)} %pad_maximum_fusion.2.refs_0_), channel_id=1, source_target_pairs={{0,16},{4,20},{8,24},{12,28},{16,0},{20,4},{24,8},{28,12},{1,17},{... | collective-permute-start | bytes 786440 | tf_op jit(solution)/shard_map/ppermute | solution.py:36
  87.6 4.8 %collective-permute-done.32 = bf16[128,512]{1,0:T(8,128)(2,1)S(1)} collective-permute-done((bf16[128,512]{1,0:T(8,128)(2,1)S(1)}, bf16[128,512]{1,0:T(8,128)(2,1)S(1)}, u32[]{:S(2)}, u32[]{:S(2)}) %collective-permute-start.32) | collective-permute-done | bytes 131104 | tf_op jit(solution)/shard_map/ppermute | solution.py:17
  92.5 1.3 %collective-permute-done.30.refs_0_ = bf16[2,128,512]{2,1,0:T(8,128)(2,1)S(1)} collective-permute-done((bf16[2,128,512]{2,1,0:T(8,128)(2,1)S(1)}, bf16[2,128,512]{2,1,0:T(8,128)(2,1)S(1)}, u32[]{:S(2)}, u32[]{:S(2)}) %collective-permute-start.30) | collective-permute-done | bytes 262176 | tf_op jit(solution)/shard_map/ppermute | solution.py:23
  93.8 1.2 collective-permute-start.35
  95.3 3.3 %backward_pair.4 = (f32[512,1024]{1,0:T(8,128)S(1)}, bf16[2,1024,2048]{2,1,0:T(8,128)(2,1)}, f32[8,128]{1,0:T(8,128)S(1)}) custom-call(s32[2]{0:T(128)S(1)} %pad_add_fusion.info_ref, bf16[2,128,512]{2,1,0:T(8,128)(2,1)S(1)} %pad_maximum_fusion.2.refs_0_, bf16[2,128,512]{2,1,0:T(8,128)(2,1)S(1)} %pad_maximum_fusion.3.refs_1_, ...), custom_call_target="tpu_custom_call" | custom-call | flops 262144 | bytes 262144 | tf_op jit(solution)/shard_map/backward_pair/pallas_call | solution.py:273
  98.7 3.8 %collective-permute-done.35.refs_1_ = bf16[2,128,512]{2,1,0:T(8,128)(2,1)S(1)} collective-permute-done((bf16[2,128,512]{2,1,0:T(8,128)(2,1)S(1)}, bf16[2,128,512]{2,1,0:T(8,128)(2,1)S(1)}, u32[]{:S(2)}, u32[]{:S(2)}) %collective-permute-start.35) | collective-permute-done | bytes 262176 | tf_op jit(solution)/shard_map/ppermute | solution.py:23
  102.5 0.5 collective-permute-start.36
  103.0 0.8 collective-permute-start.29
  104.0 0.4 collective-permute-done.36.refs_2_
  104.4 3.7 %backward_pair.5 = (f32[512,1024]{1,0:T(8,128)S(1)}, bf16[2,1024,2048]{2,1,0:T(8,128)(2,1)}, f32[8,128]{1,0:T(8,128)S(1)}) custom-call(s32[2]{0:T(128)S(1)} %pad_add_fusion.info_ref, bf16[2,128,512]{2,1,0:T(8,128)(2,1)S(1)} %collective-permute-done.30.refs_0_, ...), custom_call_target="tpu_custom_call", output_to_operand_aliasing={{0}: (7, {}), {1}: (8, {})} | custom-call | flops 262144 | bytes 262144 | tf_op jit(solution)/shard_map/backward_pair/pallas_call | solution.py:273
  108.4 0.4 collective-permute-start.39
  108.7 2.5 %collective-permute-done.29.refs_0_ = bf16[2,128,512]{2,1,0:T(8,128)(2,1)S(1)} collective-permute-done((bf16[2,128,512]{2,1,0:T(8,128)(2,1)S(1)}, bf16[2,128,512]{2,1,0:T(8,128)(2,1)S(1)}, u32[]{:S(2)}, u32[]{:S(2)}) %collective-permute-start.29) | collective-permute-done | bytes 262176 | tf_op jit(solution)/shard_map/ppermute | solution.py:23
  111.2 0.5 collective-permute-done.41.refs_1_
  111.8 3.3 %backward_pair.6 = (f32[512,1024]{1,0:T(8,128)S(1)}, bf16[2,1024,2048]{2,1,0:T(8,128)(2,1)}, f32[8,128]{1,0:T(8,128)S(1)}) custom-call(s32[2]{0:T(128)S(1)} %pad_add_fusion.info_ref, bf16[2,128,512]{2,1,0:T(8,128)(2,1)S(1)} %collective-permute-done.28.refs_0_, ...), custom_call_target="tpu_custom_call", output_to_operand_aliasing={{0}: (7, {}), {1}: (8, {})} | custom-call | flops 262144 | bytes 262144 | tf_op jit(solution)/shard_map/backward_pair/pallas_call | solution.py:273
  115.1 0.5 collective-permute-start.42
  115.6 1.0 collective-permute-done.43.refs_3_
  116.7 0.4 collective-permute-done.42.refs_2_
  117.0 3.3 %backward_pair.7 = (f32[512,1024]{1,0:T(8,128)S(1)}, bf16[2,1024,2048]{2,1,0:T(8,128)(2,1)}, f32[8,128]{1,0:T(8,128)S(1)}) custom-call(s32[2]{0:T(128)S(1)} %pad_add_fusion.info_ref, bf16[2,128,512]{2,1,0:T(8,128)(2,1)S(1)} %collective-permute-done.29.refs_0_, ...), custom_call_target="tpu_custom_call", output_to_operand_aliasing={{0}: (7, {}), {1}: (8, {})} | custom-call | flops 262144 | bytes 262144 | tf_op jit(solution)/shard_map/backward_pair/pallas_call | solution.py:273
  120.3 4.7 %encoder_grad.1 = (bf16[2048,1024]{1,0:T(8,128)(2,1)}, f32[1,1024]{1,0:T(1,128)}, f32[1,1]{1,0:T(1,128)}) custom-call(s32[2]{0:T(128)S(1)} %pad_add_fusion.info_ref, bf16[1,512,512]{2,1,0:T(8,128)(2,1)S(1)} %turned.6.refs_0_, bf16[1,512,512]{2,1,0:T(8,128)(2,1)S(1)} %turned.7.refs_1_, bf16[1,512,512]{2,1,0:T(8,128)(2,1)S(1)} %turned.8.refs_2_, ...), custom_call_target="tpu_custom_call" | custom-call | flops 2147483648 | bytes 9437184 | tf_op jit(solution)/shard_map/encoder_grad/pallas_call | solution.py:325
  (71 shorter events, 3.9 us)
Async XLA Ops:
  0.7 17.1 %copy-start.1 = (bf16[128,512]{1,0:T(8,128)(2,1)S(1)}, bf16[128,512]{1,0:T(8,128)(2,1)}, u32[]{:S(2)}) copy-start(bf16[128,512]{1,0:T(8,128)(2,1)} %param.5) | copy-start | bytes 393220
  0.7 10.7 %collective-permute-start.2 = (bf16[128,512]{1,0:T(8,128)(2,1)}, bf16[128,512]{1,0:T(8,128)(2,1)S(1)}, u32[]{:S(2)}, u32[]{:S(2)}) collective-permute-start(bf16[128,512]{1,0:T(8,128)(2,1)} %param.5), channel_id=1, source_target_pairs={{0,2},{1,3},{2,0},{3,1},{4,6},{5,7},{6,4},{7,5},{8,10},{9,11},{10,... | collective-permute-start | bytes 393224 | tf_op jit(solution)/shard_map/ppermute | solution.py:17
  4.8 8.8 %collective-permute-start.1 = (bf16[128,512]{1,0:T(8,128)(2,1)}, bf16[128,512]{1,0:T(8,128)(2,1)S(1)}, u32[]{:S(2)}, u32[]{:S(2)}) collective-permute-start(bf16[128,512]{1,0:T(8,128)(2,1)} %param.5), channel_id=1, source_target_pairs={{0,1},{1,0},{2,3},{3,2},{4,5},{5,4},{6,7},{7,6},{8,9},{9,8},{10,11... | collective-permute-start | bytes 393224 | tf_op jit(solution)/shard_map/ppermute | solution.py:17
  11.5 6.4 %collective-permute-start.3 = (bf16[128,512]{1,0:T(8,128)(2,1)S(1)}, bf16[128,512]{1,0:T(8,128)(2,1)S(1)}, u32[]{:S(2)}, u32[]{:S(2)}) collective-permute-start(bf16[128,512]{1,0:T(8,128)(2,1)S(1)} %collective-permute-done.2), channel_id=1, source_target_pairs={{0,1},{1,0},{2,3},{3,2},{4,5},{5,4},{6,7},{7,6},{8,9},{9,8},{10,11... | collective-permute-start | bytes 393224 | tf_op jit(solution)/shard_map/ppermute | solution.py:17
  12.1 6.6 %collective-permute-start = (bf16[128,512]{1,0:T(8,128)(2,1)}, bf16[128,512]{1,0:T(8,128)(2,1)S(1)}, u32[]{:S(2)}, u32[]{:S(2)}) collective-permute-start(bf16[128,512]{1,0:T(8,128)(2,1)} %param.5), channel_id=1, source_target_pairs={{0,8},{4,12},{8,0},{12,4},{16,24},{20,28},{24,16},{28,20},{1,9},{5... | collective-permute-start | bytes 393224 | tf_op jit(solution)/shard_map/ppermute | solution.py:23
  13.6 7.9 %collective-permute-start.4 = (bf16[128,512]{1,0:T(8,128)(2,1)S(1)}, bf16[128,512]{1,0:T(8,128)(2,1)S(1)}, u32[]{:S(2)}, u32[]{:S(2)}) collective-permute-start(bf16[128,512]{1,0:T(8,128)(2,1)S(1)} %collective-permute-done.1), channel_id=1, source_target_pairs={{0,8},{4,12},{8,0},{12,4},{16,24},{20,28},{24,16},{28,20},{1,9},{5... | collective-permute-start | bytes 393224 | tf_op jit(solution)/shard_map/ppermute | solution.py:23
  14.2 8.9 %collective-permute-start.5 = (bf16[128,512]{1,0:T(8,128)(2,1)S(1)}, bf16[128,512]{1,0:T(8,128)(2,1)S(1)}, u32[]{:S(2)}, u32[]{:S(2)}) collective-permute-start(bf16[128,512]{1,0:T(8,128)(2,1)S(1)} %collective-permute-done.2), channel_id=1, source_target_pairs={{0,8},{4,12},{8,0},{12,4},{16,24},{20,28},{24,16},{28,20},{1,9},{5... | collective-permute-start | bytes 393224 | tf_op jit(solution)/shard_map/ppermute | solution.py:23
  23.1 1.9 %collective-permute-start.6 = (bf16[4,128,512]{2,1,0:T(8,128)(2,1)S(1)}, bf16[4,128,512]{2,1,0:T(8,128)(2,1)S(1)}, u32[]{:S(2)}, u32[]{:S(2)}) collective-permute-start(bf16[4,128,512]{2,1,0:T(8,128)(2,1)S(1)} %pad_maximum_fusion.refs_0_), channel_id=1, source_target_pairs={{0,4},{4,0},{8,12},{12,8},{16,20},{20,16},{24,28},{28,24},{1,5},{5... | collective-permute-start | bytes 1572872 | tf_op jit(solution)/shard_map/ppermute | solution.py:23
  23.1 7.2 %collective-permute-start.7 = (bf16[128,512]{1,0:T(8,128)(2,1)S(1)}, bf16[128,512]{1,0:T(8,128)(2,1)S(1)}, u32[]{:S(2)}, u32[]{:S(2)}) collective-permute-start(bf16[128,512]{1,0:T(8,128)(2,1)S(1)} %collective-permute-done.3), channel_id=1, source_target_pairs={{0,8},{4,12},{8,0},{12,4},{16,24},{20,28},{24,16},{28,20},{1,9},{5... | collective-permute-start | bytes 393224 | tf_op jit(solution)/shard_map/ppermute | solution.py:23
  30.4 2.0 %copy-start = (f32[1024]{0:T(1024)S(1)}, f32[1024]{0:T(1024)}, u32[]{:S(2)}) copy-start(f32[1024]{0:T(1024)} %param.8) | copy-start | bytes 12292
  30.4 2.0 %collective-permute-start.8 = (bf16[4,128,512]{2,1,0:T(8,128)(2,1)S(1)}, bf16[4,128,512]{2,1,0:T(8,128)(2,1)S(1)}, u32[]{:S(2)}, u32[]{:S(2)}) collective-permute-start(bf16[4,128,512]{2,1,0:T(8,128)(2,1)S(1)} %pad_maximum_fusion.1.refs_0_), channel_id=1, source_target_pairs={{0,4},{4,0},{8,12},{12,8},{16,20},{20,16},{24,28},{28,24},{1,5},{5... | collective-permute-start | bytes 1572872 | tf_op jit(solution)/shard_map/ppermute | solution.py:23
  36.7 4.2 %collective-permute-start.14 = (bf16[2,1,128,512]{3,2,0,1:T(8,128)(2,1)S(1)}, bf16[2,1,128,512]{3,2,0,1:T(8,128)(2,1)S(1)}, u32[]{:S(2)}, u32[]{:S(2)}) collective-permute-start(bf16[2,1,128,512]{3,2,0,1:T(8,128)(2,1)S(1)} %bitcast.118), channel_id=1, source_target_pairs={{0,4},{4,0},{8,12},{12,8},{16,20},{20,16},{24,28},{28,24},{1,5},{5... | collective-permute-start | bytes 786440 | tf_op jit(solution)/shard_map/ppermute | solution.py:23
  36.9 16.7 %collective-permute-start.10 = (bf16[2,2,128,512]{3,2,1,0:T(8,128)(2,1)S(1)}, bf16[2,2,128,512]{3,2,1,0:T(8,128)(2,1)S(1)}, u32[]{:S(2)}, u32[]{:S(2)}) collective-permute-start(bf16[2,2,128,512]{3,2,1,0:T(8,128)(2,1)S(1)} %get-tuple-element.83), channel_id=1, source_target_pairs={{0,4},{4,0},{8,12},{12,8},{16,20},{20,16},{24,28},{28,24},{1,5},{5... | collective-permute-start | bytes 1572872 | tf_op jit(solution)/shard_map/ppermute | solution.py:23
  40.2 1.6 %collective-permute-start.11 = (bf16[2,1,128,512]{3,2,0,1:T(8,128)(2,1)S(1)}, bf16[2,1,128,512]{3,2,0,1:T(8,128)(2,1)S(1)}, u32[]{:S(2)}, u32[]{:S(2)}) collective-permute-start(bf16[2,1,128,512]{3,2,0,1:T(8,128)(2,1)S(1)} %bitcast.119), channel_id=1, source_target_pairs={{0,4},{4,0},{8,12},{12,8},{16,20},{20,16},{24,28},{28,24},{1,5},{5... | collective-permute-start | bytes 786440 | tf_op jit(solution)/shard_map/ppermute | solution.py:23
  40.4 3.0 %collective-permute-start.13 = (bf16[2,1,128,512]{3,2,0,1:T(8,128)(2,1)S(1)}, bf16[2,1,128,512]{3,2,0,1:T(8,128)(2,1)S(1)}, u32[]{:S(2)}, u32[]{:S(2)}) collective-permute-start(bf16[2,1,128,512]{3,2,0,1:T(8,128)(2,1)S(1)} %bitcast.116), channel_id=1, source_target_pairs={{0,4},{4,0},{8,12},{12,8},{16,20},{20,16},{24,28},{28,24},{1,5},{5... | collective-permute-start | bytes 786440 | tf_op jit(solution)/shard_map/ppermute | solution.py:23
  40.8 15.7 %collective-permute-start.9 = (bf16[2,2,128,512]{3,2,1,0:T(8,128)(2,1)S(1)}, bf16[2,2,128,512]{3,2,1,0:T(8,128)(2,1)S(1)}, u32[]{:S(2)}, u32[]{:S(2)}) collective-permute-start(bf16[2,2,128,512]{3,2,1,0:T(8,128)(2,1)S(1)} %get-tuple-element.80), channel_id=1, source_target_pairs={{0,4},{4,0},{8,12},{12,8},{16,20},{20,16},{24,28},{28,24},{1,5},{5... | collective-permute-start | bytes 1572872 | tf_op jit(solution)/shard_map/ppermute | solution.py:23
  40.9 3.1 %collective-permute-start.17 = (bf16[2,1,128,512]{3,2,0,1:T(8,128)(2,1)S(1)}, bf16[2,1,128,512]{3,2,0,1:T(8,128)(2,1)S(1)}, u32[]{:S(2)}, u32[]{:S(2)}) collective-permute-start(bf16[2,1,128,512]{3,2,0,1:T(8,128)(2,1)S(1)} %bitcast.117), channel_id=1, source_target_pairs={{0,4},{4,0},{8,12},{12,8},{16,20},{20,16},{24,28},{28,24},{1,5},{5... | collective-permute-start | bytes 786440 | tf_op jit(solution)/shard_map/ppermute | solution.py:23
  41.8 6.3 %collective-permute-start.15 = (bf16[1,1,128,512]{3,2,1,0:T(8,128)(2,1)S(1)}, bf16[1,1,128,512]{3,2,1,0:T(8,128)(2,1)S(1)}, u32[]{:S(2)}, u32[]{:S(2)}) collective-permute-start(bf16[1,1,128,512]{3,2,1,0:T(8,128)(2,1)S(1)} %slice_bitcast_fusion.10), channel_id=1, source_target_pairs={{0,8},{4,12},{8,0},{12,4},{16,24},{20,28},{24,16},{28,20},{1,9},{5... | collective-permute-start | bytes 393224 | tf_op jit(solution)/shard_map/ppermute | solution.py:23
  43.4 7.9 %collective-permute-start.18 = (bf16[1,1,128,512]{3,2,1,0:T(8,128)(2,1)S(1)}, bf16[1,1,128,512]{3,2,1,0:T(8,128)(2,1)S(1)}, u32[]{:S(2)}, u32[]{:S(2)}) collective-permute-start(bf16[1,1,128,512]{3,2,1,0:T(8,128)(2,1)S(1)} %slice_bitcast_fusion.12), channel_id=1, source_target_pairs={{0,8},{4,12},{8,0},{12,4},{16,24},{20,28},{24,16},{28,20},{1,9},{5... | collective-permute-start | bytes 393224 | tf_op jit(solution)/shard_map/ppermute | solution.py:23
  48.2 5.0 %collective-permute-start.20 = (bf16[1,1,128,512]{3,2,1,0:T(8,128)(2,1)S(1)}, bf16[1,1,128,512]{3,2,1,0:T(8,128)(2,1)S(1)}, u32[]{:S(2)}, u32[]{:S(2)}) collective-permute-start(bf16[1,1,128,512]{3,2,1,0:T(8,128)(2,1)S(1)} %fusion.16), channel_id=1, source_target_pairs={{0,16},{4,20},{8,24},{12,28},{16,0},{20,4},{24,8},{28,12},{1,17},{... | collective-permute-start | bytes 393224 | tf_op jit(solution)/shard_map/ppermute | solution.py:29
  49.8 5.6 %collective-permute-start.16 = (bf16[1,1,128,512]{3,2,1,0:T(8,128)(2,1)S(1)}, bf16[1,1,128,512]{3,2,1,0:T(8,128)(2,1)S(1)}, u32[]{:S(2)}, u32[]{:S(2)}) collective-permute-start(bf16[1,1,128,512]{3,2,1,0:T(8,128)(2,1)S(1)} %slice_bitcast_fusion.11), channel_id=1, source_target_pairs={{0,8},{4,12},{8,0},{12,4},{16,24},{20,28},{24,16},{28,20},{1,9},{5... | collective-permute-start | bytes 393224 | tf_op jit(solution)/shard_map/ppermute | solution.py:23
  51.3 13.8 %collective-permute-start.23 = (bf16[1,1,128,512]{3,2,1,0:T(8,128)(2,1)S(1)}, bf16[1,1,128,512]{3,2,1,0:T(8,128)(2,1)S(1)}, u32[]{:S(2)}, u32[]{:S(2)}) collective-permute-start(bf16[1,1,128,512]{3,2,1,0:T(8,128)(2,1)S(1)} %slice_bitcast_fusion.9), channel_id=1, source_target_pairs={{0,8},{4,12},{8,0},{12,4},{16,24},{20,28},{24,16},{28,20},{1,9},{5... | collective-permute-start | bytes 393224 | tf_op jit(solution)/shard_map/ppermute | solution.py:23
  53.3 11.9 %collective-permute-start.25 = (bf16[128,512]{1,0:T(8,128)(2,1)S(1)}, bf16[128,512]{1,0:T(8,128)(2,1)S(1)}, u32[]{:S(2)}, u32[]{:S(2)}) collective-permute-start(bf16[128,512]{1,0:T(8,128)(2,1)S(1)} %fusion.19), channel_id=1, source_target_pairs={{0,1},{1,0},{2,3},{3,2},{4,5},{5,4},{6,7},{7,6},{8,9},{9,8},{10,11... | collective-permute-start | bytes 393224 | tf_op jit(solution)/shard_map/ppermute | solution.py:17
  53.9 7.1 %collective-permute-start.12 = (bf16[1,2,128,512]{3,2,1,0:T(8,128)(2,1)S(1)}, bf16[1,2,128,512]{3,2,1,0:T(8,128)(2,1)S(1)}, u32[]{:S(2)}, u32[]{:S(2)}) collective-permute-start(bf16[1,2,128,512]{3,2,1,0:T(8,128)(2,1)S(1)} %get-tuple-element.86), channel_id=1, source_target_pairs={{0,16},{4,20},{8,24},{12,28},{16,0},{20,4},{24,8},{28,12},{1,17},{... | collective-permute-start | bytes 786440 | tf_op jit(solution)/shard_map/ppermute | solution.py:29
  55.4 9.7 %collective-permute-start.24 = (bf16[1,1,128,512]{3,2,1,0:T(8,128)(2,1)S(1)}, bf16[1,1,128,512]{3,2,1,0:T(8,128)(2,1)S(1)}, u32[]{:S(2)}, u32[]{:S(2)}) collective-permute-start(bf16[1,1,128,512]{3,2,1,0:T(8,128)(2,1)S(1)} %fusion.11), channel_id=1, source_target_pairs={{0,16},{4,20},{8,24},{12,28},{16,0},{20,4},{24,8},{28,12},{1,17},{... | collective-permute-start | bytes 393224 | tf_op jit(solution)/shard_map/ppermute | solution.py:29
  61.1 7.5 %collective-permute-start.19 = (bf16[1,2,128,512]{3,2,1,0:T(8,128)(2,1)S(1)}, bf16[1,2,128,512]{3,2,1,0:T(8,128)(2,1)S(1)}, u32[]{:S(2)}, u32[]{:S(2)}) collective-permute-start(bf16[1,2,128,512]{3,2,1,0:T(8,128)(2,1)S(1)} %fusion.2), channel_id=1, source_target_pairs={{0,8},{4,12},{8,0},{12,4},{16,24},{20,28},{24,16},{28,20},{1,9},{5... | collective-permute-start | bytes 786440 | tf_op jit(solution)/shard_map/ppermute | solution.py:23
  63.4 6.4 %collective-permute-start.21 = (bf16[1,2,128,512]{3,2,1,0:T(8,128)(2,1)S(1)}, bf16[1,2,128,512]{3,2,1,0:T(8,128)(2,1)S(1)}, u32[]{:S(2)}, u32[]{:S(2)}) collective-permute-start(bf16[1,2,128,512]{3,2,1,0:T(8,128)(2,1)S(1)} %get-tuple-element.97), channel_id=1, source_target_pairs={{0,16},{4,20},{8,24},{12,28},{16,0},{20,4},{24,8},{28,12},{1,17},{... | collective-permute-start | bytes 786440 | tf_op jit(solution)/shard_map/ppermute | solution.py:29
  65.2 10.3 %copy-start.2 = (bf16[128,512]{1,0:T(8,128)(2,1)S(1)}, bf16[128,512]{1,0:T(8,128)(2,1)}, u32[]{:S(2)}) copy-start(bf16[128,512]{1,0:T(8,128)(2,1)} %param.6) | copy-start | bytes 393220
  65.2 7.4 %collective-permute-start.26 = (bf16[128,512]{1,0:T(8,128)(2,1)S(1)}, bf16[128,512]{1,0:T(8,128)(2,1)S(1)}, u32[]{:S(2)}, u32[]{:S(2)}) collective-permute-start(bf16[128,512]{1,0:T(8,128)(2,1)S(1)} %fusion.15), channel_id=1, source_target_pairs={{0,2},{1,3},{2,0},{3,1},{4,6},{5,7},{6,4},{7,5},{8,10},{9,11},{10,... | collective-permute-start | bytes 393224 | tf_op jit(solution)/shard_map/ppermute | solution.py:17
  69.9 5.7 %collective-permute-start.22 = (bf16[128,512]{1,0:T(8,128)(2,1)S(1)}, bf16[128,512]{1,0:T(8,128)(2,1)S(1)}, u32[]{:S(2)}, u32[]{:S(2)}) collective-permute-start(bf16[128,512]{1,0:T(8,128)(2,1)S(1)} %fusion.20), channel_id=1, source_target_pairs={{0,1},{1,0},{2,3},{3,2},{4,5},{5,4},{6,7},{7,6},{8,9},{9,8},{10,11... | collective-permute-start | bytes 393224 | tf_op jit(solution)/shard_map/ppermute | solution.py:17
  76.3 5.3 %collective-permute-start.27 = (bf16[128,512]{1,0:T(8,128)(2,1)S(1)}, bf16[128,512]{1,0:T(8,128)(2,1)S(1)}, u32[]{:S(2)}, u32[]{:S(2)}) collective-permute-start(bf16[128,512]{1,0:T(8,128)(2,1)S(1)} %get-tuple-element.131), channel_id=1, source_target_pairs={{0,1},{1,0},{2,3},{3,2},{4,5},{5,4},{6,7},{7,6},{8,9},{9,8},{10,11... | collective-permute-start | bytes 393224 | tf_op jit(solution)/shard_map/ppermute | solution.py:17
  78.0 9.4 %collective-permute-start.31 = (bf16[128,512]{1,0:T(8,128)(2,1)S(1)}, bf16[128,512]{1,0:T(8,128)(2,1)S(1)}, u32[]{:S(2)}, u32[]{:S(2)}) collective-permute-start(bf16[128,512]{1,0:T(8,128)(2,1)S(1)} %get-tuple-element.131), channel_id=1, source_target_pairs={{0,2},{1,3},{2,0},{3,1},{4,6},{5,7},{6,4},{7,5},{8,10},{9,11},{10,... | collective-permute-start | bytes 393224 | tf_op jit(solution)/shard_map/ppermute | solution.py:17
  81.7 10.8 %collective-permute-start.28 = (bf16[2,128,512]{2,1,0:T(8,128)(2,1)S(1)}, bf16[2,128,512]{2,1,0:T(8,128)(2,1)S(1)}, u32[]{:S(2)}, u32[]{:S(2)}) collective-permute-start(bf16[2,128,512]{2,1,0:T(8,128)(2,1)S(1)} %pad_maximum_fusion.2.refs_0_), channel_id=1, source_target_pairs={{0,16},{4,20},{8,24},{12,28},{16,0},{20,4},{24,8},{28,12},{1,17},{... | collective-permute-start | bytes 786440 | tf_op jit(solution)/shard_map/ppermute | solution.py:36
  87.4 6.4 %collective-permute-start.30 = (bf16[2,128,512]{2,1,0:T(8,128)(2,1)S(1)}, bf16[2,128,512]{2,1,0:T(8,128)(2,1)S(1)}, u32[]{:S(2)}, u32[]{:S(2)}) collective-permute-start(bf16[2,128,512]{2,1,0:T(8,128)(2,1)S(1)} %pad_maximum_fusion.2.refs_0_), channel_id=1, source_target_pairs={{0,8},{4,12},{8,0},{12,4},{16,24},{20,28},{24,16},{28,20},{1,9},{5... | collective-permute-start | bytes 786440 | tf_op jit(solution)/shard_map/ppermute | solution.py:23
  87.4 5.0 %collective-permute-start.32 = (bf16[128,512]{1,0:T(8,128)(2,1)S(1)}, bf16[128,512]{1,0:T(8,128)(2,1)S(1)}, u32[]{:S(2)}, u32[]{:S(2)}) collective-permute-start(bf16[128,512]{1,0:T(8,128)(2,1)S(1)} %collective-permute-done.31), channel_id=1, source_target_pairs={{0,1},{1,0},{2,3},{3,2},{4,5},{5,4},{6,7},{7,6},{8,9},{9,8},{10,11... | collective-permute-start | bytes 393224 | tf_op jit(solution)/shard_map/ppermute | solution.py:17
  92.4 2.7 %collective-permute-start.34 = (bf16[2,128,512]{2,1,0:T(8,128)(2,1)S(1)}, bf16[2,128,512]{2,1,0:T(8,128)(2,1)S(1)}, u32[]{:S(2)}, u32[]{:S(2)}) collective-permute-start(bf16[2,128,512]{2,1,0:T(8,128)(2,1)S(1)} %pad_maximum_fusion.3.refs_1_), channel_id=1, source_target_pairs={{0,4},{4,0},{8,12},{12,8},{16,20},{20,16},{24,28},{28,24},{1,5},{5... | collective-permute-start | bytes 786440 | tf_op jit(solution)/shard_map/ppermute | solution.py:23
  93.8 1.5 %collective-permute-start.33 = (bf16[2,128,512]{2,1,0:T(8,128)(2,1)S(1)}, bf16[2,128,512]{2,1,0:T(8,128)(2,1)S(1)}, u32[]{:S(2)}, u32[]{:S(2)}) collective-permute-start(bf16[2,128,512]{2,1,0:T(8,128)(2,1)S(1)} %pad_maximum_fusion.2.refs_0_), channel_id=1, source_target_pairs={{0,4},{4,0},{8,12},{12,8},{16,20},{20,16},{24,28},{28,24},{1,5},{5... | collective-permute-start | bytes 786440 | tf_op jit(solution)/shard_map/ppermute | solution.py:23
  93.8 8.7 %collective-permute-start.35 = (bf16[2,128,512]{2,1,0:T(8,128)(2,1)S(1)}, bf16[2,128,512]{2,1,0:T(8,128)(2,1)S(1)}, u32[]{:S(2)}, u32[]{:S(2)}) collective-permute-start(bf16[2,128,512]{2,1,0:T(8,128)(2,1)S(1)} %pad_maximum_fusion.3.refs_1_), channel_id=1, source_target_pairs={{0,8},{4,12},{8,0},{12,4},{16,24},{20,28},{24,16},{28,20},{1,9},{5... | collective-permute-start | bytes 786440 | tf_op jit(solution)/shard_map/ppermute | solution.py:23
  95.0 8.9 %collective-permute-start.38 = (bf16[2,128,512]{2,1,0:T(8,128)(2,1)S(1)}, bf16[2,128,512]{2,1,0:T(8,128)(2,1)S(1)}, u32[]{:S(2)}, u32[]{:S(2)}) collective-permute-start(bf16[2,128,512]{2,1,0:T(8,128)(2,1)S(1)} %pad_maximum_fusion.3.refs_1_), channel_id=1, source_target_pairs={{0,16},{4,20},{8,24},{12,28},{16,0},{20,4},{24,8},{28,12},{1,17},{... | collective-permute-start | bytes 786440 | tf_op jit(solution)/shard_map/ppermute | solution.py:36
  102.5 1.5 %collective-permute-start.37 = (bf16[2,128,512]{2,1,0:T(8,128)(2,1)S(1)}, bf16[2,128,512]{2,1,0:T(8,128)(2,1)S(1)}, u32[]{:S(2)}, u32[]{:S(2)}) collective-permute-start(bf16[2,128,512]{2,1,0:T(8,128)(2,1)S(1)} %collective-permute-done.35.refs_1_), channel_id=1, source_target_pairs={{0,4},{4,0},{8,12},{12,8},{16,20},{20,16},{24,28},{28,24},{1,5},{5... | collective-permute-start | bytes 786440 | tf_op jit(solution)/shard_map/ppermute | solution.py:23
  102.5 1.9 %collective-permute-start.36 = (bf16[2,128,512]{2,1,0:T(8,128)(2,1)S(1)}, bf16[2,128,512]{2,1,0:T(8,128)(2,1)S(1)}, u32[]{:S(2)}, u32[]{:S(2)}) collective-permute-start(bf16[2,128,512]{2,1,0:T(8,128)(2,1)S(1)} %collective-permute-done.30.refs_0_), channel_id=1, source_target_pairs={{0,4},{4,0},{8,12},{12,8},{16,20},{20,16},{24,28},{28,24},{1,5},{5... | collective-permute-start | bytes 786440 | tf_op jit(solution)/shard_map/ppermute | solution.py:23
  103.0 8.2 %collective-permute-start.29 = (bf16[2,128,512]{2,1,0:T(8,128)(2,1)S(1)}, bf16[2,128,512]{2,1,0:T(8,128)(2,1)S(1)}, u32[]{:S(2)}, u32[]{:S(2)}) collective-permute-start(bf16[2,128,512]{2,1,0:T(8,128)(2,1)S(1)} %collective-permute-done.28.refs_0_), channel_id=1, source_target_pairs={{0,8},{4,12},{8,0},{12,4},{16,24},{20,28},{24,16},{28,20},{1,9},{5... | collective-permute-start | bytes 786440 | tf_op jit(solution)/shard_map/ppermute | solution.py:23
  103.8 7.9 %collective-permute-start.41 = (bf16[2,128,512]{2,1,0:T(8,128)(2,1)S(1)}, bf16[2,128,512]{2,1,0:T(8,128)(2,1)S(1)}, u32[]{:S(2)}, u32[]{:S(2)}) collective-permute-start(bf16[2,128,512]{2,1,0:T(8,128)(2,1)S(1)} %collective-permute-done.35.refs_1_), channel_id=1, source_target_pairs={{0,16},{4,20},{8,24},{12,28},{16,0},{20,4},{24,8},{28,12},{1,17},{... | collective-permute-start | bytes 786440 | tf_op jit(solution)/shard_map/ppermute | solution.py:36
  108.2 3.6 %collective-permute-start.40 = (bf16[2,128,512]{2,1,0:T(8,128)(2,1)S(1)}, bf16[2,128,512]{2,1,0:T(8,128)(2,1)S(1)}, u32[]{:S(2)}, u32[]{:S(2)}) collective-permute-start(bf16[2,128,512]{2,1,0:T(8,128)(2,1)S(1)} %collective-permute-done.38.refs_1_), channel_id=1, source_target_pairs={{0,4},{4,0},{8,12},{12,8},{16,20},{20,16},{24,28},{28,24},{1,5},{5... | collective-permute-start | bytes 786440 | tf_op jit(solution)/shard_map/ppermute | solution.py:23
  108.4 3.4 %collective-permute-start.39 = (bf16[2,128,512]{2,1,0:T(8,128)(2,1)S(1)}, bf16[2,128,512]{2,1,0:T(8,128)(2,1)S(1)}, u32[]{:S(2)}, u32[]{:S(2)}) collective-permute-start(bf16[2,128,512]{2,1,0:T(8,128)(2,1)S(1)} %collective-permute-done.28.refs_0_), channel_id=1, source_target_pairs={{0,4},{4,0},{8,12},{12,8},{16,20},{20,16},{24,28},{28,24},{1,5},{5... | collective-permute-start | bytes 786440 | tf_op jit(solution)/shard_map/ppermute | solution.py:23
  115.1 1.6 %collective-permute-start.43 = (bf16[2,128,512]{2,1,0:T(8,128)(2,1)S(1)}, bf16[2,128,512]{2,1,0:T(8,128)(2,1)S(1)}, u32[]{:S(2)}, u32[]{:S(2)}) collective-permute-start(bf16[2,128,512]{2,1,0:T(8,128)(2,1)S(1)} %collective-permute-done.41.refs_1_), channel_id=1, source_target_pairs={{0,4},{4,0},{8,12},{12,8},{16,20},{20,16},{24,28},{28,24},{1,5},{5... | collective-permute-start | bytes 786440 | tf_op jit(solution)/shard_map/ppermute | solution.py:23
  115.1 1.9 %collective-permute-start.42 = (bf16[2,128,512]{2,1,0:T(8,128)(2,1)S(1)}, bf16[2,128,512]{2,1,0:T(8,128)(2,1)S(1)}, u32[]{:S(2)}, u32[]{:S(2)}) collective-permute-start(bf16[2,128,512]{2,1,0:T(8,128)(2,1)S(1)} %collective-permute-done.29.refs_0_), channel_id=1, source_target_pairs={{0,4},{4,0},{8,12},{12,8},{16,20},{20,16},{24,28},{28,24},{1,5},{5... | collective-permute-start | bytes 786440 | tf_op jit(solution)/shard_map/ppermute | solution.py:23

commit v3 on v2

--- a/solution.py
+++ b/solution.py
@@ -23,16 +23,9 @@
     return lax.ppermute(value, "layer", pairs)
 
 
-def to_layer(value, offset, sub_count, real):
+def over_layers(value, offset, sub_count, flip=0):
     count = lax.axis_size("layer")
-    pairs = [(p, (p + offset * sub_count) % count) for p in range(count)]
-    moved = lax.ppermute(value, "layer", pairs)
-    return jnp.where(real[offset], moved, jnp.zeros_like(moved))
-
-
-def from_layer(value, offset, sub_count):
-    count = lax.axis_size("layer")
-    pairs = [(p, (p - offset * sub_count) % count) for p in range(count)]
+    pairs = [(p, ((p + offset * sub_count) % count) ^ flip) for p in range(count)]
     return lax.ppermute(value, "layer", pairs)
 
 
@@ -41,13 +34,9 @@
 
 
 def all_over_feat(value):
-    count = lax.axis_size("feat")
-    blocks = [value] + [None] * (count - 1)
-    mask = count // 2
-    while mask > 0:
-        for s in range(0, count, 2 * mask):
-            blocks[s ^ mask] = over_feat(blocks[s], mask)
-        mask //= 2
+    blocks = [value, over_feat(value, 1)]
+    for s in range(2, lax.axis_size("feat")):
+        blocks.append(over_feat(value, s))
     return blocks
 
 
@@ -356,92 +345,81 @@
     rows, cols = tokens_in.shape
     tok = feat_count * rows
     bit_count = sub_count.bit_length() - 1
-    groups = [list(range(feat_count // 2))]
-    groups += [[s] for s in range(feat_count // 2, feat_count)]
+    groups = [list(range(feat_count // 2)), list(range(feat_count // 2, feat_count))]
 
     info = jnp.stack([position % sub_count, layers - 1 - layer]).astype(jnp.int32)
     real = [layer >= k for k in range(layers)]
     tokens_in, info, *real = lax.optimization_barrier((tokens_in, info, *real))
-
     enc_weight = pltpu.with_memory_space_constraint(enc_weight, pltpu.HBM)
     dec_weight = pltpu.with_memory_space_constraint(dec_weight, pltpu.HBM)
 
-    held = {0: all_over_feat(tokens_in)}
-    for bit_level in range(bit_count - 1, 0, -1):
-        for rel in list(held):
-            held[rel ^ 2**bit_level] = [None] * feat_count
-    for s in range(feat_count):
+    order = list(range(0, sub_count, 2)) + list(range(1, sub_count, 2))
+    held = {rel: [None] * feat_count for rel in order[: sub_count // 2]}
+
+    def take(s, *others):
         known = [0]
         for bit_level in range(bit_count - 1, 0, -1):
             for rel in known:
-                held[rel ^ 2**bit_level][s] = over_members(held[rel][s], bit_level)
+                value = after(held[rel][s], *others) if others else held[rel][s]
+                held[rel ^ 2**bit_level][s] = over_members(value, bit_level)
             known += [rel ^ 2**bit_level for rel in known]
-    order = [rel for pair in sorted(held) for rel in (pair, pair ^ 1)]
-    (enc_held,) = fetch(after(enc_weight, held[0][1]))
-    early = [held[rel][s] for rel in order[2::2] for s in range(feat_count - 1)]
-    tokens = {0: after(jnp.stack(held[0], 0), enc_held, *early)}
-    tokens[1] = over_members(tokens[0], 0)
-    partial = encode(info, [0, 1], [tokens[0], tokens[1]], enc_held, None, None)
-    (dec_held,) = fetch(after(dec_weight, partial))
-    for rel in order[2::2]:
-        tokens[rel] = jnp.stack([after(block, dec_held) for block in held[rel]], 0)
+        return [held[rel][s] for rel in known[1:]]
+
+    held[0][0] = tokens_in
+    taken = take(0)
+    mask = feat_count // 2
+    while mask > 0:
+        for s in range(0, feat_count, 2 * mask):
+            value = held[0][s]
+            held[0][s ^ mask] = over_feat(after(value, taken[0]) if s > 0 else value, mask)
+        mask //= 2
+    (enc_held,) = fetch(enc_weight)
+    for s in range(1, feat_count - 1):
+        taken += take(s, *([enc_held] if s == 1 else []))
+    take(feat_count - 1, *taken)
+    (dec_held,) = fetch(after(dec_weight, held[0][feat_count - 1], enc_held))
+    tokens = {}
+    for rel in order[: sub_count // 2]:
+        tokens[rel] = after(jnp.stack(held[rel], 0), dec_held)
         tokens[rel ^ 1] = over_members(tokens[rel], 0)
-    for rel in order[2:-1]:
-        partial = encode(info, [rel], [tokens[rel]], enc_held, partial, None)
-    features = encode(info, order[-1:], [tokens[order[-1]]], enc_held, partial, enc_bias[None])
+    near, far = order[: sub_count // 2], order[sub_count // 2 :]
+    partial = encode(info, near, [tokens[rel] for rel in near], enc_held, None, None)
+    features = encode(
+        info, far, [tokens[rel] for rel in far], enc_held, partial, enc_bias[None]
+    )
 
     current, source = {}, features
     for k in reversed(range(layers)):
         sent, kept = decode(info, source, dec_held, k, groups, rows, cols)
         for place in reversed(range(len(groups))):
             current[place, k] = add_pair(kept[place], over_members(sent[place], 0))
-        source = after(features, kept[-1])
-    turns = sorted(current, reverse=True)
-    joined = {}
-    for bit_level in range(1, bit_count):
-        halves = {}
+        source = after(features, current[len(groups) - 1, k])
+    def split_pairs(value):
+        return value.reshape((value.shape[0] // 2, 2) + value.shape[1:])
+
+    for bit_level in range(1, bit_count - 1):
         for turn, value in current.items():
-            split = value.reshape((value.shape[0] // 2, 2) + value.shape[1:])
-            halves[turn] = (split[:, 0], split[:, 1])
-        if bit_level == bit_count - 1:
-            for k in range(1, layers):
-                joined[k], sent = halves.pop((0, k))
-                sent = to_layer(after(sent, halves[len(groups) - 1, 0][1]), k, sub_count, real)
-                halves[0, 0] = (halves[0, 0][0], add_pair(halves[0, 0][1], sent))
-        turns = [turn for turn in turns if turn in halves]
-        received, operands = [], []
-        for turn in turns:
-            operand = halves[turn][1]
-            if len(received) > 1:
-                operand = after(operand, received[-2], operands[-1])
-            operands.append(operand)
-            received.append(over_members(operand, bit_level))
-        for place, turn in enumerate(turns):
-            arrived = after(received[place], *operands[place + 1 :][:1])
-            if bit_level < bit_count - 1:
-                current[turn] = add_pair(halves[turn][0], arrived)
-            else:
-                current[turn] = (halves[turn][0], arrived)
-    blocks, operands = [None] * feat_count, []
+            split = split_pairs(value)
+            current[turn] = add_pair(split[:, 0], over_members(split[:, 1], bit_level))
+    top = 2 ** (bit_count - 1)
+    blocks, arrived = [None] * feat_count, []
     for place in reversed(range(len(groups))):
-        total = sum(part.astype(jnp.float32) for part in current[place, 0])
+        split = split_pairs(current[place, 0])
+        moved = over_members(after(split[:, 1], *arrived), bit_count - 1)
+        total = split[:, 0].astype(jnp.float32) + moved.astype(jnp.float32)
+        last = arrived
+        arrived = [moved]
         for k in range(1, layers):
-            if place > 0:
-                moved = to_layer(add_pair(*current[place, k]), k, sub_count, real)
-            else:
-                moved = to_layer(after(joined[k], *operands), k, sub_count, real)
-            total = total + moved.astype(jnp.float32)
+            split = split_pairs(current[place, k])
+            for half, flip in ((0, 0), (1, top)):
+                moved = over_layers(after(split[:, half], *last), k, sub_count, flip)
+                moved = jnp.where(real[k], moved, jnp.zeros_like(moved))
+                total = total + moved.astype(jnp.float32)
         for spot, block in enumerate(groups[place]):
             blocks[block] = total[0, spot]
-            if place > 0:
-                operands.append(blocks[block].astype(jnp.bfloat16))
-    mask = 1
-    while mask < feat_count:
-        for s in range(0, feat_count, 2 * mask):
-            sent = blocks[s ^ mask].astype(jnp.bfloat16)
-            blocks[s] = blocks[s] + over_feat(sent, mask).astype(jnp.float32)
-        mask *= 2
     rebuilt = blocks[0]
+    for s in reversed(range(1, feat_count)):
+        rebuilt = rebuilt + over_feat(blocks[s].astype(jnp.bfloat16), s).astype(jnp.float32)
     turned_features = turned(source, 1)[0]
     turned_tokens = [
         turned(after(tokens[rel], turned_features).reshape(1, tok, cols), 1) for rel in order
@@ -450,47 +428,36 @@
     scaled = (loss_scale / tok * recon_error).astype(jnp.bfloat16)
 
     blocks = all_over_feat(scaled)
-    stages = [[0]]
-    for level in range(bit_count - 1, 0, -1):
-        known = [rel for stage in stages for rel in stage]
-        stages.append([rel ^ 2**level for rel in known])
-    spans = [list(range(feat_count // 2)), list(range(feat_count // 2, feat_count))]
-    groups_of = {(0, k): [None] * len(spans) for k in range(layers)}
-    early, last = [], len(spans) - 1
+    spans = [[s] for s in range(min(2, feat_count))]
+    spans += [list(range(2, feat_count))] if feat_count > 2 else []
+    groups_of = {(rel, k): [] for rel in range(0, sub_count, 2) for k in range(layers)}
+    early = []
     for place, group in enumerate(spans):
         stacked = jnp.stack([blocks[s] for s in group], 0)
-        groups_of[0, 0][place] = stacked
-        for k in range(1, layers):
-            groups_of[0, k][place] = from_layer(stacked, k, sub_count)
-        known = [0]
-        for level in range(bit_count - 1, 0, -1):
-            for rel in known:
-                other = rel ^ 2**level
-                for k in range(layers):
-                    if k == 0 or place < last:
-                        part = over_members(groups_of[rel, k][place], level)
-                    else:
-                        part = from_layer(groups_of[other, 0][place], k, sub_count)
-                    groups_of.setdefault((other, k), [None] * len(spans))[place] = part
-            known += [rel ^ 2**level for rel in known]
-        if place == last - 1:
-            early = [part for parts in groups_of.values() for part in parts if part is not None]
-            early.pop()
+        for k in range(layers):
+            for rel in range(0, sub_count, 2):
+                low = rel & -rel
+                if k == 0 and rel == 0:
+                    part = stacked
+                elif rel == 0 or (k > 0 and place == len(spans) - 1):
+                    part = over_layers(stacked, -k, sub_count, rel)
+                else:
+                    part = over_members(groups_of[rel ^ low, k][place], low.bit_length() - 1)
+                groups_of[rel, k].append(part)
+                if place < len(spans) - 1:
+                    early.append(part)
+    later = early[-1:] + [groups_of[0, k][-1] for k in range(1, layers)]
+    early = early[:-1]
 
     feature_grad, dec_grad, squares = None, None, {}
-    other_rels = [rel for stage in stages[1:] for rel in stage]
     for k in range(layers):
-        for rel in [rel for stage in stages for rel in stage]:
+        for rel in range(0, sub_count, 2):
             parts = groups_of[rel, k]
             if feature_grad is None:
                 parts = [after(parts[0], *early)] + parts[1:]
             else:
                 parts = [after(part, feature_grad) for part in parts]
-                if k == 0:
-                    coming = [groups_of[0, later][-1] for later in range(1, layers)]
-                else:
-                    coming = [part for r in other_rels for part in groups_of[r, k]]
-                feature_grad = after(feature_grad, *coming)
+                feature_grad = after(feature_grad, *(later if k == 0 else groups_of[2, k]))
             feature_grad, dec_grad, squares[k, rel] = backward_pair(
                 info,
                 rel,

time: 125 us -> 124 us (level)
  starting transfers between devices: 46.1 us -> 41.3 us
  waiting for transfers between devices: 40.4 us -> 44.9 us
    ppermute x28 -> x29, waiting for transfers between devices: 20.2 us -> 25.2 us  [over_members(): return lax.ppermute(value, 'layer', pairs)]
    ppermute x9, starting transfers between devices: 17.2 us -> 12.9 us  [over_feat(): return lax.ppermute(value, 'feat', pairs)]
    ppermute x7 -> x8, starting transfers between devices: 11.8 us -> 8.58 us  [over_layers(): return lax.ppermute(value, 'layer', pairs)]
    ppermute x28 -> x29, starting transfers between devices: 17.1 us -> 19.8 us  [over_members(): return lax.ppermute(value, 'layer', pairs)]
    pallas_call x3 -> x2, Pallas kernels: 4.48 us -> 3.74 us  [encode(): pl.pallas_call(kernel, in_specs=[in_smem] + [in_vmem] * (len(pieces) + 1...]
    ppermute x7 -> x8, waiting for transfers between devices: 7.37 us -> 6.69 us  [over_layers(): return lax.ppermute(value, 'layer', pairs)]
  transfers between devices with their start and end apart: 44 -> 46, of which waited for: 22 -> 20; matrix products, arithmetic and copies ran while one was open for 1% -> 1% of each run, Pallas kernels for 16% -> 15%
where the time goes in v3:
time: 124 us
  waiting for transfers between devices  44.9 us (36%)
  starting transfers between devices  41.3 us (33%)
  Pallas kernels  34.6 us (28%)
  other arithmetic  1.92 us (2%)
    ppermute x29, waiting for transfers between devices, over_members(): return lax.ppermute(value, 'layer', pairs)  25.2 us
    ppermute x29, starting transfers between devices, over_members(): return lax.ppermute(value, 'layer', pairs)  19.8 us
    pallas_call x4, Pallas kernels, backward_pair(): pl.pallas_call(kernel, in_specs=[in_smem] + [in_vmem] * (len(inputs) + 2)...  13.6 us
    ppermute x9, waiting for transfers between devices, over_feat(): return lax.ppermute(value, 'feat', pairs)  13 us
    ppermute x9, starting transfers between devices, over_feat(): return lax.ppermute(value, 'feat', pairs)  12.9 us
    ppermute x8, starting transfers between devices, over_layers(): return lax.ppermute(value, 'layer', pairs)  8.58 us
    ppermute x8, waiting for transfers between devices, over_layers(): return lax.ppermute(value, 'layer', pairs)  6.69 us
    pallas_call x2, Pallas kernels, decode(): pl.pallas_call(kernel, in_specs=[in_smem, in_vmem, in_vmem], out_specs=[i...  5.79 us
  transfers between devices with their start and end apart: 46, of which 20 were waited for; matrix products, arithmetic and copies ran while one was open for 1% of the time, Pallas kernels for 15%

profile of v3, /device:TPU:0, one launch (start us, length us, event | category | flops | bytes accessed | tf_op | source)
XLA Modules:
  0.0 124.1 jit_solution(7981393635554816082)
XLA Ops:
  0.7 2.9 %collective-permute-start.2 = (bf16[128,512]{1,0:T(8,128)(2,1)}, bf16[128,512]{1,0:T(8,128)(2,1)S(1)}, u32[]{:S(2)}, u32[]{:S(2)}) collective-permute-start(bf16[128,512]{1,0:T(8,128)(2,1)} %param.5), channel_id=1, source_target_pairs={{0,8},{4,12},{8,0},{12,4},{16,24},{20,28},{24,16},{28,20},{1,9},{5... | collective-permute-start | bytes 393224 | tf_op jit(solution)/shard_map/ppermute | solution.py:23
  3.7 2.6 %collective-permute-start.1 = (bf16[128,512]{1,0:T(8,128)(2,1)}, bf16[128,512]{1,0:T(8,128)(2,1)S(1)}, u32[]{:S(2)}, u32[]{:S(2)}) collective-permute-start(bf16[128,512]{1,0:T(8,128)(2,1)} %param.5), channel_id=1, source_target_pairs={{0,2},{1,3},{2,0},{3,1},{4,6},{5,7},{6,4},{7,5},{8,10},{9,11},{10,... | collective-permute-start | bytes 393224 | tf_op jit(solution)/shard_map/ppermute | solution.py:17
  6.3 1.6 %collective-permute-start = (bf16[128,512]{1,0:T(8,128)(2,1)}, bf16[128,512]{1,0:T(8,128)(2,1)S(1)}, u32[]{:S(2)}, u32[]{:S(2)}) collective-permute-start(bf16[128,512]{1,0:T(8,128)(2,1)} %param.5), channel_id=1, source_target_pairs={{0,1},{1,0},{2,3},{3,2},{4,5},{5,4},{6,7},{7,6},{8,9},{9,8},{10,11... | collective-permute-start | bytes 393224 | tf_op jit(solution)/shard_map/ppermute | solution.py:17
  7.8 2.2 %fetch.2.refs_2_ = bf16[2048,1024]{1,0:T(8,128)(2,1)S(1)} custom-call(bf16[2048,1024]{1,0:T(8,128)(2,1)} %refs_0_.1), custom_call_target="tpu_custom_call" | custom-call | bytes 4194304 | tf_op jit(solution)/shard_map/fetch/pallas_call | solution.py:80
  10.1 2.6 %collective-permute-done.1 = bf16[128,512]{1,0:T(8,128)(2,1)S(1)} collective-permute-done((bf16[128,512]{1,0:T(8,128)(2,1)}, bf16[128,512]{1,0:T(8,128)(2,1)S(1)}, u32[]{:S(2)}, u32[]{:S(2)}) %collective-permute-start.1) | collective-permute-done | bytes 131104 | tf_op jit(solution)/shard_map/ppermute | solution.py:17
  12.7 0.7 collective-permute-start.3
  13.3 0.5 collective-permute-start.6
  13.9 1.5 %collective-permute-start.5 = (bf16[128,512]{1,0:T(8,128)(2,1)S(1)}, bf16[128,512]{1,0:T(8,128)(2,1)S(1)}, u32[]{:S(2)}, u32[]{:S(2)}) collective-permute-start(bf16[128,512]{1,0:T(8,128)(2,1)S(1)} %collective-permute-done), channel_id=1, source_target_pairs={{0,8},{4,12},{8,0},{12,4},{16,24},{20,28},{24,16},{28,20},{1,9},{5... | collective-permute-start | bytes 393224 | tf_op jit(solution)/shard_map/ppermute | solution.py:23
  15.4 2.3 %collective-permute-done.3 = bf16[128,512]{1,0:T(8,128)(2,1)S(1)} collective-permute-done((bf16[128,512]{1,0:T(8,128)(2,1)S(1)}, bf16[128,512]{1,0:T(8,128)(2,1)S(1)}, u32[]{:S(2)}, u32[]{:S(2)}) %collective-permute-start.3) | collective-permute-done | bytes 131104 | tf_op jit(solution)/shard_map/ppermute | solution.py:17
  17.6 2.1 %collective-permute-done.6 = bf16[128,512]{1,0:T(8,128)(2,1)S(1)} collective-permute-done((bf16[128,512]{1,0:T(8,128)(2,1)S(1)}, bf16[128,512]{1,0:T(8,128)(2,1)S(1)}, u32[]{:S(2)}, u32[]{:S(2)}) %collective-permute-start.6) | collective-permute-done | bytes 131104 | tf_op jit(solution)/shard_map/ppermute | solution.py:23
  19.7 1.5 %collective-permute-done.5 = bf16[128,512]{1,0:T(8,128)(2,1)S(1)} collective-permute-done((bf16[128,512]{1,0:T(8,128)(2,1)S(1)}, bf16[128,512]{1,0:T(8,128)(2,1)S(1)}, u32[]{:S(2)}, u32[]{:S(2)}) %collective-permute-start.5) | collective-permute-done | bytes 131104 | tf_op jit(solution)/shard_map/ppermute | solution.py:23
  21.3 0.5 collective-permute-start.7
  21.8 3.5 %fetch.3.weight_ref.refs_7_ = bf16[2,1024,2048]{2,1,0:T(8,128)(2,1)S(1)} custom-call(bf16[2,1024,2048]{2,1,0:T(8,128)(2,1)} %refs_0_.2), custom_call_target="tpu_custom_call" | custom-call | bytes 8388608 | tf_op jit(solution)/shard_map/fetch/pallas_call | solution.py:80
  25.5 0.8 collective-permute-done.7
  26.4 1.8 %encode.2.refs_3_ = f32[512,1024]{1,0:T(8,128)S(1)} custom-call(s32[2]{0:T(128)S(1)} %pad_add_fusion.info_ref, bf16[4,128,512]{2,1,0:T(8,128)(2,1)S(1)} %pad_maximum_fusion.refs_0_, bf16[4,128,512]{2,1,0:T(8,128)(2,1)S(1)} %pad_maximum_fusion.1.refs_1_, bf16[2048,1024]{1,0:T(8,128)(2,1)S(1)} %fetch.2.refs_2_), custom_call_target="tpu_custom_call" | custom-call | flops 1073741824 | bytes 3145728 | tf_op jit(solution)/shard_map/encode/pallas_call | solution.py:120
  28.3 2.0 %encode.3.feat_ref.in_ref.refs_4_ = bf16[2,512,1024]{2,1,0:T(8,128)(2,1)S(1)} custom-call(s32[2]{0:T(128)S(1)} %pad_add_fusion.info_ref, bf16[4,128,512]{2,1,0:T(8,128)(2,1)S(1)} %collective-permute-done.4.refs_0_, bf16[4,128,512]{2,1,0:T(8,128)(2,1)S(1)} %collective-permute-done.8.refs_1_, bf16[2048,1024]{1,0:T(8,128)(2,1)S(1)} %fetch.2.refs_2_, ...), custom_call_target="tpu_custom_call" | custom-call | flops 1073741824 | bytes 3145728 | tf_op jit(solution)/shard_map/encode/pallas_call | solution.py:120
  30.3 2.9 %decode.2 = (bf16[2,2,128,512]{3,2,1,0:T(8,128)(2,1)S(1)}, bf16[2,2,128,512]{3,2,1,0:T(8,128)(2,1)S(1)}, bf16[2,2,128,512]{3,2,1,0:T(8,128)(2,1)S(1)}, bf16[2,2,128,512]{3,2,1,0:T(8,128)(2,1)S(1)}) custom-call(s32[2]{0:T(128)S(1)} %pad_add_fusion.info_ref, bf16[2,512,1024]{2,1,0:T(8,128)(2,1)S(1)} %encode.3.feat_ref.in_ref.refs_4_, ...), custom_call_target="tpu_custom_call" | custom-call | flops 2147483648 | bytes 4194304 | tf_op jit(solution)/shard_map/decode/pallas_call | solution.py:158
  33.2 0.5 collective-permute-start.9
  33.7 1.4 %collective-permute-done.9 = bf16[2,2,128,512]{3,2,1,0:T(8,128)(2,1)S(1)} collective-permute-done((bf16[2,2,128,512]{3,2,1,0:T(8,128)(2,1)S(1)}, bf16[2,2,128,512]{3,2,1,0:T(8,128)(2,1)S(1)}, u32[]{:S(2)}, u32[]{:S(2)}) %collective-permute-start.9) | collective-permute-done | bytes 524320 | tf_op jit(solution)/shard_map/ppermute | solution.py:23
  35.3 2.9 %decode.3 = (bf16[2,2,128,512]{3,2,1,0:T(8,128)(2,1)S(1)}, bf16[2,2,128,512]{3,2,1,0:T(8,128)(2,1)S(1)}, bf16[2,2,128,512]{3,2,1,0:T(8,128)(2,1)S(1)}, bf16[2,2,128,512]{3,2,1,0:T(8,128)(2,1)S(1)}) custom-call(s32[2]{0:T(128)S(1)} %pad_add_fusion.info_ref, bf16[2,512,1024]{2,1,0:T(8,128)(2,1)S(1)} %encode.3.feat_ref.in_ref.refs_4_, ...), custom_call_target="tpu_custom_call" | custom-call | flops 2147483648 | bytes 4194304 | tf_op jit(solution)/shard_map/decode/pallas_call | solution.py:158
  38.2 0.4 collective-permute-start.11
  38.7 2.1 %collective-permute-start.18 = (bf16[1,2,128,512]{3,2,1,0:T(8,128)(2,1)S(1)}, bf16[1,2,128,512]{3,2,1,0:T(8,128)(2,1)S(1)}, u32[]{:S(2)}, u32[]{:S(2)}) collective-permute-start(bf16[1,2,128,512]{3,2,1,0:T(8,128)(2,1)S(1)} %get-tuple-element.118), channel_id=1, source_target_pairs={{0,24},{4,28},{8,16},{12,20},{16,8},{20,12},{24,0},{28,4},{1,25},{... | collective-permute-start | bytes 786440 | tf_op jit(solution)/shard_map/ppermute | solution.py:29
  40.8 0.5 collective-permute-start.17
  41.7 1.0 collective-permute-start.12
  42.7 0.5 collective-permute-done.10
  43.4 10.4 %collective-permute-done.12 = bf16[1,2,128,512]{3,2,1,0:T(8,128)(2,1)S(1)} collective-permute-done((bf16[1,2,128,512]{3,2,1,0:T(8,128)(2,1)S(1)}, bf16[1,2,128,512]{3,2,1,0:T(8,128)(2,1)S(1)}, u32[]{:S(2)}, u32[]{:S(2)}) %collective-permute-start.12) | collective-permute-done | bytes 262176 | tf_op jit(solution)/shard_map/ppermute | solution.py:23
  53.7 1.3 %collective-permute-start.13 = (bf16[1,2,128,512]{3,2,1,0:T(8,128)(2,1)S(1)}, bf16[1,2,128,512]{3,2,1,0:T(8,128)(2,1)S(1)}, u32[]{:S(2)}, u32[]{:S(2)}) collective-permute-start(bf16[1,2,128,512]{3,2,1,0:T(8,128)(2,1)S(1)} %slice_bitcast_fusion.7), channel_id=1, source_target_pairs={{0,8},{4,12},{8,0},{12,4},{16,24},{20,28},{24,16},{28,20},{1,9},{5... | collective-permute-start | bytes 786440 | tf_op jit(solution)/shard_map/ppermute | solution.py:23
  55.0 0.5 collective-permute-start.15
  55.5 1.7 %collective-permute-start.16 = (bf16[1,2,128,512]{3,2,1,0:T(8,128)(2,1)S(1)}, bf16[1,2,128,512]{3,2,1,0:T(8,128)(2,1)S(1)}, u32[]{:S(2)}, u32[]{:S(2)}) collective-permute-start(bf16[1,2,128,512]{3,2,1,0:T(8,128)(2,1)S(1)} %get-tuple-element.80), channel_id=1, source_target_pairs={{0,24},{4,28},{8,16},{12,20},{16,8},{20,12},{24,0},{28,4},{1,25},{... | collective-permute-start | bytes 786440 | tf_op jit(solution)/shard_map/ppermute | solution.py:29
  57.4 3.1 %collective-permute-start.19 = (bf16[128,512]{1,0:T(8,128)(2,1)S(1)}, bf16[128,512]{1,0:T(8,128)(2,1)S(1)}, u32[]{:S(2)}, u32[]{:S(2)}) collective-permute-start(bf16[128,512]{1,0:T(8,128)(2,1)S(1)} %get-tuple-element.121), channel_id=1, source_target_pairs={{0,3},{1,2},{2,1},{3,0},{4,7},{5,6},{6,5},{7,4},{8,11},{9,10},{10,... | collective-permute-start | bytes 393224 | tf_op jit(solution)/shard_map/ppermute | solution.py:17
  60.5 0.4 collective-permute-start.20
  60.8 2.1 %collective-permute-done.13 = bf16[1,2,128,512]{3,2,1,0:T(8,128)(2,1)S(1)} collective-permute-done((bf16[1,2,128,512]{3,2,1,0:T(8,128)(2,1)S(1)}, bf16[1,2,128,512]{3,2,1,0:T(8,128)(2,1)S(1)}, u32[]{:S(2)}, u32[]{:S(2)}) %collective-permute-start.13) | collective-permute-done | bytes 262176 | tf_op jit(solution)/shard_map/ppermute | solution.py:23
  63.0 5.1 %collective-permute-done.15 = bf16[1,2,128,512]{3,2,1,0:T(8,128)(2,1)S(1)} collective-permute-done((bf16[1,2,128,512]{3,2,1,0:T(8,128)(2,1)S(1)}, bf16[1,2,128,512]{3,2,1,0:T(8,128)(2,1)S(1)}, u32[]{:S(2)}, u32[]{:S(2)}) %collective-permute-start.15) | collective-permute-done | bytes 262176 | tf_op jit(solution)/shard_map/ppermute | solution.py:29
  68.3 0.4 collective-permute-start.21
  68.7 0.3 turned.5
  69.8 1.6 %collective-permute-done.20 = bf16[128,512]{1,0:T(8,128)(2,1)S(1)} collective-permute-done((bf16[128,512]{1,0:T(8,128)(2,1)S(1)}, bf16[128,512]{1,0:T(8,128)(2,1)S(1)}, u32[]{:S(2)}, u32[]{:S(2)}) %collective-permute-start.20) | collective-permute-done | bytes 131104 | tf_op jit(solution)/shard_map/ppermute | solution.py:17
  71.4 2.1 %collective-permute-done.21 = bf16[128,512]{1,0:T(8,128)(2,1)S(1)} collective-permute-done((bf16[128,512]{1,0:T(8,128)(2,1)S(1)}, bf16[128,512]{1,0:T(8,128)(2,1)S(1)}, u32[]{:S(2)}, u32[]{:S(2)}) %collective-permute-start.21) | collective-permute-done | bytes 131104 | tf_op jit(solution)/shard_map/ppermute | solution.py:17
  73.5 0.8 multiply_convert_fusion
  74.4 0.8 collective-permute-start.22
  75.3 4.1 %collective-permute-start.29 = (bf16[128,512]{1,0:T(8,128)(2,1)S(1)}, bf16[128,512]{1,0:T(8,128)(2,1)S(1)}, u32[]{:S(2)}, u32[]{:S(2)}) collective-permute-start(bf16[128,512]{1,0:T(8,128)(2,1)S(1)} %get-tuple-element.115), channel_id=1, source_target_pairs={{0,3},{1,2},{2,1},{3,0},{4,7},{5,6},{6,5},{7,4},{8,11},{9,10},{10,... | collective-permute-start | bytes 393224 | tf_op jit(solution)/shard_map/ppermute | solution.py:17
  79.4 1.2 collective-permute-start.24
  80.6 1.0 collective-permute-start.27
  81.7 1.3 %collective-permute-start.26 = (bf16[1,128,512]{2,1,0:T(8,128)(2,1)S(1)}, bf16[1,128,512]{2,1,0:T(8,128)(2,1)S(1)}, u32[]{:S(2)}, u32[]{:S(2)}) collective-permute-start(bf16[1,128,512]{2,1,0:T(8,128)(2,1)S(1)} %bitcast.80), channel_id=1, source_target_pairs={{0,8},{4,12},{8,0},{12,4},{16,24},{20,28},{24,16},{28,20},{1,9},{5... | collective-permute-start | bytes 393224 | tf_op jit(solution)/shard_map/ppermute | solution.py:23
  83.0 1.6 %collective-permute-done.29 = bf16[128,512]{1,0:T(8,128)(2,1)S(1)} collective-permute-done((bf16[128,512]{1,0:T(8,128)(2,1)S(1)}, bf16[128,512]{1,0:T(8,128)(2,1)S(1)}, u32[]{:S(2)}, u32[]{:S(2)}) %collective-permute-start.29) | collective-permute-done | bytes 131104 | tf_op jit(solution)/shard_map/ppermute | solution.py:17
  84.6 1.9 %collective-permute-start.23 = (bf16[1,128,512]{2,1,0:T(8,128)(2,1)S(1)}, bf16[1,128,512]{2,1,0:T(8,128)(2,1)S(1)}, u32[]{:S(2)}, u32[]{:S(2)}) collective-permute-start(bf16[1,128,512]{2,1,0:T(8,128)(2,1)S(1)} %collective-permute-done.22.refs_0_), channel_id=1, source_target_pairs={{0,8},{4,12},{8,0},{12,4},{16,24},{20,28},{24,16},{28,20},{1,9},{5... | collective-permute-start | bytes 393224 | tf_op jit(solution)/shard_map/ppermute | solution.py:23
  86.5 2.8 %collective-permute-done.28 = bf16[128,512]{1,0:T(8,128)(2,1)S(1)} collective-permute-done((bf16[128,512]{1,0:T(8,128)(2,1)S(1)}, bf16[128,512]{1,0:T(8,128)(2,1)S(1)}, u32[]{:S(2)}, u32[]{:S(2)}) %collective-permute-start.28) | collective-permute-done | bytes 131104 | tf_op jit(solution)/shard_map/ppermute | solution.py:17
  89.4 2.2 %collective-permute-start.33 = (bf16[2,128,512]{2,1,0:T(8,128)(2,1)S(1)}, bf16[2,128,512]{2,1,0:T(8,128)(2,1)S(1)}, u32[]{:S(2)}, u32[]{:S(2)}) collective-permute-start(bf16[2,128,512]{2,1,0:T(8,128)(2,1)S(1)} %pad_maximum_fusion.2.refs_2_), channel_id=1, source_target_pairs={{0,8},{4,12},{8,0},{12,4},{16,24},{20,28},{24,16},{28,20},{1,9},{5... | collective-permute-start | bytes 786440 | tf_op jit(solution)/shard_map/ppermute | solution.py:23
  91.8 0.4 collective-permute-start.30
  92.2 1.1 collective-permute-start.38
  93.3 3.3 %backward_pair.4 = (f32[512,1024]{1,0:T(8,128)S(1)}, bf16[2,1024,2048]{2,1,0:T(8,128)(2,1)}, f32[8,128]{1,0:T(8,128)S(1)}) custom-call(s32[2]{0:T(128)S(1)} %pad_add_fusion.info_ref, bf16[1,128,512]{2,1,0:T(8,128)(2,1)S(1)} %bitcast.78, bf16[1,128,512]{2,1,0:T(8,128)(2,1)S(1)} %bitcast.82, bf16[2,128,512]{2,1,0:T(8,128)(2,1)S(1)} %pad_maximum_fusion.2.refs_2_, ...), custom_call_target="tpu_custom_call" | custom-call | flops 262144 | bytes 262144 | tf_op jit(solution)/shard_map/backward_pair/pallas_call | solution.py:262
  96.6 1.9 %collective-permute-done.33.refs_2_ = bf16[2,128,512]{2,1,0:T(8,128)(2,1)S(1)} collective-permute-done((bf16[2,128,512]{2,1,0:T(8,128)(2,1)S(1)}, bf16[2,128,512]{2,1,0:T(8,128)(2,1)S(1)}, u32[]{:S(2)}, u32[]{:S(2)}) %collective-permute-start.33) | collective-permute-done | bytes 262176 | tf_op jit(solution)/shard_map/ppermute | solution.py:23
  98.6 1.8 %collective-permute-start.37 = (bf16[1,128,512]{2,1,0:T(8,128)(2,1)S(1)}, bf16[1,128,512]{2,1,0:T(8,128)(2,1)S(1)}, u32[]{:S(2)}, u32[]{:S(2)}) collective-permute-start(bf16[1,128,512]{2,1,0:T(8,128)(2,1)S(1)} %collective-permute-done.27.refs_1_), channel_id=1, source_target_pairs={{0,8},{4,12},{8,0},{12,4},{16,24},{20,28},{24,16},{28,20},{1,9},{5... | collective-permute-start | bytes 393224 | tf_op jit(solution)/shard_map/ppermute | solution.py:23
  100.3 0.2 collective-permute-start.34
  100.5 0.3 collective-permute-start.35
  100.8 0.8 collective-permute-start.42
  101.6 3.0 %collective-permute-done.37.refs_1_ = bf16[1,128,512]{2,1,0:T(8,128)(2,1)S(1)} collective-permute-done((bf16[1,128,512]{2,1,0:T(8,128)(2,1)S(1)}, bf16[1,128,512]{2,1,0:T(8,128)(2,1)S(1)}, u32[]{:S(2)}, u32[]{:S(2)}) %collective-permute-start.37) | collective-permute-done | bytes 131104 | tf_op jit(solution)/shard_map/ppermute | solution.py:23
  104.7 3.8 %backward_pair.5 = (f32[512,1024]{1,0:T(8,128)S(1)}, bf16[2,1024,2048]{2,1,0:T(8,128)(2,1)}, f32[8,128]{1,0:T(8,128)S(1)}) custom-call(s32[2]{0:T(128)S(1)} %pad_add_fusion.info_ref, bf16[1,128,512]{2,1,0:T(8,128)(2,1)S(1)} %collective-permute-done.24.refs_0_, ...), custom_call_target="tpu_custom_call", output_to_operand_aliasing={{0}: (9, {}), {1}: (10, {})} | custom-call | flops 262144 | bytes 262144 | tf_op jit(solution)/shard_map/backward_pair/pallas_call | solution.py:262
  108.5 0.5 collective-permute-start.39
  109.1 1.5 %collective-permute-done.42.refs_2_ = bf16[2,128,512]{2,1,0:T(8,128)(2,1)S(1)} collective-permute-done((bf16[2,128,512]{2,1,0:T(8,128)(2,1)S(1)}, bf16[2,128,512]{2,1,0:T(8,128)(2,1)S(1)}, u32[]{:S(2)}, u32[]{:S(2)}) %collective-permute-start.42) | collective-permute-done | bytes 262176 | tf_op jit(solution)/shard_map/ppermute | solution.py:29
  110.7 3.3 %backward_pair.6 = (f32[512,1024]{1,0:T(8,128)S(1)}, bf16[2,1024,2048]{2,1,0:T(8,128)(2,1)}, f32[8,128]{1,0:T(8,128)S(1)}) custom-call(s32[2]{0:T(128)S(1)} %pad_add_fusion.info_ref, bf16[1,128,512]{2,1,0:T(8,128)(2,1)S(1)} %collective-permute-done.22.refs_0_, ...), custom_call_target="tpu_custom_call", output_to_operand_aliasing={{0}: (9, {}), {1}: (10, {})} | custom-call | flops 262144 | bytes 262144 | tf_op jit(solution)/shard_map/backward_pair/pallas_call | solution.py:262
  114.0 0.5 collective-permute-start.43
  114.6 1.1 collective-permute-done.43.refs_3_
  115.9 3.3 %backward_pair.7 = (f32[512,1024]{1,0:T(8,128)S(1)}, bf16[2,1024,2048]{2,1,0:T(8,128)(2,1)}, f32[8,128]{1,0:T(8,128)S(1)}) custom-call(s32[2]{0:T(128)S(1)} %pad_add_fusion.info_ref, bf16[1,128,512]{2,1,0:T(8,128)(2,1)S(1)} %collective-permute-done.23.refs_0_, ...), custom_call_target="tpu_custom_call", output_to_operand_aliasing={{0}: (9, {}), {1}: (10, {})} | custom-call | flops 262144 | bytes 262144 | tf_op jit(solution)/shard_map/backward_pair/pallas_call | solution.py:262
  119.2 4.7 %encoder_grad.1 = (bf16[2048,1024]{1,0:T(8,128)(2,1)}, f32[1,1024]{1,0:T(1,128)}, f32[1,1]{1,0:T(1,128)}) custom-call(s32[2]{0:T(128)S(1)} %pad_add_fusion.info_ref, bf16[1,512,512]{2,1,0:T(8,128)(2,1)S(1)} %turned.6.refs_0_, bf16[1,512,512]{2,1,0:T(8,128)(2,1)S(1)} %turned.7.refs_1_, bf16[1,512,512]{2,1,0:T(8,128)(2,1)S(1)} %turned.8.refs_2_, ...), custom_call_target="tpu_custom_call" | custom-call | flops 2147483648 | bytes 9437184 | tf_op jit(solution)/shard_map/encoder_grad/pallas_call | solution.py:314
  (67 shorter events, 3.3 us)
Async XLA Ops:
  0.7 9.3 %collective-permute-start.2 = (bf16[128,512]{1,0:T(8,128)(2,1)}, bf16[128,512]{1,0:T(8,128)(2,1)S(1)}, u32[]{:S(2)}, u32[]{:S(2)}) collective-permute-start(bf16[128,512]{1,0:T(8,128)(2,1)} %param.5), channel_id=1, source_target_pairs={{0,8},{4,12},{8,0},{12,4},{16,24},{20,28},{24,16},{28,20},{1,9},{5... | collective-permute-start | bytes 393224 | tf_op jit(solution)/shard_map/ppermute | solution.py:23
  3.7 9.0 %collective-permute-start.1 = (bf16[128,512]{1,0:T(8,128)(2,1)}, bf16[128,512]{1,0:T(8,128)(2,1)S(1)}, u32[]{:S(2)}, u32[]{:S(2)}) collective-permute-start(bf16[128,512]{1,0:T(8,128)(2,1)} %param.5), channel_id=1, source_target_pairs={{0,2},{1,3},{2,0},{3,1},{4,6},{5,7},{6,4},{7,5},{8,10},{9,11},{10,... | collective-permute-start | bytes 393224 | tf_op jit(solution)/shard_map/ppermute | solution.py:17
  6.3 7.1 %collective-permute-start = (bf16[128,512]{1,0:T(8,128)(2,1)}, bf16[128,512]{1,0:T(8,128)(2,1)S(1)}, u32[]{:S(2)}, u32[]{:S(2)}) collective-permute-start(bf16[128,512]{1,0:T(8,128)(2,1)} %param.5), channel_id=1, source_target_pairs={{0,1},{1,0},{2,3},{3,2},{4,5},{5,4},{6,7},{7,6},{8,9},{9,8},{10,11... | collective-permute-start | bytes 393224 | tf_op jit(solution)/shard_map/ppermute | solution.py:17
  10.1 15.3 %copy-start.2 = (bf16[128,512]{1,0:T(8,128)(2,1)S(1)}, bf16[128,512]{1,0:T(8,128)(2,1)}, u32[]{:S(2)}) copy-start(bf16[128,512]{1,0:T(8,128)(2,1)} %param.5) | copy-start | bytes 393220
  12.7 5.0 %collective-permute-start.3 = (bf16[128,512]{1,0:T(8,128)(2,1)S(1)}, bf16[128,512]{1,0:T(8,128)(2,1)S(1)}, u32[]{:S(2)}, u32[]{:S(2)}) collective-permute-start(bf16[128,512]{1,0:T(8,128)(2,1)S(1)} %collective-permute-done.1), channel_id=1, source_target_pairs={{0,1},{1,0},{2,3},{3,2},{4,5},{5,4},{6,7},{7,6},{8,9},{9,8},{10,11... | collective-permute-start | bytes 393224 | tf_op jit(solution)/shard_map/ppermute | solution.py:17
  13.3 6.4 %collective-permute-start.6 = (bf16[128,512]{1,0:T(8,128)(2,1)S(1)}, bf16[128,512]{1,0:T(8,128)(2,1)S(1)}, u32[]{:S(2)}, u32[]{:S(2)}) collective-permute-start(bf16[128,512]{1,0:T(8,128)(2,1)S(1)} %collective-permute-done.1), channel_id=1, source_target_pairs={{0,8},{4,12},{8,0},{12,4},{16,24},{20,28},{24,16},{28,20},{1,9},{5... | collective-permute-start | bytes 393224 | tf_op jit(solution)/shard_map/ppermute | solution.py:23
  13.9 7.4 %collective-permute-start.5 = (bf16[128,512]{1,0:T(8,128)(2,1)S(1)}, bf16[128,512]{1,0:T(8,128)(2,1)S(1)}, u32[]{:S(2)}, u32[]{:S(2)}) collective-permute-start(bf16[128,512]{1,0:T(8,128)(2,1)S(1)} %collective-permute-done), channel_id=1, source_target_pairs={{0,8},{4,12},{8,0},{12,4},{16,24},{20,28},{24,16},{28,20},{1,9},{5... | collective-permute-start | bytes 393224 | tf_op jit(solution)/shard_map/ppermute | solution.py:23
  21.3 5.0 %collective-permute-start.7 = (bf16[128,512]{1,0:T(8,128)(2,1)S(1)}, bf16[128,512]{1,0:T(8,128)(2,1)S(1)}, u32[]{:S(2)}, u32[]{:S(2)}) collective-permute-start(bf16[128,512]{1,0:T(8,128)(2,1)S(1)} %collective-permute-done.3), channel_id=1, source_target_pairs={{0,8},{4,12},{8,0},{12,4},{16,24},{20,28},{24,16},{28,20},{1,9},{5... | collective-permute-start | bytes 393224 | tf_op jit(solution)/shard_map/ppermute | solution.py:23
  25.4 2.8 %collective-permute-start.4 = (bf16[4,128,512]{2,1,0:T(8,128)(2,1)S(1)}, bf16[4,128,512]{2,1,0:T(8,128)(2,1)S(1)}, u32[]{:S(2)}, u32[]{:S(2)}) collective-permute-start(bf16[4,128,512]{2,1,0:T(8,128)(2,1)S(1)} %pad_maximum_fusion.refs_0_), channel_id=1, source_target_pairs={{0,4},{4,0},{8,12},{12,8},{16,20},{20,16},{24,28},{28,24},{1,5},{5... | collective-permute-start | bytes 1572872 | tf_op jit(solution)/shard_map/ppermute | solution.py:23
  26.2 2.1 %copy-start = (f32[1024]{0:T(1024)S(1)}, f32[1024]{0:T(1024)}, u32[]{:S(2)}) copy-start(f32[1024]{0:T(1024)} %param.8) | copy-start | bytes 12292
  26.3 2.0 %collective-permute-start.8 = (bf16[4,128,512]{2,1,0:T(8,128)(2,1)S(1)}, bf16[4,128,512]{2,1,0:T(8,128)(2,1)S(1)}, u32[]{:S(2)}, u32[]{:S(2)}) collective-permute-start(bf16[4,128,512]{2,1,0:T(8,128)(2,1)S(1)} %pad_maximum_fusion.1.refs_1_), channel_id=1, source_target_pairs={{0,4},{4,0},{8,12},{12,8},{16,20},{20,16},{24,28},{28,24},{1,5},{5... | collective-permute-start | bytes 1572872 | tf_op jit(solution)/shard_map/ppermute | solution.py:23
  33.2 2.0 %collective-permute-start.9 = (bf16[2,2,128,512]{3,2,1,0:T(8,128)(2,1)S(1)}, bf16[2,2,128,512]{3,2,1,0:T(8,128)(2,1)S(1)}, u32[]{:S(2)}, u32[]{:S(2)}) collective-permute-start(bf16[2,2,128,512]{3,2,1,0:T(8,128)(2,1)S(1)} %get-tuple-element.69), channel_id=1, source_target_pairs={{0,4},{4,0},{8,12},{12,8},{16,20},{20,16},{24,28},{28,24},{1,5},{5... | collective-permute-start | bytes 1572872 | tf_op jit(solution)/shard_map/ppermute | solution.py:23
  33.6 7.6 %collective-permute-start.14 = (bf16[2,2,128,512]{3,2,1,0:T(8,128)(2,1)S(1)}, bf16[2,2,128,512]{3,2,1,0:T(8,128)(2,1)S(1)}, u32[]{:S(2)}, u32[]{:S(2)}) collective-permute-start(bf16[2,2,128,512]{3,2,1,0:T(8,128)(2,1)S(1)} %get-tuple-element.78), channel_id=1, source_target_pairs={{0,4},{4,0},{8,12},{12,8},{16,20},{20,16},{24,28},{28,24},{1,5},{5... | collective-permute-start | bytes 1572872 | tf_op jit(solution)/shard_map/ppermute | solution.py:23
  38.2 3.3 %collective-permute-start.11 = (bf16[2,2,128,512]{3,2,1,0:T(8,128)(2,1)S(1)}, bf16[2,2,128,512]{3,2,1,0:T(8,128)(2,1)S(1)}, u32[]{:S(2)}, u32[]{:S(2)}) collective-permute-start(bf16[2,2,128,512]{3,2,1,0:T(8,128)(2,1)S(1)} %get-tuple-element.74), channel_id=1, source_target_pairs={{0,4},{4,0},{8,12},{12,8},{16,20},{20,16},{24,28},{28,24},{1,5},{5... | collective-permute-start | bytes 1572872 | tf_op jit(solution)/shard_map/ppermute | solution.py:23
  38.7 18.5 %collective-permute-start.18 = (bf16[1,2,128,512]{3,2,1,0:T(8,128)(2,1)S(1)}, bf16[1,2,128,512]{3,2,1,0:T(8,128)(2,1)S(1)}, u32[]{:S(2)}, u32[]{:S(2)}) collective-permute-start(bf16[1,2,128,512]{3,2,1,0:T(8,128)(2,1)S(1)} %get-tuple-element.118), channel_id=1, source_target_pairs={{0,24},{4,28},{8,16},{12,20},{16,8},{20,12},{24,0},{28,4},{1,25},{... | collective-permute-start | bytes 786440 | tf_op jit(solution)/shard_map/ppermute | solution.py:29
  40.8 16.4 %collective-permute-start.17 = (bf16[1,2,128,512]{3,2,1,0:T(8,128)(2,1)S(1)}, bf16[1,2,128,512]{3,2,1,0:T(8,128)(2,1)S(1)}, u32[]{:S(2)}, u32[]{:S(2)}) collective-permute-start(bf16[1,2,128,512]{3,2,1,0:T(8,128)(2,1)S(1)} %get-tuple-element.117), channel_id=1, source_target_pairs={{0,16},{4,20},{8,24},{12,28},{16,0},{20,4},{24,8},{28,12},{1,17},{... | collective-permute-start | bytes 786440 | tf_op jit(solution)/shard_map/ppermute | solution.py:29
  41.3 1.9 %collective-permute-start.10 = (bf16[2,2,128,512]{3,2,1,0:T(8,128)(2,1)S(1)}, bf16[2,2,128,512]{3,2,1,0:T(8,128)(2,1)S(1)}, u32[]{:S(2)}, u32[]{:S(2)}) collective-permute-start(bf16[2,2,128,512]{3,2,1,0:T(8,128)(2,1)S(1)} %get-tuple-element.72), channel_id=1, source_target_pairs={{0,4},{4,0},{8,12},{12,8},{16,20},{20,16},{24,28},{28,24},{1,5},{5... | collective-permute-start | bytes 1572872 | tf_op jit(solution)/shard_map/ppermute | solution.py:23
  41.7 12.1 %collective-permute-start.12 = (bf16[1,2,128,512]{3,2,1,0:T(8,128)(2,1)S(1)}, bf16[1,2,128,512]{3,2,1,0:T(8,128)(2,1)S(1)}, u32[]{:S(2)}, u32[]{:S(2)}) collective-permute-start(bf16[1,2,128,512]{3,2,1,0:T(8,128)(2,1)S(1)} %slice_bitcast_fusion.6), channel_id=1, source_target_pairs={{0,8},{4,12},{8,0},{12,4},{16,24},{20,28},{24,16},{28,20},{1,9},{5... | collective-permute-start | bytes 786440 | tf_op jit(solution)/shard_map/ppermute | solution.py:23
  53.7 9.2 %collective-permute-start.13 = (bf16[1,2,128,512]{3,2,1,0:T(8,128)(2,1)S(1)}, bf16[1,2,128,512]{3,2,1,0:T(8,128)(2,1)S(1)}, u32[]{:S(2)}, u32[]{:S(2)}) collective-permute-start(bf16[1,2,128,512]{3,2,1,0:T(8,128)(2,1)S(1)} %slice_bitcast_fusion.7), channel_id=1, source_target_pairs={{0,8},{4,12},{8,0},{12,4},{16,24},{20,28},{24,16},{28,20},{1,9},{5... | collective-permute-start | bytes 786440 | tf_op jit(solution)/shard_map/ppermute | solution.py:23
  55.0 13.1 %collective-permute-start.15 = (bf16[1,2,128,512]{3,2,1,0:T(8,128)(2,1)S(1)}, bf16[1,2,128,512]{3,2,1,0:T(8,128)(2,1)S(1)}, u32[]{:S(2)}, u32[]{:S(2)}) collective-permute-start(bf16[1,2,128,512]{3,2,1,0:T(8,128)(2,1)S(1)} %get-tuple-element.79), channel_id=1, source_target_pairs={{0,16},{4,20},{8,24},{12,28},{16,0},{20,4},{24,8},{28,12},{1,17},{... | collective-permute-start | bytes 786440 | tf_op jit(solution)/shard_map/ppermute | solution.py:29
  55.5 12.6 %collective-permute-start.16 = (bf16[1,2,128,512]{3,2,1,0:T(8,128)(2,1)S(1)}, bf16[1,2,128,512]{3,2,1,0:T(8,128)(2,1)S(1)}, u32[]{:S(2)}, u32[]{:S(2)}) collective-permute-start(bf16[1,2,128,512]{3,2,1,0:T(8,128)(2,1)S(1)} %get-tuple-element.80), channel_id=1, source_target_pairs={{0,24},{4,28},{8,16},{12,20},{16,8},{20,12},{24,0},{28,4},{1,25},{... | collective-permute-start | bytes 786440 | tf_op jit(solution)/shard_map/ppermute | solution.py:29
  57.4 12.3 %collective-permute-start.19 = (bf16[128,512]{1,0:T(8,128)(2,1)S(1)}, bf16[128,512]{1,0:T(8,128)(2,1)S(1)}, u32[]{:S(2)}, u32[]{:S(2)}) collective-permute-start(bf16[128,512]{1,0:T(8,128)(2,1)S(1)} %get-tuple-element.121), channel_id=1, source_target_pairs={{0,3},{1,2},{2,1},{3,0},{4,7},{5,6},{6,5},{7,4},{8,11},{9,10},{10,... | collective-permute-start | bytes 393224 | tf_op jit(solution)/shard_map/ppermute | solution.py:17
  60.5 10.9 %collective-permute-start.20 = (bf16[128,512]{1,0:T(8,128)(2,1)S(1)}, bf16[128,512]{1,0:T(8,128)(2,1)S(1)}, u32[]{:S(2)}, u32[]{:S(2)}) collective-permute-start(bf16[128,512]{1,0:T(8,128)(2,1)S(1)} %get-tuple-element.122), channel_id=1, source_target_pairs={{0,2},{1,3},{2,0},{3,1},{4,6},{5,7},{6,4},{7,5},{8,10},{9,11},{10,... | collective-permute-start | bytes 393224 | tf_op jit(solution)/shard_map/ppermute | solution.py:17
  68.3 5.2 %copy-start.1 = (bf16[128,512]{1,0:T(8,128)(2,1)S(1)}, bf16[128,512]{1,0:T(8,128)(2,1)}, u32[]{:S(2)}) copy-start(bf16[128,512]{1,0:T(8,128)(2,1)} %param.6) | copy-start | bytes 393220
  68.3 5.2 %collective-permute-start.21 = (bf16[128,512]{1,0:T(8,128)(2,1)S(1)}, bf16[128,512]{1,0:T(8,128)(2,1)S(1)}, u32[]{:S(2)}, u32[]{:S(2)}) collective-permute-start(bf16[128,512]{1,0:T(8,128)(2,1)S(1)} %fusion.11), channel_id=1, source_target_pairs={{0,1},{1,0},{2,3},{3,2},{4,5},{5,4},{6,7},{7,6},{8,9},{9,8},{10,11... | collective-permute-start | bytes 393224 | tf_op jit(solution)/shard_map/ppermute | solution.py:17
  74.3 6.4 %collective-permute-start.25 = (bf16[128,512]{1,0:T(8,128)(2,1)S(1)}, bf16[128,512]{1,0:T(8,128)(2,1)S(1)}, u32[]{:S(2)}, u32[]{:S(2)}) collective-permute-start(bf16[128,512]{1,0:T(8,128)(2,1)S(1)} %get-tuple-element.115), channel_id=1, source_target_pairs={{0,1},{1,0},{2,3},{3,2},{4,5},{5,4},{6,7},{7,6},{8,9},{9,8},{10,11... | collective-permute-start | bytes 393224 | tf_op jit(solution)/shard_map/ppermute | solution.py:17
  74.4 7.2 %collective-permute-start.22 = (bf16[1,128,512]{2,1,0:T(8,128)(2,1)S(1)}, bf16[1,128,512]{2,1,0:T(8,128)(2,1)S(1)}, u32[]{:S(2)}, u32[]{:S(2)}) collective-permute-start(bf16[1,128,512]{2,1,0:T(8,128)(2,1)S(1)} %bitcast.75), channel_id=1, source_target_pairs={{0,16},{4,20},{8,24},{12,28},{16,0},{20,4},{24,8},{28,12},{1,17},{... | collective-permute-start | bytes 393224 | tf_op jit(solution)/shard_map/ppermute | solution.py:29
  75.3 9.3 %collective-permute-start.29 = (bf16[128,512]{1,0:T(8,128)(2,1)S(1)}, bf16[128,512]{1,0:T(8,128)(2,1)S(1)}, u32[]{:S(2)}, u32[]{:S(2)}) collective-permute-start(bf16[128,512]{1,0:T(8,128)(2,1)S(1)} %get-tuple-element.115), channel_id=1, source_target_pairs={{0,3},{1,2},{2,1},{3,0},{4,7},{5,6},{6,5},{7,4},{8,11},{9,10},{10,... | collective-permute-start | bytes 393224 | tf_op jit(solution)/shard_map/ppermute | solution.py:17
  79.4 9.9 %collective-permute-start.28 = (bf16[128,512]{1,0:T(8,128)(2,1)S(1)}, bf16[128,512]{1,0:T(8,128)(2,1)S(1)}, u32[]{:S(2)}, u32[]{:S(2)}) collective-permute-start(bf16[128,512]{1,0:T(8,128)(2,1)S(1)} %get-tuple-element.115), channel_id=1, source_target_pairs={{0,2},{1,3},{2,0},{3,1},{4,6},{5,7},{6,4},{7,5},{8,10},{9,11},{10,... | collective-permute-start | bytes 393224 | tf_op jit(solution)/shard_map/ppermute | solution.py:17
  79.4 10.0 %collective-permute-start.24 = (bf16[1,128,512]{2,1,0:T(8,128)(2,1)S(1)}, bf16[1,128,512]{2,1,0:T(8,128)(2,1)S(1)}, u32[]{:S(2)}, u32[]{:S(2)}) collective-permute-start(bf16[1,128,512]{2,1,0:T(8,128)(2,1)S(1)} %bitcast.76), channel_id=1, source_target_pairs={{0,8},{4,12},{8,0},{12,4},{16,24},{20,28},{24,16},{28,20},{1,9},{5... | collective-permute-start | bytes 393224 | tf_op jit(solution)/shard_map/ppermute | solution.py:23
  80.6 11.2 %collective-permute-start.27 = (bf16[1,128,512]{2,1,0:T(8,128)(2,1)S(1)}, bf16[1,128,512]{2,1,0:T(8,128)(2,1)S(1)}, u32[]{:S(2)}, u32[]{:S(2)}) collective-permute-start(bf16[1,128,512]{2,1,0:T(8,128)(2,1)S(1)} %bitcast.79), channel_id=1, source_target_pairs={{0,16},{4,20},{8,24},{12,28},{16,0},{20,4},{24,8},{28,12},{1,17},{... | collective-permute-start | bytes 393224 | tf_op jit(solution)/shard_map/ppermute | solution.py:29
  81.7 10.2 %collective-permute-start.26 = (bf16[1,128,512]{2,1,0:T(8,128)(2,1)S(1)}, bf16[1,128,512]{2,1,0:T(8,128)(2,1)S(1)}, u32[]{:S(2)}, u32[]{:S(2)}) collective-permute-start(bf16[1,128,512]{2,1,0:T(8,128)(2,1)S(1)} %bitcast.80), channel_id=1, source_target_pairs={{0,8},{4,12},{8,0},{12,4},{16,24},{20,28},{24,16},{28,20},{1,9},{5... | collective-permute-start | bytes 393224 | tf_op jit(solution)/shard_map/ppermute | solution.py:23
  84.6 7.1 %collective-permute-start.23 = (bf16[1,128,512]{2,1,0:T(8,128)(2,1)S(1)}, bf16[1,128,512]{2,1,0:T(8,128)(2,1)S(1)}, u32[]{:S(2)}, u32[]{:S(2)}) collective-permute-start(bf16[1,128,512]{2,1,0:T(8,128)(2,1)S(1)} %collective-permute-done.22.refs_0_), channel_id=1, source_target_pairs={{0,8},{4,12},{8,0},{12,4},{16,24},{20,28},{24,16},{28,20},{1,9},{5... | collective-permute-start | bytes 393224 | tf_op jit(solution)/shard_map/ppermute | solution.py:23
  89.3 4.0 %collective-permute-start.32 = (bf16[2,128,512]{2,1,0:T(8,128)(2,1)S(1)}, bf16[2,128,512]{2,1,0:T(8,128)(2,1)S(1)}, u32[]{:S(2)}, u32[]{:S(2)}) collective-permute-start(bf16[2,128,512]{2,1,0:T(8,128)(2,1)S(1)} %pad_maximum_fusion.2.refs_2_), channel_id=1, source_target_pairs={{0,4},{4,0},{8,12},{12,8},{16,20},{20,16},{24,28},{28,24},{1,5},{5... | collective-permute-start | bytes 786440 | tf_op jit(solution)/shard_map/ppermute | solution.py:23
  89.4 9.1 %collective-permute-start.33 = (bf16[2,128,512]{2,1,0:T(8,128)(2,1)S(1)}, bf16[2,128,512]{2,1,0:T(8,128)(2,1)S(1)}, u32[]{:S(2)}, u32[]{:S(2)}) collective-permute-start(bf16[2,128,512]{2,1,0:T(8,128)(2,1)S(1)} %pad_maximum_fusion.2.refs_2_), channel_id=1, source_target_pairs={{0,8},{4,12},{8,0},{12,4},{16,24},{20,28},{24,16},{28,20},{1,9},{5... | collective-permute-start | bytes 786440 | tf_op jit(solution)/shard_map/ppermute | solution.py:23
  91.7 1.6 %collective-permute-start.31 = (bf16[1,128,512]{2,1,0:T(8,128)(2,1)S(1)}, bf16[1,128,512]{2,1,0:T(8,128)(2,1)S(1)}, u32[]{:S(2)}, u32[]{:S(2)}) collective-permute-start(bf16[1,128,512]{2,1,0:T(8,128)(2,1)S(1)} %bitcast.81), channel_id=1, source_target_pairs={{0,4},{4,0},{8,12},{12,8},{16,20},{20,16},{24,28},{28,24},{1,5},{5... | collective-permute-start | bytes 393224 | tf_op jit(solution)/shard_map/ppermute | solution.py:23
  91.8 1.5 %collective-permute-start.30 = (bf16[1,128,512]{2,1,0:T(8,128)(2,1)S(1)}, bf16[1,128,512]{2,1,0:T(8,128)(2,1)S(1)}, u32[]{:S(2)}, u32[]{:S(2)}) collective-permute-start(bf16[1,128,512]{2,1,0:T(8,128)(2,1)S(1)} %bitcast.77), channel_id=1, source_target_pairs={{0,4},{4,0},{8,12},{12,8},{16,20},{20,16},{24,28},{28,24},{1,5},{5... | collective-permute-start | bytes 393224 | tf_op jit(solution)/shard_map/ppermute | solution.py:23
  92.2 8.6 %collective-permute-start.38 = (bf16[2,128,512]{2,1,0:T(8,128)(2,1)S(1)}, bf16[2,128,512]{2,1,0:T(8,128)(2,1)S(1)}, u32[]{:S(2)}, u32[]{:S(2)}) collective-permute-start(bf16[2,128,512]{2,1,0:T(8,128)(2,1)S(1)} %pad_maximum_fusion.2.refs_2_), channel_id=1, source_target_pairs={{0,16},{4,20},{8,24},{12,28},{16,0},{20,4},{24,8},{28,12},{1,17},{... | collective-permute-start | bytes 786440 | tf_op jit(solution)/shard_map/ppermute | solution.py:29
  98.5 6.1 %collective-permute-start.36 = (bf16[2,128,512]{2,1,0:T(8,128)(2,1)S(1)}, bf16[2,128,512]{2,1,0:T(8,128)(2,1)S(1)}, u32[]{:S(2)}, u32[]{:S(2)}) collective-permute-start(bf16[2,128,512]{2,1,0:T(8,128)(2,1)S(1)} %collective-permute-done.33.refs_2_), channel_id=1, source_target_pairs={{0,4},{4,0},{8,12},{12,8},{16,20},{20,16},{24,28},{28,24},{1,5},{5... | collective-permute-start | bytes 786440 | tf_op jit(solution)/shard_map/ppermute | solution.py:23
  98.6 6.1 %collective-permute-start.37 = (bf16[1,128,512]{2,1,0:T(8,128)(2,1)S(1)}, bf16[1,128,512]{2,1,0:T(8,128)(2,1)S(1)}, u32[]{:S(2)}, u32[]{:S(2)}) collective-permute-start(bf16[1,128,512]{2,1,0:T(8,128)(2,1)S(1)} %collective-permute-done.27.refs_1_), channel_id=1, source_target_pairs={{0,8},{4,12},{8,0},{12,4},{16,24},{20,28},{24,16},{28,20},{1,9},{5... | collective-permute-start | bytes 393224 | tf_op jit(solution)/shard_map/ppermute | solution.py:23
  100.3 4.4 %collective-permute-start.34 = (bf16[1,128,512]{2,1,0:T(8,128)(2,1)S(1)}, bf16[1,128,512]{2,1,0:T(8,128)(2,1)S(1)}, u32[]{:S(2)}, u32[]{:S(2)}) collective-permute-start(bf16[1,128,512]{2,1,0:T(8,128)(2,1)S(1)} %collective-permute-done.24.refs_0_), channel_id=1, source_target_pairs={{0,4},{4,0},{8,12},{12,8},{16,20},{20,16},{24,28},{28,24},{1,5},{5... | collective-permute-start | bytes 393224 | tf_op jit(solution)/shard_map/ppermute | solution.py:23
  100.5 4.2 %collective-permute-start.35 = (bf16[1,128,512]{2,1,0:T(8,128)(2,1)S(1)}, bf16[1,128,512]{2,1,0:T(8,128)(2,1)S(1)}, u32[]{:S(2)}, u32[]{:S(2)}) collective-permute-start(bf16[1,128,512]{2,1,0:T(8,128)(2,1)S(1)} %collective-permute-done.26.refs_1_), channel_id=1, source_target_pairs={{0,4},{4,0},{8,12},{12,8},{16,20},{20,16},{24,28},{28,24},{1,5},{5... | collective-permute-start | bytes 393224 | tf_op jit(solution)/shard_map/ppermute | solution.py:23
  100.8 9.8 %collective-permute-start.42 = (bf16[2,128,512]{2,1,0:T(8,128)(2,1)S(1)}, bf16[2,128,512]{2,1,0:T(8,128)(2,1)S(1)}, u32[]{:S(2)}, u32[]{:S(2)}) collective-permute-start(bf16[2,128,512]{2,1,0:T(8,128)(2,1)S(1)} %pad_maximum_fusion.2.refs_2_), channel_id=1, source_target_pairs={{0,24},{4,28},{8,16},{12,20},{16,8},{20,12},{24,0},{28,4},{1,25},{... | collective-permute-start | bytes 786440 | tf_op jit(solution)/shard_map/ppermute | solution.py:29
  108.5 2.2 %collective-permute-start.41 = (bf16[2,128,512]{2,1,0:T(8,128)(2,1)S(1)}, bf16[2,128,512]{2,1,0:T(8,128)(2,1)S(1)}, u32[]{:S(2)}, u32[]{:S(2)}) collective-permute-start(bf16[2,128,512]{2,1,0:T(8,128)(2,1)S(1)} %collective-permute-done.38.refs_2_), channel_id=1, source_target_pairs={{0,4},{4,0},{8,12},{12,8},{16,20},{20,16},{24,28},{28,24},{1,5},{5... | collective-permute-start | bytes 786440 | tf_op jit(solution)/shard_map/ppermute | solution.py:23
  108.5 2.1 %collective-permute-start.39 = (bf16[1,128,512]{2,1,0:T(8,128)(2,1)S(1)}, bf16[1,128,512]{2,1,0:T(8,128)(2,1)S(1)}, u32[]{:S(2)}, u32[]{:S(2)}) collective-permute-start(bf16[1,128,512]{2,1,0:T(8,128)(2,1)S(1)} %collective-permute-done.22.refs_0_), channel_id=1, source_target_pairs={{0,4},{4,0},{8,12},{12,8},{16,20},{20,16},{24,28},{28,24},{1,5},{5... | collective-permute-start | bytes 393224 | tf_op jit(solution)/shard_map/ppermute | solution.py:23
  109.0 1.6 %collective-permute-start.40 = (bf16[1,128,512]{2,1,0:T(8,128)(2,1)S(1)}, bf16[1,128,512]{2,1,0:T(8,128)(2,1)S(1)}, u32[]{:S(2)}, u32[]{:S(2)}) collective-permute-start(bf16[1,128,512]{2,1,0:T(8,128)(2,1)S(1)} %collective-permute-done.27.refs_1_), channel_id=1, source_target_pairs={{0,4},{4,0},{8,12},{12,8},{16,20},{20,16},{24,28},{28,24},{1,5},{5... | collective-permute-start | bytes 393224 | tf_op jit(solution)/shard_map/ppermute | solution.py:23
  113.9 2.0 %collective-permute-start.45 = (bf16[2,128,512]{2,1,0:T(8,128)(2,1)S(1)}, bf16[2,128,512]{2,1,0:T(8,128)(2,1)S(1)}, u32[]{:S(2)}, u32[]{:S(2)}) collective-permute-start(bf16[2,128,512]{2,1,0:T(8,128)(2,1)S(1)} %collective-permute-done.42.refs_2_), channel_id=1, source_target_pairs={{0,4},{4,0},{8,12},{12,8},{16,20},{20,16},{24,28},{28,24},{1,5},{5... | collective-permute-start | bytes 786440 | tf_op jit(solution)/shard_map/ppermute | solution.py:23
  114.0 1.7 %collective-permute-start.43 = (bf16[1,128,512]{2,1,0:T(8,128)(2,1)S(1)}, bf16[1,128,512]{2,1,0:T(8,128)(2,1)S(1)}, u32[]{:S(2)}, u32[]{:S(2)}) collective-permute-start(bf16[1,128,512]{2,1,0:T(8,128)(2,1)S(1)} %collective-permute-done.23.refs_0_), channel_id=1, source_target_pairs={{0,4},{4,0},{8,12},{12,8},{16,20},{20,16},{24,28},{28,24},{1,5},{5... | collective-permute-start | bytes 393224 | tf_op jit(solution)/shard_map/ppermute | solution.py:23
  114.5 1.4 %collective-permute-start.44 = (bf16[1,128,512]{2,1,0:T(8,128)(2,1)S(1)}, bf16[1,128,512]{2,1,0:T(8,128)(2,1)S(1)}, u32[]{:S(2)}, u32[]{:S(2)}) collective-permute-start(bf16[1,128,512]{2,1,0:T(8,128)(2,1)S(1)} %collective-permute-done.37.refs_1_), channel_id=1, source_target_pairs={{0,4},{4,0},{8,12},{12,8},{16,20},{20,16},{24,28},{28,24},{1,5},{5... | collective-permute-start | bytes 393224 | tf_op jit(solution)/shard_map/ppermute | solution.py:23

commit v4 on v1

--- a/solution.py
+++ b/solution.py
@@ -361,19 +361,20 @@
     enc_weight = pltpu.with_memory_space_constraint(enc_weight, pltpu.HBM)
     dec_weight = pltpu.with_memory_space_constraint(dec_weight, pltpu.HBM)
 
-    held = {0: all_over_feat(tokens_in)}
-    for bit_level in range(bit_count - 1, 0, -1):
-        for rel in list(held):
-            held[rel ^ 2**bit_level] = [None] * feat_count
+    order = [rel for pair in range(0, sub_count, 2) for rel in (pair, pair ^ 1)]
+    held = {rel: [None] * feat_count for rel in order[::2]}
+    held[0] = all_over_feat(tokens_in)
+    enc_held, dec_held = fetch(enc_weight, after(dec_weight, held[0][1]))
     for s in range(feat_count):
         known = [0]
         for bit_level in range(bit_count - 1, 0, -1):
             for rel in known:
-                held[rel ^ 2**bit_level][s] = over_members(held[rel][s], bit_level)
+                value = after(held[rel][s], dec_held) if s > 1 else held[rel][s]
+                held[rel ^ 2**bit_level][s] = over_members(value, bit_level)
             known += [rel ^ 2**bit_level for rel in known]
-    order = [rel for pair in sorted(held) for rel in (pair, pair ^ 1)]
-    enc_held, dec_held = fetch(enc_weight, after(dec_weight, held[0][1]))
-    early = [held[rel][s] for rel in order[2::2] for s in range(2)]
+    early = [
+        held[rel][s] for rel in order[2::2] for s in range(feat_count) if 2 * s != feat_count
+    ]
     tokens = {0: after(jnp.stack(held[0], 0), enc_held, *early)}
     tokens[1] = over_members(tokens[0], 0)
     partial = encode(info, [0, 1], [tokens[0], tokens[1]], enc_held, None, None)
@@ -470,30 +471,24 @@
             early.pop()
 
     feature_grad, dec_grad, squares = None, None, {}
-    for number, stage in enumerate(stages):
-        for k in range(layers):
-            for rel in stage:
-                parts = groups_of[rel, k]
-                if feature_grad is None:
-                    parts = [after(parts[0], *early)] + parts[1:]
-                else:
-                    parts = [after(part, feature_grad) for part in parts]
-                if k == 0 and number > 0:
-                    feature_grad = after(feature_grad, groups_of[rel, layers - 1][-1])
-                elif k > 0 and number + 1 < len(stages):
-                    coming = [groups_of[other, k - 1][-1] for other in stages[number + 1]]
-                    feature_grad = after(feature_grad, *coming)
-                feature_grad, dec_grad, squares[k, rel] = backward_pair(
-                    info,
-                    rel,
-                    k,
-                    parts,
-                    [over_members(part, 0) for part in parts],
-                    turned_features,
-                    dec_held,
-                    feature_grad,
-                    dec_grad,
-                )
+    for k in range(layers):
+        for rel in [rel for stage in stages for rel in stage]:
+            parts = groups_of[rel, k]
+            if feature_grad is None:
+                parts = [after(parts[0], *early)] + parts[1:]
+            elif rel > 0:
+                parts = [after(part, feature_grad) for part in parts]
+            feature_grad, dec_grad, squares[k, rel] = backward_pair(
+                info,
+                rel,
+                k,
+                parts,
+                [over_members(part, 0) for part in parts],
+                turned_features,
+                dec_held,
+                feature_grad,
+                dec_grad,
+            )
     scale = (tok / loss_scale) ** 2 / (layers * tok * depth)
     enc_grad, bias_grad, mean_square = encoder_grad(
         info,

time: 116 us -> 118 us (1.017)
  starting transfers between devices: 44.2 us -> 46.5 us
    ppermute x9, starting transfers between devices: 11.8 us -> 17.9 us  [over_feat(): return lax.ppermute(value, 'feat', pairs)]
    ppermute x4, waiting for transfers between devices: 4.15 us -> 0.01 us  [from_layer(): return lax.ppermute(value, 'layer', pairs)]
    ppermute x34, waiting for transfers between devices: 12.5 us -> 16.1 us  [over_members(): return lax.ppermute(value, 'layer', pairs)]
    ppermute x34, starting transfers between devices: 21.5 us -> 18.2 us  [over_members(): return lax.ppermute(value, 'layer', pairs)]
    ppermute x4, waiting for transfers between devices: 3.34 us -> 5.68 us  [to_layer(): moved = lax.ppermute(value, 'layer', pairs)]
    ppermute x9, waiting for transfers between devices: 14.3 us -> 12.2 us  [over_feat(): return lax.ppermute(value, 'feat', pairs)]
  transfers between devices with their start and end apart: 51 -> 51, of which waited for: 20 -> 19; matrix products, arithmetic and copies ran while one was open for 1% -> 1% of each run, Pallas kernels for 19% -> 19%
where the time goes in v4:
time: 118 us
  starting transfers between devices  46.5 us (39%)
  Pallas kernels  34.4 us (29%)
  waiting for transfers between devices  34 us (29%)
  other arithmetic  1.97 us (2%)
  between operations  1.21 us (1%)
    ppermute x34, starting transfers between devices, over_members(): return lax.ppermute(value, 'layer', pairs)  18.2 us
    ppermute x9, starting transfers between devices, over_feat(): return lax.ppermute(value, 'feat', pairs)  17.9 us
    ppermute x34, waiting for transfers between devices, over_members(): return lax.ppermute(value, 'layer', pairs)  16.1 us
    pallas_call x4, Pallas kernels, backward_pair(): pl.pallas_call(kernel, in_specs=[in_smem] + [in_vmem] * (len(inputs) + 2)...  13.6 us
    ppermute x9, waiting for transfers between devices, over_feat(): return lax.ppermute(value, 'feat', pairs)  12.2 us
    pallas_call x2, Pallas kernels, decode(): pl.pallas_call(kernel, in_specs=[in_smem, in_vmem, in_vmem], out_specs=[i...  5.79 us
    ppermute x4, waiting for transfers between devices, to_layer(): moved = lax.ppermute(value, 'layer', pairs)  5.68 us
    ppermute x4, starting transfers between devices, to_layer(): moved = lax.ppermute(value, 'layer', pairs)  5.33 us
  transfers between devices with their start and end apart: 51, of which 19 were waited for; matrix products, arithmetic and copies ran while one was open for 1% of the time, Pallas kernels for 19%

profile of v4, /device:TPU:0, one launch (start us, length us, event | category | flops | bytes accessed | tf_op | source)
XLA Modules:
  0.0 118.2 jit_solution(16359634386292973182)
XLA Ops:
  0.7 3.0 %collective-permute-start.1 = (bf16[128,512]{1,0:T(8,128)(2,1)}, bf16[128,512]{1,0:T(8,128)(2,1)S(1)}, u32[]{:S(2)}, u32[]{:S(2)}) collective-permute-start(bf16[128,512]{1,0:T(8,128)(2,1)} %param.5), channel_id=1, source_target_pairs={{0,1},{1,0},{2,3},{3,2},{4,5},{5,4},{6,7},{7,6},{8,9},{9,8},{10,11... | collective-permute-start | bytes 393224 | tf_op jit(solution)/shard_map/ppermute | solution.py:17
  3.8 2.5 %collective-permute-start.3 = (bf16[128,512]{1,0:T(8,128)(2,1)}, bf16[128,512]{1,0:T(8,128)(2,1)S(1)}, u32[]{:S(2)}, u32[]{:S(2)}) collective-permute-start(bf16[128,512]{1,0:T(8,128)(2,1)} %param.5), channel_id=1, source_target_pairs={{0,3},{1,2},{2,1},{3,0},{4,7},{5,6},{6,5},{7,4},{8,11},{9,10},{10,... | collective-permute-start | bytes 393224 | tf_op jit(solution)/shard_map/ppermute | solution.py:17
  6.4 1.5 %collective-permute-start = (bf16[128,512]{1,0:T(8,128)(2,1)}, bf16[128,512]{1,0:T(8,128)(2,1)S(1)}, u32[]{:S(2)}, u32[]{:S(2)}) collective-permute-start(bf16[128,512]{1,0:T(8,128)(2,1)} %param.5), channel_id=1, source_target_pairs={{0,8},{4,12},{8,0},{12,4},{16,24},{20,28},{24,16},{28,20},{1,9},{5... | collective-permute-start | bytes 393224 | tf_op jit(solution)/shard_map/ppermute | solution.py:23
  7.9 4.7 %fetch.1 = (bf16[2048,1024]{1,0:T(8,128)(2,1)S(1)}, bf16[2,1024,2048]{2,1,0:T(8,128)(2,1)S(1)}) custom-call(bf16[2048,1024]{1,0:T(8,128)(2,1)} %refs_0_.1, bf16[2,1024,2048]{2,1,0:T(8,128)(2,1)} %refs_1_), custom_call_target="tpu_custom_call" | custom-call | bytes 12582912 | tf_op jit(solution)/shard_map/fetch/pallas_call | solution.py:87
  12.6 1.1 collective-permute-done.3
  13.7 1.5 %collective-permute-start.5 = (bf16[128,512]{1,0:T(8,128)(2,1)S(1)}, bf16[128,512]{1,0:T(8,128)(2,1)S(1)}, u32[]{:S(2)}, u32[]{:S(2)}) collective-permute-start(bf16[128,512]{1,0:T(8,128)(2,1)S(1)} %collective-permute-done.3), channel_id=1, source_target_pairs={{0,8},{4,12},{8,0},{12,4},{16,24},{20,28},{24,16},{28,20},{1,9},{5... | collective-permute-start | bytes 393224 | tf_op jit(solution)/shard_map/ppermute | solution.py:23
  15.2 0.5 collective-permute-start.4
  15.8 2.5 %collective-permute-done.2 = bf16[128,512]{1,0:T(8,128)(2,1)S(1)} collective-permute-done((bf16[128,512]{1,0:T(8,128)(2,1)}, bf16[128,512]{1,0:T(8,128)(2,1)S(1)}, u32[]{:S(2)}, u32[]{:S(2)}) %collective-permute-start.2) | collective-permute-done | bytes 131104 | tf_op jit(solution)/shard_map/ppermute | solution.py:17
  18.3 0.4 collective-permute-done.5
  18.7 1.5 %collective-permute-done.4 = bf16[128,512]{1,0:T(8,128)(2,1)S(1)} collective-permute-done((bf16[128,512]{1,0:T(8,128)(2,1)S(1)}, bf16[128,512]{1,0:T(8,128)(2,1)S(1)}, u32[]{:S(2)}, u32[]{:S(2)}) %collective-permute-start.4) | collective-permute-done | bytes 131104 | tf_op jit(solution)/shard_map/ppermute | solution.py:23
  20.2 1.4 %collective-permute-start.7 = (bf16[128,512]{1,0:T(8,128)(2,1)S(1)}, bf16[128,512]{1,0:T(8,128)(2,1)S(1)}, u32[]{:S(2)}, u32[]{:S(2)}) collective-permute-start(bf16[128,512]{1,0:T(8,128)(2,1)S(1)} %collective-permute-done.2), channel_id=1, source_target_pairs={{0,8},{4,12},{8,0},{12,4},{16,24},{20,28},{24,16},{28,20},{1,9},{5... | collective-permute-start | bytes 393224 | tf_op jit(solution)/shard_map/ppermute | solution.py:23
  21.6 0.5 collective-permute-done.6.refs_1_
  22.1 1.8 %encode.3.refs_2_ = f32[512,1024]{1,0:T(8,128)S(1)} custom-call(s32[2]{0:T(128)S(1)} %pad_add_fusion.info_ref, bf16[4,128,512]{2,1,0:T(8,128)(2,1)S(1)} %pad_maximum_fusion.refs_0_, bf16[4,128,512]{2,1,0:T(8,128)(2,1)S(1)} %collective-permute-done.6.refs_1_, bf16[2048,1024]{1,0:T(8,128)(2,1)S(1)} %get-tuple-element.71.refs_2_.refs_1_), custom_call_target="tpu_custom_call" | custom-call | flops 1073741824 | bytes 3145728 | tf_op jit(solution)/shard_map/encode/pallas_call | solution.py:127
  23.9 2.2 %collective-permute-done.7 = bf16[128,512]{1,0:T(8,128)(2,1)S(1)} collective-permute-done((bf16[128,512]{1,0:T(8,128)(2,1)S(1)}, bf16[128,512]{1,0:T(8,128)(2,1)S(1)}, u32[]{:S(2)}, u32[]{:S(2)}) %collective-permute-start.7) | collective-permute-done | bytes 131104 | tf_op jit(solution)/shard_map/ppermute | solution.py:23
  26.3 1.3 %encode.4.refs_2_ = f32[512,1024]{1,0:T(8,128)S(1)} custom-call(s32[2]{0:T(128)S(1)} %pad_add_fusion.info_ref, bf16[4,128,512]{2,1,0:T(8,128)(2,1)S(1)} %pad_maximum_fusion.1.refs_0_, bf16[2048,1024]{1,0:T(8,128)(2,1)S(1)} %get-tuple-element.71.refs_2_.refs_1_, f32[512,1024]{1,0:T(8,128)S(1)} %encode.3.refs_2_), custom_call_target="tpu_custom_call" | custom-call | flops 536870912 | bytes 1572864 | tf_op jit(solution)/shard_map/encode/pallas_call | solution.py:127
  27.5 0.6 collective-permute-done.8.refs_0_
  28.2 1.4 %encode.5.feat_ref.in_ref.refs_4_ = bf16[2,512,1024]{2,1,0:T(8,128)(2,1)S(1)} custom-call(s32[2]{0:T(128)S(1)} %pad_add_fusion.info_ref, bf16[4,128,512]{2,1,0:T(8,128)(2,1)S(1)} %collective-permute-done.8.refs_0_, bf16[2048,1024]{1,0:T(8,128)(2,1)S(1)} %get-tuple-element.71.refs_2_.refs_1_, f32[512,1024]{1,0:T(8,128)S(1)} %encode.4.refs_2_, ...), custom_call_target="tpu_custom_call" | custom-call | flops 536870912 | bytes 1572864 | tf_op jit(solution)/shard_map/encode/pallas_call | solution.py:127
  29.6 2.9 %decode.2 = (bf16[2,2,128,512]{3,2,1,0:T(8,128)(2,1)S(1)}, bf16[2,1,128,512]{3,2,1,0:T(8,128)(2,1)S(1)}, bf16[2,1,128,512]{3,2,1,0:T(8,128)(2,1)S(1)}, bf16[2,2,...) custom-call(s32[2]{0:T(128)S(1)} %pad_add_fusion.info_ref, ...), custom_call_target="tpu_custom_call" | custom-call | flops 2147483648 | bytes 4194304 | tf_op jit(solution)/shard_map/decode/pallas_call | solution.py:165
  32.7 0.4 collective-permute-start.14
  33.2 0.9 collective-permute-done.9
  34.2 2.9 %decode.3 = (bf16[2,2,128,512]{3,2,1,0:T(8,128)(2,1)S(1)}, bf16[2,1,128,512]{3,2,1,0:T(8,128)(2,1)S(1)}, bf16[2,1,128,512]{3,2,1,0:T(8,128)(2,1)S(1)}, bf16[2,2,...) custom-call(s32[2]{0:T(128)S(1)} %pad_add_fusion.info_ref, ...), custom_call_target="tpu_custom_call" | custom-call | flops 2147483648 | bytes 4194304 | tf_op jit(solution)/shard_map/decode/pallas_call | solution.py:165
  37.3 0.4 collective-permute-start.12
  37.7 1.5 %collective-permute-start.15 = (bf16[1,1,128,512]{3,2,1,0:T(8,128)(2,1)S(1)}, bf16[1,1,128,512]{3,2,1,0:T(8,128)(2,1)S(1)}, u32[]{:S(2)}, u32[]{:S(2)}) collective-permute-start(bf16[1,1,128,512]{3,2,1,0:T(8,128)(2,1)S(1)} %slice_bitcast_fusion.10), channel_id=1, source_target_pairs={{0,8},{4,12},{8,0},{12,4},{16,24},{20,28},{24,16},{28,20},{1,9},{5... | collective-permute-start | bytes 393224 | tf_op jit(solution)/shard_map/ppermute | solution.py:23
  39.3 1.3 %collective-permute-start.18 = (bf16[1,1,128,512]{3,2,1,0:T(8,128)(2,1)S(1)}, bf16[1,1,128,512]{3,2,1,0:T(8,128)(2,1)S(1)}, u32[]{:S(2)}, u32[]{:S(2)}) collective-permute-start(bf16[1,1,128,512]{3,2,1,0:T(8,128)(2,1)S(1)} %slice_bitcast_fusion.12), channel_id=1, source_target_pairs={{0,8},{4,12},{8,0},{12,4},{16,24},{20,28},{24,16},{28,20},{1,9},{5... | collective-permute-start | bytes 393224 | tf_op jit(solution)/shard_map/ppermute | solution.py:23
  40.6 3.4 %collective-permute-done.15 = bf16[1,1,128,512]{3,2,1,0:T(8,128)(2,1)S(1)} collective-permute-done((bf16[1,1,128,512]{3,2,1,0:T(8,128)(2,1)S(1)}, bf16[1,1,128,512]{3,2,1,0:T(8,128)(2,1)S(1)}, u32[]{:S(2)}, u32[]{:S(2)}) %collective-permute-start.15) | collective-permute-done | bytes 131104 | tf_op jit(solution)/shard_map/ppermute | solution.py:23
  44.0 1.5 %collective-permute-start.16 = (bf16[1,1,128,512]{3,2,1,0:T(8,128)(2,1)S(1)}, bf16[1,1,128,512]{3,2,1,0:T(8,128)(2,1)S(1)}, u32[]{:S(2)}, u32[]{:S(2)}) collective-permute-start(bf16[1,1,128,512]{3,2,1,0:T(8,128)(2,1)S(1)} %slice_bitcast_fusion.11), channel_id=1, source_target_pairs={{0,8},{4,12},{8,0},{12,4},{16,24},{20,28},{24,16},{28,20},{1,9},{5... | collective-permute-start | bytes 393224 | tf_op jit(solution)/shard_map/ppermute | solution.py:23
  45.8 1.6 %collective-permute-start.13 = (bf16[1,2,128,512]{3,2,1,0:T(8,128)(2,1)S(1)}, bf16[1,2,128,512]{3,2,1,0:T(8,128)(2,1)S(1)}, u32[]{:S(2)}, u32[]{:S(2)}) collective-permute-start(bf16[1,2,128,512]{3,2,1,0:T(8,128)(2,1)S(1)} %get-tuple-element.90), channel_id=1, source_target_pairs={{0,16},{4,20},{8,24},{12,28},{16,0},{20,4},{24,8},{28,12},{1,17},{... | collective-permute-start | bytes 786440 | tf_op jit(solution)/shard_map/ppermute | solution.py:29
  47.4 0.6 collective-permute-start.20
  48.0 0.6 collective-permute-start.21
  48.5 1.2 %collective-permute-done.16 = bf16[1,1,128,512]{3,2,1,0:T(8,128)(2,1)S(1)} collective-permute-done((bf16[1,1,128,512]{3,2,1,0:T(8,128)(2,1)S(1)}, bf16[1,1,128,512]{3,2,1,0:T(8,128)(2,1)S(1)}, u32[]{:S(2)}, u32[]{:S(2)}) %collective-permute-start.16) | collective-permute-done | bytes 131104 | tf_op jit(solution)/shard_map/ppermute | solution.py:23
  49.8 1.6 %collective-permute-start.22 = (bf16[1,1,128,512]{3,2,1,0:T(8,128)(2,1)S(1)}, bf16[1,1,128,512]{3,2,1,0:T(8,128)(2,1)S(1)}, u32[]{:S(2)}, u32[]{:S(2)}) collective-permute-start(bf16[1,1,128,512]{3,2,1,0:T(8,128)(2,1)S(1)} %fusion.10), channel_id=1, source_target_pairs={{0,16},{4,20},{8,24},{12,28},{16,0},{20,4},{24,8},{28,12},{1,17},{... | collective-permute-start | bytes 393224 | tf_op jit(solution)/shard_map/ppermute | solution.py:29
  51.4 5.1 %collective-permute-done.20 = bf16[1,1,128,512]{3,2,1,0:T(8,128)(2,1)S(1)} collective-permute-done((bf16[1,1,128,512]{3,2,1,0:T(8,128)(2,1)S(1)}, bf16[1,1,128,512]{3,2,1,0:T(8,128)(2,1)S(1)}, u32[]{:S(2)}, u32[]{:S(2)}) %collective-permute-start.20) | collective-permute-done | bytes 131104 | tf_op jit(solution)/shard_map/ppermute | solution.py:29
  56.8 0.7 collective-permute-start.19
  57.5 0.4 collective-permute-done.22
  58.0 1.6 %collective-permute-start.23 = (bf16[1,2,128,512]{3,2,1,0:T(8,128)(2,1)S(1)}, bf16[1,2,128,512]{3,2,1,0:T(8,128)(2,1)S(1)}, u32[]{:S(2)}, u32[]{:S(2)}) collective-permute-start(bf16[1,2,128,512]{3,2,1,0:T(8,128)(2,1)S(1)} %get-tuple-element.102), channel_id=1, source_target_pairs={{0,16},{4,20},{8,24},{12,28},{16,0},{20,4},{24,8},{28,12},{1,17},{... | collective-permute-start | bytes 786440 | tf_op jit(solution)/shard_map/ppermute | solution.py:29
  59.5 4.4 %collective-permute-start.24 = (bf16[128,512]{1,0:T(8,128)(2,1)S(1)}, bf16[128,512]{1,0:T(8,128)(2,1)S(1)}, u32[]{:S(2)}, u32[]{:S(2)}) collective-permute-start(bf16[128,512]{1,0:T(8,128)(2,1)S(1)} %fusion.16), channel_id=1, source_target_pairs={{0,3},{1,2},{2,1},{3,0},{4,7},{5,6},{6,5},{7,4},{8,11},{9,10},{10,... | collective-permute-start | bytes 393224 | tf_op jit(solution)/shard_map/ppermute | solution.py:17
  64.0 0.2 collective-permute-start.25
  64.5 3.3 %collective-permute-start.26 = (bf16[128,512]{1,0:T(8,128)(2,1)S(1)}, bf16[128,512]{1,0:T(8,128)(2,1)S(1)}, u32[]{:S(2)}, u32[]{:S(2)}) collective-permute-start(bf16[128,512]{1,0:T(8,128)(2,1)S(1)} %fusion.18), channel_id=1, source_target_pairs={{0,1},{1,0},{2,3},{3,2},{4,5},{5,4},{6,7},{7,6},{8,9},{9,8},{10,11... | collective-permute-start | bytes 393224 | tf_op jit(solution)/shard_map/ppermute | solution.py:17
  67.8 0.3 turned.5
  68.9 4.2 %collective-permute-done.25 = bf16[128,512]{1,0:T(8,128)(2,1)S(1)} collective-permute-done((bf16[128,512]{1,0:T(8,128)(2,1)S(1)}, bf16[128,512]{1,0:T(8,128)(2,1)S(1)}, u32[]{:S(2)}, u32[]{:S(2)}) %collective-permute-start.25) | collective-permute-done | bytes 131104 | tf_op jit(solution)/shard_map/ppermute | solution.py:17
  73.1 0.8 multiply_convert_fusion
  73.9 1.1 collective-permute-start.27
  75.1 3.7 %collective-permute-start.31 = (bf16[128,512]{1,0:T(8,128)(2,1)S(1)}, bf16[128,512]{1,0:T(8,128)(2,1)S(1)}, u32[]{:S(2)}, u32[]{:S(2)}) collective-permute-start(bf16[128,512]{1,0:T(8,128)(2,1)S(1)} %get-tuple-element.131), channel_id=1, source_target_pairs={{0,2},{1,3},{2,0},{3,1},{4,6},{5,7},{6,4},{7,5},{8,10},{9,11},{10,... | collective-permute-start | bytes 393224 | tf_op jit(solution)/shard_map/ppermute | solution.py:17
  78.8 0.5 collective-permute-start.32
  79.3 0.8 collective-permute-start.37
  80.2 1.2 %collective-permute-start.28 = (bf16[1,128,512]{2,1,0:T(8,128)(2,1)S(1)}, bf16[1,128,512]{2,1,0:T(8,128)(2,1)S(1)}, u32[]{:S(2)}, u32[]{:S(2)}) collective-permute-start(bf16[1,128,512]{2,1,0:T(8,128)(2,1)S(1)} %collective-permute-done.27.refs_0_), channel_id=1, source_target_pairs={{0,8},{4,12},{8,0},{12,4},{16,24},{20,28},{24,16},{28,20},{1,9},{5... | collective-permute-start | bytes 393224 | tf_op jit(solution)/shard_map/ppermute | solution.py:23
  81.4 1.0 collective-permute-start.30
  82.3 4.4 %collective-permute-done.31 = bf16[128,512]{1,0:T(8,128)(2,1)S(1)} collective-permute-done((bf16[128,512]{1,0:T(8,128)(2,1)S(1)}, bf16[128,512]{1,0:T(8,128)(2,1)S(1)}, u32[]{:S(2)}, u32[]{:S(2)}) %collective-permute-start.31) | collective-permute-done | bytes 131104 | tf_op jit(solution)/shard_map/ppermute | solution.py:17
  87.1 1.9 %collective-permute-start.42 = (bf16[2,128,512]{2,1,0:T(8,128)(2,1)S(1)}, bf16[2,128,512]{2,1,0:T(8,128)(2,1)S(1)}, u32[]{:S(2)}, u32[]{:S(2)}) collective-permute-start(bf16[2,128,512]{2,1,0:T(8,128)(2,1)S(1)} %pad_maximum_fusion.2.refs_2_), channel_id=1, source_target_pairs={{0,8},{4,12},{8,0},{12,4},{16,24},{20,28},{24,16},{28,20},{1,9},{5... | collective-permute-start | bytes 786440 | tf_op jit(solution)/shard_map/ppermute | solution.py:23
  89.0 1.5 %collective-permute-start.33 = (bf16[2,128,512]{2,1,0:T(8,128)(2,1)S(1)}, bf16[2,128,512]{2,1,0:T(8,128)(2,1)S(1)}, u32[]{:S(2)}, u32[]{:S(2)}) collective-permute-start(bf16[2,128,512]{2,1,0:T(8,128)(2,1)S(1)} %pad_maximum_fusion.2.refs_2_), channel_id=1, source_target_pairs={{0,16},{4,20},{8,24},{12,28},{16,0},{20,4},{24,8},{28,12},{1,17},{... | collective-permute-start | bytes 786440 | tf_op jit(solution)/shard_map/ppermute | solution.py:36
  90.5 2.6 %collective-permute-done.38.refs_1_ = bf16[1,128,512]{2,1,0:T(8,128)(2,1)S(1)} collective-permute-done((bf16[1,128,512]{2,1,0:T(8,128)(2,1)S(1)}, bf16[1,128,512]{2,1,0:T(8,128)(2,1)S(1)}, u32[]{:S(2)}, u32[]{:S(2)}) %collective-permute-start.38) | collective-permute-done | bytes 131104 | tf_op jit(solution)/shard_map/ppermute | solution.py:23
  93.2 1.3 %collective-permute-done.39.refs_3_ = bf16[1,128,512]{2,1,0:T(8,128)(2,1)S(1)} collective-permute-done((bf16[1,128,512]{2,1,0:T(8,128)(2,1)S(1)}, bf16[1,128,512]{2,1,0:T(8,128)(2,1)S(1)}, u32[]{:S(2)}, u32[]{:S(2)}) %collective-permute-start.39) | collective-permute-done | bytes 131104 | tf_op jit(solution)/shard_map/ppermute | solution.py:23
  94.5 3.3 %backward_pair.4 = (f32[512,1024]{1,0:T(8,128)S(1)}, bf16[2,1024,2048]{2,1,0:T(8,128)(2,1)}, f32[8,128]{1,0:T(8,128)S(1)}) custom-call(s32[2]{0:T(128)S(1)} %pad_add_fusion.info_ref, bf16[1,128,512]{2,1,0:T(8,128)(2,1)S(1)} %bitcast.114, bf16[1,128,512]{2,1,0:T(8,128)(2,1)S(1)} %bitcast.118, bf16[2,128,512]{2,1,0:T(8,128)(2,1)S(1)} %pad_maximum_fusion.2.refs_2_, ...), custom_call_target="tpu_custom_call" | custom-call | flops 262144 | bytes 262144 | tf_op jit(solution)/shard_map/backward_pair/pallas_call | solution.py:269
  97.8 0.2 collective-permute-start.45
  98.1 0.4 collective-permute-start.44
  98.6 0.4 collective-permute-start.36
  98.9 1.5 %collective-permute-start.47 = (bf16[2,128,512]{2,1,0:T(8,128)(2,1)S(1)}, bf16[2,128,512]{2,1,0:T(8,128)(2,1)S(1)}, u32[]{:S(2)}, u32[]{:S(2)}) collective-permute-start(bf16[2,128,512]{2,1,0:T(8,128)(2,1)S(1)} %collective-permute-done.42.refs_2_), channel_id=1, source_target_pairs={{0,16},{4,20},{8,24},{12,28},{16,0},{20,4},{24,8},{28,12},{1,17},{... | collective-permute-start | bytes 786440 | tf_op jit(solution)/shard_map/ppermute | solution.py:36
  100.4 0.5 collective-permute-start.35
  101.0 3.7 %backward_pair.5 = (f32[512,1024]{1,0:T(8,128)S(1)}, bf16[2,1024,2048]{2,1,0:T(8,128)(2,1)}, f32[8,128]{1,0:T(8,128)S(1)}) custom-call(s32[2]{0:T(128)S(1)} %pad_add_fusion.info_ref, bf16[1,128,512]{2,1,0:T(8,128)(2,1)S(1)} %collective-permute-done.37.refs_0_, ...), custom_call_target="tpu_custom_call", output_to_operand_aliasing={{0}: (9, {}), {1}: (10, {})} | custom-call | flops 262144 | bytes 262144 | tf_op jit(solution)/shard_map/backward_pair/pallas_call | solution.py:269
  104.7 3.3 %backward_pair.6 = (f32[512,1024]{1,0:T(8,128)S(1)}, bf16[2,1024,2048]{2,1,0:T(8,128)(2,1)}, f32[8,128]{1,0:T(8,128)S(1)}) custom-call(s32[2]{0:T(128)S(1)} %pad_add_fusion.info_ref, bf16[1,128,512]{2,1,0:T(8,128)(2,1)S(1)} %collective-permute-done.27.refs_0_, ...), custom_call_target="tpu_custom_call", output_to_operand_aliasing={{0}: (9, {}), {1}: (10, {})} | custom-call | flops 262144 | bytes 262144 | tf_op jit(solution)/shard_map/backward_pair/pallas_call | solution.py:269
  108.2 0.4 collective-permute-start.49
  108.7 1.1 collective-permute-done.49.refs_4_
  110.0 3.3 %backward_pair.7 = (f32[512,1024]{1,0:T(8,128)S(1)}, bf16[2,1024,2048]{2,1,0:T(8,128)(2,1)}, f32[8,128]{1,0:T(8,128)S(1)}) custom-call(s32[2]{0:T(128)S(1)} %pad_add_fusion.info_ref, bf16[1,128,512]{2,1,0:T(8,128)(2,1)S(1)} %collective-permute-done.28.refs_0_, ...), custom_call_target="tpu_custom_call", output_to_operand_aliasing={{0}: (9, {}), {1}: (10, {})} | custom-call | flops 262144 | bytes 262144 | tf_op jit(solution)/shard_map/backward_pair/pallas_call | solution.py:269
  113.3 4.7 %encoder_grad.1 = (bf16[2048,1024]{1,0:T(8,128)(2,1)}, f32[1,1024]{1,0:T(1,128)}, f32[1,1]{1,0:T(1,128)}) custom-call(s32[2]{0:T(128)S(1)} %pad_add_fusion.info_ref, bf16[1,512,512]{2,1,0:T(8,128)(2,1)S(1)} %turned.6.refs_0_, bf16[1,512,512]{2,1,0:T(8,128)(2,1)S(1)} %turned.7.refs_1_, bf16[1,512,512]{2,1,0:T(8,128)(2,1)S(1)} %turned.8.refs_2_, ...), custom_call_target="tpu_custom_call" | custom-call | flops 2147483648 | bytes 9437184 | tf_op jit(solution)/shard_map/encoder_grad/pallas_call | solution.py:321
  (83 shorter events, 4.0 us)
Async XLA Ops:
  0.7 17.5 %copy-start.2 = (bf16[128,512]{1,0:T(8,128)(2,1)S(1)}, bf16[128,512]{1,0:T(8,128)(2,1)}, u32[]{:S(2)}) copy-start(bf16[128,512]{1,0:T(8,128)(2,1)} %param.5) | copy-start | bytes 393220
  0.7 7.1 %collective-permute-start.1 = (bf16[128,512]{1,0:T(8,128)(2,1)}, bf16[128,512]{1,0:T(8,128)(2,1)S(1)}, u32[]{:S(2)}, u32[]{:S(2)}) collective-permute-start(bf16[128,512]{1,0:T(8,128)(2,1)} %param.5), channel_id=1, source_target_pairs={{0,1},{1,0},{2,3},{3,2},{4,5},{5,4},{6,7},{7,6},{8,9},{9,8},{10,11... | collective-permute-start | bytes 393224 | tf_op jit(solution)/shard_map/ppermute | solution.py:17
  3.8 10.0 %collective-permute-start.3 = (bf16[128,512]{1,0:T(8,128)(2,1)}, bf16[128,512]{1,0:T(8,128)(2,1)S(1)}, u32[]{:S(2)}, u32[]{:S(2)}) collective-permute-start(bf16[128,512]{1,0:T(8,128)(2,1)} %param.5), channel_id=1, source_target_pairs={{0,3},{1,2},{2,1},{3,0},{4,7},{5,6},{6,5},{7,4},{8,11},{9,10},{10,... | collective-permute-start | bytes 393224 | tf_op jit(solution)/shard_map/ppermute | solution.py:17
  6.2 12.0 %collective-permute-start.2 = (bf16[128,512]{1,0:T(8,128)(2,1)}, bf16[128,512]{1,0:T(8,128)(2,1)S(1)}, u32[]{:S(2)}, u32[]{:S(2)}) collective-permute-start(bf16[128,512]{1,0:T(8,128)(2,1)} %param.5), channel_id=1, source_target_pairs={{0,2},{1,3},{2,0},{3,1},{4,6},{5,7},{6,4},{7,5},{8,10},{9,11},{10,... | collective-permute-start | bytes 393224 | tf_op jit(solution)/shard_map/ppermute | solution.py:17
  6.4 12.0 %collective-permute-start = (bf16[128,512]{1,0:T(8,128)(2,1)}, bf16[128,512]{1,0:T(8,128)(2,1)S(1)}, u32[]{:S(2)}, u32[]{:S(2)}) collective-permute-start(bf16[128,512]{1,0:T(8,128)(2,1)} %param.5), channel_id=1, source_target_pairs={{0,8},{4,12},{8,0},{12,4},{16,24},{20,28},{24,16},{28,20},{1,9},{5... | collective-permute-start | bytes 393224 | tf_op jit(solution)/shard_map/ppermute | solution.py:23
  13.7 5.0 %collective-permute-start.5 = (bf16[128,512]{1,0:T(8,128)(2,1)S(1)}, bf16[128,512]{1,0:T(8,128)(2,1)S(1)}, u32[]{:S(2)}, u32[]{:S(2)}) collective-permute-start(bf16[128,512]{1,0:T(8,128)(2,1)S(1)} %collective-permute-done.3), channel_id=1, source_target_pairs={{0,8},{4,12},{8,0},{12,4},{16,24},{20,28},{24,16},{28,20},{1,9},{5... | collective-permute-start | bytes 393224 | tf_op jit(solution)/shard_map/ppermute | solution.py:23
  15.2 5.0 %collective-permute-start.4 = (bf16[128,512]{1,0:T(8,128)(2,1)S(1)}, bf16[128,512]{1,0:T(8,128)(2,1)S(1)}, u32[]{:S(2)}, u32[]{:S(2)}) collective-permute-start(bf16[128,512]{1,0:T(8,128)(2,1)S(1)} %collective-permute-done.1), channel_id=1, source_target_pairs={{0,8},{4,12},{8,0},{12,4},{16,24},{20,28},{24,16},{28,20},{1,9},{5... | collective-permute-start | bytes 393224 | tf_op jit(solution)/shard_map/ppermute | solution.py:23
  20.2 1.9 %collective-permute-start.6 = (bf16[4,128,512]{2,1,0:T(8,128)(2,1)S(1)}, bf16[4,128,512]{2,1,0:T(8,128)(2,1)S(1)}, u32[]{:S(2)}, u32[]{:S(2)}) collective-permute-start(bf16[4,128,512]{2,1,0:T(8,128)(2,1)S(1)} %pad_maximum_fusion.refs_0_), channel_id=1, source_target_pairs={{0,4},{4,0},{8,12},{12,8},{16,20},{20,16},{24,28},{28,24},{1,5},{5... | collective-permute-start | bytes 1572872 | tf_op jit(solution)/shard_map/ppermute | solution.py:23
  20.2 5.9 %collective-permute-start.7 = (bf16[128,512]{1,0:T(8,128)(2,1)S(1)}, bf16[128,512]{1,0:T(8,128)(2,1)S(1)}, u32[]{:S(2)}, u32[]{:S(2)}) collective-permute-start(bf16[128,512]{1,0:T(8,128)(2,1)S(1)} %collective-permute-done.2), channel_id=1, source_target_pairs={{0,8},{4,12},{8,0},{12,4},{16,24},{20,28},{24,16},{28,20},{1,9},{5... | collective-permute-start | bytes 393224 | tf_op jit(solution)/shard_map/ppermute | solution.py:23
  26.2 2.0 %copy-start = (f32[1024]{0:T(1024)S(1)}, f32[1024]{0:T(1024)}, u32[]{:S(2)}) copy-start(f32[1024]{0:T(1024)} %param.8) | copy-start | bytes 12292
  26.2 2.0 %collective-permute-start.8 = (bf16[4,128,512]{2,1,0:T(8,128)(2,1)S(1)}, bf16[4,128,512]{2,1,0:T(8,128)(2,1)S(1)}, u32[]{:S(2)}, u32[]{:S(2)}) collective-permute-start(bf16[4,128,512]{2,1,0:T(8,128)(2,1)S(1)} %pad_maximum_fusion.1.refs_0_), channel_id=1, source_target_pairs={{0,4},{4,0},{8,12},{12,8},{16,20},{20,16},{24,28},{28,24},{1,5},{5... | collective-permute-start | bytes 1572872 | tf_op jit(solution)/shard_map/ppermute | solution.py:23
  32.5 1.6 %collective-permute-start.9 = (bf16[2,1,128,512]{3,2,0,1:T(8,128)(2,1)S(1)}, bf16[2,1,128,512]{3,2,0,1:T(8,128)(2,1)S(1)}, u32[]{:S(2)}, u32[]{:S(2)}) collective-permute-start(bf16[2,1,128,512]{3,2,0,1:T(8,128)(2,1)S(1)} %bitcast.123), channel_id=1, source_target_pairs={{0,4},{4,0},{8,12},{12,8},{16,20},{20,16},{24,28},{28,24},{1,5},{5... | collective-permute-start | bytes 786440 | tf_op jit(solution)/shard_map/ppermute | solution.py:23
  32.7 6.4 %collective-permute-start.14 = (bf16[2,1,128,512]{3,2,0,1:T(8,128)(2,1)S(1)}, bf16[2,1,128,512]{3,2,0,1:T(8,128)(2,1)S(1)}, u32[]{:S(2)}, u32[]{:S(2)}) collective-permute-start(bf16[2,1,128,512]{3,2,0,1:T(8,128)(2,1)S(1)} %bitcast.121), channel_id=1, source_target_pairs={{0,4},{4,0},{8,12},{12,8},{16,20},{20,16},{24,28},{28,24},{1,5},{5... | collective-permute-start | bytes 786440 | tf_op jit(solution)/shard_map/ppermute | solution.py:23
  33.1 12.5 %collective-permute-start.11 = (bf16[2,2,128,512]{3,2,1,0:T(8,128)(2,1)S(1)}, bf16[2,2,128,512]{3,2,1,0:T(8,128)(2,1)S(1)}, u32[]{:S(2)}, u32[]{:S(2)}) collective-permute-start(bf16[2,2,128,512]{3,2,1,0:T(8,128)(2,1)S(1)} %get-tuple-element.87), channel_id=1, source_target_pairs={{0,4},{4,0},{8,12},{12,8},{16,20},{20,16},{24,28},{28,24},{1,5},{5... | collective-permute-start | bytes 1572872 | tf_op jit(solution)/shard_map/ppermute | solution.py:23
  37.1 8.4 %collective-permute-start.17 = (bf16[2,1,128,512]{3,2,0,1:T(8,128)(2,1)S(1)}, bf16[2,1,128,512]{3,2,0,1:T(8,128)(2,1)S(1)}, u32[]{:S(2)}, u32[]{:S(2)}) collective-permute-start(bf16[2,1,128,512]{3,2,0,1:T(8,128)(2,1)S(1)} %bitcast.120), channel_id=1, source_target_pairs={{0,4},{4,0},{8,12},{12,8},{16,20},{20,16},{24,28},{28,24},{1,5},{5... | collective-permute-start | bytes 786440 | tf_op jit(solution)/shard_map/ppermute | solution.py:23
  37.3 2.0 %collective-permute-start.12 = (bf16[2,1,128,512]{3,2,0,1:T(8,128)(2,1)S(1)}, bf16[2,1,128,512]{3,2,0,1:T(8,128)(2,1)S(1)}, u32[]{:S(2)}, u32[]{:S(2)}) collective-permute-start(bf16[2,1,128,512]{3,2,0,1:T(8,128)(2,1)S(1)} %bitcast.122), channel_id=1, source_target_pairs={{0,4},{4,0},{8,12},{12,8},{16,20},{20,16},{24,28},{28,24},{1,5},{5... | collective-permute-start | bytes 786440 | tf_op jit(solution)/shard_map/ppermute | solution.py:23
  37.7 6.3 %collective-permute-start.15 = (bf16[1,1,128,512]{3,2,1,0:T(8,128)(2,1)S(1)}, bf16[1,1,128,512]{3,2,1,0:T(8,128)(2,1)S(1)}, u32[]{:S(2)}, u32[]{:S(2)}) collective-permute-start(bf16[1,1,128,512]{3,2,1,0:T(8,128)(2,1)S(1)} %slice_bitcast_fusion.10), channel_id=1, source_target_pairs={{0,8},{4,12},{8,0},{12,4},{16,24},{20,28},{24,16},{28,20},{1,9},{5... | collective-permute-start | bytes 393224 | tf_op jit(solution)/shard_map/ppermute | solution.py:23
  39.1 17.4 %collective-permute-start.10 = (bf16[2,2,128,512]{3,2,1,0:T(8,128)(2,1)S(1)}, bf16[2,2,128,512]{3,2,1,0:T(8,128)(2,1)S(1)}, u32[]{:S(2)}, u32[]{:S(2)}) collective-permute-start(bf16[2,2,128,512]{3,2,1,0:T(8,128)(2,1)S(1)} %get-tuple-element.84), channel_id=1, source_target_pairs={{0,4},{4,0},{8,12},{12,8},{16,20},{20,16},{24,28},{28,24},{1,5},{5... | collective-permute-start | bytes 1572872 | tf_op jit(solution)/shard_map/ppermute | solution.py:23
  39.3 8.6 %collective-permute-start.18 = (bf16[1,1,128,512]{3,2,1,0:T(8,128)(2,1)S(1)}, bf16[1,1,128,512]{3,2,1,0:T(8,128)(2,1)S(1)}, u32[]{:S(2)}, u32[]{:S(2)}) collective-permute-start(bf16[1,1,128,512]{3,2,1,0:T(8,128)(2,1)S(1)} %slice_bitcast_fusion.12), channel_id=1, source_target_pairs={{0,8},{4,12},{8,0},{12,4},{16,24},{20,28},{24,16},{28,20},{1,9},{5... | collective-permute-start | bytes 393224 | tf_op jit(solution)/shard_map/ppermute | solution.py:23
  44.0 5.8 %collective-permute-start.16 = (bf16[1,1,128,512]{3,2,1,0:T(8,128)(2,1)S(1)}, bf16[1,1,128,512]{3,2,1,0:T(8,128)(2,1)S(1)}, u32[]{:S(2)}, u32[]{:S(2)}) collective-permute-start(bf16[1,1,128,512]{3,2,1,0:T(8,128)(2,1)S(1)} %slice_bitcast_fusion.11), channel_id=1, source_target_pairs={{0,8},{4,12},{8,0},{12,4},{16,24},{20,28},{24,16},{28,20},{1,9},{5... | collective-permute-start | bytes 393224 | tf_op jit(solution)/shard_map/ppermute | solution.py:23
  45.8 10.9 %collective-permute-start.13 = (bf16[1,2,128,512]{3,2,1,0:T(8,128)(2,1)S(1)}, bf16[1,2,128,512]{3,2,1,0:T(8,128)(2,1)S(1)}, u32[]{:S(2)}, u32[]{:S(2)}) collective-permute-start(bf16[1,2,128,512]{3,2,1,0:T(8,128)(2,1)S(1)} %get-tuple-element.90), channel_id=1, source_target_pairs={{0,16},{4,20},{8,24},{12,28},{16,0},{20,4},{24,8},{28,12},{1,17},{... | collective-permute-start | bytes 786440 | tf_op jit(solution)/shard_map/ppermute | solution.py:29
  47.4 9.1 %collective-permute-start.20 = (bf16[1,1,128,512]{3,2,1,0:T(8,128)(2,1)S(1)}, bf16[1,1,128,512]{3,2,1,0:T(8,128)(2,1)S(1)}, u32[]{:S(2)}, u32[]{:S(2)}) collective-permute-start(bf16[1,1,128,512]{3,2,1,0:T(8,128)(2,1)S(1)} %fusion.13), channel_id=1, source_target_pairs={{0,16},{4,20},{8,24},{12,28},{16,0},{20,4},{24,8},{28,12},{1,17},{... | collective-permute-start | bytes 393224 | tf_op jit(solution)/shard_map/ppermute | solution.py:29
  48.0 9.5 %collective-permute-start.21 = (bf16[1,1,128,512]{3,2,1,0:T(8,128)(2,1)S(1)}, bf16[1,1,128,512]{3,2,1,0:T(8,128)(2,1)S(1)}, u32[]{:S(2)}, u32[]{:S(2)}) collective-permute-start(bf16[1,1,128,512]{3,2,1,0:T(8,128)(2,1)S(1)} %slice_bitcast_fusion.9), channel_id=1, source_target_pairs={{0,8},{4,12},{8,0},{12,4},{16,24},{20,28},{24,16},{28,20},{1,9},{5... | collective-permute-start | bytes 393224 | tf_op jit(solution)/shard_map/ppermute | solution.py:23
  49.8 8.1 %collective-permute-start.22 = (bf16[1,1,128,512]{3,2,1,0:T(8,128)(2,1)S(1)}, bf16[1,1,128,512]{3,2,1,0:T(8,128)(2,1)S(1)}, u32[]{:S(2)}, u32[]{:S(2)}) collective-permute-start(bf16[1,1,128,512]{3,2,1,0:T(8,128)(2,1)S(1)} %fusion.10), channel_id=1, source_target_pairs={{0,16},{4,20},{8,24},{12,28},{16,0},{20,4},{24,8},{28,12},{1,17},{... | collective-permute-start | bytes 393224 | tf_op jit(solution)/shard_map/ppermute | solution.py:29
  56.8 7.4 %collective-permute-start.19 = (bf16[1,2,128,512]{3,2,1,0:T(8,128)(2,1)S(1)}, bf16[1,2,128,512]{3,2,1,0:T(8,128)(2,1)S(1)}, u32[]{:S(2)}, u32[]{:S(2)}) collective-permute-start(bf16[1,2,128,512]{3,2,1,0:T(8,128)(2,1)S(1)} %fusion.2), channel_id=1, source_target_pairs={{0,8},{4,12},{8,0},{12,4},{16,24},{20,28},{24,16},{28,20},{1,9},{5... | collective-permute-start | bytes 786440 | tf_op jit(solution)/shard_map/ppermute | solution.py:23
  58.0 15.1 %copy-start.1 = (bf16[128,512]{1,0:T(8,128)(2,1)S(1)}, bf16[128,512]{1,0:T(8,128)(2,1)}, u32[]{:S(2)}) copy-start(bf16[128,512]{1,0:T(8,128)(2,1)} %param.6) | copy-start | bytes 393220
  58.0 6.4 %collective-permute-start.23 = (bf16[1,2,128,512]{3,2,1,0:T(8,128)(2,1)S(1)}, bf16[1,2,128,512]{3,2,1,0:T(8,128)(2,1)S(1)}, u32[]{:S(2)}, u32[]{:S(2)}) collective-permute-start(bf16[1,2,128,512]{3,2,1,0:T(8,128)(2,1)S(1)} %get-tuple-element.102), channel_id=1, source_target_pairs={{0,16},{4,20},{8,24},{12,28},{16,0},{20,4},{24,8},{28,12},{1,17},{... | collective-permute-start | bytes 786440 | tf_op jit(solution)/shard_map/ppermute | solution.py:29
  59.5 9.4 %collective-permute-start.24 = (bf16[128,512]{1,0:T(8,128)(2,1)S(1)}, bf16[128,512]{1,0:T(8,128)(2,1)S(1)}, u32[]{:S(2)}, u32[]{:S(2)}) collective-permute-start(bf16[128,512]{1,0:T(8,128)(2,1)S(1)} %fusion.16), channel_id=1, source_target_pairs={{0,3},{1,2},{2,1},{3,0},{4,7},{5,6},{6,5},{7,4},{8,11},{9,10},{10,... | collective-permute-start | bytes 393224 | tf_op jit(solution)/shard_map/ppermute | solution.py:17
  64.0 9.1 %collective-permute-start.25 = (bf16[128,512]{1,0:T(8,128)(2,1)S(1)}, bf16[128,512]{1,0:T(8,128)(2,1)S(1)}, u32[]{:S(2)}, u32[]{:S(2)}) collective-permute-start(bf16[128,512]{1,0:T(8,128)(2,1)S(1)} %fusion.17), channel_id=1, source_target_pairs={{0,2},{1,3},{2,0},{3,1},{4,6},{5,7},{6,4},{7,5},{8,10},{9,11},{10,... | collective-permute-start | bytes 393224 | tf_op jit(solution)/shard_map/ppermute | solution.py:17
  64.5 8.5 %collective-permute-start.26 = (bf16[128,512]{1,0:T(8,128)(2,1)S(1)}, bf16[128,512]{1,0:T(8,128)(2,1)S(1)}, u32[]{:S(2)}, u32[]{:S(2)}) collective-permute-start(bf16[128,512]{1,0:T(8,128)(2,1)S(1)} %fusion.18), channel_id=1, source_target_pairs={{0,1},{1,0},{2,3},{3,2},{4,5},{5,4},{6,7},{7,6},{8,9},{9,8},{10,11... | collective-permute-start | bytes 393224 | tf_op jit(solution)/shard_map/ppermute | solution.py:17
  73.9 6.3 %collective-permute-start.27 = (bf16[1,128,512]{2,1,0:T(8,128)(2,1)S(1)}, bf16[1,128,512]{2,1,0:T(8,128)(2,1)S(1)}, u32[]{:S(2)}, u32[]{:S(2)}) collective-permute-start(bf16[1,128,512]{2,1,0:T(8,128)(2,1)S(1)} %bitcast.111), channel_id=1, source_target_pairs={{0,16},{4,20},{8,24},{12,28},{16,0},{20,4},{24,8},{28,12},{1,17},{... | collective-permute-start | bytes 393224 | tf_op jit(solution)/shard_map/ppermute | solution.py:36
  74.9 6.4 %collective-permute-start.29 = (bf16[128,512]{1,0:T(8,128)(2,1)S(1)}, bf16[128,512]{1,0:T(8,128)(2,1)S(1)}, u32[]{:S(2)}, u32[]{:S(2)}) collective-permute-start(bf16[128,512]{1,0:T(8,128)(2,1)S(1)} %get-tuple-element.131), channel_id=1, source_target_pairs={{0,1},{1,0},{2,3},{3,2},{4,5},{5,4},{6,7},{7,6},{8,9},{9,8},{10,11... | collective-permute-start | bytes 393224 | tf_op jit(solution)/shard_map/ppermute | solution.py:17
  75.1 11.7 %collective-permute-start.31 = (bf16[128,512]{1,0:T(8,128)(2,1)S(1)}, bf16[128,512]{1,0:T(8,128)(2,1)S(1)}, u32[]{:S(2)}, u32[]{:S(2)}) collective-permute-start(bf16[128,512]{1,0:T(8,128)(2,1)S(1)} %get-tuple-element.131), channel_id=1, source_target_pairs={{0,2},{1,3},{2,0},{3,1},{4,6},{5,7},{6,4},{7,5},{8,10},{9,11},{10,... | collective-permute-start | bytes 393224 | tf_op jit(solution)/shard_map/ppermute | solution.py:17
  78.8 8.2 %collective-permute-start.32 = (bf16[128,512]{1,0:T(8,128)(2,1)S(1)}, bf16[128,512]{1,0:T(8,128)(2,1)S(1)}, u32[]{:S(2)}, u32[]{:S(2)}) collective-permute-start(bf16[128,512]{1,0:T(8,128)(2,1)S(1)} %get-tuple-element.131), channel_id=1, source_target_pairs={{0,3},{1,2},{2,1},{3,0},{4,7},{5,6},{6,5},{7,4},{8,11},{9,10},{10,... | collective-permute-start | bytes 393224 | tf_op jit(solution)/shard_map/ppermute | solution.py:17
  79.3 7.8 %collective-permute-start.37 = (bf16[1,128,512]{2,1,0:T(8,128)(2,1)S(1)}, bf16[1,128,512]{2,1,0:T(8,128)(2,1)S(1)}, u32[]{:S(2)}, u32[]{:S(2)}) collective-permute-start(bf16[1,128,512]{2,1,0:T(8,128)(2,1)S(1)} %bitcast.112), channel_id=1, source_target_pairs={{0,8},{4,12},{8,0},{12,4},{16,24},{20,28},{24,16},{28,20},{1,9},{5... | collective-permute-start | bytes 393224 | tf_op jit(solution)/shard_map/ppermute | solution.py:23
  80.2 8.8 %collective-permute-start.28 = (bf16[1,128,512]{2,1,0:T(8,128)(2,1)S(1)}, bf16[1,128,512]{2,1,0:T(8,128)(2,1)S(1)}, u32[]{:S(2)}, u32[]{:S(2)}) collective-permute-start(bf16[1,128,512]{2,1,0:T(8,128)(2,1)S(1)} %collective-permute-done.27.refs_0_), channel_id=1, source_target_pairs={{0,8},{4,12},{8,0},{12,4},{16,24},{20,28},{24,16},{28,20},{1,9},{5... | collective-permute-start | bytes 393224 | tf_op jit(solution)/shard_map/ppermute | solution.py:23
  81.4 9.1 %collective-permute-start.30 = (bf16[1,128,512]{2,1,0:T(8,128)(2,1)S(1)}, bf16[1,128,512]{2,1,0:T(8,128)(2,1)S(1)}, u32[]{:S(2)}, u32[]{:S(2)}) collective-permute-start(bf16[1,128,512]{2,1,0:T(8,128)(2,1)S(1)} %bitcast.115), channel_id=1, source_target_pairs={{0,16},{4,20},{8,24},{12,28},{16,0},{20,4},{24,8},{28,12},{1,17},{... | collective-permute-start | bytes 393224 | tf_op jit(solution)/shard_map/ppermute | solution.py:36
  86.8 6.4 %collective-permute-start.38 = (bf16[1,128,512]{2,1,0:T(8,128)(2,1)S(1)}, bf16[1,128,512]{2,1,0:T(8,128)(2,1)S(1)}, u32[]{:S(2)}, u32[]{:S(2)}) collective-permute-start(bf16[1,128,512]{2,1,0:T(8,128)(2,1)S(1)} %bitcast.116), channel_id=1, source_target_pairs={{0,8},{4,12},{8,0},{12,4},{16,24},{20,28},{24,16},{28,20},{1,9},{5... | collective-permute-start | bytes 393224 | tf_op jit(solution)/shard_map/ppermute | solution.py:23
  87.0 6.1 %collective-permute-start.41 = (bf16[2,128,512]{2,1,0:T(8,128)(2,1)S(1)}, bf16[2,128,512]{2,1,0:T(8,128)(2,1)S(1)}, u32[]{:S(2)}, u32[]{:S(2)}) collective-permute-start(bf16[2,128,512]{2,1,0:T(8,128)(2,1)S(1)} %pad_maximum_fusion.2.refs_2_), channel_id=1, source_target_pairs={{0,4},{4,0},{8,12},{12,8},{16,20},{20,16},{24,28},{28,24},{1,5},{5... | collective-permute-start | bytes 786440 | tf_op jit(solution)/shard_map/ppermute | solution.py:23
  87.1 10.7 %collective-permute-start.42 = (bf16[2,128,512]{2,1,0:T(8,128)(2,1)S(1)}, bf16[2,128,512]{2,1,0:T(8,128)(2,1)S(1)}, u32[]{:S(2)}, u32[]{:S(2)}) collective-permute-start(bf16[2,128,512]{2,1,0:T(8,128)(2,1)S(1)} %pad_maximum_fusion.2.refs_2_), channel_id=1, source_target_pairs={{0,8},{4,12},{8,0},{12,4},{16,24},{20,28},{24,16},{28,20},{1,9},{5... | collective-permute-start | bytes 786440 | tf_op jit(solution)/shard_map/ppermute | solution.py:23
  89.0 9.6 %collective-permute-start.33 = (bf16[2,128,512]{2,1,0:T(8,128)(2,1)S(1)}, bf16[2,128,512]{2,1,0:T(8,128)(2,1)S(1)}, u32[]{:S(2)}, u32[]{:S(2)}) collective-permute-start(bf16[2,128,512]{2,1,0:T(8,128)(2,1)S(1)} %pad_maximum_fusion.2.refs_2_), channel_id=1, source_target_pairs={{0,16},{4,20},{8,24},{12,28},{16,0},{20,4},{24,8},{28,12},{1,17},{... | collective-permute-start | bytes 786440 | tf_op jit(solution)/shard_map/ppermute | solution.py:36
  90.5 2.7 %collective-permute-start.40 = (bf16[1,128,512]{2,1,0:T(8,128)(2,1)S(1)}, bf16[1,128,512]{2,1,0:T(8,128)(2,1)S(1)}, u32[]{:S(2)}, u32[]{:S(2)}) collective-permute-start(bf16[1,128,512]{2,1,0:T(8,128)(2,1)S(1)} %bitcast.117), channel_id=1, source_target_pairs={{0,4},{4,0},{8,12},{12,8},{16,20},{20,16},{24,28},{28,24},{1,5},{5... | collective-permute-start | bytes 393224 | tf_op jit(solution)/shard_map/ppermute | solution.py:23
  93.1 1.3 %collective-permute-start.39 = (bf16[1,128,512]{2,1,0:T(8,128)(2,1)S(1)}, bf16[1,128,512]{2,1,0:T(8,128)(2,1)S(1)}, u32[]{:S(2)}, u32[]{:S(2)}) collective-permute-start(bf16[1,128,512]{2,1,0:T(8,128)(2,1)S(1)} %bitcast.113), channel_id=1, source_target_pairs={{0,4},{4,0},{8,12},{12,8},{16,20},{20,16},{24,28},{28,24},{1,5},{5... | collective-permute-start | bytes 393224 | tf_op jit(solution)/shard_map/ppermute | solution.py:23
  97.8 3.1 %collective-permute-start.45 = (bf16[2,128,512]{2,1,0:T(8,128)(2,1)S(1)}, bf16[2,128,512]{2,1,0:T(8,128)(2,1)S(1)}, u32[]{:S(2)}, u32[]{:S(2)}) collective-permute-start(bf16[2,128,512]{2,1,0:T(8,128)(2,1)S(1)} %collective-permute-done.42.refs_2_), channel_id=1, source_target_pairs={{0,4},{4,0},{8,12},{12,8},{16,20},{20,16},{24,28},{28,24},{1,5},{5... | collective-permute-start | bytes 786440 | tf_op jit(solution)/shard_map/ppermute | solution.py:23
  98.1 2.4 %collective-permute-start.44 = (bf16[1,128,512]{2,1,0:T(8,128)(2,1)S(1)}, bf16[1,128,512]{2,1,0:T(8,128)(2,1)S(1)}, u32[]{:S(2)}, u32[]{:S(2)}) collective-permute-start(bf16[1,128,512]{2,1,0:T(8,128)(2,1)S(1)} %collective-permute-done.38.refs_1_), channel_id=1, source_target_pairs={{0,4},{4,0},{8,12},{12,8},{16,20},{20,16},{24,28},{28,24},{1,5},{5... | collective-permute-start | bytes 393224 | tf_op jit(solution)/shard_map/ppermute | solution.py:23
  98.4 2.0 %collective-permute-start.43 = (bf16[1,128,512]{2,1,0:T(8,128)(2,1)S(1)}, bf16[1,128,512]{2,1,0:T(8,128)(2,1)S(1)}, u32[]{:S(2)}, u32[]{:S(2)}) collective-permute-start(bf16[1,128,512]{2,1,0:T(8,128)(2,1)S(1)} %collective-permute-done.37.refs_0_), channel_id=1, source_target_pairs={{0,4},{4,0},{8,12},{12,8},{16,20},{20,16},{24,28},{28,24},{1,5},{5... | collective-permute-start | bytes 393224 | tf_op jit(solution)/shard_map/ppermute | solution.py:23
  98.6 6.2 %collective-permute-start.36 = (bf16[2,128,512]{2,1,0:T(8,128)(2,1)S(1)}, bf16[2,128,512]{2,1,0:T(8,128)(2,1)S(1)}, u32[]{:S(2)}, u32[]{:S(2)}) collective-permute-start(bf16[2,128,512]{2,1,0:T(8,128)(2,1)S(1)} %collective-permute-done.33.refs_2_), channel_id=1, source_target_pairs={{0,4},{4,0},{8,12},{12,8},{16,20},{20,16},{24,28},{28,24},{1,5},{5... | collective-permute-start | bytes 786440 | tf_op jit(solution)/shard_map/ppermute | solution.py:23
  98.9 9.1 %collective-permute-start.47 = (bf16[2,128,512]{2,1,0:T(8,128)(2,1)S(1)}, bf16[2,128,512]{2,1,0:T(8,128)(2,1)S(1)}, u32[]{:S(2)}, u32[]{:S(2)}) collective-permute-start(bf16[2,128,512]{2,1,0:T(8,128)(2,1)S(1)} %collective-permute-done.42.refs_2_), channel_id=1, source_target_pairs={{0,16},{4,20},{8,24},{12,28},{16,0},{20,4},{24,8},{28,12},{1,17},{... | collective-permute-start | bytes 786440 | tf_op jit(solution)/shard_map/ppermute | solution.py:36
  100.4 4.3 %collective-permute-start.34 = (bf16[1,128,512]{2,1,0:T(8,128)(2,1)S(1)}, bf16[1,128,512]{2,1,0:T(8,128)(2,1)S(1)}, u32[]{:S(2)}, u32[]{:S(2)}) collective-permute-start(bf16[1,128,512]{2,1,0:T(8,128)(2,1)S(1)} %collective-permute-done.27.refs_0_), channel_id=1, source_target_pairs={{0,4},{4,0},{8,12},{12,8},{16,20},{20,16},{24,28},{28,24},{1,5},{5... | collective-permute-start | bytes 393224 | tf_op jit(solution)/shard_map/ppermute | solution.py:23
  100.4 4.3 %collective-permute-start.35 = (bf16[1,128,512]{2,1,0:T(8,128)(2,1)S(1)}, bf16[1,128,512]{2,1,0:T(8,128)(2,1)S(1)}, u32[]{:S(2)}, u32[]{:S(2)}) collective-permute-start(bf16[1,128,512]{2,1,0:T(8,128)(2,1)S(1)} %collective-permute-done.30.refs_1_), channel_id=1, source_target_pairs={{0,4},{4,0},{8,12},{12,8},{16,20},{20,16},{24,28},{28,24},{1,5},{5... | collective-permute-start | bytes 393224 | tf_op jit(solution)/shard_map/ppermute | solution.py:23
  101.0 7.2 %collective-permute-start.46 = (bf16[1,128,512]{2,1,0:T(8,128)(2,1)S(1)}, bf16[1,128,512]{2,1,0:T(8,128)(2,1)S(1)}, u32[]{:S(2)}, u32[]{:S(2)}) collective-permute-start(bf16[1,128,512]{2,1,0:T(8,128)(2,1)S(1)} %collective-permute-done.30.refs_1_), channel_id=1, source_target_pairs={{0,8},{4,12},{8,0},{12,4},{16,24},{20,28},{24,16},{28,20},{1,9},{5... | collective-permute-start | bytes 393224 | tf_op jit(solution)/shard_map/ppermute | solution.py:23
  108.0 2.0 %collective-permute-start.50 = (bf16[2,128,512]{2,1,0:T(8,128)(2,1)S(1)}, bf16[2,128,512]{2,1,0:T(8,128)(2,1)S(1)}, u32[]{:S(2)}, u32[]{:S(2)}) collective-permute-start(bf16[2,128,512]{2,1,0:T(8,128)(2,1)S(1)} %collective-permute-done.47.refs_2_), channel_id=1, source_target_pairs={{0,4},{4,0},{8,12},{12,8},{16,20},{20,16},{24,28},{28,24},{1,5},{5... | collective-permute-start | bytes 786440 | tf_op jit(solution)/shard_map/ppermute | solution.py:23
  108.2 1.6 %collective-permute-start.49 = (bf16[1,128,512]{2,1,0:T(8,128)(2,1)S(1)}, bf16[1,128,512]{2,1,0:T(8,128)(2,1)S(1)}, u32[]{:S(2)}, u32[]{:S(2)}) collective-permute-start(bf16[1,128,512]{2,1,0:T(8,128)(2,1)S(1)} %collective-permute-done.46.refs_1_), channel_id=1, source_target_pairs={{0,4},{4,0},{8,12},{12,8},{16,20},{20,16},{24,28},{28,24},{1,5},{5... | collective-permute-start | bytes 393224 | tf_op jit(solution)/shard_map/ppermute | solution.py:23
  108.6 1.4 %collective-permute-start.48 = (bf16[1,128,512]{2,1,0:T(8,128)(2,1)S(1)}, bf16[1,128,512]{2,1,0:T(8,128)(2,1)S(1)}, u32[]{:S(2)}, u32[]{:S(2)}) collective-permute-start(bf16[1,128,512]{2,1,0:T(8,128)(2,1)S(1)} %collective-permute-done.28.refs_0_), channel_id=1, source_target_pairs={{0,4},{4,0},{8,12},{12,8},{16,20},{20,16},{24,28},{28,24},{1,5},{5... | collective-permute-start | bytes 393224 | tf_op jit(solution)/shard_map/ppermute | solution.py:23

commit v5 on v4

--- a/solution.py
+++ b/solution.py
@@ -199,18 +199,24 @@
     return values[0]
 
 
-def backward_pair(info, rel, offset, own, other, turned_features, dec_weight, feature_grad, dec_grad):
+def backward_pair(
+    info, rel, offset, own, other, turned_features, dec_weight, feature_grad, dec_grad, features
+):
     layers, width, depth = dec_weight.shape
     tok = turned_features.shape[1]
     cols = own[0].shape[2]
     first = feature_grad is None
     extra = [] if first else [feature_grad, dec_grad]
+    final = features is not None
+    if final:
+        extra.append(features)
     inputs = [*own, *other]
 
     def kernel(info_ref, *refs):
         grad_refs = refs[: len(inputs)]
         feat_ref, weight_ref = refs[len(inputs) : len(inputs) + 2]
-        out_ref, dec_ref, square_ref, held, sems = refs[-5:]
+        held, sems = refs[-2:]
+        out_ref, dec_ref, square_ref = refs[len(inputs) + 2 + len(extra) :][:3]
         columns = span((info_ref[0] ^ rel) // 2, 2 * cols)
         starts = range(0, width, tile)
         copies = [
@@ -250,13 +256,24 @@
                 product = dot(grad, weight_ref[offset, here, columns], (1, 1))
                 if not first:
                     product += refs[len(inputs) + 2][:, here]
-                out_ref[:, here] = product
+                store(here, product)
+
+        def store(here, total):
+            if not final:
+                out_ref[:, here] = total
+                return
+            mask_ref, bias_ref = refs[len(inputs) + 4], refs[-3]
+            kept = jnp.where(mask_ref[1, :, here] > 0.0, total, 0.0).astype(jnp.bfloat16)
+            out_ref[:, here] = kept
+            bias_ref[:, here] = jnp.sum(kept.astype(jnp.float32), 0, keepdims=True)
 
         def nothing():
             held[...] = jnp.zeros_like(held)
             for copy in copies:
                 copy.start()
-            out_ref[...] = refs[len(inputs) + 2][...]
+            for start in starts:
+                here = slice(start, start + tile)
+                store(here, refs[len(inputs) + 2][:, here])
 
         if offset == 0:
             products()
@@ -266,77 +283,77 @@
         for copy in copies:
             copy.wait()
 
+    out_shape = [
+        jax.ShapeDtypeStruct((tok, width), jnp.bfloat16 if final else jnp.float32),
+        jax.ShapeDtypeStruct((layers, width, depth), jnp.bfloat16),
+        jax.ShapeDtypeStruct((8, 128), jnp.float32),
+    ]
+    aliases = {} if first else {len(inputs) + 4: 1}
+    if not first and not final:
+        aliases[len(inputs) + 3] = 0
+    if final:
+        out_shape.append(jax.ShapeDtypeStruct((1, width), jnp.float32))
     return pl.pallas_call(
         kernel,
         in_specs=[in_smem]
         + [in_vmem] * (len(inputs) + 2)
-        + ([] if first else [in_vmem, in_hbm]),
-        out_specs=[in_vmem, in_hbm, in_vmem],
-        out_shape=[
-            jax.ShapeDtypeStruct((tok, width), jnp.float32),
-            jax.ShapeDtypeStruct((layers, width, depth), jnp.bfloat16),
-            jax.ShapeDtypeStruct((8, 128), jnp.float32),
-        ],
+        + ([] if first else [in_vmem, in_hbm])
+        + ([in_vmem] if final else []),
+        out_specs=[in_vmem, in_hbm, in_vmem] + ([in_vmem] if final else []),
+        out_shape=out_shape,
         scratch_shapes=[
             pltpu.VMEM((width, 2 * cols), jnp.bfloat16),
             pltpu.SemaphoreType.DMA((width // tile,)),
         ],
-        input_output_aliases={} if first else {len(inputs) + 3: 0, len(inputs) + 4: 1},
+        input_output_aliases=aliases,
         name="backward_pair",
         **params(tok * cols, tok * cols, 8),
     )(info, *inputs, turned_features, dec_weight, *extra)
 
 
-def encoder_grad(info, rels, turned_tokens, features, feature_grad, squares, scale):
-    count, cols, tok = turned_tokens[0].shape
-    width = features.shape[2]
-    pieces = len(turned_tokens) * count
+def encoder_grad(info, rels, turned_tokens, preact_grad, squares, scale):
+    _, cols, tok = turned_tokens[0].shape
+    width = preact_grad.shape[1]
+    pieces = len(turned_tokens)
+    step = min(tile, cols)
+    parts = [(piece, start) for piece in range(pieces) for start in range(0, cols, step)]
 
     def kernel(info_ref, *refs):
-        token_refs = refs[: len(turned_tokens)]
-        mask_ref, grad_ref = refs[len(turned_tokens) : len(turned_tokens) + 2]
-        square_refs = refs[len(turned_tokens) + 2 : -6]
-        enc_ref, bias_ref, mean_ref, preact, held, sems = refs[-6:]
+        token_refs, grad_ref = refs[:pieces], refs[pieces]
+        square_refs = refs[pieces + 1 : -4]
+        enc_ref, mean_ref, held, sems = refs[-4:]
+        copies = []
+        for place, (piece, start) in enumerate(parts):
+            held[piece, start : start + step] = dot(
+                token_refs[piece][0, start : start + step], grad_ref[...], (1, 0)
+            ).astype(jnp.bfloat16)
+            row = pl.multiple_of((info_ref[0] ^ rels[piece]) * cols + start, step)
+            copy = pltpu.make_async_copy(
+                held.at[piece, pl.ds(start, step)], enc_ref.at[pl.ds(row, step)], sems.at[place]
+            )
+            copy.start()
+            copies.append(copy)
         mean_ref[...] = scale * jnp.sum(
             tree_sum([ref[...] for ref in square_refs]), (0, 1), keepdims=True
         )
-        for start in range(0, width, tile):
-            here = slice(start, start + tile)
-            kept = jnp.where(mask_ref[1, :, here] > 0.0, grad_ref[:, here], 0.0).astype(jnp.bfloat16)
-            preact[:, here] = kept
-            bias_ref[:, here] = jnp.sum(kept.astype(jnp.float32), 0, keepdims=True)
-        copies = []
-        for piece in range(pieces):
-            held[piece] = dot(
-                token_refs[piece // count][piece % count], preact[...], (1, 0)
-            ).astype(jnp.bfloat16)
-            copy = pltpu.make_async_copy(
-                held.at[piece], enc_ref.at[span(info_ref[0] ^ rels[piece], cols)], sems.at[piece]
-            )
-            copy.start()
-            copies.append(copy)
         for copy in copies:
             copy.wait()
 
     return pl.pallas_call(
         kernel,
-        in_specs=[in_smem] + [in_vmem] * (len(turned_tokens) + 2 + len(squares)),
-        out_specs=[in_hbm, in_vmem, in_vmem],
+        in_specs=[in_smem] + [in_vmem] * (pieces + 1 + len(squares)),
+        out_specs=[in_hbm, in_vmem],
         out_shape=[
             jax.ShapeDtypeStruct((pieces * cols, width), jnp.bfloat16),
-            jax.ShapeDtypeStruct((1, width), jnp.float32),
             jax.ShapeDtypeStruct((1, 1), jnp.float32),
         ],
         scratch_shapes=[
-            pltpu.VMEM((tok, width), jnp.bfloat16),
             pltpu.VMEM((pieces, cols, width), jnp.bfloat16),
-            pltpu.SemaphoreType.DMA((pieces,)),
+            pltpu.SemaphoreType.DMA((len(parts),)),
         ],
         name="encoder_grad",
-        **params(
-            2 * pieces * tok * cols * width, 2 * pieces * cols * (tok + width) + 6 * tok * width, 10
-        ),
-    )(info, *turned_tokens, features, feature_grad, *squares)
+        **params(2 * pieces * tok * cols * width, 2 * pieces * cols * (tok + width), 8),
+    )(info, *turned_tokens, preact_grad, *squares)
 
 
 def add_pair(left, right):
@@ -363,6 +380,9 @@
 
     order = [rel for pair in range(0, sub_count, 2) for rel in (pair, pair ^ 1)]
     held = {rel: [None] * feat_count for rel in order[::2]}
+    first = tokens_in
+    if bit_count > 1:
+        first = over_members(tokens_in, bit_count - 1)
     held[0] = all_over_feat(tokens_in)
     enc_held, dec_held = fetch(enc_weight, after(dec_weight, held[0][1]))
     for s in range(feat_count):
@@ -370,7 +390,10 @@
         for bit_level in range(bit_count - 1, 0, -1):
             for rel in known:
                 value = after(held[rel][s], dec_held) if s > 1 else held[rel][s]
-                held[rel ^ 2**bit_level][s] = over_members(value, bit_level)
+                if s == 0 and bit_level == bit_count - 1:
+                    held[rel ^ 2**bit_level][s] = first
+                else:
+                    held[rel ^ 2**bit_level][s] = over_members(value, bit_level)
             known += [rel ^ 2**bit_level for rel in known]
     early = [
         held[rel][s] for rel in order[2::2] for s in range(feat_count) if 2 * s != feat_count
@@ -392,21 +415,12 @@
             current[place, k] = add_pair(kept[place], over_members(sent[place], 0))
         source = after(features, current[len(groups) - 1, k])
     turns = sorted(current, reverse=True)
-    joined = {}
     for bit_level in range(1, bit_count):
-        halves = {}
-        for turn, value in current.items():
+        kept, received, operands = {}, [], []
+        for turn in turns:
+            value = current[turn]
             split = value.reshape((value.shape[0] // 2, 2) + value.shape[1:])
-            halves[turn] = (split[:, 0], split[:, 1])
-        if bit_level == bit_count - 1:
-            for k in range(1, layers):
-                joined[k], sent = halves.pop((0, k))
-                sent = to_layer(after(sent, halves[len(groups) - 1, 0][1]), k, sub_count, real)
-                halves[0, 0] = (halves[0, 0][0], add_pair(halves[0, 0][1], sent))
-        turns = [turn for turn in turns if turn in halves]
-        received, operands = [], []
-        for turn in turns:
-            operand = halves[turn][1]
+            kept[turn], operand = split[:, 0], split[:, 1]
             if len(received) > 1:
                 operand = after(operand, received[-2], operands[-1])
             operands.append(operand)
@@ -414,18 +428,17 @@
         for place, turn in enumerate(turns):
             arrived = after(received[place], *operands[place + 1 :][:1])
             if bit_level < bit_count - 1:
-                current[turn] = add_pair(halves[turn][0], arrived)
+                current[turn] = add_pair(kept[turn], arrived)
             else:
-                current[turn] = (halves[turn][0], arrived)
+                current[turn] = (kept[turn], arrived)
     blocks, operands = [None] * feat_count, []
     for place in reversed(range(len(groups))):
         total = sum(part.astype(jnp.float32) for part in current[place, 0])
         for k in range(1, layers):
-            if place > 0:
-                moved = to_layer(add_pair(*current[place, k]), k, sub_count, real)
-            else:
-                moved = to_layer(after(joined[k], *operands), k, sub_count, real)
-            total = total + moved.astype(jnp.float32)
+            value = add_pair(*current[place, k])
+            if place == 0:
+                value = after(value, *operands)
+            total = total + to_layer(value, k, sub_count, real).astype(jnp.float32)
         for spot, block in enumerate(groups[place]):
             if block == 0:
                 rebuilt = total[0, spot]
@@ -467,39 +480,39 @@
                     groups_of.setdefault((other, k), [None] * len(spans))[place] = part
             known += [rel ^ 2**level for rel in known]
         if place == last - 1:
-            early = [part for parts in groups_of.values() for part in parts if part is not None]
-            early.pop()
+            early = [groups_of[rel, k][spot] for rel, k in groups_of for spot in range(place)]
+            early += [groups_of[0, k][place] for k in range(1, layers)]
 
     feature_grad, dec_grad, squares = None, None, {}
-    for k in range(layers):
-        for rel in [rel for stage in stages for rel in stage]:
-            parts = groups_of[rel, k]
-            if feature_grad is None:
-                parts = [after(parts[0], *early)] + parts[1:]
-            elif rel > 0:
-                parts = [after(part, feature_grad) for part in parts]
-            feature_grad, dec_grad, squares[k, rel] = backward_pair(
-                info,
-                rel,
-                k,
-                parts,
-                [over_members(part, 0) for part in parts],
-                turned_features,
-                dec_held,
-                feature_grad,
-                dec_grad,
-            )
+    uses = [(rel, k) for k in range(layers) for stage in stages for rel in stage]
+    for rel, k in uses:
+        parts = groups_of[rel, k]
+        if feature_grad is None:
+            parts = [after(parts[0], *early)] + parts[1:]
+        elif rel > 0:
+            parts = [after(part, feature_grad) for part in parts]
+        feature_grad, dec_grad, squares[k, rel], *sums = backward_pair(
+            info,
+            rel,
+            k,
+            parts,
+            [over_members(part, 0) for part in parts],
+            turned_features,
+            dec_held,
+            feature_grad,
+            dec_grad,
+            features if (rel, k) == uses[-1] else None,
+        )
     scale = (tok / loss_scale) ** 2 / (layers * tok * depth)
-    enc_grad, bias_grad, mean_square = encoder_grad(
+    enc_grad, mean_square = encoder_grad(
         info,
         order,
         turned_tokens,
-        features,
         feature_grad,
         [squares[key] for key in sorted(squares)],
         scale,
     )
-    return (recon_error, mean_square[0, 0], enc_grad, bias_grad[0], dec_grad)
+    return (recon_error, mean_square[0, 0], enc_grad, sums[0][0], dec_grad)
 
 
 def solution(mesh):

time: 118 us -> 124 us (1.051)
  waiting for transfers between devices: 34 us -> 37.5 us
  starting transfers between devices: 46.5 us -> 48 us
    ppermute x34 -> x35, waiting for transfers between devices: 16.1 us -> 22.8 us  [over_members(): return lax.ppermute(value, 'layer', pairs)]
    ppermute x4 -> x3, waiting for transfers between devices: 5.68 us -> 2.29 us  [to_layer(): moved = lax.ppermute(value, 'layer', pairs)]
    ppermute x34 -> x35, starting transfers between devices: 18.2 us -> 20.7 us  [over_members(): return lax.ppermute(value, 'layer', pairs)]
    ppermute x9, starting transfers between devices: 17.9 us -> 19.7 us  [over_feat(): return lax.ppermute(value, 'feat', pairs)]
    ppermute x4 -> x3, starting transfers between devices: 5.33 us -> 3.74 us  [to_layer(): moved = lax.ppermute(value, 'layer', pairs)]
  transfers between devices with their start and end apart: 51 -> 51, of which waited for: 19 -> 22; matrix products, arithmetic and copies ran while one was open for 1% -> 1% of each run, Pallas kernels for 19% -> 18%
where the time goes in v5:
time: 124 us
  starting transfers between devices  48 us (39%)
  waiting for transfers between devices  37.5 us (30%)
  Pallas kernels  34.9 us (28%)
  other arithmetic  1.94 us (2%)
    ppermute x35, waiting for transfers between devices, over_members(): return lax.ppermute(value, 'layer', pairs)  22.8 us
    ppermute x35, starting transfers between devices, over_members(): return lax.ppermute(value, 'layer', pairs)  20.7 us
    ppermute x9, starting transfers between devices, over_feat(): return lax.ppermute(value, 'feat', pairs)  19.7 us
    pallas_call x4, Pallas kernels, backward_pair(): pl.pallas_call(kernel, in_specs=[in_smem] + [in_vmem] * (len(inputs) + 2)...  14.5 us
    ppermute x9, waiting for transfers between devices, over_feat(): return lax.ppermute(value, 'feat', pairs)  12.4 us
    pallas_call x2, Pallas kernels, decode(): pl.pallas_call(kernel, in_specs=[in_smem, in_vmem, in_vmem], out_specs=[i...  5.79 us
    pallas_call x1, Pallas kernels, fetch(): pl.pallas_call(kernel, in_specs=[in_hbm] * len(arrays), out_specs=[in_vme...  4.74 us
    pallas_call x3, Pallas kernels, encode(): pl.pallas_call(kernel, in_specs=[in_smem] + [in_vmem] * (len(pieces) + 1...  4.48 us
  transfers between devices with their start and end apart: 51, of which 22 were waited for; matrix products, arithmetic and copies ran while one was open for 1% of the time, Pallas kernels for 18%

profile of v5, /device:TPU:0, one launch (start us, length us, event | category | flops | bytes accessed | tf_op | source)
XLA Modules:
  0.0 123.6 jit_solution(12837736241118879302)
XLA Ops:
  0.7 3.0 %collective-permute-start.1 = (bf16[128,512]{1,0:T(8,128)(2,1)}, bf16[128,512]{1,0:T(8,128)(2,1)S(1)}, u32[]{:S(2)}, u32[]{:S(2)}) collective-permute-start(bf16[128,512]{1,0:T(8,128)(2,1)} %param.5), channel_id=1, source_target_pairs={{0,1},{1,0},{2,3},{3,2},{4,5},{5,4},{6,7},{7,6},{8,9},{9,8},{10,11... | collective-permute-start | bytes 393224 | tf_op jit(solution)/shard_map/ppermute | solution.py:17
  3.8 2.5 %collective-permute-start.3 = (bf16[128,512]{1,0:T(8,128)(2,1)}, bf16[128,512]{1,0:T(8,128)(2,1)S(1)}, u32[]{:S(2)}, u32[]{:S(2)}) collective-permute-start(bf16[128,512]{1,0:T(8,128)(2,1)} %param.5), channel_id=1, source_target_pairs={{0,3},{1,2},{2,1},{3,0},{4,7},{5,6},{6,5},{7,4},{8,11},{9,10},{10,... | collective-permute-start | bytes 393224 | tf_op jit(solution)/shard_map/ppermute | solution.py:17
  6.4 1.5 %collective-permute-start = (bf16[128,512]{1,0:T(8,128)(2,1)}, bf16[128,512]{1,0:T(8,128)(2,1)S(1)}, u32[]{:S(2)}, u32[]{:S(2)}) collective-permute-start(bf16[128,512]{1,0:T(8,128)(2,1)} %param.5), channel_id=1, source_target_pairs={{0,8},{4,12},{8,0},{12,4},{16,24},{20,28},{24,16},{28,20},{1,9},{5... | collective-permute-start | bytes 393224 | tf_op jit(solution)/shard_map/ppermute | solution.py:23
  7.9 4.7 %fetch.1 = (bf16[2048,1024]{1,0:T(8,128)(2,1)S(1)}, bf16[2,1024,2048]{2,1,0:T(8,128)(2,1)S(1)}) custom-call(bf16[2048,1024]{1,0:T(8,128)(2,1)} %refs_0_.1, bf16[2,1024,2048]{2,1,0:T(8,128)(2,1)} %refs_1_), custom_call_target="tpu_custom_call" | custom-call | bytes 12582912 | tf_op jit(solution)/shard_map/fetch/pallas_call | solution.py:87
  12.6 1.1 collective-permute-done.3
  13.7 1.5 %collective-permute-start.5 = (bf16[128,512]{1,0:T(8,128)(2,1)S(1)}, bf16[128,512]{1,0:T(8,128)(2,1)S(1)}, u32[]{:S(2)}, u32[]{:S(2)}) collective-permute-start(bf16[128,512]{1,0:T(8,128)(2,1)S(1)} %collective-permute-done.3), channel_id=1, source_target_pairs={{0,8},{4,12},{8,0},{12,4},{16,24},{20,28},{24,16},{28,20},{1,9},{5... | collective-permute-start | bytes 393224 | tf_op jit(solution)/shard_map/ppermute | solution.py:23
  15.2 0.5 collective-permute-start.4
  15.8 2.5 %collective-permute-done.2 = bf16[128,512]{1,0:T(8,128)(2,1)S(1)} collective-permute-done((bf16[128,512]{1,0:T(8,128)(2,1)}, bf16[128,512]{1,0:T(8,128)(2,1)S(1)}, u32[]{:S(2)}, u32[]{:S(2)}) %collective-permute-start.2) | collective-permute-done | bytes 131104 | tf_op jit(solution)/shard_map/ppermute | solution.py:17
  18.3 0.4 collective-permute-done.5
  18.7 1.5 %collective-permute-done.4 = bf16[128,512]{1,0:T(8,128)(2,1)S(1)} collective-permute-done((bf16[128,512]{1,0:T(8,128)(2,1)S(1)}, bf16[128,512]{1,0:T(8,128)(2,1)S(1)}, u32[]{:S(2)}, u32[]{:S(2)}) %collective-permute-start.4) | collective-permute-done | bytes 131104 | tf_op jit(solution)/shard_map/ppermute | solution.py:23
  20.2 1.4 %collective-permute-start.7 = (bf16[128,512]{1,0:T(8,128)(2,1)S(1)}, bf16[128,512]{1,0:T(8,128)(2,1)S(1)}, u32[]{:S(2)}, u32[]{:S(2)}) collective-permute-start(bf16[128,512]{1,0:T(8,128)(2,1)S(1)} %collective-permute-done.2), channel_id=1, source_target_pairs={{0,8},{4,12},{8,0},{12,4},{16,24},{20,28},{24,16},{28,20},{1,9},{5... | collective-permute-start | bytes 393224 | tf_op jit(solution)/shard_map/ppermute | solution.py:23
  21.6 0.5 collective-permute-done.6.refs_1_
  22.1 1.8 %encode.3.refs_2_ = f32[512,1024]{1,0:T(8,128)S(1)} custom-call(s32[2]{0:T(128)S(1)} %pad_add_fusion.info_ref, bf16[4,128,512]{2,1,0:T(8,128)(2,1)S(1)} %pad_maximum_fusion.refs_0_, bf16[4,128,512]{2,1,0:T(8,128)(2,1)S(1)} %collective-permute-done.6.refs_1_, bf16[2048,1024]{1,0:T(8,128)(2,1)S(1)} %get-tuple-element.72.refs_2_.refs_1_), custom_call_target="tpu_custom_call" | custom-call | flops 1073741824 | bytes 3145728 | tf_op jit(solution)/shard_map/encode/pallas_call | solution.py:127
  23.9 2.2 %collective-permute-done.7 = bf16[128,512]{1,0:T(8,128)(2,1)S(1)} collective-permute-done((bf16[128,512]{1,0:T(8,128)(2,1)S(1)}, bf16[128,512]{1,0:T(8,128)(2,1)S(1)}, u32[]{:S(2)}, u32[]{:S(2)}) %collective-permute-start.7) | collective-permute-done | bytes 131104 | tf_op jit(solution)/shard_map/ppermute | solution.py:23
  26.3 1.3 %encode.4.refs_2_ = f32[512,1024]{1,0:T(8,128)S(1)} custom-call(s32[2]{0:T(128)S(1)} %pad_add_fusion.info_ref, bf16[4,128,512]{2,1,0:T(8,128)(2,1)S(1)} %pad_maximum_fusion.1.refs_0_, bf16[2048,1024]{1,0:T(8,128)(2,1)S(1)} %get-tuple-element.72.refs_2_.refs_1_, f32[512,1024]{1,0:T(8,128)S(1)} %encode.3.refs_2_), custom_call_target="tpu_custom_call" | custom-call | flops 536870912 | bytes 1572864 | tf_op jit(solution)/shard_map/encode/pallas_call | solution.py:127
  27.5 0.6 collective-permute-done.8.refs_0_
  28.2 1.4 %encode.5.feat_ref.in_ref.refs_10_ = bf16[2,512,1024]{2,1,0:T(8,128)(2,1)S(1)} custom-call(s32[2]{0:T(128)S(1)} %pad_add_fusion.info_ref, bf16[4,128,512]{2,1,0:T(8,128)(2,1)S(1)} %collective-permute-done.8.refs_0_, bf16[2048,1024]{1,0:T(8,128)(2,1)S(1)} %get-tuple-element.72.refs_2_.refs_1_, f32[512,1024]{1,0:T(8,128)S(1)} %encode.4.refs_2_, ...), custom_call_target="tpu_custom_call" | custom-call | flops 536870912 | bytes 1572864 | tf_op jit(solution)/shard_map/encode/pallas_call | solution.py:127
  29.6 2.9 %decode.2 = (bf16[2,2,128,512]{3,2,1,0:T(8,128)(2,1)S(1)}, bf16[2,1,128,512]{3,2,1,0:T(8,128)(2,1)S(1)}, bf16[2,1,128,512]{3,2,1,0:T(8,128)(2,1)S(1)}, bf16[2,2,...) custom-call(s32[2]{0:T(128)S(1)} %pad_add_fusion.info_ref, ...), custom_call_target="tpu_custom_call" | custom-call | flops 2147483648 | bytes 4194304 | tf_op jit(solution)/shard_map/decode/pallas_call | solution.py:165
  32.7 0.4 collective-permute-start.14
  33.2 0.9 collective-permute-done.9
  34.2 2.9 %decode.3 = (bf16[2,2,128,512]{3,2,1,0:T(8,128)(2,1)S(1)}, bf16[2,1,128,512]{3,2,1,0:T(8,128)(2,1)S(1)}, bf16[2,1,128,512]{3,2,1,0:T(8,128)(2,1)S(1)}, bf16[2,2,...) custom-call(s32[2]{0:T(128)S(1)} %pad_add_fusion.info_ref, ...), custom_call_target="tpu_custom_call" | custom-call | flops 2147483648 | bytes 4194304 | tf_op jit(solution)/shard_map/decode/pallas_call | solution.py:165
  37.4 1.5 %collective-permute-start.15 = (bf16[1,1,128,512]{3,2,1,0:T(8,128)(2,1)S(1)}, bf16[1,1,128,512]{3,2,1,0:T(8,128)(2,1)S(1)}, u32[]{:S(2)}, u32[]{:S(2)}) collective-permute-start(bf16[1,1,128,512]{3,2,1,0:T(8,128)(2,1)S(1)} %slice_bitcast_fusion.9), channel_id=1, source_target_pairs={{0,8},{4,12},{8,0},{12,4},{16,24},{20,28},{24,16},{28,20},{1,9},{5... | collective-permute-start | bytes 393224 | tf_op jit(solution)/shard_map/ppermute | solution.py:23
  38.9 0.4 collective-permute-start.10
  39.5 0.8 collective-permute-start.13
  40.2 3.5 %collective-permute-done.15 = bf16[1,1,128,512]{3,2,1,0:T(8,128)(2,1)S(1)} collective-permute-done((bf16[1,1,128,512]{3,2,1,0:T(8,128)(2,1)S(1)}, bf16[1,1,128,512]{3,2,1,0:T(8,128)(2,1)S(1)}, u32[]{:S(2)}, u32[]{:S(2)}) %collective-permute-start.15) | collective-permute-done | bytes 131104 | tf_op jit(solution)/shard_map/ppermute | solution.py:23
  43.8 1.4 %collective-permute-start.18 = (bf16[1,1,128,512]{3,2,1,0:T(8,128)(2,1)S(1)}, bf16[1,1,128,512]{3,2,1,0:T(8,128)(2,1)S(1)}, u32[]{:S(2)}, u32[]{:S(2)}) collective-permute-start(bf16[1,1,128,512]{3,2,1,0:T(8,128)(2,1)S(1)} %slice_bitcast_fusion.10), channel_id=1, source_target_pairs={{0,8},{4,12},{8,0},{12,4},{16,24},{20,28},{24,16},{28,20},{1,9},{5... | collective-permute-start | bytes 393224 | tf_op jit(solution)/shard_map/ppermute | solution.py:23
  45.5 1.6 %collective-permute-start.21 = (bf16[1,1,128,512]{3,2,1,0:T(8,128)(2,1)S(1)}, bf16[1,1,128,512]{3,2,1,0:T(8,128)(2,1)S(1)}, u32[]{:S(2)}, u32[]{:S(2)}) collective-permute-start(bf16[1,1,128,512]{3,2,1,0:T(8,128)(2,1)S(1)} %fusion.13), channel_id=1, source_target_pairs={{0,16},{4,20},{8,24},{12,28},{16,0},{20,4},{24,8},{28,12},{1,17},{... | collective-permute-start | bytes 393224 | tf_op jit(solution)/shard_map/ppermute | solution.py:29
  47.1 0.9 collective-permute-start.16
  48.0 1.5 %collective-permute-done.18 = bf16[1,1,128,512]{3,2,1,0:T(8,128)(2,1)S(1)} collective-permute-done((bf16[1,1,128,512]{3,2,1,0:T(8,128)(2,1)S(1)}, bf16[1,1,128,512]{3,2,1,0:T(8,128)(2,1)S(1)}, u32[]{:S(2)}, u32[]{:S(2)}) %collective-permute-start.18) | collective-permute-done | bytes 131104 | tf_op jit(solution)/shard_map/ppermute | solution.py:23
  49.6 1.6 %collective-permute-start.22 = (bf16[1,1,128,512]{3,2,1,0:T(8,128)(2,1)S(1)}, bf16[1,1,128,512]{3,2,1,0:T(8,128)(2,1)S(1)}, u32[]{:S(2)}, u32[]{:S(2)}) collective-permute-start(bf16[1,1,128,512]{3,2,1,0:T(8,128)(2,1)S(1)} %fusion.10), channel_id=1, source_target_pairs={{0,16},{4,20},{8,24},{12,28},{16,0},{20,4},{24,8},{28,12},{1,17},{... | collective-permute-start | bytes 393224 | tf_op jit(solution)/shard_map/ppermute | solution.py:29
  51.1 1.4 %collective-permute-start.20 = (bf16[1,2,128,512]{3,2,1,0:T(8,128)(2,1)S(1)}, bf16[1,2,128,512]{3,2,1,0:T(8,128)(2,1)S(1)}, u32[]{:S(2)}, u32[]{:S(2)}) collective-permute-start(bf16[1,2,128,512]{3,2,1,0:T(8,128)(2,1)S(1)} %slice_bitcast_fusion.2), channel_id=1, source_target_pairs={{0,8},{4,12},{8,0},{12,4},{16,24},{20,28},{24,16},{28,20},{1,9},{5... | collective-permute-start | bytes 786440 | tf_op jit(solution)/shard_map/ppermute | solution.py:23
  52.8 0.7 collective-permute-start.19
  53.5 1.1 collective-permute-done.22
  54.7 5.7 %collective-permute-done.20 = bf16[1,2,128,512]{3,2,1,0:T(8,128)(2,1)S(1)} collective-permute-done((bf16[1,2,128,512]{3,2,1,0:T(8,128)(2,1)S(1)}, bf16[1,2,128,512]{3,2,1,0:T(8,128)(2,1)S(1)}, u32[]{:S(2)}, u32[]{:S(2)}) %collective-permute-start.20) | collective-permute-done | bytes 262176 | tf_op jit(solution)/shard_map/ppermute | solution.py:23
  60.5 0.6 collective-permute-start.23
  61.0 4.4 %collective-permute-start.24 = (bf16[128,512]{1,0:T(8,128)(2,1)S(1)}, bf16[128,512]{1,0:T(8,128)(2,1)S(1)}, u32[]{:S(2)}, u32[]{:S(2)}) collective-permute-start(bf16[128,512]{1,0:T(8,128)(2,1)S(1)} %fusion.16), channel_id=1, source_target_pairs={{0,3},{1,2},{2,1},{3,0},{4,7},{5,6},{6,5},{7,4},{8,11},{9,10},{10,... | collective-permute-start | bytes 393224 | tf_op jit(solution)/shard_map/ppermute | solution.py:17
  65.7 1.2 collective-permute-done.23
  67.0 3.3 %collective-permute-start.26 = (bf16[128,512]{1,0:T(8,128)(2,1)S(1)}, bf16[128,512]{1,0:T(8,128)(2,1)S(1)}, u32[]{:S(2)}, u32[]{:S(2)}) collective-permute-start(bf16[128,512]{1,0:T(8,128)(2,1)S(1)} %fusion.18), channel_id=1, source_target_pairs={{0,1},{1,0},{2,3},{3,2},{4,5},{5,4},{6,7},{7,6},{8,9},{9,8},{10,11... | collective-permute-start | bytes 393224 | tf_op jit(solution)/shard_map/ppermute | solution.py:17
  70.3 0.3 turned.5
  71.4 1.9 %collective-permute-done.25 = bf16[128,512]{1,0:T(8,128)(2,1)S(1)} collective-permute-done((bf16[128,512]{1,0:T(8,128)(2,1)S(1)}, bf16[128,512]{1,0:T(8,128)(2,1)S(1)}, u32[]{:S(2)}, u32[]{:S(2)}) %collective-permute-start.25) | collective-permute-done | bytes 131104 | tf_op jit(solution)/shard_map/ppermute | solution.py:17
  73.3 3.4 %collective-permute-done.26 = bf16[128,512]{1,0:T(8,128)(2,1)S(1)} collective-permute-done((bf16[128,512]{1,0:T(8,128)(2,1)S(1)}, bf16[128,512]{1,0:T(8,128)(2,1)S(1)}, u32[]{:S(2)}, u32[]{:S(2)}) %collective-permute-start.26) | collective-permute-done | bytes 131104 | tf_op jit(solution)/shard_map/ppermute | solution.py:17
  76.7 0.8 multiply_convert_fusion
  77.6 6.1 %collective-permute-start.31 = (bf16[128,512]{1,0:T(8,128)(2,1)S(1)}, bf16[128,512]{1,0:T(8,128)(2,1)S(1)}, u32[]{:S(2)}, u32[]{:S(2)}) collective-permute-start(bf16[128,512]{1,0:T(8,128)(2,1)S(1)} %get-tuple-element.133), channel_id=1, source_target_pairs={{0,2},{1,3},{2,0},{3,1},{4,6},{5,7},{6,4},{7,5},{8,10},{9,11},{10,... | collective-permute-start | bytes 393224 | tf_op jit(solution)/shard_map/ppermute | solution.py:17
  83.7 1.6 %collective-permute-start.37 = (bf16[1,128,512]{2,1,0:T(8,128)(2,1)S(1)}, bf16[1,128,512]{2,1,0:T(8,128)(2,1)S(1)}, u32[]{:S(2)}, u32[]{:S(2)}) collective-permute-start(bf16[1,128,512]{2,1,0:T(8,128)(2,1)S(1)} %bitcast.112), channel_id=1, source_target_pairs={{0,8},{4,12},{8,0},{12,4},{16,24},{20,28},{24,16},{28,20},{1,9},{5... | collective-permute-start | bytes 393224 | tf_op jit(solution)/shard_map/ppermute | solution.py:23
  85.3 0.5 collective-permute-start.28
  85.7 1.3 %collective-permute-start.30 = (bf16[1,128,512]{2,1,0:T(8,128)(2,1)S(1)}, bf16[1,128,512]{2,1,0:T(8,128)(2,1)S(1)}, u32[]{:S(2)}, u32[]{:S(2)}) collective-permute-start(bf16[1,128,512]{2,1,0:T(8,128)(2,1)S(1)} %bitcast.115), channel_id=1, source_target_pairs={{0,16},{4,20},{8,24},{12,28},{16,0},{20,4},{24,8},{28,12},{1,17},{... | collective-permute-start | bytes 393224 | tf_op jit(solution)/shard_map/ppermute | solution.py:36
  87.0 1.0 collective-permute-done.31
  88.0 2.5 %collective-permute-done.32 = bf16[128,512]{1,0:T(8,128)(2,1)S(1)} collective-permute-done((bf16[128,512]{1,0:T(8,128)(2,1)S(1)}, bf16[128,512]{1,0:T(8,128)(2,1)S(1)}, u32[]{:S(2)}, u32[]{:S(2)}) %collective-permute-start.32) | collective-permute-done | bytes 131104 | tf_op jit(solution)/shard_map/ppermute | solution.py:17
  90.7 1.6 %collective-permute-start.42 = (bf16[2,128,512]{2,1,0:T(8,128)(2,1)S(1)}, bf16[2,128,512]{2,1,0:T(8,128)(2,1)S(1)}, u32[]{:S(2)}, u32[]{:S(2)}) collective-permute-start(bf16[2,128,512]{2,1,0:T(8,128)(2,1)S(1)} %pad_maximum_fusion.2.refs_2_), channel_id=1, source_target_pairs={{0,8},{4,12},{8,0},{12,4},{16,24},{20,28},{24,16},{28,20},{1,9},{5... | collective-permute-start | bytes 786440 | tf_op jit(solution)/shard_map/ppermute | solution.py:23
  92.5 1.1 collective-permute-start.33
  93.6 0.7 collective-permute-start.41
  94.3 0.6 collective-permute-done.38.refs_3_
  94.9 3.3 %backward_pair.4 = (f32[512,1024]{1,0:T(8,128)S(1)}, bf16[2,1024,2048]{2,1,0:T(8,128)(2,1)}, f32[8,128]{1,0:T(8,128)S(1)}) custom-call(s32[2]{0:T(128)S(1)} %pad_add_fusion.info_ref, bf16[1,128,512]{2,1,0:T(8,128)(2,1)S(1)} %bitcast.114, bf16[1,128,512]{2,1,0:T(8,128)(2,1)S(1)} %bitcast.118, bf16[2,128,512]{2,1,0:T(8,128)(2,1)S(1)} %pad_maximum_fusion.2.refs_2_, ...), custom_call_target="tpu_custom_call" | custom-call | flops 262144 | bytes 262144 | tf_op jit(solution)/shard_map/backward_pair/pallas_call | solution.py:296
  98.3 1.6 %collective-permute-done.42.refs_2_ = bf16[2,128,512]{2,1,0:T(8,128)(2,1)S(1)} collective-permute-done((bf16[2,128,512]{2,1,0:T(8,128)(2,1)S(1)}, bf16[2,128,512]{2,1,0:T(8,128)(2,1)S(1)}, u32[]{:S(2)}, u32[]{:S(2)}) %collective-permute-start.42) | collective-permute-done | bytes 262176 | tf_op jit(solution)/shard_map/ppermute | solution.py:23
  99.8 2.4 %collective-permute-done.41.refs_1_ = bf16[1,128,512]{2,1,0:T(8,128)(2,1)S(1)} collective-permute-done((bf16[1,128,512]{2,1,0:T(8,128)(2,1)S(1)}, bf16[1,128,512]{2,1,0:T(8,128)(2,1)S(1)}, u32[]{:S(2)}, u32[]{:S(2)}) %collective-permute-start.41) | collective-permute-done | bytes 131104 | tf_op jit(solution)/shard_map/ppermute | solution.py:23
  102.2 0.5 collective-permute-start.43
  102.7 1.3 %collective-permute-start.47 = (bf16[2,128,512]{2,1,0:T(8,128)(2,1)S(1)}, bf16[2,128,512]{2,1,0:T(8,128)(2,1)S(1)}, u32[]{:S(2)}, u32[]{:S(2)}) collective-permute-start(bf16[2,128,512]{2,1,0:T(8,128)(2,1)S(1)} %collective-permute-done.42.refs_2_), channel_id=1, source_target_pairs={{0,16},{4,20},{8,24},{12,28},{16,0},{20,4},{24,8},{28,12},{1,17},{... | collective-permute-start | bytes 786440 | tf_op jit(solution)/shard_map/ppermute | solution.py:36
  104.6 1.3 %collective-permute-start.46 = (bf16[1,128,512]{2,1,0:T(8,128)(2,1)S(1)}, bf16[1,128,512]{2,1,0:T(8,128)(2,1)S(1)}, u32[]{:S(2)}, u32[]{:S(2)}) collective-permute-start(bf16[1,128,512]{2,1,0:T(8,128)(2,1)S(1)} %collective-permute-done.30.refs_1_), channel_id=1, source_target_pairs={{0,8},{4,12},{8,0},{12,4},{16,24},{20,28},{24,16},{28,20},{1,9},{5... | collective-permute-start | bytes 393224 | tf_op jit(solution)/shard_map/ppermute | solution.py:23
  105.9 3.7 %backward_pair.5 = (f32[512,1024]{1,0:T(8,128)S(1)}, bf16[2,1024,2048]{2,1,0:T(8,128)(2,1)}, f32[8,128]{1,0:T(8,128)S(1)}) custom-call(s32[2]{0:T(128)S(1)} %pad_add_fusion.info_ref, bf16[1,128,512]{2,1,0:T(8,128)(2,1)S(1)} %collective-permute-done.37.refs_0_, ...), custom_call_target="tpu_custom_call", output_to_operand_aliasing={{1}: (10, {}), {0}: (9, {})} | custom-call | flops 262144 | bytes 262144 | tf_op jit(solution)/shard_map/backward_pair/pallas_call | solution.py:296
  109.7 3.3 %backward_pair.6 = (f32[512,1024]{1,0:T(8,128)S(1)}, bf16[2,1024,2048]{2,1,0:T(8,128)(2,1)}, f32[8,128]{1,0:T(8,128)S(1)}) custom-call(s32[2]{0:T(128)S(1)} %pad_add_fusion.info_ref, bf16[1,128,512]{2,1,0:T(8,128)(2,1)S(1)} %collective-permute-done.27.refs_0_, ...), custom_call_target="tpu_custom_call", output_to_operand_aliasing={{1}: (10, {}), {0}: (9, {})} | custom-call | flops 262144 | bytes 262144 | tf_op jit(solution)/shard_map/backward_pair/pallas_call | solution.py:296
  113.1 0.5 collective-permute-start.49
  113.7 1.1 collective-permute-done.49.refs_4_
  115.0 4.1 %backward_pair.7 = (bf16[512,1024]{1,0:T(8,128)(2,1)S(1)}, bf16[2,1024,2048]{2,1,0:T(8,128)(2,1)}, f32[8,128]{1,0:T(8,128)S(1)}, f32[1,1024]{1,0:T(1,128)}) custom-call(s32[2]{0:T(128)S(1)} %pad_add_fusion.info_ref, bf16[1,128,512]{2,1,0:T(8,128)(2,1)S(1)} %collective-permute-done.28.refs_0_, ...), custom_call_target="tpu_custom_call", output_to_operand_aliasing={{1}: (10, {})} | custom-call | flops 262144 | bytes 262144 | tf_op jit(solution)/shard_map/backward_pair/pallas_call | solution.py:296
  119.1 4.4 %encoder_grad.1 = (bf16[2048,1024]{1,0:T(8,128)(2,1)}, f32[1,1]{1,0:T(1,128)}) custom-call(s32[2]{0:T(128)S(1)} %pad_add_fusion.info_ref, bf16[1,512,512]{2,1,0:T(8,128)(2,1)S(1)} %turned.6.refs_0_, bf16[1,512,512]{2,1,0:T(8,128)(2,1)S(1)} %turned.7.refs_1_, bf16[1,512,512]{2,1,0:T(8,128)(2,1)S(1)} %turned.8.refs_2_, ...), custom_call_target="tpu_custom_call" | custom-call | flops 2147483648 | bytes 6291456 | tf_op jit(solution)/shard_map/encoder_grad/pallas_call | solution.py:342
  (84 shorter events, 4.4 us)
Async XLA Ops:
  0.7 17.5 %copy-start.2 = (bf16[128,512]{1,0:T(8,128)(2,1)S(1)}, bf16[128,512]{1,0:T(8,128)(2,1)}, u32[]{:S(2)}) copy-start(bf16[128,512]{1,0:T(8,128)(2,1)} %param.5) | copy-start | bytes 393220
  0.7 7.1 %collective-permute-start.1 = (bf16[128,512]{1,0:T(8,128)(2,1)}, bf16[128,512]{1,0:T(8,128)(2,1)S(1)}, u32[]{:S(2)}, u32[]{:S(2)}) collective-permute-start(bf16[128,512]{1,0:T(8,128)(2,1)} %param.5), channel_id=1, source_target_pairs={{0,1},{1,0},{2,3},{3,2},{4,5},{5,4},{6,7},{7,6},{8,9},{9,8},{10,11... | collective-permute-start | bytes 393224 | tf_op jit(solution)/shard_map/ppermute | solution.py:17
  3.8 10.0 %collective-permute-start.3 = (bf16[128,512]{1,0:T(8,128)(2,1)}, bf16[128,512]{1,0:T(8,128)(2,1)S(1)}, u32[]{:S(2)}, u32[]{:S(2)}) collective-permute-start(bf16[128,512]{1,0:T(8,128)(2,1)} %param.5), channel_id=1, source_target_pairs={{0,3},{1,2},{2,1},{3,0},{4,7},{5,6},{6,5},{7,4},{8,11},{9,10},{10,... | collective-permute-start | bytes 393224 | tf_op jit(solution)/shard_map/ppermute | solution.py:17
  6.2 12.0 %collective-permute-start.2 = (bf16[128,512]{1,0:T(8,128)(2,1)}, bf16[128,512]{1,0:T(8,128)(2,1)S(1)}, u32[]{:S(2)}, u32[]{:S(2)}) collective-permute-start(bf16[128,512]{1,0:T(8,128)(2,1)} %param.5), channel_id=1, source_target_pairs={{0,2},{1,3},{2,0},{3,1},{4,6},{5,7},{6,4},{7,5},{8,10},{9,11},{10,... | collective-permute-start | bytes 393224 | tf_op jit(solution)/shard_map/ppermute | solution.py:17
  6.4 12.0 %collective-permute-start = (bf16[128,512]{1,0:T(8,128)(2,1)}, bf16[128,512]{1,0:T(8,128)(2,1)S(1)}, u32[]{:S(2)}, u32[]{:S(2)}) collective-permute-start(bf16[128,512]{1,0:T(8,128)(2,1)} %param.5), channel_id=1, source_target_pairs={{0,8},{4,12},{8,0},{12,4},{16,24},{20,28},{24,16},{28,20},{1,9},{5... | collective-permute-start | bytes 393224 | tf_op jit(solution)/shard_map/ppermute | solution.py:23
  13.7 5.0 %collective-permute-start.5 = (bf16[128,512]{1,0:T(8,128)(2,1)S(1)}, bf16[128,512]{1,0:T(8,128)(2,1)S(1)}, u32[]{:S(2)}, u32[]{:S(2)}) collective-permute-start(bf16[128,512]{1,0:T(8,128)(2,1)S(1)} %collective-permute-done.3), channel_id=1, source_target_pairs={{0,8},{4,12},{8,0},{12,4},{16,24},{20,28},{24,16},{28,20},{1,9},{5... | collective-permute-start | bytes 393224 | tf_op jit(solution)/shard_map/ppermute | solution.py:23
  15.2 5.0 %collective-permute-start.4 = (bf16[128,512]{1,0:T(8,128)(2,1)S(1)}, bf16[128,512]{1,0:T(8,128)(2,1)S(1)}, u32[]{:S(2)}, u32[]{:S(2)}) collective-permute-start(bf16[128,512]{1,0:T(8,128)(2,1)S(1)} %collective-permute-done.1), channel_id=1, source_target_pairs={{0,8},{4,12},{8,0},{12,4},{16,24},{20,28},{24,16},{28,20},{1,9},{5... | collective-permute-start | bytes 393224 | tf_op jit(solution)/shard_map/ppermute | solution.py:23
  20.2 1.9 %collective-permute-start.6 = (bf16[4,128,512]{2,1,0:T(8,128)(2,1)S(1)}, bf16[4,128,512]{2,1,0:T(8,128)(2,1)S(1)}, u32[]{:S(2)}, u32[]{:S(2)}) collective-permute-start(bf16[4,128,512]{2,1,0:T(8,128)(2,1)S(1)} %pad_maximum_fusion.refs_0_), channel_id=1, source_target_pairs={{0,4},{4,0},{8,12},{12,8},{16,20},{20,16},{24,28},{28,24},{1,5},{5... | collective-permute-start | bytes 1572872 | tf_op jit(solution)/shard_map/ppermute | solution.py:23
  20.2 5.9 %collective-permute-start.7 = (bf16[128,512]{1,0:T(8,128)(2,1)S(1)}, bf16[128,512]{1,0:T(8,128)(2,1)S(1)}, u32[]{:S(2)}, u32[]{:S(2)}) collective-permute-start(bf16[128,512]{1,0:T(8,128)(2,1)S(1)} %collective-permute-done.2), channel_id=1, source_target_pairs={{0,8},{4,12},{8,0},{12,4},{16,24},{20,28},{24,16},{28,20},{1,9},{5... | collective-permute-start | bytes 393224 | tf_op jit(solution)/shard_map/ppermute | solution.py:23
  26.2 2.0 %copy-start = (f32[1024]{0:T(1024)S(1)}, f32[1024]{0:T(1024)}, u32[]{:S(2)}) copy-start(f32[1024]{0:T(1024)} %param.8) | copy-start | bytes 12292
  26.2 2.0 %collective-permute-start.8 = (bf16[4,128,512]{2,1,0:T(8,128)(2,1)S(1)}, bf16[4,128,512]{2,1,0:T(8,128)(2,1)S(1)}, u32[]{:S(2)}, u32[]{:S(2)}) collective-permute-start(bf16[4,128,512]{2,1,0:T(8,128)(2,1)S(1)} %pad_maximum_fusion.1.refs_0_), channel_id=1, source_target_pairs={{0,4},{4,0},{8,12},{12,8},{16,20},{20,16},{24,28},{28,24},{1,5},{5... | collective-permute-start | bytes 1572872 | tf_op jit(solution)/shard_map/ppermute | solution.py:23
  32.5 1.6 %collective-permute-start.9 = (bf16[2,1,128,512]{3,2,0,1:T(8,128)(2,1)S(1)}, bf16[2,1,128,512]{3,2,0,1:T(8,128)(2,1)S(1)}, u32[]{:S(2)}, u32[]{:S(2)}) collective-permute-start(bf16[2,1,128,512]{3,2,0,1:T(8,128)(2,1)S(1)} %bitcast.123), channel_id=1, source_target_pairs={{0,4},{4,0},{8,12},{12,8},{16,20},{20,16},{24,28},{28,24},{1,5},{5... | collective-permute-start | bytes 786440 | tf_op jit(solution)/shard_map/ppermute | solution.py:23
  32.7 4.6 %collective-permute-start.14 = (bf16[2,1,128,512]{3,2,0,1:T(8,128)(2,1)S(1)}, bf16[2,1,128,512]{3,2,0,1:T(8,128)(2,1)S(1)}, u32[]{:S(2)}, u32[]{:S(2)}) collective-permute-start(bf16[2,1,128,512]{3,2,0,1:T(8,128)(2,1)S(1)} %bitcast.121), channel_id=1, source_target_pairs={{0,4},{4,0},{8,12},{12,8},{16,20},{20,16},{24,28},{28,24},{1,5},{5... | collective-permute-start | bytes 786440 | tf_op jit(solution)/shard_map/ppermute | solution.py:23
  33.1 12.1 %collective-permute-start.17 = (bf16[2,2,128,512]{3,2,1,0:T(8,128)(2,1)S(1)}, bf16[2,2,128,512]{3,2,1,0:T(8,128)(2,1)S(1)}, u32[]{:S(2)}, u32[]{:S(2)}) collective-permute-start(bf16[2,2,128,512]{3,2,1,0:T(8,128)(2,1)S(1)} %get-tuple-element.95), channel_id=1, source_target_pairs={{0,4},{4,0},{8,12},{12,8},{16,20},{20,16},{24,28},{28,24},{1,5},{5... | collective-permute-start | bytes 1572872 | tf_op jit(solution)/shard_map/ppermute | solution.py:23
  37.1 2.3 %collective-permute-start.12 = (bf16[2,1,128,512]{3,2,0,1:T(8,128)(2,1)S(1)}, bf16[2,1,128,512]{3,2,0,1:T(8,128)(2,1)S(1)}, u32[]{:S(2)}, u32[]{:S(2)}) collective-permute-start(bf16[2,1,128,512]{3,2,0,1:T(8,128)(2,1)S(1)} %bitcast.122), channel_id=1, source_target_pairs={{0,4},{4,0},{8,12},{12,8},{16,20},{20,16},{24,28},{28,24},{1,5},{5... | collective-permute-start | bytes 786440 | tf_op jit(solution)/shard_map/ppermute | solution.py:23
  37.4 6.4 %collective-permute-start.15 = (bf16[1,1,128,512]{3,2,1,0:T(8,128)(2,1)S(1)}, bf16[1,1,128,512]{3,2,1,0:T(8,128)(2,1)S(1)}, u32[]{:S(2)}, u32[]{:S(2)}) collective-permute-start(bf16[1,1,128,512]{3,2,1,0:T(8,128)(2,1)S(1)} %slice_bitcast_fusion.9), channel_id=1, source_target_pairs={{0,8},{4,12},{8,0},{12,4},{16,24},{20,28},{24,16},{28,20},{1,9},{5... | collective-permute-start | bytes 393224 | tf_op jit(solution)/shard_map/ppermute | solution.py:23
  38.9 6.5 %collective-permute-start.11 = (bf16[2,1,128,512]{3,2,0,1:T(8,128)(2,1)S(1)}, bf16[2,1,128,512]{3,2,0,1:T(8,128)(2,1)S(1)}, u32[]{:S(2)}, u32[]{:S(2)}) collective-permute-start(bf16[2,1,128,512]{3,2,0,1:T(8,128)(2,1)S(1)} %bitcast.120), channel_id=1, source_target_pairs={{0,4},{4,0},{8,12},{12,8},{16,20},{20,16},{24,28},{28,24},{1,5},{5... | collective-permute-start | bytes 786440 | tf_op jit(solution)/shard_map/ppermute | solution.py:23
  38.9 13.7 %collective-permute-start.10 = (bf16[2,2,128,512]{3,2,1,0:T(8,128)(2,1)S(1)}, bf16[2,2,128,512]{3,2,1,0:T(8,128)(2,1)S(1)}, u32[]{:S(2)}, u32[]{:S(2)}) collective-permute-start(bf16[2,2,128,512]{3,2,1,0:T(8,128)(2,1)S(1)} %get-tuple-element.85), channel_id=1, source_target_pairs={{0,4},{4,0},{8,12},{12,8},{16,20},{20,16},{24,28},{28,24},{1,5},{5... | collective-permute-start | bytes 1572872 | tf_op jit(solution)/shard_map/ppermute | solution.py:23
  39.5 7.6 %collective-permute-start.13 = (bf16[1,1,128,512]{3,2,1,0:T(8,128)(2,1)S(1)}, bf16[1,1,128,512]{3,2,1,0:T(8,128)(2,1)S(1)}, u32[]{:S(2)}, u32[]{:S(2)}) collective-permute-start(bf16[1,1,128,512]{3,2,1,0:T(8,128)(2,1)S(1)} %slice_bitcast_fusion.11), channel_id=1, source_target_pairs={{0,8},{4,12},{8,0},{12,4},{16,24},{20,28},{24,16},{28,20},{1,9},{5... | collective-permute-start | bytes 393224 | tf_op jit(solution)/shard_map/ppermute | solution.py:23
  43.8 5.7 %collective-permute-start.18 = (bf16[1,1,128,512]{3,2,1,0:T(8,128)(2,1)S(1)}, bf16[1,1,128,512]{3,2,1,0:T(8,128)(2,1)S(1)}, u32[]{:S(2)}, u32[]{:S(2)}) collective-permute-start(bf16[1,1,128,512]{3,2,1,0:T(8,128)(2,1)S(1)} %slice_bitcast_fusion.10), channel_id=1, source_target_pairs={{0,8},{4,12},{8,0},{12,4},{16,24},{20,28},{24,16},{28,20},{1,9},{5... | collective-permute-start | bytes 393224 | tf_op jit(solution)/shard_map/ppermute | solution.py:23
  45.5 7.0 %collective-permute-start.21 = (bf16[1,1,128,512]{3,2,1,0:T(8,128)(2,1)S(1)}, bf16[1,1,128,512]{3,2,1,0:T(8,128)(2,1)S(1)}, u32[]{:S(2)}, u32[]{:S(2)}) collective-permute-start(bf16[1,1,128,512]{3,2,1,0:T(8,128)(2,1)S(1)} %fusion.13), channel_id=1, source_target_pairs={{0,16},{4,20},{8,24},{12,28},{16,0},{20,4},{24,8},{28,12},{1,17},{... | collective-permute-start | bytes 393224 | tf_op jit(solution)/shard_map/ppermute | solution.py:29
  47.1 5.7 %collective-permute-start.16 = (bf16[1,1,128,512]{3,2,1,0:T(8,128)(2,1)S(1)}, bf16[1,1,128,512]{3,2,1,0:T(8,128)(2,1)S(1)}, u32[]{:S(2)}, u32[]{:S(2)}) collective-permute-start(bf16[1,1,128,512]{3,2,1,0:T(8,128)(2,1)S(1)} %slice_bitcast_fusion.12), channel_id=1, source_target_pairs={{0,8},{4,12},{8,0},{12,4},{16,24},{20,28},{24,16},{28,20},{1,9},{5... | collective-permute-start | bytes 393224 | tf_op jit(solution)/shard_map/ppermute | solution.py:23
  49.6 5.0 %collective-permute-start.22 = (bf16[1,1,128,512]{3,2,1,0:T(8,128)(2,1)S(1)}, bf16[1,1,128,512]{3,2,1,0:T(8,128)(2,1)S(1)}, u32[]{:S(2)}, u32[]{:S(2)}) collective-permute-start(bf16[1,1,128,512]{3,2,1,0:T(8,128)(2,1)S(1)} %fusion.10), channel_id=1, source_target_pairs={{0,16},{4,20},{8,24},{12,28},{16,0},{20,4},{24,8},{28,12},{1,17},{... | collective-permute-start | bytes 393224 | tf_op jit(solution)/shard_map/ppermute | solution.py:29
  51.1 9.2 %collective-permute-start.20 = (bf16[1,2,128,512]{3,2,1,0:T(8,128)(2,1)S(1)}, bf16[1,2,128,512]{3,2,1,0:T(8,128)(2,1)S(1)}, u32[]{:S(2)}, u32[]{:S(2)}) collective-permute-start(bf16[1,2,128,512]{3,2,1,0:T(8,128)(2,1)S(1)} %slice_bitcast_fusion.2), channel_id=1, source_target_pairs={{0,8},{4,12},{8,0},{12,4},{16,24},{20,28},{24,16},{28,20},{1,9},{5... | collective-permute-start | bytes 786440 | tf_op jit(solution)/shard_map/ppermute | solution.py:23
  52.8 12.9 %collective-permute-start.19 = (bf16[1,2,128,512]{3,2,1,0:T(8,128)(2,1)S(1)}, bf16[1,2,128,512]{3,2,1,0:T(8,128)(2,1)S(1)}, u32[]{:S(2)}, u32[]{:S(2)}) collective-permute-start(bf16[1,2,128,512]{3,2,1,0:T(8,128)(2,1)S(1)} %slice_bitcast_fusion.3), channel_id=1, source_target_pairs={{0,8},{4,12},{8,0},{12,4},{16,24},{20,28},{24,16},{28,20},{1,9},{5... | collective-permute-start | bytes 786440 | tf_op jit(solution)/shard_map/ppermute | solution.py:23
  60.5 16.3 %copy-start.1 = (bf16[128,512]{1,0:T(8,128)(2,1)S(1)}, bf16[128,512]{1,0:T(8,128)(2,1)}, u32[]{:S(2)}) copy-start(bf16[128,512]{1,0:T(8,128)(2,1)} %param.6) | copy-start | bytes 393220
  60.5 6.4 %collective-permute-start.23 = (bf16[1,2,128,512]{3,2,1,0:T(8,128)(2,1)S(1)}, bf16[1,2,128,512]{3,2,1,0:T(8,128)(2,1)S(1)}, u32[]{:S(2)}, u32[]{:S(2)}) collective-permute-start(bf16[1,2,128,512]{3,2,1,0:T(8,128)(2,1)S(1)} %fusion.2), channel_id=1, source_target_pairs={{0,16},{4,20},{8,24},{12,28},{16,0},{20,4},{24,8},{28,12},{1,17},{... | collective-permute-start | bytes 786440 | tf_op jit(solution)/shard_map/ppermute | solution.py:29
  61.0 10.4 %collective-permute-start.24 = (bf16[128,512]{1,0:T(8,128)(2,1)S(1)}, bf16[128,512]{1,0:T(8,128)(2,1)S(1)}, u32[]{:S(2)}, u32[]{:S(2)}) collective-permute-start(bf16[128,512]{1,0:T(8,128)(2,1)S(1)} %fusion.16), channel_id=1, source_target_pairs={{0,3},{1,2},{2,1},{3,0},{4,7},{5,6},{6,5},{7,4},{8,11},{9,10},{10,... | collective-permute-start | bytes 393224 | tf_op jit(solution)/shard_map/ppermute | solution.py:17
  65.5 7.9 %collective-permute-start.25 = (bf16[128,512]{1,0:T(8,128)(2,1)S(1)}, bf16[128,512]{1,0:T(8,128)(2,1)S(1)}, u32[]{:S(2)}, u32[]{:S(2)}) collective-permute-start(bf16[128,512]{1,0:T(8,128)(2,1)S(1)} %fusion.17), channel_id=1, source_target_pairs={{0,2},{1,3},{2,0},{3,1},{4,6},{5,7},{6,4},{7,5},{8,10},{9,11},{10,... | collective-permute-start | bytes 393224 | tf_op jit(solution)/shard_map/ppermute | solution.py:17
  67.0 9.7 %collective-permute-start.26 = (bf16[128,512]{1,0:T(8,128)(2,1)S(1)}, bf16[128,512]{1,0:T(8,128)(2,1)S(1)}, u32[]{:S(2)}, u32[]{:S(2)}) collective-permute-start(bf16[128,512]{1,0:T(8,128)(2,1)S(1)} %fusion.18), channel_id=1, source_target_pairs={{0,1},{1,0},{2,3},{3,2},{4,5},{5,4},{6,7},{7,6},{8,9},{9,8},{10,11... | collective-permute-start | bytes 393224 | tf_op jit(solution)/shard_map/ppermute | solution.py:17
  77.5 7.7 %collective-permute-start.27 = (bf16[1,128,512]{2,1,0:T(8,128)(2,1)S(1)}, bf16[1,128,512]{2,1,0:T(8,128)(2,1)S(1)}, u32[]{:S(2)}, u32[]{:S(2)}) collective-permute-start(bf16[1,128,512]{2,1,0:T(8,128)(2,1)S(1)} %bitcast.111), channel_id=1, source_target_pairs={{0,16},{4,20},{8,24},{12,28},{16,0},{20,4},{24,8},{28,12},{1,17},{... | collective-permute-start | bytes 393224 | tf_op jit(solution)/shard_map/ppermute | solution.py:36
  77.5 8.2 %collective-permute-start.29 = (bf16[128,512]{1,0:T(8,128)(2,1)S(1)}, bf16[128,512]{1,0:T(8,128)(2,1)S(1)}, u32[]{:S(2)}, u32[]{:S(2)}) collective-permute-start(bf16[128,512]{1,0:T(8,128)(2,1)S(1)} %get-tuple-element.133), channel_id=1, source_target_pairs={{0,1},{1,0},{2,3},{3,2},{4,5},{5,4},{6,7},{7,6},{8,9},{9,8},{10,11... | collective-permute-start | bytes 393224 | tf_op jit(solution)/shard_map/ppermute | solution.py:17
  77.6 10.4 %collective-permute-start.31 = (bf16[128,512]{1,0:T(8,128)(2,1)S(1)}, bf16[128,512]{1,0:T(8,128)(2,1)S(1)}, u32[]{:S(2)}, u32[]{:S(2)}) collective-permute-start(bf16[128,512]{1,0:T(8,128)(2,1)S(1)} %get-tuple-element.133), channel_id=1, source_target_pairs={{0,2},{1,3},{2,0},{3,1},{4,6},{5,7},{6,4},{7,5},{8,10},{9,11},{10,... | collective-permute-start | bytes 393224 | tf_op jit(solution)/shard_map/ppermute | solution.py:17
  83.7 6.9 %collective-permute-start.32 = (bf16[128,512]{1,0:T(8,128)(2,1)S(1)}, bf16[128,512]{1,0:T(8,128)(2,1)S(1)}, u32[]{:S(2)}, u32[]{:S(2)}) collective-permute-start(bf16[128,512]{1,0:T(8,128)(2,1)S(1)} %get-tuple-element.133), channel_id=1, source_target_pairs={{0,3},{1,2},{2,1},{3,0},{4,7},{5,6},{6,5},{7,4},{8,11},{9,10},{10,... | collective-permute-start | bytes 393224 | tf_op jit(solution)/shard_map/ppermute | solution.py:17
  83.7 8.6 %collective-permute-start.37 = (bf16[1,128,512]{2,1,0:T(8,128)(2,1)S(1)}, bf16[1,128,512]{2,1,0:T(8,128)(2,1)S(1)}, u32[]{:S(2)}, u32[]{:S(2)}) collective-permute-start(bf16[1,128,512]{2,1,0:T(8,128)(2,1)S(1)} %bitcast.112), channel_id=1, source_target_pairs={{0,8},{4,12},{8,0},{12,4},{16,24},{20,28},{24,16},{28,20},{1,9},{5... | collective-permute-start | bytes 393224 | tf_op jit(solution)/shard_map/ppermute | solution.py:23
  85.3 7.2 %collective-permute-start.28 = (bf16[1,128,512]{2,1,0:T(8,128)(2,1)S(1)}, bf16[1,128,512]{2,1,0:T(8,128)(2,1)S(1)}, u32[]{:S(2)}, u32[]{:S(2)}) collective-permute-start(bf16[1,128,512]{2,1,0:T(8,128)(2,1)S(1)} %collective-permute-done.27.refs_0_), channel_id=1, source_target_pairs={{0,8},{4,12},{8,0},{12,4},{16,24},{20,28},{24,16},{28,20},{1,9},{5... | collective-permute-start | bytes 393224 | tf_op jit(solution)/shard_map/ppermute | solution.py:23
  85.7 7.9 %collective-permute-start.30 = (bf16[1,128,512]{2,1,0:T(8,128)(2,1)S(1)}, bf16[1,128,512]{2,1,0:T(8,128)(2,1)S(1)}, u32[]{:S(2)}, u32[]{:S(2)}) collective-permute-start(bf16[1,128,512]{2,1,0:T(8,128)(2,1)S(1)} %bitcast.115), channel_id=1, source_target_pairs={{0,16},{4,20},{8,24},{12,28},{16,0},{20,4},{24,8},{28,12},{1,17},{... | collective-permute-start | bytes 393224 | tf_op jit(solution)/shard_map/ppermute | solution.py:36
  90.6 3.8 %collective-permute-start.40 = (bf16[2,128,512]{2,1,0:T(8,128)(2,1)S(1)}, bf16[2,128,512]{2,1,0:T(8,128)(2,1)S(1)}, u32[]{:S(2)}, u32[]{:S(2)}) collective-permute-start(bf16[2,128,512]{2,1,0:T(8,128)(2,1)S(1)} %pad_maximum_fusion.2.refs_2_), channel_id=1, source_target_pairs={{0,4},{4,0},{8,12},{12,8},{16,20},{20,16},{24,28},{28,24},{1,5},{5... | collective-permute-start | bytes 786440 | tf_op jit(solution)/shard_map/ppermute | solution.py:23
  90.7 9.2 %collective-permute-start.42 = (bf16[2,128,512]{2,1,0:T(8,128)(2,1)S(1)}, bf16[2,128,512]{2,1,0:T(8,128)(2,1)S(1)}, u32[]{:S(2)}, u32[]{:S(2)}) collective-permute-start(bf16[2,128,512]{2,1,0:T(8,128)(2,1)S(1)} %pad_maximum_fusion.2.refs_2_), channel_id=1, source_target_pairs={{0,8},{4,12},{8,0},{12,4},{16,24},{20,28},{24,16},{28,20},{1,9},{5... | collective-permute-start | bytes 786440 | tf_op jit(solution)/shard_map/ppermute | solution.py:23
  92.3 1.4 %collective-permute-start.39 = (bf16[1,128,512]{2,1,0:T(8,128)(2,1)S(1)}, bf16[1,128,512]{2,1,0:T(8,128)(2,1)S(1)}, u32[]{:S(2)}, u32[]{:S(2)}) collective-permute-start(bf16[1,128,512]{2,1,0:T(8,128)(2,1)S(1)} %bitcast.116), channel_id=1, source_target_pairs={{0,4},{4,0},{8,12},{12,8},{16,20},{20,16},{24,28},{28,24},{1,5},{5... | collective-permute-start | bytes 393224 | tf_op jit(solution)/shard_map/ppermute | solution.py:23
  92.5 10.2 %collective-permute-start.33 = (bf16[2,128,512]{2,1,0:T(8,128)(2,1)S(1)}, bf16[2,128,512]{2,1,0:T(8,128)(2,1)S(1)}, u32[]{:S(2)}, u32[]{:S(2)}) collective-permute-start(bf16[2,128,512]{2,1,0:T(8,128)(2,1)S(1)} %pad_maximum_fusion.2.refs_2_), channel_id=1, source_target_pairs={{0,16},{4,20},{8,24},{12,28},{16,0},{20,4},{24,8},{28,12},{1,17},{... | collective-permute-start | bytes 786440 | tf_op jit(solution)/shard_map/ppermute | solution.py:36
  93.6 1.3 %collective-permute-start.38 = (bf16[1,128,512]{2,1,0:T(8,128)(2,1)S(1)}, bf16[1,128,512]{2,1,0:T(8,128)(2,1)S(1)}, u32[]{:S(2)}, u32[]{:S(2)}) collective-permute-start(bf16[1,128,512]{2,1,0:T(8,128)(2,1)S(1)} %bitcast.113), channel_id=1, source_target_pairs={{0,4},{4,0},{8,12},{12,8},{16,20},{20,16},{24,28},{28,24},{1,5},{5... | collective-permute-start | bytes 393224 | tf_op jit(solution)/shard_map/ppermute | solution.py:23
  93.6 8.5 %collective-permute-start.41 = (bf16[1,128,512]{2,1,0:T(8,128)(2,1)S(1)}, bf16[1,128,512]{2,1,0:T(8,128)(2,1)S(1)}, u32[]{:S(2)}, u32[]{:S(2)}) collective-permute-start(bf16[1,128,512]{2,1,0:T(8,128)(2,1)S(1)} %bitcast.117), channel_id=1, source_target_pairs={{0,8},{4,12},{8,0},{12,4},{16,24},{20,28},{24,16},{28,20},{1,9},{5... | collective-permute-start | bytes 393224 | tf_op jit(solution)/shard_map/ppermute | solution.py:23
  99.8 4.7 %collective-permute-start.45 = (bf16[2,128,512]{2,1,0:T(8,128)(2,1)S(1)}, bf16[2,128,512]{2,1,0:T(8,128)(2,1)S(1)}, u32[]{:S(2)}, u32[]{:S(2)}) collective-permute-start(bf16[2,128,512]{2,1,0:T(8,128)(2,1)S(1)} %collective-permute-done.42.refs_2_), channel_id=1, source_target_pairs={{0,4},{4,0},{8,12},{12,8},{16,20},{20,16},{24,28},{28,24},{1,5},{5... | collective-permute-start | bytes 786440 | tf_op jit(solution)/shard_map/ppermute | solution.py:23
  102.2 1.9 %collective-permute-start.44 = (bf16[1,128,512]{2,1,0:T(8,128)(2,1)S(1)}, bf16[1,128,512]{2,1,0:T(8,128)(2,1)S(1)}, u32[]{:S(2)}, u32[]{:S(2)}) collective-permute-start(bf16[1,128,512]{2,1,0:T(8,128)(2,1)S(1)} %collective-permute-done.41.refs_1_), channel_id=1, source_target_pairs={{0,4},{4,0},{8,12},{12,8},{16,20},{20,16},{24,28},{28,24},{1,5},{5... | collective-permute-start | bytes 393224 | tf_op jit(solution)/shard_map/ppermute | solution.py:23
  102.2 2.1 %collective-permute-start.43 = (bf16[1,128,512]{2,1,0:T(8,128)(2,1)S(1)}, bf16[1,128,512]{2,1,0:T(8,128)(2,1)S(1)}, u32[]{:S(2)}, u32[]{:S(2)}) collective-permute-start(bf16[1,128,512]{2,1,0:T(8,128)(2,1)S(1)} %collective-permute-done.37.refs_0_), channel_id=1, source_target_pairs={{0,4},{4,0},{8,12},{12,8},{16,20},{20,16},{24,28},{28,24},{1,5},{5... | collective-permute-start | bytes 393224 | tf_op jit(solution)/shard_map/ppermute | solution.py:23
  102.7 7.0 %collective-permute-start.36 = (bf16[2,128,512]{2,1,0:T(8,128)(2,1)S(1)}, bf16[2,128,512]{2,1,0:T(8,128)(2,1)S(1)}, u32[]{:S(2)}, u32[]{:S(2)}) collective-permute-start(bf16[2,128,512]{2,1,0:T(8,128)(2,1)S(1)} %collective-permute-done.33.refs_2_), channel_id=1, source_target_pairs={{0,4},{4,0},{8,12},{12,8},{16,20},{20,16},{24,28},{28,24},{1,5},{5... | collective-permute-start | bytes 786440 | tf_op jit(solution)/shard_map/ppermute | solution.py:23
  102.7 10.3 %collective-permute-start.47 = (bf16[2,128,512]{2,1,0:T(8,128)(2,1)S(1)}, bf16[2,128,512]{2,1,0:T(8,128)(2,1)S(1)}, u32[]{:S(2)}, u32[]{:S(2)}) collective-permute-start(bf16[2,128,512]{2,1,0:T(8,128)(2,1)S(1)} %collective-permute-done.42.refs_2_), channel_id=1, source_target_pairs={{0,16},{4,20},{8,24},{12,28},{16,0},{20,4},{24,8},{28,12},{1,17},{... | collective-permute-start | bytes 786440 | tf_op jit(solution)/shard_map/ppermute | solution.py:36
  104.0 5.6 %collective-permute-start.34 = (bf16[1,128,512]{2,1,0:T(8,128)(2,1)S(1)}, bf16[1,128,512]{2,1,0:T(8,128)(2,1)S(1)}, u32[]{:S(2)}, u32[]{:S(2)}) collective-permute-start(bf16[1,128,512]{2,1,0:T(8,128)(2,1)S(1)} %collective-permute-done.27.refs_0_), channel_id=1, source_target_pairs={{0,4},{4,0},{8,12},{12,8},{16,20},{20,16},{24,28},{28,24},{1,5},{5... | collective-permute-start | bytes 393224 | tf_op jit(solution)/shard_map/ppermute | solution.py:23
  104.3 5.4 %collective-permute-start.35 = (bf16[1,128,512]{2,1,0:T(8,128)(2,1)S(1)}, bf16[1,128,512]{2,1,0:T(8,128)(2,1)S(1)}, u32[]{:S(2)}, u32[]{:S(2)}) collective-permute-start(bf16[1,128,512]{2,1,0:T(8,128)(2,1)S(1)} %collective-permute-done.30.refs_1_), channel_id=1, source_target_pairs={{0,4},{4,0},{8,12},{12,8},{16,20},{20,16},{24,28},{28,24},{1,5},{5... | collective-permute-start | bytes 393224 | tf_op jit(solution)/shard_map/ppermute | solution.py:23
  104.6 8.5 %collective-permute-start.46 = (bf16[1,128,512]{2,1,0:T(8,128)(2,1)S(1)}, bf16[1,128,512]{2,1,0:T(8,128)(2,1)S(1)}, u32[]{:S(2)}, u32[]{:S(2)}) collective-permute-start(bf16[1,128,512]{2,1,0:T(8,128)(2,1)S(1)} %collective-permute-done.30.refs_1_), channel_id=1, source_target_pairs={{0,8},{4,12},{8,0},{12,4},{16,24},{20,28},{24,16},{28,20},{1,9},{5... | collective-permute-start | bytes 393224 | tf_op jit(solution)/shard_map/ppermute | solution.py:23
  113.0 2.0 %collective-permute-start.50 = (bf16[2,128,512]{2,1,0:T(8,128)(2,1)S(1)}, bf16[2,128,512]{2,1,0:T(8,128)(2,1)S(1)}, u32[]{:S(2)}, u32[]{:S(2)}) collective-permute-start(bf16[2,128,512]{2,1,0:T(8,128)(2,1)S(1)} %collective-permute-done.47.refs_2_), channel_id=1, source_target_pairs={{0,4},{4,0},{8,12},{12,8},{16,20},{20,16},{24,28},{28,24},{1,5},{5... | collective-permute-start | bytes 786440 | tf_op jit(solution)/shard_map/ppermute | solution.py:23
  113.1 1.7 %collective-permute-start.49 = (bf16[1,128,512]{2,1,0:T(8,128)(2,1)S(1)}, bf16[1,128,512]{2,1,0:T(8,128)(2,1)S(1)}, u32[]{:S(2)}, u32[]{:S(2)}) collective-permute-start(bf16[1,128,512]{2,1,0:T(8,128)(2,1)S(1)} %collective-permute-done.46.refs_1_), channel_id=1, source_target_pairs={{0,4},{4,0},{8,12},{12,8},{16,20},{20,16},{24,28},{28,24},{1,5},{5... | collective-permute-start | bytes 393224 | tf_op jit(solution)/shard_map/ppermute | solution.py:23
  113.6 1.4 %collective-permute-start.48 = (bf16[1,128,512]{2,1,0:T(8,128)(2,1)S(1)}, bf16[1,128,512]{2,1,0:T(8,128)(2,1)S(1)}, u32[]{:S(2)}, u32[]{:S(2)}) collective-permute-start(bf16[1,128,512]{2,1,0:T(8,128)(2,1)S(1)} %collective-permute-done.28.refs_0_), channel_id=1, source_target_pairs={{0,4},{4,0},{8,12},{12,8},{16,20},{20,16},{24,28},{28,24},{1,5},{5... | collective-permute-start | bytes 393224 | tf_op jit(solution)/shard_map/ppermute | solution.py:23

commit v6 on v4

--- a/solution.py
+++ b/solution.py
@@ -40,10 +40,11 @@
     return lax.optimization_barrier((value, *others))[0]
 
 
-def all_over_feat(value):
-    blocks = [value, over_feat(value, 1)]
-    for s in range(2, lax.axis_size("feat")):
-        blocks.append(over_feat(value, s))
+def all_over_feat(value, turn=0):
+    count = lax.axis_size("feat")
+    blocks = [value] + [None] * (count - 1)
+    for s in (range(1, count) if turn == 0 else reversed(range(1, count))):
+        blocks[s] = over_feat(value, s)
     return blocks
 
 
@@ -352,8 +353,7 @@
     rows, cols = tokens_in.shape
     tok = feat_count * rows
     bit_count = sub_count.bit_length() - 1
-    groups = [list(range(feat_count // 2))]
-    groups += [[s] for s in range(feat_count // 2, feat_count)]
+    groups = [list(range(feat_count // 2)), list(range(feat_count // 2, feat_count))]
 
     info = jnp.stack([position % sub_count, layers - 1 - layer]).astype(jnp.int32)
     real = [layer >= k for k in range(layers)]
@@ -363,7 +363,7 @@
 
     order = [rel for pair in range(0, sub_count, 2) for rel in (pair, pair ^ 1)]
     held = {rel: [None] * feat_count for rel in order[::2]}
-    held[0] = all_over_feat(tokens_in)
+    held[0] = all_over_feat(tokens_in, 0)
     enc_held, dec_held = fetch(enc_weight, after(dec_weight, held[0][1]))
     for s in range(feat_count):
         known = [0]
@@ -390,7 +390,7 @@
         sent, kept = decode(info, source, dec_held, k, groups, rows, cols)
         for place in reversed(range(len(groups))):
             current[place, k] = add_pair(kept[place], over_members(sent[place], 0))
-        source = after(features, current[len(groups) - 1, k])
+        source = after(features, kept[-1])
     turns = sorted(current, reverse=True)
     joined = {}
     for bit_level in range(1, bit_count):
@@ -401,7 +401,8 @@
         if bit_level == bit_count - 1:
             for k in range(1, layers):
                 joined[k], sent = halves.pop((0, k))
-                sent = to_layer(after(sent, halves[len(groups) - 1, 0][1]), k, sub_count, real)
+                sent = to_layer(sent, k, sub_count, real)
+                ahead = sent
                 halves[0, 0] = (halves[0, 0][0], add_pair(halves[0, 0][1], sent))
         turns = [turn for turn in turns if turn in halves]
         received, operands = [], []
@@ -422,9 +423,11 @@
         total = sum(part.astype(jnp.float32) for part in current[place, 0])
         for k in range(1, layers):
             if place > 0:
-                moved = to_layer(add_pair(*current[place, k]), k, sub_count, real)
+                value = add_pair(*current[place, k])
+                value = after(value, ahead) if place == 1 else value
+                moved = to_layer(value, k, sub_count, real)
             else:
-                moved = to_layer(after(joined[k], *operands), k, sub_count, real)
+                moved = to_layer(after(joined[k], *operands[:1]), k, sub_count, real)
             total = total + moved.astype(jnp.float32)
         for spot, block in enumerate(groups[place]):
             if block == 0:
@@ -441,7 +444,7 @@
     recon_error = rebuilt - after(targets, turned_features, *turned_tokens).astype(jnp.float32)
     scaled = (loss_scale / tok * recon_error).astype(jnp.bfloat16)
 
-    blocks = all_over_feat(scaled)
+    blocks = all_over_feat(scaled, 0)
     stages = [[0]]
     for level in range(bit_count - 1, 0, -1):
         known = [rel for stage in stages for rel in stage]
@@ -452,6 +455,8 @@
     early, last = [], len(spans) - 1
     for place, group in enumerate(spans):
         stacked = jnp.stack([blocks[s] for s in group], 0)
+        if place == last:
+            stacked = after(stacked, groups_of[2, 0][1])
         groups_of[0, 0][place] = stacked
         for k in range(1, layers):
             groups_of[0, k][place] = from_layer(stacked, k, sub_count)
@@ -475,9 +480,12 @@
         for rel in [rel for stage in stages for rel in stage]:
             parts = groups_of[rel, k]
             if feature_grad is None:
-                parts = [after(parts[0], *early)] + parts[1:]
-            elif rel > 0:
+                parts = [after(parts[0], groups_of[2, 0][0], groups_of[0, 1][0], groups_of[2, 0][1], groups_of[0, 1][1])] + parts[1:]
+            elif (rel > 0 and k == 0) or (rel == 0 and k > 0):
                 parts = [after(part, feature_grad) for part in parts]
+            if feature_grad is not None:
+                if rel > 0 and k == 0:
+                    feature_grad = after(feature_grad, groups_of[0, layers - 1][-1])
             feature_grad, dec_grad, squares[k, rel] = backward_pair(
                 info,
                 rel,

time: 118 us -> 117 us (level)
  starting transfers between devices: 46.5 us -> 41.6 us
  waiting for transfers between devices: 34 us -> 37.7 us
    ppermute x4, waiting for transfers between devices: 0.01 us -> 6.44 us  [from_layer(): return lax.ppermute(value, 'layer', pairs)]
    ppermute x4 -> x3, waiting for transfers between devices: 5.68 us -> 2.82 us  [to_layer(): moved = lax.ppermute(value, 'layer', pairs)]
    ppermute x4, starting transfers between devices: 5.01 us -> 2.46 us  [from_layer(): return lax.ppermute(value, 'layer', pairs)]
    ppermute x34 -> x30, starting transfers between devices: 18.2 us -> 16.2 us  [over_members(): return lax.ppermute(value, 'layer', pairs)]
    ppermute x9, waiting for transfers between devices: 12.2 us -> 14.1 us  [over_feat(): return lax.ppermute(value, 'feat', pairs)]
    ppermute x34 -> x30, waiting for transfers between devices: 16.1 us -> 14.3 us  [over_members(): return lax.ppermute(value, 'layer', pairs)]
    ppermute x4 -> x3, starting transfers between devices: 5.33 us -> 4.76 us  [to_layer(): moved = lax.ppermute(value, 'layer', pairs)]
  transfers between devices with their start and end apart: 51 -> 46, of which waited for: 19 -> 21; matrix products, arithmetic and copies ran while one was open for 1% -> 1% of each run, Pallas kernels for 19% -> 19%
where the time goes in v6:
time: 117 us
  starting transfers between devices  41.6 us (36%)
  waiting for transfers between devices  37.7 us (32%)
  Pallas kernels  34.4 us (29%)
  other arithmetic  1.96 us (2%)
    ppermute x9, starting transfers between devices, over_feat(): return lax.ppermute(value, 'feat', pairs)  18.1 us
    ppermute x30, starting transfers between devices, over_members(): return lax.ppermute(value, 'layer', pairs)  16.2 us
    ppermute x30, waiting for transfers between devices, over_members(): return lax.ppermute(value, 'layer', pairs)  14.3 us
    ppermute x9, waiting for transfers between devices, over_feat(): return lax.ppermute(value, 'feat', pairs)  14.1 us
    pallas_call x4, Pallas kernels, backward_pair(): pl.pallas_call(kernel, in_specs=[in_smem] + [in_vmem] * (len(inputs) + 2)...  13.6 us
    ppermute x4, waiting for transfers between devices, from_layer(): return lax.ppermute(value, 'layer', pairs)  6.44 us
    pallas_call x2, Pallas kernels, decode(): pl.pallas_call(kernel, in_specs=[in_smem, in_vmem, in_vmem], out_specs=[i...  5.79 us
    ppermute x3, starting transfers between devices, to_layer(): moved = lax.ppermute(value, 'layer', pairs)  4.76 us
  transfers between devices with their start and end apart: 46, of which 21 were waited for; matrix products, arithmetic and copies ran while one was open for 1% of the time, Pallas kernels for 19%

profile of v6, /device:TPU:0, one launch (start us, length us, event | category | flops | bytes accessed | tf_op | source)
XLA Modules:
  0.0 116.9 jit_solution(2611986515408899640)
XLA Ops:
  0.7 3.0 %collective-permute-start.1 = (bf16[128,512]{1,0:T(8,128)(2,1)}, bf16[128,512]{1,0:T(8,128)(2,1)S(1)}, u32[]{:S(2)}, u32[]{:S(2)}) collective-permute-start(bf16[128,512]{1,0:T(8,128)(2,1)} %param.5), channel_id=1, source_target_pairs={{0,1},{1,0},{2,3},{3,2},{4,5},{5,4},{6,7},{7,6},{8,9},{9,8},{10,11... | collective-permute-start | bytes 393224 | tf_op jit(solution)/shard_map/ppermute | solution.py:17
  3.8 2.5 %collective-permute-start.3 = (bf16[128,512]{1,0:T(8,128)(2,1)}, bf16[128,512]{1,0:T(8,128)(2,1)S(1)}, u32[]{:S(2)}, u32[]{:S(2)}) collective-permute-start(bf16[128,512]{1,0:T(8,128)(2,1)} %param.5), channel_id=1, source_target_pairs={{0,3},{1,2},{2,1},{3,0},{4,7},{5,6},{6,5},{7,4},{8,11},{9,10},{10,... | collective-permute-start | bytes 393224 | tf_op jit(solution)/shard_map/ppermute | solution.py:17
  6.4 1.5 %collective-permute-start = (bf16[128,512]{1,0:T(8,128)(2,1)}, bf16[128,512]{1,0:T(8,128)(2,1)S(1)}, u32[]{:S(2)}, u32[]{:S(2)}) collective-permute-start(bf16[128,512]{1,0:T(8,128)(2,1)} %param.5), channel_id=1, source_target_pairs={{0,8},{4,12},{8,0},{12,4},{16,24},{20,28},{24,16},{28,20},{1,9},{5... | collective-permute-start | bytes 393224 | tf_op jit(solution)/shard_map/ppermute | solution.py:23
  7.9 4.7 %fetch.1 = (bf16[2048,1024]{1,0:T(8,128)(2,1)S(1)}, bf16[2,1024,2048]{2,1,0:T(8,128)(2,1)S(1)}) custom-call(bf16[2048,1024]{1,0:T(8,128)(2,1)} %refs_0_.1, bf16[2,1024,2048]{2,1,0:T(8,128)(2,1)} %refs_1_), custom_call_target="tpu_custom_call" | custom-call | bytes 12582912 | tf_op jit(solution)/shard_map/fetch/pallas_call | solution.py:88
  12.6 1.1 collective-permute-done.3
  13.7 1.5 %collective-permute-start.5 = (bf16[128,512]{1,0:T(8,128)(2,1)S(1)}, bf16[128,512]{1,0:T(8,128)(2,1)S(1)}, u32[]{:S(2)}, u32[]{:S(2)}) collective-permute-start(bf16[128,512]{1,0:T(8,128)(2,1)S(1)} %collective-permute-done.3), channel_id=1, source_target_pairs={{0,8},{4,12},{8,0},{12,4},{16,24},{20,28},{24,16},{28,20},{1,9},{5... | collective-permute-start | bytes 393224 | tf_op jit(solution)/shard_map/ppermute | solution.py:23
  15.2 0.5 collective-permute-start.4
  15.8 2.5 %collective-permute-done.2 = bf16[128,512]{1,0:T(8,128)(2,1)S(1)} collective-permute-done((bf16[128,512]{1,0:T(8,128)(2,1)}, bf16[128,512]{1,0:T(8,128)(2,1)S(1)}, u32[]{:S(2)}, u32[]{:S(2)}) %collective-permute-start.2) | collective-permute-done | bytes 131104 | tf_op jit(solution)/shard_map/ppermute | solution.py:17
  18.3 0.4 collective-permute-done.5
  18.7 1.5 %collective-permute-done.4 = bf16[128,512]{1,0:T(8,128)(2,1)S(1)} collective-permute-done((bf16[128,512]{1,0:T(8,128)(2,1)S(1)}, bf16[128,512]{1,0:T(8,128)(2,1)S(1)}, u32[]{:S(2)}, u32[]{:S(2)}) %collective-permute-start.4) | collective-permute-done | bytes 131104 | tf_op jit(solution)/shard_map/ppermute | solution.py:23
  20.2 1.4 %collective-permute-start.7 = (bf16[128,512]{1,0:T(8,128)(2,1)S(1)}, bf16[128,512]{1,0:T(8,128)(2,1)S(1)}, u32[]{:S(2)}, u32[]{:S(2)}) collective-permute-start(bf16[128,512]{1,0:T(8,128)(2,1)S(1)} %collective-permute-done.2), channel_id=1, source_target_pairs={{0,8},{4,12},{8,0},{12,4},{16,24},{20,28},{24,16},{28,20},{1,9},{5... | collective-permute-start | bytes 393224 | tf_op jit(solution)/shard_map/ppermute | solution.py:23
  21.6 0.5 collective-permute-done.6.refs_1_
  22.1 1.8 %encode.3.refs_2_ = f32[512,1024]{1,0:T(8,128)S(1)} custom-call(s32[2]{0:T(128)S(1)} %pad_add_fusion.info_ref, bf16[4,128,512]{2,1,0:T(8,128)(2,1)S(1)} %pad_maximum_fusion.refs_0_, bf16[4,128,512]{2,1,0:T(8,128)(2,1)S(1)} %collective-permute-done.6.refs_1_, bf16[2048,1024]{1,0:T(8,128)(2,1)S(1)} %get-tuple-element.65.refs_2_.refs_1_), custom_call_target="tpu_custom_call" | custom-call | flops 1073741824 | bytes 3145728 | tf_op jit(solution)/shard_map/encode/pallas_call | solution.py:128
  23.9 2.2 %collective-permute-done.7 = bf16[128,512]{1,0:T(8,128)(2,1)S(1)} collective-permute-done((bf16[128,512]{1,0:T(8,128)(2,1)S(1)}, bf16[128,512]{1,0:T(8,128)(2,1)S(1)}, u32[]{:S(2)}, u32[]{:S(2)}) %collective-permute-start.7) | collective-permute-done | bytes 131104 | tf_op jit(solution)/shard_map/ppermute | solution.py:23
  26.3 1.3 %encode.4.refs_2_ = f32[512,1024]{1,0:T(8,128)S(1)} custom-call(s32[2]{0:T(128)S(1)} %pad_add_fusion.info_ref, bf16[4,128,512]{2,1,0:T(8,128)(2,1)S(1)} %pad_maximum_fusion.1.refs_0_, bf16[2048,1024]{1,0:T(8,128)(2,1)S(1)} %get-tuple-element.65.refs_2_.refs_1_, f32[512,1024]{1,0:T(8,128)S(1)} %encode.3.refs_2_), custom_call_target="tpu_custom_call" | custom-call | flops 536870912 | bytes 1572864 | tf_op jit(solution)/shard_map/encode/pallas_call | solution.py:128
  27.5 0.6 collective-permute-done.8.refs_0_
  28.2 1.4 %encode.5.feat_ref.in_ref.refs_4_ = bf16[2,512,1024]{2,1,0:T(8,128)(2,1)S(1)} custom-call(s32[2]{0:T(128)S(1)} %pad_add_fusion.info_ref, bf16[4,128,512]{2,1,0:T(8,128)(2,1)S(1)} %collective-permute-done.8.refs_0_, bf16[2048,1024]{1,0:T(8,128)(2,1)S(1)} %get-tuple-element.65.refs_2_.refs_1_, f32[512,1024]{1,0:T(8,128)S(1)} %encode.4.refs_2_, ...), custom_call_target="tpu_custom_call" | custom-call | flops 536870912 | bytes 1572864 | tf_op jit(solution)/shard_map/encode/pallas_call | solution.py:128
  29.6 2.9 %decode.2 = (bf16[2,2,128,512]{3,2,1,0:T(8,128)(2,1)S(1)}, bf16[2,2,128,512]{3,2,1,0:T(8,128)(2,1)S(1)}, bf16[2,2,128,512]{3,2,1,0:T(8,128)(2,1)S(1)}, bf16[2,2,128,512]{3,2,1,0:T(8,128)(2,1)S(1)}) custom-call(s32[2]{0:T(128)S(1)} %pad_add_fusion.info_ref, bf16[2,512,1024]{2,1,0:T(8,128)(2,1)S(1)} %encode.5.feat_ref.in_ref.refs_4_, ...), custom_call_target="tpu_custom_call" | custom-call | flops 2147483648 | bytes 4194304 | tf_op jit(solution)/shard_map/decode/pallas_call | solution.py:166
  32.7 0.4 collective-permute-start.10
  33.1 2.9 %decode.3 = (bf16[2,2,128,512]{3,2,1,0:T(8,128)(2,1)S(1)}, bf16[2,2,128,512]{3,2,1,0:T(8,128)(2,1)S(1)}, bf16[2,2,128,512]{3,2,1,0:T(8,128)(2,1)S(1)}, bf16[2,2,128,512]{3,2,1,0:T(8,128)(2,1)S(1)}) custom-call(s32[2]{0:T(128)S(1)} %pad_add_fusion.info_ref, bf16[2,512,1024]{2,1,0:T(8,128)(2,1)S(1)} %encode.5.feat_ref.in_ref.refs_4_, ...), custom_call_target="tpu_custom_call" | custom-call | flops 2147483648 | bytes 4194304 | tf_op jit(solution)/shard_map/decode/pallas_call | solution.py:166
  36.2 0.4 collective-permute-start.9
  36.7 1.5 %collective-permute-start.13 = (bf16[1,2,128,512]{3,2,1,0:T(8,128)(2,1)S(1)}, bf16[1,2,128,512]{3,2,1,0:T(8,128)(2,1)S(1)}, u32[]{:S(2)}, u32[]{:S(2)}) collective-permute-start(bf16[1,2,128,512]{3,2,1,0:T(8,128)(2,1)S(1)} %slice_bitcast_fusion.5), channel_id=1, source_target_pairs={{0,8},{4,12},{8,0},{12,4},{16,24},{20,28},{24,16},{28,20},{1,9},{5... | collective-permute-start | bytes 786440 | tf_op jit(solution)/shard_map/ppermute | solution.py:23
  38.4 1.6 %collective-permute-start.11 = (bf16[1,2,128,512]{3,2,1,0:T(8,128)(2,1)S(1)}, bf16[1,2,128,512]{3,2,1,0:T(8,128)(2,1)S(1)}, u32[]{:S(2)}, u32[]{:S(2)}) collective-permute-start(bf16[1,2,128,512]{3,2,1,0:T(8,128)(2,1)S(1)} %get-tuple-element.124), channel_id=1, source_target_pairs={{0,16},{4,20},{8,24},{12,28},{16,0},{20,4},{24,8},{28,12},{1,17},{... | collective-permute-start | bytes 786440 | tf_op jit(solution)/shard_map/ppermute | solution.py:29
  40.1 0.7 collective-permute-start.16
  41.0 5.0 %collective-permute-done.13 = bf16[1,2,128,512]{3,2,1,0:T(8,128)(2,1)S(1)} collective-permute-done((bf16[1,2,128,512]{3,2,1,0:T(8,128)(2,1)S(1)}, bf16[1,2,128,512]{3,2,1,0:T(8,128)(2,1)S(1)}, u32[]{:S(2)}, u32[]{:S(2)}) %collective-permute-start.13) | collective-permute-done | bytes 262176 | tf_op jit(solution)/shard_map/ppermute | solution.py:23
  46.0 0.5 collective-permute-done.11
  46.6 1.6 %collective-permute-start.17 = (bf16[1,2,128,512]{3,2,1,0:T(8,128)(2,1)S(1)}, bf16[1,2,128,512]{3,2,1,0:T(8,128)(2,1)S(1)}, u32[]{:S(2)}, u32[]{:S(2)}) collective-permute-start(bf16[1,2,128,512]{3,2,1,0:T(8,128)(2,1)S(1)} %fusion.4), channel_id=1, source_target_pairs={{0,16},{4,20},{8,24},{12,28},{16,0},{20,4},{24,8},{28,12},{1,17},{... | collective-permute-start | bytes 786440 | tf_op jit(solution)/shard_map/ppermute | solution.py:29
  48.2 0.9 collective-permute-start.15
  49.1 2.5 %collective-permute-done.16 = bf16[1,2,128,512]{3,2,1,0:T(8,128)(2,1)S(1)} collective-permute-done((bf16[1,2,128,512]{3,2,1,0:T(8,128)(2,1)S(1)}, bf16[1,2,128,512]{3,2,1,0:T(8,128)(2,1)S(1)}, u32[]{:S(2)}, u32[]{:S(2)}) %collective-permute-start.16) | collective-permute-done | bytes 262176 | tf_op jit(solution)/shard_map/ppermute | solution.py:23
  51.5 2.3 %collective-permute-done.17 = bf16[1,2,128,512]{3,2,1,0:T(8,128)(2,1)S(1)} collective-permute-done((bf16[1,2,128,512]{3,2,1,0:T(8,128)(2,1)S(1)}, bf16[1,2,128,512]{3,2,1,0:T(8,128)(2,1)S(1)}, u32[]{:S(2)}, u32[]{:S(2)}) %collective-permute-start.17) | collective-permute-done | bytes 262176 | tf_op jit(solution)/shard_map/ppermute | solution.py:29
  54.0 1.6 %collective-permute-start.18 = (bf16[1,2,128,512]{3,2,1,0:T(8,128)(2,1)S(1)}, bf16[1,2,128,512]{3,2,1,0:T(8,128)(2,1)S(1)}, u32[]{:S(2)}, u32[]{:S(2)}) collective-permute-start(bf16[1,2,128,512]{3,2,1,0:T(8,128)(2,1)S(1)} %get-tuple-element.88), channel_id=1, source_target_pairs={{0,16},{4,20},{8,24},{12,28},{16,0},{20,4},{24,8},{28,12},{1,17},{... | collective-permute-start | bytes 786440 | tf_op jit(solution)/shard_map/ppermute | solution.py:29
  55.6 4.6 %collective-permute-start.20 = (bf16[128,512]{1,0:T(8,128)(2,1)S(1)}, bf16[128,512]{1,0:T(8,128)(2,1)S(1)}, u32[]{:S(2)}, u32[]{:S(2)}) collective-permute-start(bf16[128,512]{1,0:T(8,128)(2,1)S(1)} %get-tuple-element.126), channel_id=1, source_target_pairs={{0,2},{1,3},{2,0},{3,1},{4,6},{5,7},{6,4},{7,5},{8,10},{9,11},{10,... | collective-permute-start | bytes 393224 | tf_op jit(solution)/shard_map/ppermute | solution.py:17
  60.2 1.0 collective-permute-start.19
  61.3 2.5 %collective-permute-start.21 = (bf16[128,512]{1,0:T(8,128)(2,1)S(1)}, bf16[128,512]{1,0:T(8,128)(2,1)S(1)}, u32[]{:S(2)}, u32[]{:S(2)}) collective-permute-start(bf16[128,512]{1,0:T(8,128)(2,1)S(1)} %fusion.13), channel_id=1, source_target_pairs={{0,1},{1,0},{2,3},{3,2},{4,5},{5,4},{6,7},{7,6},{8,9},{9,8},{10,11... | collective-permute-start | bytes 393224 | tf_op jit(solution)/shard_map/ppermute | solution.py:17
  63.8 0.3 turned.5
  64.9 2.8 %collective-permute-done.19 = bf16[128,512]{1,0:T(8,128)(2,1)S(1)} collective-permute-done((bf16[128,512]{1,0:T(8,128)(2,1)S(1)}, bf16[128,512]{1,0:T(8,128)(2,1)S(1)}, u32[]{:S(2)}, u32[]{:S(2)}) %collective-permute-start.19) | collective-permute-done | bytes 131104 | tf_op jit(solution)/shard_map/ppermute | solution.py:17
  67.8 0.9 collective-permute-done.20
  68.6 0.5 collective-permute-done.21
  69.2 0.8 multiply_convert_fusion
  70.0 1.4 %collective-permute-start.24 = (bf16[128,512]{1,0:T(8,128)(2,1)S(1)}, bf16[128,512]{1,0:T(8,128)(2,1)S(1)}, u32[]{:S(2)}, u32[]{:S(2)}) collective-permute-start(bf16[128,512]{1,0:T(8,128)(2,1)S(1)} %get-tuple-element.119), channel_id=1, source_target_pairs={{0,1},{1,0},{2,3},{3,2},{4,5},{5,4},{6,7},{7,6},{8,9},{9,8},{10,11... | collective-permute-start | bytes 393224 | tf_op jit(solution)/shard_map/ppermute | solution.py:17
  71.4 1.5 %collective-permute-start.27 = (bf16[128,512]{1,0:T(8,128)(2,1)S(1)}, bf16[128,512]{1,0:T(8,128)(2,1)S(1)}, u32[]{:S(2)}, u32[]{:S(2)}) collective-permute-start(bf16[128,512]{1,0:T(8,128)(2,1)S(1)} %get-tuple-element.119), channel_id=1, source_target_pairs={{0,2},{1,3},{2,0},{3,1},{4,6},{5,7},{6,4},{7,5},{8,10},{9,11},{10,... | collective-permute-start | bytes 393224 | tf_op jit(solution)/shard_map/ppermute | solution.py:17
  72.9 1.4 %collective-permute-start.28 = (bf16[128,512]{1,0:T(8,128)(2,1)S(1)}, bf16[128,512]{1,0:T(8,128)(2,1)S(1)}, u32[]{:S(2)}, u32[]{:S(2)}) collective-permute-start(bf16[128,512]{1,0:T(8,128)(2,1)S(1)} %get-tuple-element.119), channel_id=1, source_target_pairs={{0,3},{1,2},{2,1},{3,0},{4,7},{5,6},{6,5},{7,4},{8,11},{9,10},{10,... | collective-permute-start | bytes 393224 | tf_op jit(solution)/shard_map/ppermute | solution.py:17
  74.3 1.6 %collective-permute-done.24 = bf16[128,512]{1,0:T(8,128)(2,1)S(1)} collective-permute-done((bf16[128,512]{1,0:T(8,128)(2,1)S(1)}, bf16[128,512]{1,0:T(8,128)(2,1)S(1)}, u32[]{:S(2)}, u32[]{:S(2)}) %collective-permute-start.24) | collective-permute-done | bytes 131104 | tf_op jit(solution)/shard_map/ppermute | solution.py:17
  76.0 0.5 collective-permute-start.22
  76.5 2.0 %collective-permute-start.35 = (bf16[1,128,512]{2,1,0:T(8,128)(2,1)S(1)}, bf16[1,128,512]{2,1,0:T(8,128)(2,1)S(1)}, u32[]{:S(2)}, u32[]{:S(2)}) collective-permute-start(bf16[1,128,512]{2,1,0:T(8,128)(2,1)S(1)} %bitcast.84), channel_id=1, source_target_pairs={{0,8},{4,12},{8,0},{12,4},{16,24},{20,28},{24,16},{28,20},{1,9},{5... | collective-permute-start | bytes 393224 | tf_op jit(solution)/shard_map/ppermute | solution.py:23
  78.5 4.7 %collective-permute-done.27 = bf16[128,512]{1,0:T(8,128)(2,1)S(1)} collective-permute-done((bf16[128,512]{1,0:T(8,128)(2,1)S(1)}, bf16[128,512]{1,0:T(8,128)(2,1)S(1)}, u32[]{:S(2)}, u32[]{:S(2)}) %collective-permute-start.27) | collective-permute-done | bytes 131104 | tf_op jit(solution)/shard_map/ppermute | solution.py:17
  83.2 0.5 collective-permute-start.25
  83.8 0.4 collective-permute-start.30
  84.4 3.8 %collective-permute-done.25.refs_1_ = bf16[1,128,512]{2,1,0:T(8,128)(2,1)S(1)} collective-permute-done((bf16[1,128,512]{2,1,0:T(8,128)(2,1)S(1)}, bf16[1,128,512]{2,1,0:T(8,128)(2,1)S(1)}, u32[]{:S(2)}, u32[]{:S(2)}) %collective-permute-start.25) | collective-permute-done | bytes 131104 | tf_op jit(solution)/shard_map/ppermute | solution.py:36
  88.2 0.5 collective-permute-start.42
  88.6 0.9 collective-permute-done.36.refs_3_
  89.5 3.3 %backward_pair.4 = (f32[512,1024]{1,0:T(8,128)S(1)}, bf16[2,1024,2048]{2,1,0:T(8,128)(2,1)}, f32[8,128]{1,0:T(8,128)S(1)}) custom-call(s32[2]{0:T(128)S(1)} %pad_add_fusion.info_ref, bf16[1,128,512]{2,1,0:T(8,128)(2,1)S(1)} %bitcast.86, bf16[1,128,512]{2,1,0:T(8,128)(2,1)S(1)} %bitcast.90, bf16[2,128,512]{2,1,0:T(8,128)(2,1)S(1)} %pad_maximum_fusion.2.refs_2_, ...), custom_call_target="tpu_custom_call" | custom-call | flops 262144 | bytes 262144 | tf_op jit(solution)/shard_map/backward_pair/pallas_call | solution.py:270
  93.1 1.0 collective-permute-start.31
  94.6 2.7 %collective-permute-done.42.refs_2_ = bf16[2,128,512]{2,1,0:T(8,128)(2,1)S(1)} collective-permute-done((bf16[2,128,512]{2,1,0:T(8,128)(2,1)S(1)}, bf16[2,128,512]{2,1,0:T(8,128)(2,1)S(1)}, u32[]{:S(2)}, u32[]{:S(2)}) %collective-permute-start.42) | collective-permute-done | bytes 262176 | tf_op jit(solution)/shard_map/ppermute | solution.py:36
  97.3 0.3 collective-permute-start.23
  97.6 1.7 %collective-permute-start.26 = (bf16[1,128,512]{2,1,0:T(8,128)(2,1)S(1)}, bf16[1,128,512]{2,1,0:T(8,128)(2,1)S(1)}, u32[]{:S(2)}, u32[]{:S(2)}) collective-permute-start(bf16[1,128,512]{2,1,0:T(8,128)(2,1)S(1)} %collective-permute-done.25.refs_1_), channel_id=1, source_target_pairs={{0,8},{4,12},{8,0},{12,4},{16,24},{20,28},{24,16},{28,20},{1,9},{5... | collective-permute-start | bytes 393224 | tf_op jit(solution)/shard_map/ppermute | solution.py:23
  99.3 3.7 %backward_pair.5 = (f32[512,1024]{1,0:T(8,128)S(1)}, bf16[2,1024,2048]{2,1,0:T(8,128)(2,1)}, f32[8,128]{1,0:T(8,128)S(1)}) custom-call(s32[2]{0:T(128)S(1)} %pad_add_fusion.info_ref, bf16[1,128,512]{2,1,0:T(8,128)(2,1)S(1)} %collective-permute-done.35.refs_0_, ...), custom_call_target="tpu_custom_call", output_to_operand_aliasing={{0}: (9, {}), {1}: (10, {})} | custom-call | flops 262144 | bytes 262144 | tf_op jit(solution)/shard_map/backward_pair/pallas_call | solution.py:270
  103.1 0.5 collective-permute-start.44
  103.7 0.4 collective-permute-start.43
  104.2 0.7 collective-permute-done.26.refs_1_
  104.9 0.5 collective-permute-start.33
  105.4 3.3 %backward_pair.6 = (f32[512,1024]{1,0:T(8,128)S(1)}, bf16[2,1024,2048]{2,1,0:T(8,128)(2,1)}, f32[8,128]{1,0:T(8,128)S(1)}) custom-call(s32[2]{0:T(128)S(1)} %pad_add_fusion.info_ref, bf16[1,128,512]{2,1,0:T(8,128)(2,1)S(1)} %collective-permute-done.22.refs_0_, ...), custom_call_target="tpu_custom_call", output_to_operand_aliasing={{0}: (9, {}), {1}: (10, {})} | custom-call | flops 262144 | bytes 262144 | tf_op jit(solution)/shard_map/backward_pair/pallas_call | solution.py:270
  108.7 3.3 %backward_pair.7 = (f32[512,1024]{1,0:T(8,128)S(1)}, bf16[2,1024,2048]{2,1,0:T(8,128)(2,1)}, f32[8,128]{1,0:T(8,128)S(1)}) custom-call(s32[2]{0:T(128)S(1)} %pad_add_fusion.info_ref, bf16[1,128,512]{2,1,0:T(8,128)(2,1)S(1)} %collective-permute-done.23.refs_0_, ...), custom_call_target="tpu_custom_call", output_to_operand_aliasing={{0}: (9, {}), {1}: (10, {})} | custom-call | flops 262144 | bytes 262144 | tf_op jit(solution)/shard_map/backward_pair/pallas_call | solution.py:270
  112.0 4.7 %encoder_grad.1 = (bf16[2048,1024]{1,0:T(8,128)(2,1)}, f32[1,1024]{1,0:T(1,128)}, f32[1,1]{1,0:T(1,128)}) custom-call(s32[2]{0:T(128)S(1)} %pad_add_fusion.info_ref, bf16[1,512,512]{2,1,0:T(8,128)(2,1)S(1)} %turned.6.refs_0_, bf16[1,512,512]{2,1,0:T(8,128)(2,1)S(1)} %turned.7.refs_1_, bf16[1,512,512]{2,1,0:T(8,128)(2,1)S(1)} %turned.8.refs_2_, ...), custom_call_target="tpu_custom_call" | custom-call | flops 2147483648 | bytes 9437184 | tf_op jit(solution)/shard_map/encoder_grad/pallas_call | solution.py:322
  (68 shorter events, 3.9 us)
Async XLA Ops:
  0.7 17.5 %copy-start.2 = (bf16[128,512]{1,0:T(8,128)(2,1)S(1)}, bf16[128,512]{1,0:T(8,128)(2,1)}, u32[]{:S(2)}) copy-start(bf16[128,512]{1,0:T(8,128)(2,1)} %param.5) | copy-start | bytes 393220
  0.7 7.1 %collective-permute-start.1 = (bf16[128,512]{1,0:T(8,128)(2,1)}, bf16[128,512]{1,0:T(8,128)(2,1)S(1)}, u32[]{:S(2)}, u32[]{:S(2)}) collective-permute-start(bf16[128,512]{1,0:T(8,128)(2,1)} %param.5), channel_id=1, source_target_pairs={{0,1},{1,0},{2,3},{3,2},{4,5},{5,4},{6,7},{7,6},{8,9},{9,8},{10,11... | collective-permute-start | bytes 393224 | tf_op jit(solution)/shard_map/ppermute | solution.py:17
  3.8 10.0 %collective-permute-start.3 = (bf16[128,512]{1,0:T(8,128)(2,1)}, bf16[128,512]{1,0:T(8,128)(2,1)S(1)}, u32[]{:S(2)}, u32[]{:S(2)}) collective-permute-start(bf16[128,512]{1,0:T(8,128)(2,1)} %param.5), channel_id=1, source_target_pairs={{0,3},{1,2},{2,1},{3,0},{4,7},{5,6},{6,5},{7,4},{8,11},{9,10},{10,... | collective-permute-start | bytes 393224 | tf_op jit(solution)/shard_map/ppermute | solution.py:17
  6.2 12.0 %collective-permute-start.2 = (bf16[128,512]{1,0:T(8,128)(2,1)}, bf16[128,512]{1,0:T(8,128)(2,1)S(1)}, u32[]{:S(2)}, u32[]{:S(2)}) collective-permute-start(bf16[128,512]{1,0:T(8,128)(2,1)} %param.5), channel_id=1, source_target_pairs={{0,2},{1,3},{2,0},{3,1},{4,6},{5,7},{6,4},{7,5},{8,10},{9,11},{10,... | collective-permute-start | bytes 393224 | tf_op jit(solution)/shard_map/ppermute | solution.py:17
  6.4 12.0 %collective-permute-start = (bf16[128,512]{1,0:T(8,128)(2,1)}, bf16[128,512]{1,0:T(8,128)(2,1)S(1)}, u32[]{:S(2)}, u32[]{:S(2)}) collective-permute-start(bf16[128,512]{1,0:T(8,128)(2,1)} %param.5), channel_id=1, source_target_pairs={{0,8},{4,12},{8,0},{12,4},{16,24},{20,28},{24,16},{28,20},{1,9},{5... | collective-permute-start | bytes 393224 | tf_op jit(solution)/shard_map/ppermute | solution.py:23
  13.7 5.0 %collective-permute-start.5 = (bf16[128,512]{1,0:T(8,128)(2,1)S(1)}, bf16[128,512]{1,0:T(8,128)(2,1)S(1)}, u32[]{:S(2)}, u32[]{:S(2)}) collective-permute-start(bf16[128,512]{1,0:T(8,128)(2,1)S(1)} %collective-permute-done.3), channel_id=1, source_target_pairs={{0,8},{4,12},{8,0},{12,4},{16,24},{20,28},{24,16},{28,20},{1,9},{5... | collective-permute-start | bytes 393224 | tf_op jit(solution)/shard_map/ppermute | solution.py:23
  15.2 5.0 %collective-permute-start.4 = (bf16[128,512]{1,0:T(8,128)(2,1)S(1)}, bf16[128,512]{1,0:T(8,128)(2,1)S(1)}, u32[]{:S(2)}, u32[]{:S(2)}) collective-permute-start(bf16[128,512]{1,0:T(8,128)(2,1)S(1)} %collective-permute-done.1), channel_id=1, source_target_pairs={{0,8},{4,12},{8,0},{12,4},{16,24},{20,28},{24,16},{28,20},{1,9},{5... | collective-permute-start | bytes 393224 | tf_op jit(solution)/shard_map/ppermute | solution.py:23
  20.2 1.9 %collective-permute-start.6 = (bf16[4,128,512]{2,1,0:T(8,128)(2,1)S(1)}, bf16[4,128,512]{2,1,0:T(8,128)(2,1)S(1)}, u32[]{:S(2)}, u32[]{:S(2)}) collective-permute-start(bf16[4,128,512]{2,1,0:T(8,128)(2,1)S(1)} %pad_maximum_fusion.refs_0_), channel_id=1, source_target_pairs={{0,4},{4,0},{8,12},{12,8},{16,20},{20,16},{24,28},{28,24},{1,5},{5... | collective-permute-start | bytes 1572872 | tf_op jit(solution)/shard_map/ppermute | solution.py:23
  20.2 5.9 %collective-permute-start.7 = (bf16[128,512]{1,0:T(8,128)(2,1)S(1)}, bf16[128,512]{1,0:T(8,128)(2,1)S(1)}, u32[]{:S(2)}, u32[]{:S(2)}) collective-permute-start(bf16[128,512]{1,0:T(8,128)(2,1)S(1)} %collective-permute-done.2), channel_id=1, source_target_pairs={{0,8},{4,12},{8,0},{12,4},{16,24},{20,28},{24,16},{28,20},{1,9},{5... | collective-permute-start | bytes 393224 | tf_op jit(solution)/shard_map/ppermute | solution.py:23
  26.2 2.0 %copy-start = (f32[1024]{0:T(1024)S(1)}, f32[1024]{0:T(1024)}, u32[]{:S(2)}) copy-start(f32[1024]{0:T(1024)} %param.8) | copy-start | bytes 12292
  26.2 2.0 %collective-permute-start.8 = (bf16[4,128,512]{2,1,0:T(8,128)(2,1)S(1)}, bf16[4,128,512]{2,1,0:T(8,128)(2,1)S(1)}, u32[]{:S(2)}, u32[]{:S(2)}) collective-permute-start(bf16[4,128,512]{2,1,0:T(8,128)(2,1)S(1)} %pad_maximum_fusion.1.refs_0_), channel_id=1, source_target_pairs={{0,4},{4,0},{8,12},{12,8},{16,20},{20,16},{24,28},{28,24},{1,5},{5... | collective-permute-start | bytes 1572872 | tf_op jit(solution)/shard_map/ppermute | solution.py:23
  32.5 4.1 %collective-permute-start.12 = (bf16[2,2,128,512]{3,2,1,0:T(8,128)(2,1)S(1)}, bf16[2,2,128,512]{3,2,1,0:T(8,128)(2,1)S(1)}, u32[]{:S(2)}, u32[]{:S(2)}) collective-permute-start(bf16[2,2,128,512]{3,2,1,0:T(8,128)(2,1)S(1)} %get-tuple-element.81), channel_id=1, source_target_pairs={{0,4},{4,0},{8,12},{12,8},{16,20},{20,16},{24,28},{28,24},{1,5},{5... | collective-permute-start | bytes 1572872 | tf_op jit(solution)/shard_map/ppermute | solution.py:23
  32.7 5.5 %collective-permute-start.10 = (bf16[2,2,128,512]{3,2,1,0:T(8,128)(2,1)S(1)}, bf16[2,2,128,512]{3,2,1,0:T(8,128)(2,1)S(1)}, u32[]{:S(2)}, u32[]{:S(2)}) collective-permute-start(bf16[2,2,128,512]{3,2,1,0:T(8,128)(2,1)S(1)} %get-tuple-element.80), channel_id=1, source_target_pairs={{0,4},{4,0},{8,12},{12,8},{16,20},{20,16},{24,28},{28,24},{1,5},{5... | collective-permute-start | bytes 1572872 | tf_op jit(solution)/shard_map/ppermute | solution.py:23
  36.0 4.0 %collective-permute-start.14 = (bf16[2,2,128,512]{3,2,1,0:T(8,128)(2,1)S(1)}, bf16[2,2,128,512]{3,2,1,0:T(8,128)(2,1)S(1)}, u32[]{:S(2)}, u32[]{:S(2)}) collective-permute-start(bf16[2,2,128,512]{3,2,1,0:T(8,128)(2,1)S(1)} %get-tuple-element.83), channel_id=1, source_target_pairs={{0,4},{4,0},{8,12},{12,8},{16,20},{20,16},{24,28},{28,24},{1,5},{5... | collective-permute-start | bytes 1572872 | tf_op jit(solution)/shard_map/ppermute | solution.py:23
  36.2 4.7 %collective-permute-start.9 = (bf16[2,2,128,512]{3,2,1,0:T(8,128)(2,1)S(1)}, bf16[2,2,128,512]{3,2,1,0:T(8,128)(2,1)S(1)}, u32[]{:S(2)}, u32[]{:S(2)}) collective-permute-start(bf16[2,2,128,512]{3,2,1,0:T(8,128)(2,1)S(1)} %get-tuple-element.77), channel_id=1, source_target_pairs={{0,4},{4,0},{8,12},{12,8},{16,20},{20,16},{24,28},{28,24},{1,5},{5... | collective-permute-start | bytes 1572872 | tf_op jit(solution)/shard_map/ppermute | solution.py:23
  36.7 9.2 %collective-permute-start.13 = (bf16[1,2,128,512]{3,2,1,0:T(8,128)(2,1)S(1)}, bf16[1,2,128,512]{3,2,1,0:T(8,128)(2,1)S(1)}, u32[]{:S(2)}, u32[]{:S(2)}) collective-permute-start(bf16[1,2,128,512]{3,2,1,0:T(8,128)(2,1)S(1)} %slice_bitcast_fusion.5), channel_id=1, source_target_pairs={{0,8},{4,12},{8,0},{12,4},{16,24},{20,28},{24,16},{28,20},{1,9},{5... | collective-permute-start | bytes 786440 | tf_op jit(solution)/shard_map/ppermute | solution.py:23
  38.4 8.1 %collective-permute-start.11 = (bf16[1,2,128,512]{3,2,1,0:T(8,128)(2,1)S(1)}, bf16[1,2,128,512]{3,2,1,0:T(8,128)(2,1)S(1)}, u32[]{:S(2)}, u32[]{:S(2)}) collective-permute-start(bf16[1,2,128,512]{3,2,1,0:T(8,128)(2,1)S(1)} %get-tuple-element.124), channel_id=1, source_target_pairs={{0,16},{4,20},{8,24},{12,28},{16,0},{20,4},{24,8},{28,12},{1,17},{... | collective-permute-start | bytes 786440 | tf_op jit(solution)/shard_map/ppermute | solution.py:29
  40.1 11.4 %collective-permute-start.16 = (bf16[1,2,128,512]{3,2,1,0:T(8,128)(2,1)S(1)}, bf16[1,2,128,512]{3,2,1,0:T(8,128)(2,1)S(1)}, u32[]{:S(2)}, u32[]{:S(2)}) collective-permute-start(bf16[1,2,128,512]{3,2,1,0:T(8,128)(2,1)S(1)} %slice_bitcast_fusion.4), channel_id=1, source_target_pairs={{0,8},{4,12},{8,0},{12,4},{16,24},{20,28},{24,16},{28,20},{1,9},{5... | collective-permute-start | bytes 786440 | tf_op jit(solution)/shard_map/ppermute | solution.py:23
  46.6 7.3 %collective-permute-start.17 = (bf16[1,2,128,512]{3,2,1,0:T(8,128)(2,1)S(1)}, bf16[1,2,128,512]{3,2,1,0:T(8,128)(2,1)S(1)}, u32[]{:S(2)}, u32[]{:S(2)}) collective-permute-start(bf16[1,2,128,512]{3,2,1,0:T(8,128)(2,1)S(1)} %fusion.4), channel_id=1, source_target_pairs={{0,16},{4,20},{8,24},{12,28},{16,0},{20,4},{24,8},{28,12},{1,17},{... | collective-permute-start | bytes 786440 | tf_op jit(solution)/shard_map/ppermute | solution.py:29
  48.2 13.0 %collective-permute-start.15 = (bf16[1,2,128,512]{3,2,1,0:T(8,128)(2,1)S(1)}, bf16[1,2,128,512]{3,2,1,0:T(8,128)(2,1)S(1)}, u32[]{:S(2)}, u32[]{:S(2)}) collective-permute-start(bf16[1,2,128,512]{3,2,1,0:T(8,128)(2,1)S(1)} %fusion.7), channel_id=1, source_target_pairs={{0,8},{4,12},{8,0},{12,4},{16,24},{20,28},{24,16},{28,20},{1,9},{5... | collective-permute-start | bytes 786440 | tf_op jit(solution)/shard_map/ppermute | solution.py:23
  54.0 7.2 %collective-permute-start.18 = (bf16[1,2,128,512]{3,2,1,0:T(8,128)(2,1)S(1)}, bf16[1,2,128,512]{3,2,1,0:T(8,128)(2,1)S(1)}, u32[]{:S(2)}, u32[]{:S(2)}) collective-permute-start(bf16[1,2,128,512]{3,2,1,0:T(8,128)(2,1)S(1)} %get-tuple-element.88), channel_id=1, source_target_pairs={{0,16},{4,20},{8,24},{12,28},{16,0},{20,4},{24,8},{28,12},{1,17},{... | collective-permute-start | bytes 786440 | tf_op jit(solution)/shard_map/ppermute | solution.py:29
  55.6 13.0 %collective-permute-start.20 = (bf16[128,512]{1,0:T(8,128)(2,1)S(1)}, bf16[128,512]{1,0:T(8,128)(2,1)S(1)}, u32[]{:S(2)}, u32[]{:S(2)}) collective-permute-start(bf16[128,512]{1,0:T(8,128)(2,1)S(1)} %get-tuple-element.126), channel_id=1, source_target_pairs={{0,2},{1,3},{2,0},{3,1},{4,6},{5,7},{6,4},{7,5},{8,10},{9,11},{10,... | collective-permute-start | bytes 393224 | tf_op jit(solution)/shard_map/ppermute | solution.py:17
  60.2 9.0 %copy-start.1 = (bf16[128,512]{1,0:T(8,128)(2,1)S(1)}, bf16[128,512]{1,0:T(8,128)(2,1)}, u32[]{:S(2)}) copy-start(bf16[128,512]{1,0:T(8,128)(2,1)} %param.6) | copy-start | bytes 393220
  60.2 7.6 %collective-permute-start.19 = (bf16[128,512]{1,0:T(8,128)(2,1)S(1)}, bf16[128,512]{1,0:T(8,128)(2,1)S(1)}, u32[]{:S(2)}, u32[]{:S(2)}) collective-permute-start(bf16[128,512]{1,0:T(8,128)(2,1)S(1)} %get-tuple-element.125), channel_id=1, source_target_pairs={{0,3},{1,2},{2,1},{3,0},{4,7},{5,6},{6,5},{7,4},{8,11},{9,10},{10,... | collective-permute-start | bytes 393224 | tf_op jit(solution)/shard_map/ppermute | solution.py:17
  61.3 7.9 %collective-permute-start.21 = (bf16[128,512]{1,0:T(8,128)(2,1)S(1)}, bf16[128,512]{1,0:T(8,128)(2,1)S(1)}, u32[]{:S(2)}, u32[]{:S(2)}) collective-permute-start(bf16[128,512]{1,0:T(8,128)(2,1)S(1)} %fusion.13), channel_id=1, source_target_pairs={{0,1},{1,0},{2,3},{3,2},{4,5},{5,4},{6,7},{7,6},{8,9},{9,8},{10,11... | collective-permute-start | bytes 393224 | tf_op jit(solution)/shard_map/ppermute | solution.py:17
  70.0 6.0 %collective-permute-start.24 = (bf16[128,512]{1,0:T(8,128)(2,1)S(1)}, bf16[128,512]{1,0:T(8,128)(2,1)S(1)}, u32[]{:S(2)}, u32[]{:S(2)}) collective-permute-start(bf16[128,512]{1,0:T(8,128)(2,1)S(1)} %get-tuple-element.119), channel_id=1, source_target_pairs={{0,1},{1,0},{2,3},{3,2},{4,5},{5,4},{6,7},{7,6},{8,9},{9,8},{10,11... | collective-permute-start | bytes 393224 | tf_op jit(solution)/shard_map/ppermute | solution.py:17
  71.4 11.8 %collective-permute-start.27 = (bf16[128,512]{1,0:T(8,128)(2,1)S(1)}, bf16[128,512]{1,0:T(8,128)(2,1)S(1)}, u32[]{:S(2)}, u32[]{:S(2)}) collective-permute-start(bf16[128,512]{1,0:T(8,128)(2,1)S(1)} %get-tuple-element.119), channel_id=1, source_target_pairs={{0,2},{1,3},{2,0},{3,1},{4,6},{5,7},{6,4},{7,5},{8,10},{9,11},{10,... | collective-permute-start | bytes 393224 | tf_op jit(solution)/shard_map/ppermute | solution.py:17
  72.9 10.8 %collective-permute-start.28 = (bf16[128,512]{1,0:T(8,128)(2,1)S(1)}, bf16[128,512]{1,0:T(8,128)(2,1)S(1)}, u32[]{:S(2)}, u32[]{:S(2)}) collective-permute-start(bf16[128,512]{1,0:T(8,128)(2,1)S(1)} %get-tuple-element.119), channel_id=1, source_target_pairs={{0,3},{1,2},{2,1},{3,0},{4,7},{5,6},{6,5},{7,4},{8,11},{9,10},{10,... | collective-permute-start | bytes 393224 | tf_op jit(solution)/shard_map/ppermute | solution.py:17
  76.0 7.7 %collective-permute-start.29 = (bf16[1,128,512]{2,1,0:T(8,128)(2,1)S(1)}, bf16[1,128,512]{2,1,0:T(8,128)(2,1)S(1)}, u32[]{:S(2)}, u32[]{:S(2)}) collective-permute-start(bf16[1,128,512]{2,1,0:T(8,128)(2,1)S(1)} %bitcast.87), channel_id=1, source_target_pairs={{0,8},{4,12},{8,0},{12,4},{16,24},{20,28},{24,16},{28,20},{1,9},{5... | collective-permute-start | bytes 393224 | tf_op jit(solution)/shard_map/ppermute | solution.py:23
  76.0 8.3 %collective-permute-start.22 = (bf16[1,128,512]{2,1,0:T(8,128)(2,1)S(1)}, bf16[1,128,512]{2,1,0:T(8,128)(2,1)S(1)}, u32[]{:S(2)}, u32[]{:S(2)}) collective-permute-start(bf16[1,128,512]{2,1,0:T(8,128)(2,1)S(1)} %bitcast.83), channel_id=1, source_target_pairs={{0,16},{4,20},{8,24},{12,28},{16,0},{20,4},{24,8},{28,12},{1,17},{... | collective-permute-start | bytes 393224 | tf_op jit(solution)/shard_map/ppermute | solution.py:36
  76.5 7.9 %collective-permute-start.35 = (bf16[1,128,512]{2,1,0:T(8,128)(2,1)S(1)}, bf16[1,128,512]{2,1,0:T(8,128)(2,1)S(1)}, u32[]{:S(2)}, u32[]{:S(2)}) collective-permute-start(bf16[1,128,512]{2,1,0:T(8,128)(2,1)S(1)} %bitcast.84), channel_id=1, source_target_pairs={{0,8},{4,12},{8,0},{12,4},{16,24},{20,28},{24,16},{28,20},{1,9},{5... | collective-permute-start | bytes 393224 | tf_op jit(solution)/shard_map/ppermute | solution.py:23
  83.2 5.0 %collective-permute-start.25 = (bf16[1,128,512]{2,1,0:T(8,128)(2,1)S(1)}, bf16[1,128,512]{2,1,0:T(8,128)(2,1)S(1)}, u32[]{:S(2)}, u32[]{:S(2)}) collective-permute-start(bf16[1,128,512]{2,1,0:T(8,128)(2,1)S(1)} %bitcast.88), channel_id=1, source_target_pairs={{0,16},{4,20},{8,24},{12,28},{16,0},{20,4},{24,8},{28,12},{1,17},{... | collective-permute-start | bytes 393224 | tf_op jit(solution)/shard_map/ppermute | solution.py:36
  83.7 5.8 %collective-permute-start.38 = (bf16[2,128,512]{2,1,0:T(8,128)(2,1)S(1)}, bf16[2,128,512]{2,1,0:T(8,128)(2,1)S(1)}, u32[]{:S(2)}, u32[]{:S(2)}) collective-permute-start(bf16[2,128,512]{2,1,0:T(8,128)(2,1)S(1)} %pad_maximum_fusion.2.refs_2_), channel_id=1, source_target_pairs={{0,4},{4,0},{8,12},{12,8},{16,20},{20,16},{24,28},{28,24},{1,5},{5... | collective-permute-start | bytes 786440 | tf_op jit(solution)/shard_map/ppermute | solution.py:23
  83.8 9.1 %collective-permute-start.30 = (bf16[2,128,512]{2,1,0:T(8,128)(2,1)S(1)}, bf16[2,128,512]{2,1,0:T(8,128)(2,1)S(1)}, u32[]{:S(2)}, u32[]{:S(2)}) collective-permute-start(bf16[2,128,512]{2,1,0:T(8,128)(2,1)S(1)} %pad_maximum_fusion.2.refs_2_), channel_id=1, source_target_pairs={{0,8},{4,12},{8,0},{12,4},{16,24},{20,28},{24,16},{28,20},{1,9},{5... | collective-permute-start | bytes 786440 | tf_op jit(solution)/shard_map/ppermute | solution.py:23
  84.2 4.4 %collective-permute-start.37 = (bf16[1,128,512]{2,1,0:T(8,128)(2,1)S(1)}, bf16[1,128,512]{2,1,0:T(8,128)(2,1)S(1)}, u32[]{:S(2)}, u32[]{:S(2)}) collective-permute-start(bf16[1,128,512]{2,1,0:T(8,128)(2,1)S(1)} %bitcast.89), channel_id=1, source_target_pairs={{0,4},{4,0},{8,12},{12,8},{16,20},{20,16},{24,28},{28,24},{1,5},{5... | collective-permute-start | bytes 393224 | tf_op jit(solution)/shard_map/ppermute | solution.py:23
  88.2 1.3 %collective-permute-start.36 = (bf16[1,128,512]{2,1,0:T(8,128)(2,1)S(1)}, bf16[1,128,512]{2,1,0:T(8,128)(2,1)S(1)}, u32[]{:S(2)}, u32[]{:S(2)}) collective-permute-start(bf16[1,128,512]{2,1,0:T(8,128)(2,1)S(1)} %bitcast.85), channel_id=1, source_target_pairs={{0,4},{4,0},{8,12},{12,8},{16,20},{20,16},{24,28},{28,24},{1,5},{5... | collective-permute-start | bytes 393224 | tf_op jit(solution)/shard_map/ppermute | solution.py:23
  88.2 9.1 %collective-permute-start.42 = (bf16[2,128,512]{2,1,0:T(8,128)(2,1)S(1)}, bf16[2,128,512]{2,1,0:T(8,128)(2,1)S(1)}, u32[]{:S(2)}, u32[]{:S(2)}) collective-permute-start(bf16[2,128,512]{2,1,0:T(8,128)(2,1)S(1)} %pad_maximum_fusion.2.refs_2_), channel_id=1, source_target_pairs={{0,16},{4,20},{8,24},{12,28},{16,0},{20,4},{24,8},{28,12},{1,17},{... | collective-permute-start | bytes 786440 | tf_op jit(solution)/shard_map/ppermute | solution.py:36
  92.9 6.4 %collective-permute-start.41 = (bf16[2,128,512]{2,1,0:T(8,128)(2,1)S(1)}, bf16[2,128,512]{2,1,0:T(8,128)(2,1)S(1)}, u32[]{:S(2)}, u32[]{:S(2)}) collective-permute-start(bf16[2,128,512]{2,1,0:T(8,128)(2,1)S(1)} %collective-permute-done.30.refs_2_), channel_id=1, source_target_pairs={{0,4},{4,0},{8,12},{12,8},{16,20},{20,16},{24,28},{28,24},{1,5},{5... | collective-permute-start | bytes 786440 | tf_op jit(solution)/shard_map/ppermute | solution.py:23
  93.1 10.6 %collective-permute-start.31 = (bf16[2,128,512]{2,1,0:T(8,128)(2,1)S(1)}, bf16[2,128,512]{2,1,0:T(8,128)(2,1)S(1)}, u32[]{:S(2)}, u32[]{:S(2)}) collective-permute-start(bf16[2,128,512]{2,1,0:T(8,128)(2,1)S(1)} %collective-permute-done.30.refs_2_), channel_id=1, source_target_pairs={{0,16},{4,20},{8,24},{12,28},{16,0},{20,4},{24,8},{28,12},{1,17},{... | collective-permute-start | bytes 786440 | tf_op jit(solution)/shard_map/ppermute | solution.py:36
  94.1 3.5 %collective-permute-start.40 = (bf16[1,128,512]{2,1,0:T(8,128)(2,1)S(1)}, bf16[1,128,512]{2,1,0:T(8,128)(2,1)S(1)}, u32[]{:S(2)}, u32[]{:S(2)}) collective-permute-start(bf16[1,128,512]{2,1,0:T(8,128)(2,1)S(1)} %collective-permute-done.29.refs_1_), channel_id=1, source_target_pairs={{0,4},{4,0},{8,12},{12,8},{16,20},{20,16},{24,28},{28,24},{1,5},{5... | collective-permute-start | bytes 393224 | tf_op jit(solution)/shard_map/ppermute | solution.py:23
  94.3 5.0 %collective-permute-start.39 = (bf16[1,128,512]{2,1,0:T(8,128)(2,1)S(1)}, bf16[1,128,512]{2,1,0:T(8,128)(2,1)S(1)}, u32[]{:S(2)}, u32[]{:S(2)}) collective-permute-start(bf16[1,128,512]{2,1,0:T(8,128)(2,1)S(1)} %collective-permute-done.35.refs_0_), channel_id=1, source_target_pairs={{0,4},{4,0},{8,12},{12,8},{16,20},{20,16},{24,28},{28,24},{1,5},{5... | collective-permute-start | bytes 393224 | tf_op jit(solution)/shard_map/ppermute | solution.py:23
  97.3 6.5 %collective-permute-start.23 = (bf16[1,128,512]{2,1,0:T(8,128)(2,1)S(1)}, bf16[1,128,512]{2,1,0:T(8,128)(2,1)S(1)}, u32[]{:S(2)}, u32[]{:S(2)}) collective-permute-start(bf16[1,128,512]{2,1,0:T(8,128)(2,1)S(1)} %collective-permute-done.22.refs_0_), channel_id=1, source_target_pairs={{0,8},{4,12},{8,0},{12,4},{16,24},{20,28},{24,16},{28,20},{1,9},{5... | collective-permute-start | bytes 393224 | tf_op jit(solution)/shard_map/ppermute | solution.py:23
  97.6 7.2 %collective-permute-start.26 = (bf16[1,128,512]{2,1,0:T(8,128)(2,1)S(1)}, bf16[1,128,512]{2,1,0:T(8,128)(2,1)S(1)}, u32[]{:S(2)}, u32[]{:S(2)}) collective-permute-start(bf16[1,128,512]{2,1,0:T(8,128)(2,1)S(1)} %collective-permute-done.25.refs_1_), channel_id=1, source_target_pairs={{0,8},{4,12},{8,0},{12,4},{16,24},{20,28},{24,16},{28,20},{1,9},{5... | collective-permute-start | bytes 393224 | tf_op jit(solution)/shard_map/ppermute | solution.py:23
  103.1 2.4 %collective-permute-start.45 = (bf16[2,128,512]{2,1,0:T(8,128)(2,1)S(1)}, bf16[2,128,512]{2,1,0:T(8,128)(2,1)S(1)}, u32[]{:S(2)}, u32[]{:S(2)}) collective-permute-start(bf16[2,128,512]{2,1,0:T(8,128)(2,1)S(1)} %collective-permute-done.42.refs_2_), channel_id=1, source_target_pairs={{0,4},{4,0},{8,12},{12,8},{16,20},{20,16},{24,28},{28,24},{1,5},{5... | collective-permute-start | bytes 786440 | tf_op jit(solution)/shard_map/ppermute | solution.py:23
  103.1 1.7 %collective-permute-start.44 = (bf16[1,128,512]{2,1,0:T(8,128)(2,1)S(1)}, bf16[1,128,512]{2,1,0:T(8,128)(2,1)S(1)}, u32[]{:S(2)}, u32[]{:S(2)}) collective-permute-start(bf16[1,128,512]{2,1,0:T(8,128)(2,1)S(1)} %collective-permute-done.25.refs_1_), channel_id=1, source_target_pairs={{0,4},{4,0},{8,12},{12,8},{16,20},{20,16},{24,28},{28,24},{1,5},{5... | collective-permute-start | bytes 393224 | tf_op jit(solution)/shard_map/ppermute | solution.py:23
  103.6 5.1 %collective-permute-start.34 = (bf16[2,128,512]{2,1,0:T(8,128)(2,1)S(1)}, bf16[2,128,512]{2,1,0:T(8,128)(2,1)S(1)}, u32[]{:S(2)}, u32[]{:S(2)}) collective-permute-start(bf16[2,128,512]{2,1,0:T(8,128)(2,1)S(1)} %collective-permute-done.31.refs_2_), channel_id=1, source_target_pairs={{0,4},{4,0},{8,12},{12,8},{16,20},{20,16},{24,28},{28,24},{1,5},{5... | collective-permute-start | bytes 786440 | tf_op jit(solution)/shard_map/ppermute | solution.py:23
  103.7 1.7 %collective-permute-start.43 = (bf16[1,128,512]{2,1,0:T(8,128)(2,1)S(1)}, bf16[1,128,512]{2,1,0:T(8,128)(2,1)S(1)}, u32[]{:S(2)}, u32[]{:S(2)}) collective-permute-start(bf16[1,128,512]{2,1,0:T(8,128)(2,1)S(1)} %collective-permute-done.22.refs_0_), channel_id=1, source_target_pairs={{0,4},{4,0},{8,12},{12,8},{16,20},{20,16},{24,28},{28,24},{1,5},{5... | collective-permute-start | bytes 393224 | tf_op jit(solution)/shard_map/ppermute | solution.py:23
  104.8 3.9 %collective-permute-start.32 = (bf16[1,128,512]{2,1,0:T(8,128)(2,1)S(1)}, bf16[1,128,512]{2,1,0:T(8,128)(2,1)S(1)}, u32[]{:S(2)}, u32[]{:S(2)}) collective-permute-start(bf16[1,128,512]{2,1,0:T(8,128)(2,1)S(1)} %collective-permute-done.23.refs_0_), channel_id=1, source_target_pairs={{0,4},{4,0},{8,12},{12,8},{16,20},{20,16},{24,28},{28,24},{1,5},{5... | collective-permute-start | bytes 393224 | tf_op jit(solution)/shard_map/ppermute | solution.py:23
  104.9 3.9 %collective-permute-start.33 = (bf16[1,128,512]{2,1,0:T(8,128)(2,1)S(1)}, bf16[1,128,512]{2,1,0:T(8,128)(2,1)S(1)}, u32[]{:S(2)}, u32[]{:S(2)}) collective-permute-start(bf16[1,128,512]{2,1,0:T(8,128)(2,1)S(1)} %collective-permute-done.26.refs_1_), channel_id=1, source_target_pairs={{0,4},{4,0},{8,12},{12,8},{16,20},{20,16},{24,28},{28,24},{1,5},{5... | collective-permute-start | bytes 393224 | tf_op jit(solution)/shard_map/ppermute | solution.py:23

commit v7 on v6

--- a/solution.py
+++ b/solution.py
@@ -6,7 +6,7 @@
 from jax.sharding import PartitionSpec as P
 
 loss_scale = 64.0
-tile = 256
+tile = 512
 in_vmem = pl.BlockSpec(memory_space=pltpu.VMEM)
 in_smem = pl.BlockSpec(memory_space=pltpu.SMEM)
 in_hbm = pl.BlockSpec(memory_space=pltpu.HBM)
@@ -144,11 +144,12 @@
     def kernel(info_ref, feat_ref, weight_ref, *out_refs):
         left = feat_ref[0]
         even = info_ref[0] % 2 == 0
+        step = min(tile, cols)
         for pair in range(count):
             piece = pair ^ (info_ref[0] // 2)
-            for start in range(0, cols, tile):
+            for start in range(0, cols, step):
                 low, high = (
-                    dot(left, weight_ref[offset, :, base + start : base + start + tile], (1, 0)).astype(
+                    dot(left, weight_ref[offset, :, base + start : base + start + step], (1, 0)).astype(
                         jnp.bfloat16
                     )
                     for base in (2 * pair * cols, (2 * pair + 1) * cols)
@@ -158,7 +159,7 @@
                     for number, group in enumerate(groups):
                         for place, block in enumerate(group):
                             out_refs[side * len(groups) + number][
-                                piece, place, :, start : start + tile
+                                piece, place, :, start : start + step
                             ] = product[block * rows : (block + 1) * rows]
     out_shape = [
         jax.ShapeDtypeStruct((count, len(group), rows, cols), jnp.bfloat16) for group in groups
@@ -177,11 +178,13 @@
 def turned(value, count):
     _, tok, width = value.shape
 
+    step = min(tile, width)
+
     def kernel(in_ref, out_ref):
         for piece in range(count):
-            for start in range(0, width, tile):
-                out_ref[piece, start : start + tile, :] = in_ref[
-                    piece, :, start : start + tile
+            for start in range(0, width, step):
+                out_ref[piece, start : start + step, :] = in_ref[
+                    piece, :, start : start + step
                 ].T
 
     return pl.pallas_call(
@@ -311,11 +314,16 @@
             held[piece] = dot(
                 token_refs[piece // count][piece % count], preact[...], (1, 0)
             ).astype(jnp.bfloat16)
-            copy = pltpu.make_async_copy(
-                held.at[piece], enc_ref.at[span(info_ref[0] ^ rels[piece], cols)], sems.at[piece]
-            )
-            copy.start()
-            copies.append(copy)
+            size = cols // 4
+            for part in range(4):
+                row = (info_ref[0] ^ rels[piece]) * 4 + part
+                copy = pltpu.make_async_copy(
+                    held.at[piece, pl.ds(part * size, size)],
+                    enc_ref.at[span(row, size)],
+                    sems.at[4 * piece + part],
+                )
+                copy.start()
+                copies.append(copy)
         for copy in copies:
             copy.wait()
 
@@ -331,7 +339,7 @@
         scratch_shapes=[
             pltpu.VMEM((tok, width), jnp.bfloat16),
             pltpu.VMEM((pieces, cols, width), jnp.bfloat16),
-            pltpu.SemaphoreType.DMA((pieces,)),
+            pltpu.SemaphoreType.DMA((4 * pieces,)),
         ],
         name="encoder_grad",
         **params(
@@ -455,8 +463,6 @@
     early, last = [], len(spans) - 1
     for place, group in enumerate(spans):
         stacked = jnp.stack([blocks[s] for s in group], 0)
-        if place == last:
-            stacked = after(stacked, groups_of[2, 0][1])
         groups_of[0, 0][place] = stacked
         for k in range(1, layers):
             groups_of[0, k][place] = from_layer(stacked, k, sub_count)
@@ -480,12 +486,9 @@
         for rel in [rel for stage in stages for rel in stage]:
             parts = groups_of[rel, k]
             if feature_grad is None:
-                parts = [after(parts[0], groups_of[2, 0][0], groups_of[0, 1][0], groups_of[2, 0][1], groups_of[0, 1][1])] + parts[1:]
-            elif (rel > 0 and k == 0) or (rel == 0 and k > 0):
+                parts = [after(parts[0], groups_of[2, 0][0], groups_of[0, 1][0], groups_of[2, 1][0], groups_of[2, 0][1], groups_of[0, 1][1])] + parts[1:]
+            elif (rel > 0 and k == 0) or (rel > 0 and k > 0):
                 parts = [after(part, feature_grad) for part in parts]
-            if feature_grad is not None:
-                if rel > 0 and k == 0:
-                    feature_grad = after(feature_grad, groups_of[0, layers - 1][-1])
             feature_grad, dec_grad, squares[k, rel] = backward_pair(
                 info,
                 rel,

time: 117 us -> 114 us (0.974)
  waiting for transfers between devices: 37.7 us -> 33.5 us
  starting transfers between devices: 41.6 us -> 43.7 us
    ppermute x4, waiting for transfers between devices: 6.44 us -> 0.01 us  [from_layer(): return lax.ppermute(value, 'layer', pairs)]
    ppermute x30, waiting for transfers between devices: 14.3 us -> 17.9 us  [over_members(): return lax.ppermute(value, 'layer', pairs)]
    ppermute x4, starting transfers between devices: 2.46 us -> 5.17 us  [from_layer(): return lax.ppermute(value, 'layer', pairs)]
    ppermute x9, waiting for transfers between devices: 14.1 us -> 12.8 us  [over_feat(): return lax.ppermute(value, 'feat', pairs)]
  transfers between devices with their start and end apart: 46 -> 46, of which waited for: 21 -> 19; matrix products, arithmetic and copies ran while one was open for 1% -> 1% of each run, Pallas kernels for 19% -> 19%
where the time goes in v7:
time: 114 us
  starting transfers between devices  43.7 us (38%)
  Pallas kernels  33.6 us (29%)
  waiting for transfers between devices  33.5 us (29%)
  other arithmetic  1.96 us (2%)
    ppermute x9, starting transfers between devices, over_feat(): return lax.ppermute(value, 'feat', pairs)  18.1 us
    ppermute x30, waiting for transfers between devices, over_members(): return lax.ppermute(value, 'layer', pairs)  17.9 us
    ppermute x30, starting transfers between devices, over_members(): return lax.ppermute(value, 'layer', pairs)  15.7 us
    ppermute x9, waiting for transfers between devices, over_feat(): return lax.ppermute(value, 'feat', pairs)  12.8 us
    pallas_call x4, Pallas kernels, backward_pair(): pl.pallas_call(kernel, in_specs=[in_smem] + [in_vmem] * (len(inputs) + 2)...  12.8 us
    pallas_call x2, Pallas kernels, decode(): pl.pallas_call(kernel, in_specs=[in_smem, in_vmem, in_vmem], out_specs=[i...  5.78 us
    ppermute x4, starting transfers between devices, from_layer(): return lax.ppermute(value, 'layer', pairs)  5.17 us
    pallas_call x1, Pallas kernels, encoder_grad(): pl.pallas_call(kernel, in_specs=[in_smem] + [in_vmem] * (len(turned_token...  4.79 us
  transfers between devices with their start and end apart: 46, of which 19 were waited for; matrix products, arithmetic and copies ran while one was open for 1% of the time, Pallas kernels for 19%

profile of v7, /device:TPU:0, one launch (start us, length us, event | category | flops | bytes accessed | tf_op | source)
XLA Modules:
  0.0 114.0 jit_solution(17251302328816878296)
XLA Ops:
  0.7 3.0 %collective-permute-start.1 = (bf16[128,512]{1,0:T(8,128)(2,1)}, bf16[128,512]{1,0:T(8,128)(2,1)S(1)}, u32[]{:S(2)}, u32[]{:S(2)}) collective-permute-start(bf16[128,512]{1,0:T(8,128)(2,1)} %param.5), channel_id=1, source_target_pairs={{0,1},{1,0},{2,3},{3,2},{4,5},{5,4},{6,7},{7,6},{8,9},{9,8},{10,11... | collective-permute-start | bytes 393224 | tf_op jit(solution)/shard_map/ppermute | solution.py:17
  3.8 2.5 %collective-permute-start.3 = (bf16[128,512]{1,0:T(8,128)(2,1)}, bf16[128,512]{1,0:T(8,128)(2,1)S(1)}, u32[]{:S(2)}, u32[]{:S(2)}) collective-permute-start(bf16[128,512]{1,0:T(8,128)(2,1)} %param.5), channel_id=1, source_target_pairs={{0,3},{1,2},{2,1},{3,0},{4,7},{5,6},{6,5},{7,4},{8,11},{9,10},{10,... | collective-permute-start | bytes 393224 | tf_op jit(solution)/shard_map/ppermute | solution.py:17
  6.4 1.5 %collective-permute-start = (bf16[128,512]{1,0:T(8,128)(2,1)}, bf16[128,512]{1,0:T(8,128)(2,1)S(1)}, u32[]{:S(2)}, u32[]{:S(2)}) collective-permute-start(bf16[128,512]{1,0:T(8,128)(2,1)} %param.5), channel_id=1, source_target_pairs={{0,8},{4,12},{8,0},{12,4},{16,24},{20,28},{24,16},{28,20},{1,9},{5... | collective-permute-start | bytes 393224 | tf_op jit(solution)/shard_map/ppermute | solution.py:23
  7.9 4.7 %fetch.1 = (bf16[2048,1024]{1,0:T(8,128)(2,1)S(1)}, bf16[2,1024,2048]{2,1,0:T(8,128)(2,1)S(1)}) custom-call(bf16[2048,1024]{1,0:T(8,128)(2,1)} %refs_0_.1, bf16[2,1024,2048]{2,1,0:T(8,128)(2,1)} %refs_1_), custom_call_target="tpu_custom_call" | custom-call | bytes 12582912 | tf_op jit(solution)/shard_map/fetch/pallas_call | solution.py:88
  12.6 1.1 collective-permute-done.3
  13.7 1.5 %collective-permute-start.5 = (bf16[128,512]{1,0:T(8,128)(2,1)S(1)}, bf16[128,512]{1,0:T(8,128)(2,1)S(1)}, u32[]{:S(2)}, u32[]{:S(2)}) collective-permute-start(bf16[128,512]{1,0:T(8,128)(2,1)S(1)} %collective-permute-done.3), channel_id=1, source_target_pairs={{0,8},{4,12},{8,0},{12,4},{16,24},{20,28},{24,16},{28,20},{1,9},{5... | collective-permute-start | bytes 393224 | tf_op jit(solution)/shard_map/ppermute | solution.py:23
  15.2 0.5 collective-permute-start.4
  15.8 2.5 %collective-permute-done.2 = bf16[128,512]{1,0:T(8,128)(2,1)S(1)} collective-permute-done((bf16[128,512]{1,0:T(8,128)(2,1)}, bf16[128,512]{1,0:T(8,128)(2,1)S(1)}, u32[]{:S(2)}, u32[]{:S(2)}) %collective-permute-start.2) | collective-permute-done | bytes 131104 | tf_op jit(solution)/shard_map/ppermute | solution.py:17
  18.3 0.4 collective-permute-done.5
  18.7 1.5 %collective-permute-done.4 = bf16[128,512]{1,0:T(8,128)(2,1)S(1)} collective-permute-done((bf16[128,512]{1,0:T(8,128)(2,1)S(1)}, bf16[128,512]{1,0:T(8,128)(2,1)S(1)}, u32[]{:S(2)}, u32[]{:S(2)}) %collective-permute-start.4) | collective-permute-done | bytes 131104 | tf_op jit(solution)/shard_map/ppermute | solution.py:23
  20.2 1.4 %collective-permute-start.7 = (bf16[128,512]{1,0:T(8,128)(2,1)S(1)}, bf16[128,512]{1,0:T(8,128)(2,1)S(1)}, u32[]{:S(2)}, u32[]{:S(2)}) collective-permute-start(bf16[128,512]{1,0:T(8,128)(2,1)S(1)} %collective-permute-done.2), channel_id=1, source_target_pairs={{0,8},{4,12},{8,0},{12,4},{16,24},{20,28},{24,16},{28,20},{1,9},{5... | collective-permute-start | bytes 393224 | tf_op jit(solution)/shard_map/ppermute | solution.py:23
  21.6 0.5 collective-permute-done.6.refs_1_
  22.1 1.8 %encode.3.refs_2_ = f32[512,1024]{1,0:T(8,128)S(1)} custom-call(s32[2]{0:T(128)S(1)} %pad_add_fusion.info_ref, bf16[4,128,512]{2,1,0:T(8,128)(2,1)S(1)} %pad_maximum_fusion.refs_0_, bf16[4,128,512]{2,1,0:T(8,128)(2,1)S(1)} %collective-permute-done.6.refs_1_, bf16[2048,1024]{1,0:T(8,128)(2,1)S(1)} %get-tuple-element.63.refs_2_.refs_1_), custom_call_target="tpu_custom_call" | custom-call | flops 1073741824 | bytes 3145728 | tf_op jit(solution)/shard_map/encode/pallas_call | solution.py:128
  23.9 2.2 %collective-permute-done.7 = bf16[128,512]{1,0:T(8,128)(2,1)S(1)} collective-permute-done((bf16[128,512]{1,0:T(8,128)(2,1)S(1)}, bf16[128,512]{1,0:T(8,128)(2,1)S(1)}, u32[]{:S(2)}, u32[]{:S(2)}) %collective-permute-start.7) | collective-permute-done | bytes 131104 | tf_op jit(solution)/shard_map/ppermute | solution.py:23
  26.3 1.3 %encode.4.refs_2_ = f32[512,1024]{1,0:T(8,128)S(1)} custom-call(s32[2]{0:T(128)S(1)} %pad_add_fusion.info_ref, bf16[4,128,512]{2,1,0:T(8,128)(2,1)S(1)} %pad_maximum_fusion.1.refs_0_, bf16[2048,1024]{1,0:T(8,128)(2,1)S(1)} %get-tuple-element.63.refs_2_.refs_1_, f32[512,1024]{1,0:T(8,128)S(1)} %encode.3.refs_2_), custom_call_target="tpu_custom_call" | custom-call | flops 536870912 | bytes 1572864 | tf_op jit(solution)/shard_map/encode/pallas_call | solution.py:128
  27.5 0.6 collective-permute-done.8.refs_0_
  28.2 1.4 %encode.5.feat_ref.in_ref.refs_4_ = bf16[2,512,1024]{2,1,0:T(8,128)(2,1)S(1)} custom-call(s32[2]{0:T(128)S(1)} %pad_add_fusion.info_ref, bf16[4,128,512]{2,1,0:T(8,128)(2,1)S(1)} %collective-permute-done.8.refs_0_, bf16[2048,1024]{1,0:T(8,128)(2,1)S(1)} %get-tuple-element.63.refs_2_.refs_1_, f32[512,1024]{1,0:T(8,128)S(1)} %encode.4.refs_2_, ...), custom_call_target="tpu_custom_call" | custom-call | flops 536870912 | bytes 1572864 | tf_op jit(solution)/shard_map/encode/pallas_call | solution.py:128
  29.6 2.9 %decode.2 = (bf16[2,2,128,512]{3,2,1,0:T(8,128)(2,1)S(1)}, bf16[2,2,128,512]{3,2,1,0:T(8,128)(2,1)S(1)}, bf16[2,2,128,512]{3,2,1,0:T(8,128)(2,1)S(1)}, bf16[2,2,128,512]{3,2,1,0:T(8,128)(2,1)S(1)}) custom-call(s32[2]{0:T(128)S(1)} %pad_add_fusion.info_ref, bf16[2,512,1024]{2,1,0:T(8,128)(2,1)S(1)} %encode.5.feat_ref.in_ref.refs_4_, ...), custom_call_target="tpu_custom_call" | custom-call | flops 2147483648 | bytes 4194304 | tf_op jit(solution)/shard_map/decode/pallas_call | solution.py:167
  32.7 0.4 collective-permute-start.10
  33.1 2.9 %decode.3 = (bf16[2,2,128,512]{3,2,1,0:T(8,128)(2,1)S(1)}, bf16[2,2,128,512]{3,2,1,0:T(8,128)(2,1)S(1)}, bf16[2,2,128,512]{3,2,1,0:T(8,128)(2,1)S(1)}, bf16[2,2,128,512]{3,2,1,0:T(8,128)(2,1)S(1)}) custom-call(s32[2]{0:T(128)S(1)} %pad_add_fusion.info_ref, bf16[2,512,1024]{2,1,0:T(8,128)(2,1)S(1)} %encode.5.feat_ref.in_ref.refs_4_, ...), custom_call_target="tpu_custom_call" | custom-call | flops 2147483648 | bytes 4194304 | tf_op jit(solution)/shard_map/decode/pallas_call | solution.py:167
  36.2 0.4 collective-permute-start.9
  36.7 1.5 %collective-permute-start.13 = (bf16[1,2,128,512]{3,2,1,0:T(8,128)(2,1)S(1)}, bf16[1,2,128,512]{3,2,1,0:T(8,128)(2,1)S(1)}, u32[]{:S(2)}, u32[]{:S(2)}) collective-permute-start(bf16[1,2,128,512]{3,2,1,0:T(8,128)(2,1)S(1)} %slice_bitcast_fusion.5), channel_id=1, source_target_pairs={{0,8},{4,12},{8,0},{12,4},{16,24},{20,28},{24,16},{28,20},{1,9},{5... | collective-permute-start | bytes 786440 | tf_op jit(solution)/shard_map/ppermute | solution.py:23
  38.4 1.6 %collective-permute-start.11 = (bf16[1,2,128,512]{3,2,1,0:T(8,128)(2,1)S(1)}, bf16[1,2,128,512]{3,2,1,0:T(8,128)(2,1)S(1)}, u32[]{:S(2)}, u32[]{:S(2)}) collective-permute-start(bf16[1,2,128,512]{3,2,1,0:T(8,128)(2,1)S(1)} %get-tuple-element.120), channel_id=1, source_target_pairs={{0,16},{4,20},{8,24},{12,28},{16,0},{20,4},{24,8},{28,12},{1,17},{... | collective-permute-start | bytes 786440 | tf_op jit(solution)/shard_map/ppermute | solution.py:29
  40.1 0.7 collective-permute-start.16
  41.0 5.0 %collective-permute-done.13 = bf16[1,2,128,512]{3,2,1,0:T(8,128)(2,1)S(1)} collective-permute-done((bf16[1,2,128,512]{3,2,1,0:T(8,128)(2,1)S(1)}, bf16[1,2,128,512]{3,2,1,0:T(8,128)(2,1)S(1)}, u32[]{:S(2)}, u32[]{:S(2)}) %collective-permute-start.13) | collective-permute-done | bytes 262176 | tf_op jit(solution)/shard_map/ppermute | solution.py:23
  46.0 0.5 collective-permute-done.11
  46.6 1.6 %collective-permute-start.17 = (bf16[1,2,128,512]{3,2,1,0:T(8,128)(2,1)S(1)}, bf16[1,2,128,512]{3,2,1,0:T(8,128)(2,1)S(1)}, u32[]{:S(2)}, u32[]{:S(2)}) collective-permute-start(bf16[1,2,128,512]{3,2,1,0:T(8,128)(2,1)S(1)} %fusion.4), channel_id=1, source_target_pairs={{0,16},{4,20},{8,24},{12,28},{16,0},{20,4},{24,8},{28,12},{1,17},{... | collective-permute-start | bytes 786440 | tf_op jit(solution)/shard_map/ppermute | solution.py:29
  48.2 0.9 collective-permute-start.15
  49.1 2.5 %collective-permute-done.16 = bf16[1,2,128,512]{3,2,1,0:T(8,128)(2,1)S(1)} collective-permute-done((bf16[1,2,128,512]{3,2,1,0:T(8,128)(2,1)S(1)}, bf16[1,2,128,512]{3,2,1,0:T(8,128)(2,1)S(1)}, u32[]{:S(2)}, u32[]{:S(2)}) %collective-permute-start.16) | collective-permute-done | bytes 262176 | tf_op jit(solution)/shard_map/ppermute | solution.py:23
  51.5 2.3 %collective-permute-done.17 = bf16[1,2,128,512]{3,2,1,0:T(8,128)(2,1)S(1)} collective-permute-done((bf16[1,2,128,512]{3,2,1,0:T(8,128)(2,1)S(1)}, bf16[1,2,128,512]{3,2,1,0:T(8,128)(2,1)S(1)}, u32[]{:S(2)}, u32[]{:S(2)}) %collective-permute-start.17) | collective-permute-done | bytes 262176 | tf_op jit(solution)/shard_map/ppermute | solution.py:29
  54.0 1.6 %collective-permute-start.18 = (bf16[1,2,128,512]{3,2,1,0:T(8,128)(2,1)S(1)}, bf16[1,2,128,512]{3,2,1,0:T(8,128)(2,1)S(1)}, u32[]{:S(2)}, u32[]{:S(2)}) collective-permute-start(bf16[1,2,128,512]{3,2,1,0:T(8,128)(2,1)S(1)} %get-tuple-element.86), channel_id=1, source_target_pairs={{0,16},{4,20},{8,24},{12,28},{16,0},{20,4},{24,8},{28,12},{1,17},{... | collective-permute-start | bytes 786440 | tf_op jit(solution)/shard_map/ppermute | solution.py:29
  55.6 4.6 %collective-permute-start.20 = (bf16[128,512]{1,0:T(8,128)(2,1)S(1)}, bf16[128,512]{1,0:T(8,128)(2,1)S(1)}, u32[]{:S(2)}, u32[]{:S(2)}) collective-permute-start(bf16[128,512]{1,0:T(8,128)(2,1)S(1)} %get-tuple-element.122), channel_id=1, source_target_pairs={{0,2},{1,3},{2,0},{3,1},{4,6},{5,7},{6,4},{7,5},{8,10},{9,11},{10,... | collective-permute-start | bytes 393224 | tf_op jit(solution)/shard_map/ppermute | solution.py:17
  60.1 1.0 collective-permute-start.19
  61.3 2.5 %collective-permute-start.21 = (bf16[128,512]{1,0:T(8,128)(2,1)S(1)}, bf16[128,512]{1,0:T(8,128)(2,1)S(1)}, u32[]{:S(2)}, u32[]{:S(2)}) collective-permute-start(bf16[128,512]{1,0:T(8,128)(2,1)S(1)} %fusion.13), channel_id=1, source_target_pairs={{0,1},{1,0},{2,3},{3,2},{4,5},{5,4},{6,7},{7,6},{8,9},{9,8},{10,11... | collective-permute-start | bytes 393224 | tf_op jit(solution)/shard_map/ppermute | solution.py:17
  63.8 0.3 turned.5
  64.9 2.8 %collective-permute-done.19 = bf16[128,512]{1,0:T(8,128)(2,1)S(1)} collective-permute-done((bf16[128,512]{1,0:T(8,128)(2,1)S(1)}, bf16[128,512]{1,0:T(8,128)(2,1)S(1)}, u32[]{:S(2)}, u32[]{:S(2)}) %collective-permute-start.19) | collective-permute-done | bytes 131104 | tf_op jit(solution)/shard_map/ppermute | solution.py:17
  67.7 0.9 collective-permute-done.20
  68.6 0.5 collective-permute-done.21
  69.2 0.8 multiply_convert_fusion
  69.9 0.8 collective-permute-start.22
  70.8 1.1 %collective-permute-start.24 = (bf16[128,512]{1,0:T(8,128)(2,1)S(1)}, bf16[128,512]{1,0:T(8,128)(2,1)S(1)}, u32[]{:S(2)}, u32[]{:S(2)}) collective-permute-start(bf16[128,512]{1,0:T(8,128)(2,1)S(1)} %get-tuple-element.115), channel_id=1, source_target_pairs={{0,1},{1,0},{2,3},{3,2},{4,5},{5,4},{6,7},{7,6},{8,9},{9,8},{10,11... | collective-permute-start | bytes 393224 | tf_op jit(solution)/shard_map/ppermute | solution.py:17
  71.9 1.7 %collective-permute-start.26 = (bf16[128,512]{1,0:T(8,128)(2,1)S(1)}, bf16[128,512]{1,0:T(8,128)(2,1)S(1)}, u32[]{:S(2)}, u32[]{:S(2)}) collective-permute-start(bf16[128,512]{1,0:T(8,128)(2,1)S(1)} %get-tuple-element.115), channel_id=1, source_target_pairs={{0,2},{1,3},{2,0},{3,1},{4,6},{5,7},{6,4},{7,5},{8,10},{9,11},{10,... | collective-permute-start | bytes 393224 | tf_op jit(solution)/shard_map/ppermute | solution.py:17
  73.6 1.5 %collective-permute-start.27 = (bf16[128,512]{1,0:T(8,128)(2,1)S(1)}, bf16[128,512]{1,0:T(8,128)(2,1)S(1)}, u32[]{:S(2)}, u32[]{:S(2)}) collective-permute-start(bf16[128,512]{1,0:T(8,128)(2,1)S(1)} %get-tuple-element.115), channel_id=1, source_target_pairs={{0,3},{1,2},{2,1},{3,0},{4,7},{5,6},{6,5},{7,4},{8,11},{9,10},{10,... | collective-permute-start | bytes 393224 | tf_op jit(solution)/shard_map/ppermute | solution.py:17
  75.1 0.6 collective-permute-start.32
  75.8 1.4 %collective-permute-start.23 = (bf16[1,128,512]{2,1,0:T(8,128)(2,1)S(1)}, bf16[1,128,512]{2,1,0:T(8,128)(2,1)S(1)}, u32[]{:S(2)}, u32[]{:S(2)}) collective-permute-start(bf16[1,128,512]{2,1,0:T(8,128)(2,1)S(1)} %collective-permute-done.22.refs_0_), channel_id=1, source_target_pairs={{0,8},{4,12},{8,0},{12,4},{16,24},{20,28},{24,16},{28,20},{1,9},{5... | collective-permute-start | bytes 393224 | tf_op jit(solution)/shard_map/ppermute | solution.py:23
  77.2 1.2 %collective-permute-start.25 = (bf16[1,128,512]{2,1,0:T(8,128)(2,1)S(1)}, bf16[1,128,512]{2,1,0:T(8,128)(2,1)S(1)}, u32[]{:S(2)}, u32[]{:S(2)}) collective-permute-start(bf16[1,128,512]{2,1,0:T(8,128)(2,1)S(1)} %bitcast.87), channel_id=1, source_target_pairs={{0,16},{4,20},{8,24},{12,28},{16,0},{20,4},{24,8},{28,12},{1,17},{... | collective-permute-start | bytes 393224 | tf_op jit(solution)/shard_map/ppermute | solution.py:36
  78.4 5.0 %collective-permute-done.26 = bf16[128,512]{1,0:T(8,128)(2,1)S(1)} collective-permute-done((bf16[128,512]{1,0:T(8,128)(2,1)S(1)}, bf16[128,512]{1,0:T(8,128)(2,1)S(1)}, u32[]{:S(2)}, u32[]{:S(2)}) %collective-permute-start.26) | collective-permute-done | bytes 131104 | tf_op jit(solution)/shard_map/ppermute | solution.py:17
  83.4 0.4 collective-permute-start.33
  83.9 1.7 %collective-permute-start.37 = (bf16[2,128,512]{2,1,0:T(8,128)(2,1)S(1)}, bf16[2,128,512]{2,1,0:T(8,128)(2,1)S(1)}, u32[]{:S(2)}, u32[]{:S(2)}) collective-permute-start(bf16[2,128,512]{2,1,0:T(8,128)(2,1)S(1)} %pad_maximum_fusion.2.refs_2_), channel_id=1, source_target_pairs={{0,8},{4,12},{8,0},{12,4},{16,24},{20,28},{24,16},{28,20},{1,9},{5... | collective-permute-start | bytes 786440 | tf_op jit(solution)/shard_map/ppermute | solution.py:23
  85.6 1.6 %collective-permute-start.28 = (bf16[2,128,512]{2,1,0:T(8,128)(2,1)S(1)}, bf16[2,128,512]{2,1,0:T(8,128)(2,1)S(1)}, u32[]{:S(2)}, u32[]{:S(2)}) collective-permute-start(bf16[2,128,512]{2,1,0:T(8,128)(2,1)S(1)} %pad_maximum_fusion.2.refs_2_), channel_id=1, source_target_pairs={{0,16},{4,20},{8,24},{12,28},{16,0},{20,4},{24,8},{28,12},{1,17},{... | collective-permute-start | bytes 786440 | tf_op jit(solution)/shard_map/ppermute | solution.py:36
  87.1 2.6 %collective-permute-done.33.refs_1_ = bf16[1,128,512]{2,1,0:T(8,128)(2,1)S(1)} collective-permute-done((bf16[1,128,512]{2,1,0:T(8,128)(2,1)S(1)}, bf16[1,128,512]{2,1,0:T(8,128)(2,1)S(1)}, u32[]{:S(2)}, u32[]{:S(2)}) %collective-permute-start.33) | collective-permute-done | bytes 131104 | tf_op jit(solution)/shard_map/ppermute | solution.py:23
  89.7 1.3 %collective-permute-done.34.refs_3_ = bf16[1,128,512]{2,1,0:T(8,128)(2,1)S(1)} collective-permute-done((bf16[1,128,512]{2,1,0:T(8,128)(2,1)S(1)}, bf16[1,128,512]{2,1,0:T(8,128)(2,1)S(1)}, u32[]{:S(2)}, u32[]{:S(2)}) %collective-permute-start.34) | collective-permute-done | bytes 131104 | tf_op jit(solution)/shard_map/ppermute | solution.py:23
  91.1 3.2 %backward_pair.4 = (f32[512,1024]{1,0:T(8,128)S(1)}, bf16[2,1024,2048]{2,1,0:T(8,128)(2,1)}, f32[8,128]{1,0:T(8,128)S(1)}) custom-call(s32[2]{0:T(128)S(1)} %pad_add_fusion.info_ref, bf16[1,128,512]{2,1,0:T(8,128)(2,1)S(1)} %bitcast.86, bf16[1,128,512]{2,1,0:T(8,128)(2,1)S(1)} %bitcast.90, bf16[2,128,512]{2,1,0:T(8,128)(2,1)S(1)} %pad_maximum_fusion.2.refs_2_, ...), custom_call_target="tpu_custom_call" | custom-call | flops 262144 | bytes 262144 | tf_op jit(solution)/shard_map/backward_pair/pallas_call | solution.py:273
  94.3 0.2 collective-permute-start.40
  94.5 0.4 collective-permute-start.39
  95.0 0.4 collective-permute-start.31
  95.4 1.6 %collective-permute-start.42 = (bf16[2,128,512]{2,1,0:T(8,128)(2,1)S(1)}, bf16[2,128,512]{2,1,0:T(8,128)(2,1)S(1)}, u32[]{:S(2)}, u32[]{:S(2)}) collective-permute-start(bf16[2,128,512]{2,1,0:T(8,128)(2,1)S(1)} %collective-permute-done.37.refs_2_), channel_id=1, source_target_pairs={{0,16},{4,20},{8,24},{12,28},{16,0},{20,4},{24,8},{28,12},{1,17},{... | collective-permute-start | bytes 786440 | tf_op jit(solution)/shard_map/ppermute | solution.py:36
  96.9 0.5 collective-permute-start.30
  97.5 3.1 %backward_pair.5 = (f32[512,1024]{1,0:T(8,128)S(1)}, bf16[2,1024,2048]{2,1,0:T(8,128)(2,1)}, f32[8,128]{1,0:T(8,128)S(1)}) custom-call(s32[2]{0:T(128)S(1)} %pad_add_fusion.info_ref, bf16[1,128,512]{2,1,0:T(8,128)(2,1)S(1)} %collective-permute-done.32.refs_0_, ...), custom_call_target="tpu_custom_call", output_to_operand_aliasing={{0}: (9, {}), {1}: (10, {})} | custom-call | flops 262144 | bytes 262144 | tf_op jit(solution)/shard_map/backward_pair/pallas_call | solution.py:273
  100.6 3.2 %backward_pair.6 = (f32[512,1024]{1,0:T(8,128)S(1)}, bf16[2,1024,2048]{2,1,0:T(8,128)(2,1)}, f32[8,128]{1,0:T(8,128)S(1)}) custom-call(s32[2]{0:T(128)S(1)} %pad_add_fusion.info_ref, bf16[1,128,512]{2,1,0:T(8,128)(2,1)S(1)} %collective-permute-done.22.refs_0_, ...), custom_call_target="tpu_custom_call", output_to_operand_aliasing={{0}: (9, {}), {1}: (10, {})} | custom-call | flops 262144 | bytes 262144 | tf_op jit(solution)/shard_map/backward_pair/pallas_call | solution.py:273
  104.0 0.4 collective-permute-start.44
  104.6 1.1 collective-permute-done.44.refs_4_
  105.9 3.2 %backward_pair.7 = (f32[512,1024]{1,0:T(8,128)S(1)}, bf16[2,1024,2048]{2,1,0:T(8,128)(2,1)}, f32[8,128]{1,0:T(8,128)S(1)}) custom-call(s32[2]{0:T(128)S(1)} %pad_add_fusion.info_ref, bf16[1,128,512]{2,1,0:T(8,128)(2,1)S(1)} %collective-permute-done.23.refs_0_, ...), custom_call_target="tpu_custom_call", output_to_operand_aliasing={{0}: (9, {}), {1}: (10, {})} | custom-call | flops 262144 | bytes 262144 | tf_op jit(solution)/shard_map/backward_pair/pallas_call | solution.py:273
  109.1 4.8 %encoder_grad.1 = (bf16[2048,1024]{1,0:T(8,128)(2,1)}, f32[1,1024]{1,0:T(1,128)}, f32[1,1]{1,0:T(1,128)}) custom-call(s32[2]{0:T(128)S(1)} %pad_add_fusion.info_ref, bf16[1,512,512]{2,1,0:T(8,128)(2,1)S(1)} %turned.6.refs_0_, bf16[1,512,512]{2,1,0:T(8,128)(2,1)S(1)} %turned.7.refs_1_, bf16[1,512,512]{2,1,0:T(8,128)(2,1)S(1)} %turned.8.refs_2_, ...), custom_call_target="tpu_custom_call" | custom-call | flops 2147483648 | bytes 9437184 | tf_op jit(solution)/shard_map/encoder_grad/pallas_call | solution.py:330
  (68 shorter events, 3.4 us)
Async XLA Ops:
  0.7 17.5 %copy-start.2 = (bf16[128,512]{1,0:T(8,128)(2,1)S(1)}, bf16[128,512]{1,0:T(8,128)(2,1)}, u32[]{:S(2)}) copy-start(bf16[128,512]{1,0:T(8,128)(2,1)} %param.5) | copy-start | bytes 393220
  0.7 7.1 %collective-permute-start.1 = (bf16[128,512]{1,0:T(8,128)(2,1)}, bf16[128,512]{1,0:T(8,128)(2,1)S(1)}, u32[]{:S(2)}, u32[]{:S(2)}) collective-permute-start(bf16[128,512]{1,0:T(8,128)(2,1)} %param.5), channel_id=1, source_target_pairs={{0,1},{1,0},{2,3},{3,2},{4,5},{5,4},{6,7},{7,6},{8,9},{9,8},{10,11... | collective-permute-start | bytes 393224 | tf_op jit(solution)/shard_map/ppermute | solution.py:17
  3.8 10.0 %collective-permute-start.3 = (bf16[128,512]{1,0:T(8,128)(2,1)}, bf16[128,512]{1,0:T(8,128)(2,1)S(1)}, u32[]{:S(2)}, u32[]{:S(2)}) collective-permute-start(bf16[128,512]{1,0:T(8,128)(2,1)} %param.5), channel_id=1, source_target_pairs={{0,3},{1,2},{2,1},{3,0},{4,7},{5,6},{6,5},{7,4},{8,11},{9,10},{10,... | collective-permute-start | bytes 393224 | tf_op jit(solution)/shard_map/ppermute | solution.py:17
  6.2 12.0 %collective-permute-start.2 = (bf16[128,512]{1,0:T(8,128)(2,1)}, bf16[128,512]{1,0:T(8,128)(2,1)S(1)}, u32[]{:S(2)}, u32[]{:S(2)}) collective-permute-start(bf16[128,512]{1,0:T(8,128)(2,1)} %param.5), channel_id=1, source_target_pairs={{0,2},{1,3},{2,0},{3,1},{4,6},{5,7},{6,4},{7,5},{8,10},{9,11},{10,... | collective-permute-start | bytes 393224 | tf_op jit(solution)/shard_map/ppermute | solution.py:17
  6.4 12.0 %collective-permute-start = (bf16[128,512]{1,0:T(8,128)(2,1)}, bf16[128,512]{1,0:T(8,128)(2,1)S(1)}, u32[]{:S(2)}, u32[]{:S(2)}) collective-permute-start(bf16[128,512]{1,0:T(8,128)(2,1)} %param.5), channel_id=1, source_target_pairs={{0,8},{4,12},{8,0},{12,4},{16,24},{20,28},{24,16},{28,20},{1,9},{5... | collective-permute-start | bytes 393224 | tf_op jit(solution)/shard_map/ppermute | solution.py:23
  13.7 5.0 %collective-permute-start.5 = (bf16[128,512]{1,0:T(8,128)(2,1)S(1)}, bf16[128,512]{1,0:T(8,128)(2,1)S(1)}, u32[]{:S(2)}, u32[]{:S(2)}) collective-permute-start(bf16[128,512]{1,0:T(8,128)(2,1)S(1)} %collective-permute-done.3), channel_id=1, source_target_pairs={{0,8},{4,12},{8,0},{12,4},{16,24},{20,28},{24,16},{28,20},{1,9},{5... | collective-permute-start | bytes 393224 | tf_op jit(solution)/shard_map/ppermute | solution.py:23
  15.2 5.0 %collective-permute-start.4 = (bf16[128,512]{1,0:T(8,128)(2,1)S(1)}, bf16[128,512]{1,0:T(8,128)(2,1)S(1)}, u32[]{:S(2)}, u32[]{:S(2)}) collective-permute-start(bf16[128,512]{1,0:T(8,128)(2,1)S(1)} %collective-permute-done.1), channel_id=1, source_target_pairs={{0,8},{4,12},{8,0},{12,4},{16,24},{20,28},{24,16},{28,20},{1,9},{5... | collective-permute-start | bytes 393224 | tf_op jit(solution)/shard_map/ppermute | solution.py:23
  20.2 1.9 %collective-permute-start.6 = (bf16[4,128,512]{2,1,0:T(8,128)(2,1)S(1)}, bf16[4,128,512]{2,1,0:T(8,128)(2,1)S(1)}, u32[]{:S(2)}, u32[]{:S(2)}) collective-permute-start(bf16[4,128,512]{2,1,0:T(8,128)(2,1)S(1)} %pad_maximum_fusion.refs_0_), channel_id=1, source_target_pairs={{0,4},{4,0},{8,12},{12,8},{16,20},{20,16},{24,28},{28,24},{1,5},{5... | collective-permute-start | bytes 1572872 | tf_op jit(solution)/shard_map/ppermute | solution.py:23
  20.2 5.9 %collective-permute-start.7 = (bf16[128,512]{1,0:T(8,128)(2,1)S(1)}, bf16[128,512]{1,0:T(8,128)(2,1)S(1)}, u32[]{:S(2)}, u32[]{:S(2)}) collective-permute-start(bf16[128,512]{1,0:T(8,128)(2,1)S(1)} %collective-permute-done.2), channel_id=1, source_target_pairs={{0,8},{4,12},{8,0},{12,4},{16,24},{20,28},{24,16},{28,20},{1,9},{5... | collective-permute-start | bytes 393224 | tf_op jit(solution)/shard_map/ppermute | solution.py:23
  26.2 2.0 %copy-start = (f32[1024]{0:T(1024)S(1)}, f32[1024]{0:T(1024)}, u32[]{:S(2)}) copy-start(f32[1024]{0:T(1024)} %param.8) | copy-start | bytes 12292
  26.2 2.0 %collective-permute-start.8 = (bf16[4,128,512]{2,1,0:T(8,128)(2,1)S(1)}, bf16[4,128,512]{2,1,0:T(8,128)(2,1)S(1)}, u32[]{:S(2)}, u32[]{:S(2)}) collective-permute-start(bf16[4,128,512]{2,1,0:T(8,128)(2,1)S(1)} %pad_maximum_fusion.1.refs_0_), channel_id=1, source_target_pairs={{0,4},{4,0},{8,12},{12,8},{16,20},{20,16},{24,28},{28,24},{1,5},{5... | collective-permute-start | bytes 1572872 | tf_op jit(solution)/shard_map/ppermute | solution.py:23
  32.5 4.0 %collective-permute-start.12 = (bf16[2,2,128,512]{3,2,1,0:T(8,128)(2,1)S(1)}, bf16[2,2,128,512]{3,2,1,0:T(8,128)(2,1)S(1)}, u32[]{:S(2)}, u32[]{:S(2)}) collective-permute-start(bf16[2,2,128,512]{3,2,1,0:T(8,128)(2,1)S(1)} %get-tuple-element.79), channel_id=1, source_target_pairs={{0,4},{4,0},{8,12},{12,8},{16,20},{20,16},{24,28},{28,24},{1,5},{5... | collective-permute-start | bytes 1572872 | tf_op jit(solution)/shard_map/ppermute | solution.py:23
  32.7 5.5 %collective-permute-start.10 = (bf16[2,2,128,512]{3,2,1,0:T(8,128)(2,1)S(1)}, bf16[2,2,128,512]{3,2,1,0:T(8,128)(2,1)S(1)}, u32[]{:S(2)}, u32[]{:S(2)}) collective-permute-start(bf16[2,2,128,512]{3,2,1,0:T(8,128)(2,1)S(1)} %get-tuple-element.78), channel_id=1, source_target_pairs={{0,4},{4,0},{8,12},{12,8},{16,20},{20,16},{24,28},{28,24},{1,5},{5... | collective-permute-start | bytes 1572872 | tf_op jit(solution)/shard_map/ppermute | solution.py:23
  36.0 4.0 %collective-permute-start.14 = (bf16[2,2,128,512]{3,2,1,0:T(8,128)(2,1)S(1)}, bf16[2,2,128,512]{3,2,1,0:T(8,128)(2,1)S(1)}, u32[]{:S(2)}, u32[]{:S(2)}) collective-permute-start(bf16[2,2,128,512]{3,2,1,0:T(8,128)(2,1)S(1)} %get-tuple-element.81), channel_id=1, source_target_pairs={{0,4},{4,0},{8,12},{12,8},{16,20},{20,16},{24,28},{28,24},{1,5},{5... | collective-permute-start | bytes 1572872 | tf_op jit(solution)/shard_map/ppermute | solution.py:23
  36.2 4.7 %collective-permute-start.9 = (bf16[2,2,128,512]{3,2,1,0:T(8,128)(2,1)S(1)}, bf16[2,2,128,512]{3,2,1,0:T(8,128)(2,1)S(1)}, u32[]{:S(2)}, u32[]{:S(2)}) collective-permute-start(bf16[2,2,128,512]{3,2,1,0:T(8,128)(2,1)S(1)} %get-tuple-element.75), channel_id=1, source_target_pairs={{0,4},{4,0},{8,12},{12,8},{16,20},{20,16},{24,28},{28,24},{1,5},{5... | collective-permute-start | bytes 1572872 | tf_op jit(solution)/shard_map/ppermute | solution.py:23
  36.7 9.2 %collective-permute-start.13 = (bf16[1,2,128,512]{3,2,1,0:T(8,128)(2,1)S(1)}, bf16[1,2,128,512]{3,2,1,0:T(8,128)(2,1)S(1)}, u32[]{:S(2)}, u32[]{:S(2)}) collective-permute-start(bf16[1,2,128,512]{3,2,1,0:T(8,128)(2,1)S(1)} %slice_bitcast_fusion.5), channel_id=1, source_target_pairs={{0,8},{4,12},{8,0},{12,4},{16,24},{20,28},{24,16},{28,20},{1,9},{5... | collective-permute-start | bytes 786440 | tf_op jit(solution)/shard_map/ppermute | solution.py:23
  38.4 8.1 %collective-permute-start.11 = (bf16[1,2,128,512]{3,2,1,0:T(8,128)(2,1)S(1)}, bf16[1,2,128,512]{3,2,1,0:T(8,128)(2,1)S(1)}, u32[]{:S(2)}, u32[]{:S(2)}) collective-permute-start(bf16[1,2,128,512]{3,2,1,0:T(8,128)(2,1)S(1)} %get-tuple-element.120), channel_id=1, source_target_pairs={{0,16},{4,20},{8,24},{12,28},{16,0},{20,4},{24,8},{28,12},{1,17},{... | collective-permute-start | bytes 786440 | tf_op jit(solution)/shard_map/ppermute | solution.py:29
  40.1 11.4 %collective-permute-start.16 = (bf16[1,2,128,512]{3,2,1,0:T(8,128)(2,1)S(1)}, bf16[1,2,128,512]{3,2,1,0:T(8,128)(2,1)S(1)}, u32[]{:S(2)}, u32[]{:S(2)}) collective-permute-start(bf16[1,2,128,512]{3,2,1,0:T(8,128)(2,1)S(1)} %slice_bitcast_fusion.4), channel_id=1, source_target_pairs={{0,8},{4,12},{8,0},{12,4},{16,24},{20,28},{24,16},{28,20},{1,9},{5... | collective-permute-start | bytes 786440 | tf_op jit(solution)/shard_map/ppermute | solution.py:23
  46.6 7.3 %collective-permute-start.17 = (bf16[1,2,128,512]{3,2,1,0:T(8,128)(2,1)S(1)}, bf16[1,2,128,512]{3,2,1,0:T(8,128)(2,1)S(1)}, u32[]{:S(2)}, u32[]{:S(2)}) collective-permute-start(bf16[1,2,128,512]{3,2,1,0:T(8,128)(2,1)S(1)} %fusion.4), channel_id=1, source_target_pairs={{0,16},{4,20},{8,24},{12,28},{16,0},{20,4},{24,8},{28,12},{1,17},{... | collective-permute-start | bytes 786440 | tf_op jit(solution)/shard_map/ppermute | solution.py:29
  48.2 13.0 %collective-permute-start.15 = (bf16[1,2,128,512]{3,2,1,0:T(8,128)(2,1)S(1)}, bf16[1,2,128,512]{3,2,1,0:T(8,128)(2,1)S(1)}, u32[]{:S(2)}, u32[]{:S(2)}) collective-permute-start(bf16[1,2,128,512]{3,2,1,0:T(8,128)(2,1)S(1)} %fusion.7), channel_id=1, source_target_pairs={{0,8},{4,12},{8,0},{12,4},{16,24},{20,28},{24,16},{28,20},{1,9},{5... | collective-permute-start | bytes 786440 | tf_op jit(solution)/shard_map/ppermute | solution.py:23
  54.0 7.2 %collective-permute-start.18 = (bf16[1,2,128,512]{3,2,1,0:T(8,128)(2,1)S(1)}, bf16[1,2,128,512]{3,2,1,0:T(8,128)(2,1)S(1)}, u32[]{:S(2)}, u32[]{:S(2)}) collective-permute-start(bf16[1,2,128,512]{3,2,1,0:T(8,128)(2,1)S(1)} %get-tuple-element.86), channel_id=1, source_target_pairs={{0,16},{4,20},{8,24},{12,28},{16,0},{20,4},{24,8},{28,12},{1,17},{... | collective-permute-start | bytes 786440 | tf_op jit(solution)/shard_map/ppermute | solution.py:29
  55.6 13.0 %collective-permute-start.20 = (bf16[128,512]{1,0:T(8,128)(2,1)S(1)}, bf16[128,512]{1,0:T(8,128)(2,1)S(1)}, u32[]{:S(2)}, u32[]{:S(2)}) collective-permute-start(bf16[128,512]{1,0:T(8,128)(2,1)S(1)} %get-tuple-element.122), channel_id=1, source_target_pairs={{0,2},{1,3},{2,0},{3,1},{4,6},{5,7},{6,4},{7,5},{8,10},{9,11},{10,... | collective-permute-start | bytes 393224 | tf_op jit(solution)/shard_map/ppermute | solution.py:17
  60.1 9.0 %copy-start.1 = (bf16[128,512]{1,0:T(8,128)(2,1)S(1)}, bf16[128,512]{1,0:T(8,128)(2,1)}, u32[]{:S(2)}) copy-start(bf16[128,512]{1,0:T(8,128)(2,1)} %param.6) | copy-start | bytes 393220
  60.1 7.6 %collective-permute-start.19 = (bf16[128,512]{1,0:T(8,128)(2,1)S(1)}, bf16[128,512]{1,0:T(8,128)(2,1)S(1)}, u32[]{:S(2)}, u32[]{:S(2)}) collective-permute-start(bf16[128,512]{1,0:T(8,128)(2,1)S(1)} %get-tuple-element.121), channel_id=1, source_target_pairs={{0,3},{1,2},{2,1},{3,0},{4,7},{5,6},{6,5},{7,4},{8,11},{9,10},{10,... | collective-permute-start | bytes 393224 | tf_op jit(solution)/shard_map/ppermute | solution.py:17
  61.3 7.9 %collective-permute-start.21 = (bf16[128,512]{1,0:T(8,128)(2,1)S(1)}, bf16[128,512]{1,0:T(8,128)(2,1)S(1)}, u32[]{:S(2)}, u32[]{:S(2)}) collective-permute-start(bf16[128,512]{1,0:T(8,128)(2,1)S(1)} %fusion.13), channel_id=1, source_target_pairs={{0,1},{1,0},{2,3},{3,2},{4,5},{5,4},{6,7},{7,6},{8,9},{9,8},{10,11... | collective-permute-start | bytes 393224 | tf_op jit(solution)/shard_map/ppermute | solution.py:17
  69.9 5.8 %collective-permute-start.22 = (bf16[1,128,512]{2,1,0:T(8,128)(2,1)S(1)}, bf16[1,128,512]{2,1,0:T(8,128)(2,1)S(1)}, u32[]{:S(2)}, u32[]{:S(2)}) collective-permute-start(bf16[1,128,512]{2,1,0:T(8,128)(2,1)S(1)} %bitcast.83), channel_id=1, source_target_pairs={{0,16},{4,20},{8,24},{12,28},{16,0},{20,4},{24,8},{28,12},{1,17},{... | collective-permute-start | bytes 393224 | tf_op jit(solution)/shard_map/ppermute | solution.py:36
  70.8 6.4 %collective-permute-start.24 = (bf16[128,512]{1,0:T(8,128)(2,1)S(1)}, bf16[128,512]{1,0:T(8,128)(2,1)S(1)}, u32[]{:S(2)}, u32[]{:S(2)}) collective-permute-start(bf16[128,512]{1,0:T(8,128)(2,1)S(1)} %get-tuple-element.115), channel_id=1, source_target_pairs={{0,1},{1,0},{2,3},{3,2},{4,5},{5,4},{6,7},{7,6},{8,9},{9,8},{10,11... | collective-permute-start | bytes 393224 | tf_op jit(solution)/shard_map/ppermute | solution.py:17
  71.9 11.5 %collective-permute-start.26 = (bf16[128,512]{1,0:T(8,128)(2,1)S(1)}, bf16[128,512]{1,0:T(8,128)(2,1)S(1)}, u32[]{:S(2)}, u32[]{:S(2)}) collective-permute-start(bf16[128,512]{1,0:T(8,128)(2,1)S(1)} %get-tuple-element.115), channel_id=1, source_target_pairs={{0,2},{1,3},{2,0},{3,1},{4,6},{5,7},{6,4},{7,5},{8,10},{9,11},{10,... | collective-permute-start | bytes 393224 | tf_op jit(solution)/shard_map/ppermute | solution.py:17
  73.6 10.1 %collective-permute-start.27 = (bf16[128,512]{1,0:T(8,128)(2,1)S(1)}, bf16[128,512]{1,0:T(8,128)(2,1)S(1)}, u32[]{:S(2)}, u32[]{:S(2)}) collective-permute-start(bf16[128,512]{1,0:T(8,128)(2,1)S(1)} %get-tuple-element.115), channel_id=1, source_target_pairs={{0,3},{1,2},{2,1},{3,0},{4,7},{5,6},{6,5},{7,4},{8,11},{9,10},{10,... | collective-permute-start | bytes 393224 | tf_op jit(solution)/shard_map/ppermute | solution.py:17
  75.1 8.7 %collective-permute-start.32 = (bf16[1,128,512]{2,1,0:T(8,128)(2,1)S(1)}, bf16[1,128,512]{2,1,0:T(8,128)(2,1)S(1)}, u32[]{:S(2)}, u32[]{:S(2)}) collective-permute-start(bf16[1,128,512]{2,1,0:T(8,128)(2,1)S(1)} %bitcast.84), channel_id=1, source_target_pairs={{0,8},{4,12},{8,0},{12,4},{16,24},{20,28},{24,16},{28,20},{1,9},{5... | collective-permute-start | bytes 393224 | tf_op jit(solution)/shard_map/ppermute | solution.py:23
  75.8 9.8 %collective-permute-start.23 = (bf16[1,128,512]{2,1,0:T(8,128)(2,1)S(1)}, bf16[1,128,512]{2,1,0:T(8,128)(2,1)S(1)}, u32[]{:S(2)}, u32[]{:S(2)}) collective-permute-start(bf16[1,128,512]{2,1,0:T(8,128)(2,1)S(1)} %collective-permute-done.22.refs_0_), channel_id=1, source_target_pairs={{0,8},{4,12},{8,0},{12,4},{16,24},{20,28},{24,16},{28,20},{1,9},{5... | collective-permute-start | bytes 393224 | tf_op jit(solution)/shard_map/ppermute | solution.py:23
  77.2 10.0 %collective-permute-start.25 = (bf16[1,128,512]{2,1,0:T(8,128)(2,1)S(1)}, bf16[1,128,512]{2,1,0:T(8,128)(2,1)S(1)}, u32[]{:S(2)}, u32[]{:S(2)}) collective-permute-start(bf16[1,128,512]{2,1,0:T(8,128)(2,1)S(1)} %bitcast.87), channel_id=1, source_target_pairs={{0,16},{4,20},{8,24},{12,28},{16,0},{20,4},{24,8},{28,12},{1,17},{... | collective-permute-start | bytes 393224 | tf_op jit(solution)/shard_map/ppermute | solution.py:36
  83.4 6.3 %collective-permute-start.33 = (bf16[1,128,512]{2,1,0:T(8,128)(2,1)S(1)}, bf16[1,128,512]{2,1,0:T(8,128)(2,1)S(1)}, u32[]{:S(2)}, u32[]{:S(2)}) collective-permute-start(bf16[1,128,512]{2,1,0:T(8,128)(2,1)S(1)} %bitcast.88), channel_id=1, source_target_pairs={{0,8},{4,12},{8,0},{12,4},{16,24},{20,28},{24,16},{28,20},{1,9},{5... | collective-permute-start | bytes 393224 | tf_op jit(solution)/shard_map/ppermute | solution.py:23
  83.8 6.0 %collective-permute-start.36 = (bf16[2,128,512]{2,1,0:T(8,128)(2,1)S(1)}, bf16[2,128,512]{2,1,0:T(8,128)(2,1)S(1)}, u32[]{:S(2)}, u32[]{:S(2)}) collective-permute-start(bf16[2,128,512]{2,1,0:T(8,128)(2,1)S(1)} %pad_maximum_fusion.2.refs_2_), channel_id=1, source_target_pairs={{0,4},{4,0},{8,12},{12,8},{16,20},{20,16},{24,28},{28,24},{1,5},{5... | collective-permute-start | bytes 786440 | tf_op jit(solution)/shard_map/ppermute | solution.py:23
  83.9 10.4 %collective-permute-start.37 = (bf16[2,128,512]{2,1,0:T(8,128)(2,1)S(1)}, bf16[2,128,512]{2,1,0:T(8,128)(2,1)S(1)}, u32[]{:S(2)}, u32[]{:S(2)}) collective-permute-start(bf16[2,128,512]{2,1,0:T(8,128)(2,1)S(1)} %pad_maximum_fusion.2.refs_2_), channel_id=1, source_target_pairs={{0,8},{4,12},{8,0},{12,4},{16,24},{20,28},{24,16},{28,20},{1,9},{5... | collective-permute-start | bytes 786440 | tf_op jit(solution)/shard_map/ppermute | solution.py:23
  85.6 9.4 %collective-permute-start.28 = (bf16[2,128,512]{2,1,0:T(8,128)(2,1)S(1)}, bf16[2,128,512]{2,1,0:T(8,128)(2,1)S(1)}, u32[]{:S(2)}, u32[]{:S(2)}) collective-permute-start(bf16[2,128,512]{2,1,0:T(8,128)(2,1)S(1)} %pad_maximum_fusion.2.refs_2_), channel_id=1, source_target_pairs={{0,16},{4,20},{8,24},{12,28},{16,0},{20,4},{24,8},{28,12},{1,17},{... | collective-permute-start | bytes 786440 | tf_op jit(solution)/shard_map/ppermute | solution.py:36
  87.1 2.6 %collective-permute-start.35 = (bf16[1,128,512]{2,1,0:T(8,128)(2,1)S(1)}, bf16[1,128,512]{2,1,0:T(8,128)(2,1)S(1)}, u32[]{:S(2)}, u32[]{:S(2)}) collective-permute-start(bf16[1,128,512]{2,1,0:T(8,128)(2,1)S(1)} %bitcast.89), channel_id=1, source_target_pairs={{0,4},{4,0},{8,12},{12,8},{16,20},{20,16},{24,28},{28,24},{1,5},{5... | collective-permute-start | bytes 393224 | tf_op jit(solution)/shard_map/ppermute | solution.py:23
  89.7 1.3 %collective-permute-start.34 = (bf16[1,128,512]{2,1,0:T(8,128)(2,1)S(1)}, bf16[1,128,512]{2,1,0:T(8,128)(2,1)S(1)}, u32[]{:S(2)}, u32[]{:S(2)}) collective-permute-start(bf16[1,128,512]{2,1,0:T(8,128)(2,1)S(1)} %bitcast.85), channel_id=1, source_target_pairs={{0,4},{4,0},{8,12},{12,8},{16,20},{20,16},{24,28},{28,24},{1,5},{5... | collective-permute-start | bytes 393224 | tf_op jit(solution)/shard_map/ppermute | solution.py:23
  94.3 3.2 %collective-permute-start.40 = (bf16[2,128,512]{2,1,0:T(8,128)(2,1)S(1)}, bf16[2,128,512]{2,1,0:T(8,128)(2,1)S(1)}, u32[]{:S(2)}, u32[]{:S(2)}) collective-permute-start(bf16[2,128,512]{2,1,0:T(8,128)(2,1)S(1)} %collective-permute-done.37.refs_2_), channel_id=1, source_target_pairs={{0,4},{4,0},{8,12},{12,8},{16,20},{20,16},{24,28},{28,24},{1,5},{5... | collective-permute-start | bytes 786440 | tf_op jit(solution)/shard_map/ppermute | solution.py:23
  94.5 2.5 %collective-permute-start.39 = (bf16[1,128,512]{2,1,0:T(8,128)(2,1)S(1)}, bf16[1,128,512]{2,1,0:T(8,128)(2,1)S(1)}, u32[]{:S(2)}, u32[]{:S(2)}) collective-permute-start(bf16[1,128,512]{2,1,0:T(8,128)(2,1)S(1)} %collective-permute-done.33.refs_1_), channel_id=1, source_target_pairs={{0,4},{4,0},{8,12},{12,8},{16,20},{20,16},{24,28},{28,24},{1,5},{5... | collective-permute-start | bytes 393224 | tf_op jit(solution)/shard_map/ppermute | solution.py:23
  94.8 2.1 %collective-permute-start.38 = (bf16[1,128,512]{2,1,0:T(8,128)(2,1)S(1)}, bf16[1,128,512]{2,1,0:T(8,128)(2,1)S(1)}, u32[]{:S(2)}, u32[]{:S(2)}) collective-permute-start(bf16[1,128,512]{2,1,0:T(8,128)(2,1)S(1)} %collective-permute-done.32.refs_0_), channel_id=1, source_target_pairs={{0,4},{4,0},{8,12},{12,8},{16,20},{20,16},{24,28},{28,24},{1,5},{5... | collective-permute-start | bytes 393224 | tf_op jit(solution)/shard_map/ppermute | solution.py:23
  95.0 5.6 %collective-permute-start.31 = (bf16[2,128,512]{2,1,0:T(8,128)(2,1)S(1)}, bf16[2,128,512]{2,1,0:T(8,128)(2,1)S(1)}, u32[]{:S(2)}, u32[]{:S(2)}) collective-permute-start(bf16[2,128,512]{2,1,0:T(8,128)(2,1)S(1)} %collective-permute-done.28.refs_2_), channel_id=1, source_target_pairs={{0,4},{4,0},{8,12},{12,8},{16,20},{20,16},{24,28},{28,24},{1,5},{5... | collective-permute-start | bytes 786440 | tf_op jit(solution)/shard_map/ppermute | solution.py:23
  95.4 8.5 %collective-permute-start.42 = (bf16[2,128,512]{2,1,0:T(8,128)(2,1)S(1)}, bf16[2,128,512]{2,1,0:T(8,128)(2,1)S(1)}, u32[]{:S(2)}, u32[]{:S(2)}) collective-permute-start(bf16[2,128,512]{2,1,0:T(8,128)(2,1)S(1)} %collective-permute-done.37.refs_2_), channel_id=1, source_target_pairs={{0,16},{4,20},{8,24},{12,28},{16,0},{20,4},{24,8},{28,12},{1,17},{... | collective-permute-start | bytes 786440 | tf_op jit(solution)/shard_map/ppermute | solution.py:36
  96.9 3.7 %collective-permute-start.29 = (bf16[1,128,512]{2,1,0:T(8,128)(2,1)S(1)}, bf16[1,128,512]{2,1,0:T(8,128)(2,1)S(1)}, u32[]{:S(2)}, u32[]{:S(2)}) collective-permute-start(bf16[1,128,512]{2,1,0:T(8,128)(2,1)S(1)} %collective-permute-done.22.refs_0_), channel_id=1, source_target_pairs={{0,4},{4,0},{8,12},{12,8},{16,20},{20,16},{24,28},{28,24},{1,5},{5... | collective-permute-start | bytes 393224 | tf_op jit(solution)/shard_map/ppermute | solution.py:23
  96.9 3.7 %collective-permute-start.30 = (bf16[1,128,512]{2,1,0:T(8,128)(2,1)S(1)}, bf16[1,128,512]{2,1,0:T(8,128)(2,1)S(1)}, u32[]{:S(2)}, u32[]{:S(2)}) collective-permute-start(bf16[1,128,512]{2,1,0:T(8,128)(2,1)S(1)} %collective-permute-done.25.refs_1_), channel_id=1, source_target_pairs={{0,4},{4,0},{8,12},{12,8},{16,20},{20,16},{24,28},{28,24},{1,5},{5... | collective-permute-start | bytes 393224 | tf_op jit(solution)/shard_map/ppermute | solution.py:23
  97.5 6.6 %collective-permute-start.41 = (bf16[1,128,512]{2,1,0:T(8,128)(2,1)S(1)}, bf16[1,128,512]{2,1,0:T(8,128)(2,1)S(1)}, u32[]{:S(2)}, u32[]{:S(2)}) collective-permute-start(bf16[1,128,512]{2,1,0:T(8,128)(2,1)S(1)} %collective-permute-done.25.refs_1_), channel_id=1, source_target_pairs={{0,8},{4,12},{8,0},{12,4},{16,24},{20,28},{24,16},{28,20},{1,9},{5... | collective-permute-start | bytes 393224 | tf_op jit(solution)/shard_map/ppermute | solution.py:23
  103.9 2.0 %collective-permute-start.45 = (bf16[2,128,512]{2,1,0:T(8,128)(2,1)S(1)}, bf16[2,128,512]{2,1,0:T(8,128)(2,1)S(1)}, u32[]{:S(2)}, u32[]{:S(2)}) collective-permute-start(bf16[2,128,512]{2,1,0:T(8,128)(2,1)S(1)} %collective-permute-done.42.refs_2_), channel_id=1, source_target_pairs={{0,4},{4,0},{8,12},{12,8},{16,20},{20,16},{24,28},{28,24},{1,5},{5... | collective-permute-start | bytes 786440 | tf_op jit(solution)/shard_map/ppermute | solution.py:23
  104.0 1.6 %collective-permute-start.44 = (bf16[1,128,512]{2,1,0:T(8,128)(2,1)S(1)}, bf16[1,128,512]{2,1,0:T(8,128)(2,1)S(1)}, u32[]{:S(2)}, u32[]{:S(2)}) collective-permute-start(bf16[1,128,512]{2,1,0:T(8,128)(2,1)S(1)} %collective-permute-done.41.refs_1_), channel_id=1, source_target_pairs={{0,4},{4,0},{8,12},{12,8},{16,20},{20,16},{24,28},{28,24},{1,5},{5... | collective-permute-start | bytes 393224 | tf_op jit(solution)/shard_map/ppermute | solution.py:23
  104.5 1.4 %collective-permute-start.43 = (bf16[1,128,512]{2,1,0:T(8,128)(2,1)S(1)}, bf16[1,128,512]{2,1,0:T(8,128)(2,1)S(1)}, u32[]{:S(2)}, u32[]{:S(2)}) collective-permute-start(bf16[1,128,512]{2,1,0:T(8,128)(2,1)S(1)} %collective-permute-done.23.refs_0_), channel_id=1, source_target_pairs={{0,4},{4,0},{8,12},{12,8},{16,20},{20,16},{24,28},{28,24},{1,5},{5... | collective-permute-start | bytes 393224 | tf_op jit(solution)/shard_map/ppermute | solution.py:23

commit v8 on v6

--- a/solution.py
+++ b/solution.py
@@ -6,7 +6,7 @@
 from jax.sharding import PartitionSpec as P
 
 loss_scale = 64.0
-tile = 256
+tile = 512
 in_vmem = pl.BlockSpec(memory_space=pltpu.VMEM)
 in_smem = pl.BlockSpec(memory_space=pltpu.SMEM)
 in_hbm = pl.BlockSpec(memory_space=pltpu.HBM)
@@ -144,11 +144,12 @@
     def kernel(info_ref, feat_ref, weight_ref, *out_refs):
         left = feat_ref[0]
         even = info_ref[0] % 2 == 0
+        step = min(tile, cols)
         for pair in range(count):
             piece = pair ^ (info_ref[0] // 2)
-            for start in range(0, cols, tile):
+            for start in range(0, cols, step):
                 low, high = (
-                    dot(left, weight_ref[offset, :, base + start : base + start + tile], (1, 0)).astype(
+                    dot(left, weight_ref[offset, :, base + start : base + start + step], (1, 0)).astype(
                         jnp.bfloat16
                     )
                     for base in (2 * pair * cols, (2 * pair + 1) * cols)
@@ -158,7 +159,7 @@
                     for number, group in enumerate(groups):
                         for place, block in enumerate(group):
                             out_refs[side * len(groups) + number][
-                                piece, place, :, start : start + tile
+                                piece, place, :, start : start + step
                             ] = product[block * rows : (block + 1) * rows]
     out_shape = [
         jax.ShapeDtypeStruct((count, len(group), rows, cols), jnp.bfloat16) for group in groups
@@ -177,11 +178,13 @@
 def turned(value, count):
     _, tok, width = value.shape
 
+    step = min(tile, width)
+
     def kernel(in_ref, out_ref):
         for piece in range(count):
-            for start in range(0, width, tile):
-                out_ref[piece, start : start + tile, :] = in_ref[
-                    piece, :, start : start + tile
+            for start in range(0, width, step):
+                out_ref[piece, start : start + step, :] = in_ref[
+                    piece, :, start : start + step
                 ].T
 
     return pl.pallas_call(
@@ -301,16 +304,18 @@
         mean_ref[...] = scale * jnp.sum(
             tree_sum([ref[...] for ref in square_refs]), (0, 1), keepdims=True
         )
-        for start in range(0, width, tile):
-            here = slice(start, start + tile)
+        copies = []
+        for start in range(0, width, 256):
+            here = slice(start, start + 256)
             kept = jnp.where(mask_ref[1, :, here] > 0.0, grad_ref[:, here], 0.0).astype(jnp.bfloat16)
             preact[:, here] = kept
+            held[0, :, here] = dot(token_refs[0][0], kept, (1, 0)).astype(jnp.bfloat16)
             bias_ref[:, here] = jnp.sum(kept.astype(jnp.float32), 0, keepdims=True)
-        copies = []
         for piece in range(pieces):
-            held[piece] = dot(
-                token_refs[piece // count][piece % count], preact[...], (1, 0)
-            ).astype(jnp.bfloat16)
+            if piece > 0:
+                held[piece] = dot(
+                    token_refs[piece // count][piece % count], preact[...], (1, 0)
+                ).astype(jnp.bfloat16)
             copy = pltpu.make_async_copy(
                 held.at[piece], enc_ref.at[span(info_ref[0] ^ rels[piece], cols)], sems.at[piece]
             )
@@ -480,12 +485,12 @@
         for rel in [rel for stage in stages for rel in stage]:
             parts = groups_of[rel, k]
             if feature_grad is None:
-                parts = [after(parts[0], groups_of[2, 0][0], groups_of[0, 1][0], groups_of[2, 0][1], groups_of[0, 1][1])] + parts[1:]
-            elif (rel > 0 and k == 0) or (rel == 0 and k > 0):
+                parts = [after(parts[0], groups_of[2, 0][0], groups_of[0, 1][0], groups_of[2, 1][0], groups_of[0, 1][1])] + parts[1:]
+            elif (rel > 0 and k == 0) or (rel > 0 and k > 0):
                 parts = [after(part, feature_grad) for part in parts]
             if feature_grad is not None:
                 if rel > 0 and k == 0:
-                    feature_grad = after(feature_grad, groups_of[0, layers - 1][-1])
+                    feature_grad = after(feature_grad, groups_of[2, layers - 1][0], groups_of[2, layers - 1][1])
             feature_grad, dec_grad, squares[k, rel] = backward_pair(
                 info,
                 rel,

time: 117 us -> 114 us (0.974)
  starting transfers between devices: 41.6 us -> 40.4 us
    ppermute x4, waiting for transfers between devices: 6.44 us -> 3.1 us  [from_layer(): return lax.ppermute(value, 'layer', pairs)]
    ppermute x30, waiting for transfers between devices: 14.3 us -> 17.3 us  [over_members(): return lax.ppermute(value, 'layer', pairs)]
    ppermute x30, starting transfers between devices: 16.2 us -> 13.9 us  [over_members(): return lax.ppermute(value, 'layer', pairs)]
  transfers between devices with their start and end apart: 46 -> 46, of which waited for: 21 -> 23; matrix products, arithmetic and copies ran while one was open for 1% -> 1% of each run, Pallas kernels for 19% -> 19%
where the time goes in v8:
time: 114 us
  starting transfers between devices  40.4 us (35%)
  waiting for transfers between devices  37 us (32%)
  Pallas kernels  33.5 us (29%)
  other arithmetic  1.96 us (2%)
    ppermute x9, starting transfers between devices, over_feat(): return lax.ppermute(value, 'feat', pairs)  18.4 us
    ppermute x30, waiting for transfers between devices, over_members(): return lax.ppermute(value, 'layer', pairs)  17.3 us
    ppermute x30, starting transfers between devices, over_members(): return lax.ppermute(value, 'layer', pairs)  13.9 us
    ppermute x9, waiting for transfers between devices, over_feat(): return lax.ppermute(value, 'feat', pairs)  13.8 us
    pallas_call x4, Pallas kernels, backward_pair(): pl.pallas_call(kernel, in_specs=[in_smem] + [in_vmem] * (len(inputs) + 2)...  12.8 us
    pallas_call x2, Pallas kernels, decode(): pl.pallas_call(kernel, in_specs=[in_smem, in_vmem, in_vmem], out_specs=[i...  5.78 us
    ppermute x3, starting transfers between devices, to_layer(): moved = lax.ppermute(value, 'layer', pairs)  4.75 us
    pallas_call x1, Pallas kernels, fetch(): pl.pallas_call(kernel, in_specs=[in_hbm] * len(arrays), out_specs=[in_vme...  4.74 us
  transfers between devices with their start and end apart: 46, of which 23 were waited for; matrix products, arithmetic and copies ran while one was open for 1% of the time, Pallas kernels for 19%

profile of v8, /device:TPU:0, one launch (start us, length us, event | category | flops | bytes accessed | tf_op | source)
XLA Modules:
  0.0 114.2 jit_solution(16990528710058052900)
XLA Ops:
  0.7 3.0 %collective-permute-start.1 = (bf16[128,512]{1,0:T(8,128)(2,1)}, bf16[128,512]{1,0:T(8,128)(2,1)S(1)}, u32[]{:S(2)}, u32[]{:S(2)}) collective-permute-start(bf16[128,512]{1,0:T(8,128)(2,1)} %param.5), channel_id=1, source_target_pairs={{0,1},{1,0},{2,3},{3,2},{4,5},{5,4},{6,7},{7,6},{8,9},{9,8},{10,11... | collective-permute-start | bytes 393224 | tf_op jit(solution)/shard_map/ppermute | solution.py:17
  3.8 2.5 %collective-permute-start.3 = (bf16[128,512]{1,0:T(8,128)(2,1)}, bf16[128,512]{1,0:T(8,128)(2,1)S(1)}, u32[]{:S(2)}, u32[]{:S(2)}) collective-permute-start(bf16[128,512]{1,0:T(8,128)(2,1)} %param.5), channel_id=1, source_target_pairs={{0,3},{1,2},{2,1},{3,0},{4,7},{5,6},{6,5},{7,4},{8,11},{9,10},{10,... | collective-permute-start | bytes 393224 | tf_op jit(solution)/shard_map/ppermute | solution.py:17
  6.4 1.5 %collective-permute-start = (bf16[128,512]{1,0:T(8,128)(2,1)}, bf16[128,512]{1,0:T(8,128)(2,1)S(1)}, u32[]{:S(2)}, u32[]{:S(2)}) collective-permute-start(bf16[128,512]{1,0:T(8,128)(2,1)} %param.5), channel_id=1, source_target_pairs={{0,8},{4,12},{8,0},{12,4},{16,24},{20,28},{24,16},{28,20},{1,9},{5... | collective-permute-start | bytes 393224 | tf_op jit(solution)/shard_map/ppermute | solution.py:23
  7.9 4.7 %fetch.1 = (bf16[2048,1024]{1,0:T(8,128)(2,1)S(1)}, bf16[2,1024,2048]{2,1,0:T(8,128)(2,1)S(1)}) custom-call(bf16[2048,1024]{1,0:T(8,128)(2,1)} %refs_0_.1, bf16[2,1024,2048]{2,1,0:T(8,128)(2,1)} %refs_1_), custom_call_target="tpu_custom_call" | custom-call | bytes 12582912 | tf_op jit(solution)/shard_map/fetch/pallas_call | solution.py:88
  12.6 1.1 collective-permute-done.3
  13.7 1.5 %collective-permute-start.5 = (bf16[128,512]{1,0:T(8,128)(2,1)S(1)}, bf16[128,512]{1,0:T(8,128)(2,1)S(1)}, u32[]{:S(2)}, u32[]{:S(2)}) collective-permute-start(bf16[128,512]{1,0:T(8,128)(2,1)S(1)} %collective-permute-done.3), channel_id=1, source_target_pairs={{0,8},{4,12},{8,0},{12,4},{16,24},{20,28},{24,16},{28,20},{1,9},{5... | collective-permute-start | bytes 393224 | tf_op jit(solution)/shard_map/ppermute | solution.py:23
  15.2 0.5 collective-permute-start.4
  15.8 2.5 %collective-permute-done.2 = bf16[128,512]{1,0:T(8,128)(2,1)S(1)} collective-permute-done((bf16[128,512]{1,0:T(8,128)(2,1)}, bf16[128,512]{1,0:T(8,128)(2,1)S(1)}, u32[]{:S(2)}, u32[]{:S(2)}) %collective-permute-start.2) | collective-permute-done | bytes 131104 | tf_op jit(solution)/shard_map/ppermute | solution.py:17
  18.3 0.4 collective-permute-done.5
  18.7 1.5 %collective-permute-done.4 = bf16[128,512]{1,0:T(8,128)(2,1)S(1)} collective-permute-done((bf16[128,512]{1,0:T(8,128)(2,1)S(1)}, bf16[128,512]{1,0:T(8,128)(2,1)S(1)}, u32[]{:S(2)}, u32[]{:S(2)}) %collective-permute-start.4) | collective-permute-done | bytes 131104 | tf_op jit(solution)/shard_map/ppermute | solution.py:23
  20.2 1.4 %collective-permute-start.7 = (bf16[128,512]{1,0:T(8,128)(2,1)S(1)}, bf16[128,512]{1,0:T(8,128)(2,1)S(1)}, u32[]{:S(2)}, u32[]{:S(2)}) collective-permute-start(bf16[128,512]{1,0:T(8,128)(2,1)S(1)} %collective-permute-done.2), channel_id=1, source_target_pairs={{0,8},{4,12},{8,0},{12,4},{16,24},{20,28},{24,16},{28,20},{1,9},{5... | collective-permute-start | bytes 393224 | tf_op jit(solution)/shard_map/ppermute | solution.py:23
  21.6 0.5 collective-permute-done.6.refs_1_
  22.1 1.8 %encode.3.refs_2_ = f32[512,1024]{1,0:T(8,128)S(1)} custom-call(s32[2]{0:T(128)S(1)} %pad_add_fusion.info_ref, bf16[4,128,512]{2,1,0:T(8,128)(2,1)S(1)} %pad_maximum_fusion.refs_0_, bf16[4,128,512]{2,1,0:T(8,128)(2,1)S(1)} %collective-permute-done.6.refs_1_, bf16[2048,1024]{1,0:T(8,128)(2,1)S(1)} %get-tuple-element.65.refs_2_.refs_1_), custom_call_target="tpu_custom_call" | custom-call | flops 1073741824 | bytes 3145728 | tf_op jit(solution)/shard_map/encode/pallas_call | solution.py:128
  23.9 2.2 %collective-permute-done.7 = bf16[128,512]{1,0:T(8,128)(2,1)S(1)} collective-permute-done((bf16[128,512]{1,0:T(8,128)(2,1)S(1)}, bf16[128,512]{1,0:T(8,128)(2,1)S(1)}, u32[]{:S(2)}, u32[]{:S(2)}) %collective-permute-start.7) | collective-permute-done | bytes 131104 | tf_op jit(solution)/shard_map/ppermute | solution.py:23
  26.3 1.3 %encode.4.refs_2_ = f32[512,1024]{1,0:T(8,128)S(1)} custom-call(s32[2]{0:T(128)S(1)} %pad_add_fusion.info_ref, bf16[4,128,512]{2,1,0:T(8,128)(2,1)S(1)} %pad_maximum_fusion.1.refs_0_, bf16[2048,1024]{1,0:T(8,128)(2,1)S(1)} %get-tuple-element.65.refs_2_.refs_1_, f32[512,1024]{1,0:T(8,128)S(1)} %encode.3.refs_2_), custom_call_target="tpu_custom_call" | custom-call | flops 536870912 | bytes 1572864 | tf_op jit(solution)/shard_map/encode/pallas_call | solution.py:128
  27.5 0.6 collective-permute-done.8.refs_0_
  28.2 1.4 %encode.5.feat_ref.in_ref.refs_4_ = bf16[2,512,1024]{2,1,0:T(8,128)(2,1)S(1)} custom-call(s32[2]{0:T(128)S(1)} %pad_add_fusion.info_ref, bf16[4,128,512]{2,1,0:T(8,128)(2,1)S(1)} %collective-permute-done.8.refs_0_, bf16[2048,1024]{1,0:T(8,128)(2,1)S(1)} %get-tuple-element.65.refs_2_.refs_1_, f32[512,1024]{1,0:T(8,128)S(1)} %encode.4.refs_2_, ...), custom_call_target="tpu_custom_call" | custom-call | flops 536870912 | bytes 1572864 | tf_op jit(solution)/shard_map/encode/pallas_call | solution.py:128
  29.6 2.9 %decode.2 = (bf16[2,2,128,512]{3,2,1,0:T(8,128)(2,1)S(1)}, bf16[2,2,128,512]{3,2,1,0:T(8,128)(2,1)S(1)}, bf16[2,2,128,512]{3,2,1,0:T(8,128)(2,1)S(1)}, bf16[2,2,128,512]{3,2,1,0:T(8,128)(2,1)S(1)}) custom-call(s32[2]{0:T(128)S(1)} %pad_add_fusion.info_ref, bf16[2,512,1024]{2,1,0:T(8,128)(2,1)S(1)} %encode.5.feat_ref.in_ref.refs_4_, ...), custom_call_target="tpu_custom_call" | custom-call | flops 2147483648 | bytes 4194304 | tf_op jit(solution)/shard_map/decode/pallas_call | solution.py:167
  32.7 0.4 collective-permute-start.10
  33.1 2.9 %decode.3 = (bf16[2,2,128,512]{3,2,1,0:T(8,128)(2,1)S(1)}, bf16[2,2,128,512]{3,2,1,0:T(8,128)(2,1)S(1)}, bf16[2,2,128,512]{3,2,1,0:T(8,128)(2,1)S(1)}, bf16[2,2,128,512]{3,2,1,0:T(8,128)(2,1)S(1)}) custom-call(s32[2]{0:T(128)S(1)} %pad_add_fusion.info_ref, bf16[2,512,1024]{2,1,0:T(8,128)(2,1)S(1)} %encode.5.feat_ref.in_ref.refs_4_, ...), custom_call_target="tpu_custom_call" | custom-call | flops 2147483648 | bytes 4194304 | tf_op jit(solution)/shard_map/decode/pallas_call | solution.py:167
  36.2 0.4 collective-permute-start.9
  36.7 1.5 %collective-permute-start.13 = (bf16[1,2,128,512]{3,2,1,0:T(8,128)(2,1)S(1)}, bf16[1,2,128,512]{3,2,1,0:T(8,128)(2,1)S(1)}, u32[]{:S(2)}, u32[]{:S(2)}) collective-permute-start(bf16[1,2,128,512]{3,2,1,0:T(8,128)(2,1)S(1)} %slice_bitcast_fusion.5), channel_id=1, source_target_pairs={{0,8},{4,12},{8,0},{12,4},{16,24},{20,28},{24,16},{28,20},{1,9},{5... | collective-permute-start | bytes 786440 | tf_op jit(solution)/shard_map/ppermute | solution.py:23
  38.4 1.6 %collective-permute-start.11 = (bf16[1,2,128,512]{3,2,1,0:T(8,128)(2,1)S(1)}, bf16[1,2,128,512]{3,2,1,0:T(8,128)(2,1)S(1)}, u32[]{:S(2)}, u32[]{:S(2)}) collective-permute-start(bf16[1,2,128,512]{3,2,1,0:T(8,128)(2,1)S(1)} %get-tuple-element.124), channel_id=1, source_target_pairs={{0,16},{4,20},{8,24},{12,28},{16,0},{20,4},{24,8},{28,12},{1,17},{... | collective-permute-start | bytes 786440 | tf_op jit(solution)/shard_map/ppermute | solution.py:29
  40.1 0.7 collective-permute-start.16
  41.0 5.0 %collective-permute-done.13 = bf16[1,2,128,512]{3,2,1,0:T(8,128)(2,1)S(1)} collective-permute-done((bf16[1,2,128,512]{3,2,1,0:T(8,128)(2,1)S(1)}, bf16[1,2,128,512]{3,2,1,0:T(8,128)(2,1)S(1)}, u32[]{:S(2)}, u32[]{:S(2)}) %collective-permute-start.13) | collective-permute-done | bytes 262176 | tf_op jit(solution)/shard_map/ppermute | solution.py:23
  46.0 0.5 collective-permute-done.11
  46.6 1.6 %collective-permute-start.17 = (bf16[1,2,128,512]{3,2,1,0:T(8,128)(2,1)S(1)}, bf16[1,2,128,512]{3,2,1,0:T(8,128)(2,1)S(1)}, u32[]{:S(2)}, u32[]{:S(2)}) collective-permute-start(bf16[1,2,128,512]{3,2,1,0:T(8,128)(2,1)S(1)} %fusion.4), channel_id=1, source_target_pairs={{0,16},{4,20},{8,24},{12,28},{16,0},{20,4},{24,8},{28,12},{1,17},{... | collective-permute-start | bytes 786440 | tf_op jit(solution)/shard_map/ppermute | solution.py:29
  48.2 0.9 collective-permute-start.15
  49.1 2.5 %collective-permute-done.16 = bf16[1,2,128,512]{3,2,1,0:T(8,128)(2,1)S(1)} collective-permute-done((bf16[1,2,128,512]{3,2,1,0:T(8,128)(2,1)S(1)}, bf16[1,2,128,512]{3,2,1,0:T(8,128)(2,1)S(1)}, u32[]{:S(2)}, u32[]{:S(2)}) %collective-permute-start.16) | collective-permute-done | bytes 262176 | tf_op jit(solution)/shard_map/ppermute | solution.py:23
  51.5 2.3 %collective-permute-done.17 = bf16[1,2,128,512]{3,2,1,0:T(8,128)(2,1)S(1)} collective-permute-done((bf16[1,2,128,512]{3,2,1,0:T(8,128)(2,1)S(1)}, bf16[1,2,128,512]{3,2,1,0:T(8,128)(2,1)S(1)}, u32[]{:S(2)}, u32[]{:S(2)}) %collective-permute-start.17) | collective-permute-done | bytes 262176 | tf_op jit(solution)/shard_map/ppermute | solution.py:29
  54.0 1.6 %collective-permute-start.18 = (bf16[1,2,128,512]{3,2,1,0:T(8,128)(2,1)S(1)}, bf16[1,2,128,512]{3,2,1,0:T(8,128)(2,1)S(1)}, u32[]{:S(2)}, u32[]{:S(2)}) collective-permute-start(bf16[1,2,128,512]{3,2,1,0:T(8,128)(2,1)S(1)} %get-tuple-element.88), channel_id=1, source_target_pairs={{0,16},{4,20},{8,24},{12,28},{16,0},{20,4},{24,8},{28,12},{1,17},{... | collective-permute-start | bytes 786440 | tf_op jit(solution)/shard_map/ppermute | solution.py:29
  55.6 4.6 %collective-permute-start.20 = (bf16[128,512]{1,0:T(8,128)(2,1)S(1)}, bf16[128,512]{1,0:T(8,128)(2,1)S(1)}, u32[]{:S(2)}, u32[]{:S(2)}) collective-permute-start(bf16[128,512]{1,0:T(8,128)(2,1)S(1)} %get-tuple-element.126), channel_id=1, source_target_pairs={{0,2},{1,3},{2,0},{3,1},{4,6},{5,7},{6,4},{7,5},{8,10},{9,11},{10,... | collective-permute-start | bytes 393224 | tf_op jit(solution)/shard_map/ppermute | solution.py:17
  60.1 1.0 collective-permute-start.19
  61.3 2.5 %collective-permute-start.21 = (bf16[128,512]{1,0:T(8,128)(2,1)S(1)}, bf16[128,512]{1,0:T(8,128)(2,1)S(1)}, u32[]{:S(2)}, u32[]{:S(2)}) collective-permute-start(bf16[128,512]{1,0:T(8,128)(2,1)S(1)} %fusion.13), channel_id=1, source_target_pairs={{0,1},{1,0},{2,3},{3,2},{4,5},{5,4},{6,7},{7,6},{8,9},{9,8},{10,11... | collective-permute-start | bytes 393224 | tf_op jit(solution)/shard_map/ppermute | solution.py:17
  64.9 2.8 %collective-permute-done.19 = bf16[128,512]{1,0:T(8,128)(2,1)S(1)} collective-permute-done((bf16[128,512]{1,0:T(8,128)(2,1)S(1)}, bf16[128,512]{1,0:T(8,128)(2,1)S(1)}, u32[]{:S(2)}, u32[]{:S(2)}) %collective-permute-start.19) | collective-permute-done | bytes 131104 | tf_op jit(solution)/shard_map/ppermute | solution.py:17
  67.7 0.9 collective-permute-done.20
  68.6 0.5 collective-permute-done.21
  69.2 0.8 multiply_convert_fusion
  69.9 1.4 %collective-permute-start.24 = (bf16[128,512]{1,0:T(8,128)(2,1)S(1)}, bf16[128,512]{1,0:T(8,128)(2,1)S(1)}, u32[]{:S(2)}, u32[]{:S(2)}) collective-permute-start(bf16[128,512]{1,0:T(8,128)(2,1)S(1)} %get-tuple-element.119), channel_id=1, source_target_pairs={{0,1},{1,0},{2,3},{3,2},{4,5},{5,4},{6,7},{7,6},{8,9},{9,8},{10,11... | collective-permute-start | bytes 393224 | tf_op jit(solution)/shard_map/ppermute | solution.py:17
  71.4 0.5 collective-permute-start.22
  71.9 1.7 %collective-permute-start.26 = (bf16[128,512]{1,0:T(8,128)(2,1)S(1)}, bf16[128,512]{1,0:T(8,128)(2,1)S(1)}, u32[]{:S(2)}, u32[]{:S(2)}) collective-permute-start(bf16[128,512]{1,0:T(8,128)(2,1)S(1)} %get-tuple-element.119), channel_id=1, source_target_pairs={{0,2},{1,3},{2,0},{3,1},{4,6},{5,7},{6,4},{7,5},{8,10},{9,11},{10,... | collective-permute-start | bytes 393224 | tf_op jit(solution)/shard_map/ppermute | solution.py:17
  73.6 1.5 %collective-permute-start.27 = (bf16[128,512]{1,0:T(8,128)(2,1)S(1)}, bf16[128,512]{1,0:T(8,128)(2,1)S(1)}, u32[]{:S(2)}, u32[]{:S(2)}) collective-permute-start(bf16[128,512]{1,0:T(8,128)(2,1)S(1)} %get-tuple-element.119), channel_id=1, source_target_pairs={{0,3},{1,2},{2,1},{3,0},{4,7},{5,6},{6,5},{7,4},{8,11},{9,10},{10,... | collective-permute-start | bytes 393224 | tf_op jit(solution)/shard_map/ppermute | solution.py:17
  75.1 1.0 collective-permute-done.24
  76.2 2.0 %collective-permute-start.33 = (bf16[1,128,512]{2,1,0:T(8,128)(2,1)S(1)}, bf16[1,128,512]{2,1,0:T(8,128)(2,1)S(1)}, u32[]{:S(2)}, u32[]{:S(2)}) collective-permute-start(bf16[1,128,512]{2,1,0:T(8,128)(2,1)S(1)} %bitcast.84), channel_id=1, source_target_pairs={{0,8},{4,12},{8,0},{12,4},{16,24},{20,28},{24,16},{28,20},{1,9},{5... | collective-permute-start | bytes 393224 | tf_op jit(solution)/shard_map/ppermute | solution.py:23
  78.3 4.9 %collective-permute-done.26 = bf16[128,512]{1,0:T(8,128)(2,1)S(1)} collective-permute-done((bf16[128,512]{1,0:T(8,128)(2,1)S(1)}, bf16[128,512]{1,0:T(8,128)(2,1)S(1)}, u32[]{:S(2)}, u32[]{:S(2)}) %collective-permute-start.26) | collective-permute-done | bytes 131104 | tf_op jit(solution)/shard_map/ppermute | solution.py:17
  83.2 1.4 %collective-permute-start.25 = (bf16[1,128,512]{2,1,0:T(8,128)(2,1)S(1)}, bf16[1,128,512]{2,1,0:T(8,128)(2,1)S(1)}, u32[]{:S(2)}, u32[]{:S(2)}) collective-permute-start(bf16[1,128,512]{2,1,0:T(8,128)(2,1)S(1)} %bitcast.88), channel_id=1, source_target_pairs={{0,16},{4,20},{8,24},{12,28},{16,0},{20,4},{24,8},{28,12},{1,17},{... | collective-permute-start | bytes 393224 | tf_op jit(solution)/shard_map/ppermute | solution.py:36
  84.9 0.8 collective-permute-start.29
  85.7 2.7 %collective-permute-done.25.refs_1_ = bf16[1,128,512]{2,1,0:T(8,128)(2,1)S(1)} collective-permute-done((bf16[1,128,512]{2,1,0:T(8,128)(2,1)S(1)}, bf16[1,128,512]{2,1,0:T(8,128)(2,1)S(1)}, u32[]{:S(2)}, u32[]{:S(2)}) %collective-permute-start.25) | collective-permute-done | bytes 131104 | tf_op jit(solution)/shard_map/ppermute | solution.py:36
  88.5 0.3 collective-permute-start.41
  88.8 1.0 collective-permute-done.34.refs_3_
  89.8 3.2 %backward_pair.4 = (f32[512,1024]{1,0:T(8,128)S(1)}, bf16[2,1024,2048]{2,1,0:T(8,128)(2,1)}, f32[8,128]{1,0:T(8,128)S(1)}) custom-call(s32[2]{0:T(128)S(1)} %pad_add_fusion.info_ref, bf16[1,128,512]{2,1,0:T(8,128)(2,1)S(1)} %bitcast.86, bf16[1,128,512]{2,1,0:T(8,128)(2,1)S(1)} %bitcast.90, bf16[2,128,512]{2,1,0:T(8,128)(2,1)S(1)} %pad_maximum_fusion.2.refs_2_, ...), custom_call_target="tpu_custom_call" | custom-call | flops 262144 | bytes 262144 | tf_op jit(solution)/shard_map/backward_pair/pallas_call | solution.py:273
  93.0 0.9 collective-permute-done.37.refs_2_
  94.0 0.5 collective-permute-start.39
  94.5 0.5 collective-permute-start.32
  95.0 1.3 %collective-permute-done.41.refs_1_ = bf16[1,128,512]{2,1,0:T(8,128)(2,1)S(1)} collective-permute-done((bf16[1,128,512]{2,1,0:T(8,128)(2,1)S(1)}, bf16[1,128,512]{2,1,0:T(8,128)(2,1)S(1)}, u32[]{:S(2)}, u32[]{:S(2)}) %collective-permute-start.41) | collective-permute-done | bytes 131104 | tf_op jit(solution)/shard_map/ppermute | solution.py:23
  96.3 0.6 collective-permute-start.42
  96.9 0.5 collective-permute-start.31
  97.4 3.1 %backward_pair.5 = (f32[512,1024]{1,0:T(8,128)S(1)}, bf16[2,1024,2048]{2,1,0:T(8,128)(2,1)}, f32[8,128]{1,0:T(8,128)S(1)}) custom-call(s32[2]{0:T(128)S(1)} %pad_add_fusion.info_ref, bf16[1,128,512]{2,1,0:T(8,128)(2,1)S(1)} %collective-permute-done.33.refs_0_, ...), custom_call_target="tpu_custom_call", output_to_operand_aliasing={{0}: (9, {}), {1}: (10, {})} | custom-call | flops 262144 | bytes 262144 | tf_op jit(solution)/shard_map/backward_pair/pallas_call | solution.py:273
  100.6 3.2 %backward_pair.6 = (f32[512,1024]{1,0:T(8,128)S(1)}, bf16[2,1024,2048]{2,1,0:T(8,128)(2,1)}, f32[8,128]{1,0:T(8,128)S(1)}) custom-call(s32[2]{0:T(128)S(1)} %pad_add_fusion.info_ref, bf16[1,128,512]{2,1,0:T(8,128)(2,1)S(1)} %collective-permute-done.22.refs_0_, ...), custom_call_target="tpu_custom_call", output_to_operand_aliasing={{0}: (9, {}), {1}: (10, {})} | custom-call | flops 262144 | bytes 262144 | tf_op jit(solution)/shard_map/backward_pair/pallas_call | solution.py:273
  103.8 0.3 collective-permute-done.42.refs_2_
  104.2 0.5 collective-permute-start.44
  104.7 1.2 %collective-permute-done.44.refs_4_ = bf16[1,128,512]{2,1,0:T(8,128)(2,1)S(1)} collective-permute-done((bf16[1,128,512]{2,1,0:T(8,128)(2,1)S(1)}, bf16[1,128,512]{2,1,0:T(8,128)(2,1)S(1)}, u32[]{:S(2)}, u32[]{:S(2)}) %collective-permute-start.44) | collective-permute-done | bytes 131104 | tf_op jit(solution)/shard_map/ppermute | solution.py:23
  106.1 3.2 %backward_pair.7 = (f32[512,1024]{1,0:T(8,128)S(1)}, bf16[2,1024,2048]{2,1,0:T(8,128)(2,1)}, f32[8,128]{1,0:T(8,128)S(1)}) custom-call(s32[2]{0:T(128)S(1)} %pad_add_fusion.info_ref, bf16[1,128,512]{2,1,0:T(8,128)(2,1)S(1)} %collective-permute-done.23.refs_0_, ...), custom_call_target="tpu_custom_call", output_to_operand_aliasing={{0}: (9, {}), {1}: (10, {})} | custom-call | flops 262144 | bytes 262144 | tf_op jit(solution)/shard_map/backward_pair/pallas_call | solution.py:273
  109.3 4.7 %encoder_grad.1 = (bf16[2048,1024]{1,0:T(8,128)(2,1)}, f32[1,1024]{1,0:T(1,128)}, f32[1,1]{1,0:T(1,128)}) custom-call(s32[2]{0:T(128)S(1)} %pad_add_fusion.info_ref, bf16[1,512,512]{2,1,0:T(8,128)(2,1)S(1)} %turned.6.refs_0_, bf16[1,512,512]{2,1,0:T(8,128)(2,1)S(1)} %turned.7.refs_1_, bf16[1,512,512]{2,1,0:T(8,128)(2,1)S(1)} %turned.8.refs_2_, ...), custom_call_target="tpu_custom_call" | custom-call | flops 2147483648 | bytes 9437184 | tf_op jit(solution)/shard_map/encoder_grad/pallas_call | solution.py:327
  (68 shorter events, 3.5 us)
Async XLA Ops:
  0.7 17.5 %copy-start.2 = (bf16[128,512]{1,0:T(8,128)(2,1)S(1)}, bf16[128,512]{1,0:T(8,128)(2,1)}, u32[]{:S(2)}) copy-start(bf16[128,512]{1,0:T(8,128)(2,1)} %param.5) | copy-start | bytes 393220
  0.7 7.1 %collective-permute-start.1 = (bf16[128,512]{1,0:T(8,128)(2,1)}, bf16[128,512]{1,0:T(8,128)(2,1)S(1)}, u32[]{:S(2)}, u32[]{:S(2)}) collective-permute-start(bf16[128,512]{1,0:T(8,128)(2,1)} %param.5), channel_id=1, source_target_pairs={{0,1},{1,0},{2,3},{3,2},{4,5},{5,4},{6,7},{7,6},{8,9},{9,8},{10,11... | collective-permute-start | bytes 393224 | tf_op jit(solution)/shard_map/ppermute | solution.py:17
  3.8 10.0 %collective-permute-start.3 = (bf16[128,512]{1,0:T(8,128)(2,1)}, bf16[128,512]{1,0:T(8,128)(2,1)S(1)}, u32[]{:S(2)}, u32[]{:S(2)}) collective-permute-start(bf16[128,512]{1,0:T(8,128)(2,1)} %param.5), channel_id=1, source_target_pairs={{0,3},{1,2},{2,1},{3,0},{4,7},{5,6},{6,5},{7,4},{8,11},{9,10},{10,... | collective-permute-start | bytes 393224 | tf_op jit(solution)/shard_map/ppermute | solution.py:17
  6.2 12.0 %collective-permute-start.2 = (bf16[128,512]{1,0:T(8,128)(2,1)}, bf16[128,512]{1,0:T(8,128)(2,1)S(1)}, u32[]{:S(2)}, u32[]{:S(2)}) collective-permute-start(bf16[128,512]{1,0:T(8,128)(2,1)} %param.5), channel_id=1, source_target_pairs={{0,2},{1,3},{2,0},{3,1},{4,6},{5,7},{6,4},{7,5},{8,10},{9,11},{10,... | collective-permute-start | bytes 393224 | tf_op jit(solution)/shard_map/ppermute | solution.py:17
  6.4 12.0 %collective-permute-start = (bf16[128,512]{1,0:T(8,128)(2,1)}, bf16[128,512]{1,0:T(8,128)(2,1)S(1)}, u32[]{:S(2)}, u32[]{:S(2)}) collective-permute-start(bf16[128,512]{1,0:T(8,128)(2,1)} %param.5), channel_id=1, source_target_pairs={{0,8},{4,12},{8,0},{12,4},{16,24},{20,28},{24,16},{28,20},{1,9},{5... | collective-permute-start | bytes 393224 | tf_op jit(solution)/shard_map/ppermute | solution.py:23
  13.7 5.0 %collective-permute-start.5 = (bf16[128,512]{1,0:T(8,128)(2,1)S(1)}, bf16[128,512]{1,0:T(8,128)(2,1)S(1)}, u32[]{:S(2)}, u32[]{:S(2)}) collective-permute-start(bf16[128,512]{1,0:T(8,128)(2,1)S(1)} %collective-permute-done.3), channel_id=1, source_target_pairs={{0,8},{4,12},{8,0},{12,4},{16,24},{20,28},{24,16},{28,20},{1,9},{5... | collective-permute-start | bytes 393224 | tf_op jit(solution)/shard_map/ppermute | solution.py:23
  15.2 5.0 %collective-permute-start.4 = (bf16[128,512]{1,0:T(8,128)(2,1)S(1)}, bf16[128,512]{1,0:T(8,128)(2,1)S(1)}, u32[]{:S(2)}, u32[]{:S(2)}) collective-permute-start(bf16[128,512]{1,0:T(8,128)(2,1)S(1)} %collective-permute-done.1), channel_id=1, source_target_pairs={{0,8},{4,12},{8,0},{12,4},{16,24},{20,28},{24,16},{28,20},{1,9},{5... | collective-permute-start | bytes 393224 | tf_op jit(solution)/shard_map/ppermute | solution.py:23
  20.2 1.9 %collective-permute-start.6 = (bf16[4,128,512]{2,1,0:T(8,128)(2,1)S(1)}, bf16[4,128,512]{2,1,0:T(8,128)(2,1)S(1)}, u32[]{:S(2)}, u32[]{:S(2)}) collective-permute-start(bf16[4,128,512]{2,1,0:T(8,128)(2,1)S(1)} %pad_maximum_fusion.refs_0_), channel_id=1, source_target_pairs={{0,4},{4,0},{8,12},{12,8},{16,20},{20,16},{24,28},{28,24},{1,5},{5... | collective-permute-start | bytes 1572872 | tf_op jit(solution)/shard_map/ppermute | solution.py:23
  20.2 5.9 %collective-permute-start.7 = (bf16[128,512]{1,0:T(8,128)(2,1)S(1)}, bf16[128,512]{1,0:T(8,128)(2,1)S(1)}, u32[]{:S(2)}, u32[]{:S(2)}) collective-permute-start(bf16[128,512]{1,0:T(8,128)(2,1)S(1)} %collective-permute-done.2), channel_id=1, source_target_pairs={{0,8},{4,12},{8,0},{12,4},{16,24},{20,28},{24,16},{28,20},{1,9},{5... | collective-permute-start | bytes 393224 | tf_op jit(solution)/shard_map/ppermute | solution.py:23
  26.2 2.0 %copy-start = (f32[1024]{0:T(1024)S(1)}, f32[1024]{0:T(1024)}, u32[]{:S(2)}) copy-start(f32[1024]{0:T(1024)} %param.8) | copy-start | bytes 12292
  26.2 2.0 %collective-permute-start.8 = (bf16[4,128,512]{2,1,0:T(8,128)(2,1)S(1)}, bf16[4,128,512]{2,1,0:T(8,128)(2,1)S(1)}, u32[]{:S(2)}, u32[]{:S(2)}) collective-permute-start(bf16[4,128,512]{2,1,0:T(8,128)(2,1)S(1)} %pad_maximum_fusion.1.refs_0_), channel_id=1, source_target_pairs={{0,4},{4,0},{8,12},{12,8},{16,20},{20,16},{24,28},{28,24},{1,5},{5... | collective-permute-start | bytes 1572872 | tf_op jit(solution)/shard_map/ppermute | solution.py:23
  32.5 4.0 %collective-permute-start.12 = (bf16[2,2,128,512]{3,2,1,0:T(8,128)(2,1)S(1)}, bf16[2,2,128,512]{3,2,1,0:T(8,128)(2,1)S(1)}, u32[]{:S(2)}, u32[]{:S(2)}) collective-permute-start(bf16[2,2,128,512]{3,2,1,0:T(8,128)(2,1)S(1)} %get-tuple-element.81), channel_id=1, source_target_pairs={{0,4},{4,0},{8,12},{12,8},{16,20},{20,16},{24,28},{28,24},{1,5},{5... | collective-permute-start | bytes 1572872 | tf_op jit(solution)/shard_map/ppermute | solution.py:23
  32.7 5.5 %collective-permute-start.10 = (bf16[2,2,128,512]{3,2,1,0:T(8,128)(2,1)S(1)}, bf16[2,2,128,512]{3,2,1,0:T(8,128)(2,1)S(1)}, u32[]{:S(2)}, u32[]{:S(2)}) collective-permute-start(bf16[2,2,128,512]{3,2,1,0:T(8,128)(2,1)S(1)} %get-tuple-element.80), channel_id=1, source_target_pairs={{0,4},{4,0},{8,12},{12,8},{16,20},{20,16},{24,28},{28,24},{1,5},{5... | collective-permute-start | bytes 1572872 | tf_op jit(solution)/shard_map/ppermute | solution.py:23
  36.0 4.0 %collective-permute-start.14 = (bf16[2,2,128,512]{3,2,1,0:T(8,128)(2,1)S(1)}, bf16[2,2,128,512]{3,2,1,0:T(8,128)(2,1)S(1)}, u32[]{:S(2)}, u32[]{:S(2)}) collective-permute-start(bf16[2,2,128,512]{3,2,1,0:T(8,128)(2,1)S(1)} %get-tuple-element.83), channel_id=1, source_target_pairs={{0,4},{4,0},{8,12},{12,8},{16,20},{20,16},{24,28},{28,24},{1,5},{5... | collective-permute-start | bytes 1572872 | tf_op jit(solution)/shard_map/ppermute | solution.py:23
  36.2 4.7 %collective-permute-start.9 = (bf16[2,2,128,512]{3,2,1,0:T(8,128)(2,1)S(1)}, bf16[2,2,128,512]{3,2,1,0:T(8,128)(2,1)S(1)}, u32[]{:S(2)}, u32[]{:S(2)}) collective-permute-start(bf16[2,2,128,512]{3,2,1,0:T(8,128)(2,1)S(1)} %get-tuple-element.77), channel_id=1, source_target_pairs={{0,4},{4,0},{8,12},{12,8},{16,20},{20,16},{24,28},{28,24},{1,5},{5... | collective-permute-start | bytes 1572872 | tf_op jit(solution)/shard_map/ppermute | solution.py:23
  36.7 9.2 %collective-permute-start.13 = (bf16[1,2,128,512]{3,2,1,0:T(8,128)(2,1)S(1)}, bf16[1,2,128,512]{3,2,1,0:T(8,128)(2,1)S(1)}, u32[]{:S(2)}, u32[]{:S(2)}) collective-permute-start(bf16[1,2,128,512]{3,2,1,0:T(8,128)(2,1)S(1)} %slice_bitcast_fusion.5), channel_id=1, source_target_pairs={{0,8},{4,12},{8,0},{12,4},{16,24},{20,28},{24,16},{28,20},{1,9},{5... | collective-permute-start | bytes 786440 | tf_op jit(solution)/shard_map/ppermute | solution.py:23
  38.4 8.1 %collective-permute-start.11 = (bf16[1,2,128,512]{3,2,1,0:T(8,128)(2,1)S(1)}, bf16[1,2,128,512]{3,2,1,0:T(8,128)(2,1)S(1)}, u32[]{:S(2)}, u32[]{:S(2)}) collective-permute-start(bf16[1,2,128,512]{3,2,1,0:T(8,128)(2,1)S(1)} %get-tuple-element.124), channel_id=1, source_target_pairs={{0,16},{4,20},{8,24},{12,28},{16,0},{20,4},{24,8},{28,12},{1,17},{... | collective-permute-start | bytes 786440 | tf_op jit(solution)/shard_map/ppermute | solution.py:29
  40.1 11.4 %collective-permute-start.16 = (bf16[1,2,128,512]{3,2,1,0:T(8,128)(2,1)S(1)}, bf16[1,2,128,512]{3,2,1,0:T(8,128)(2,1)S(1)}, u32[]{:S(2)}, u32[]{:S(2)}) collective-permute-start(bf16[1,2,128,512]{3,2,1,0:T(8,128)(2,1)S(1)} %slice_bitcast_fusion.4), channel_id=1, source_target_pairs={{0,8},{4,12},{8,0},{12,4},{16,24},{20,28},{24,16},{28,20},{1,9},{5... | collective-permute-start | bytes 786440 | tf_op jit(solution)/shard_map/ppermute | solution.py:23
  46.6 7.3 %collective-permute-start.17 = (bf16[1,2,128,512]{3,2,1,0:T(8,128)(2,1)S(1)}, bf16[1,2,128,512]{3,2,1,0:T(8,128)(2,1)S(1)}, u32[]{:S(2)}, u32[]{:S(2)}) collective-permute-start(bf16[1,2,128,512]{3,2,1,0:T(8,128)(2,1)S(1)} %fusion.4), channel_id=1, source_target_pairs={{0,16},{4,20},{8,24},{12,28},{16,0},{20,4},{24,8},{28,12},{1,17},{... | collective-permute-start | bytes 786440 | tf_op jit(solution)/shard_map/ppermute | solution.py:29
  48.2 13.0 %collective-permute-start.15 = (bf16[1,2,128,512]{3,2,1,0:T(8,128)(2,1)S(1)}, bf16[1,2,128,512]{3,2,1,0:T(8,128)(2,1)S(1)}, u32[]{:S(2)}, u32[]{:S(2)}) collective-permute-start(bf16[1,2,128,512]{3,2,1,0:T(8,128)(2,1)S(1)} %fusion.7), channel_id=1, source_target_pairs={{0,8},{4,12},{8,0},{12,4},{16,24},{20,28},{24,16},{28,20},{1,9},{5... | collective-permute-start | bytes 786440 | tf_op jit(solution)/shard_map/ppermute | solution.py:23
  54.0 7.2 %collective-permute-start.18 = (bf16[1,2,128,512]{3,2,1,0:T(8,128)(2,1)S(1)}, bf16[1,2,128,512]{3,2,1,0:T(8,128)(2,1)S(1)}, u32[]{:S(2)}, u32[]{:S(2)}) collective-permute-start(bf16[1,2,128,512]{3,2,1,0:T(8,128)(2,1)S(1)} %get-tuple-element.88), channel_id=1, source_target_pairs={{0,16},{4,20},{8,24},{12,28},{16,0},{20,4},{24,8},{28,12},{1,17},{... | collective-permute-start | bytes 786440 | tf_op jit(solution)/shard_map/ppermute | solution.py:29
  55.6 13.0 %collective-permute-start.20 = (bf16[128,512]{1,0:T(8,128)(2,1)S(1)}, bf16[128,512]{1,0:T(8,128)(2,1)S(1)}, u32[]{:S(2)}, u32[]{:S(2)}) collective-permute-start(bf16[128,512]{1,0:T(8,128)(2,1)S(1)} %get-tuple-element.126), channel_id=1, source_target_pairs={{0,2},{1,3},{2,0},{3,1},{4,6},{5,7},{6,4},{7,5},{8,10},{9,11},{10,... | collective-permute-start | bytes 393224 | tf_op jit(solution)/shard_map/ppermute | solution.py:17
  60.1 9.0 %copy-start.1 = (bf16[128,512]{1,0:T(8,128)(2,1)S(1)}, bf16[128,512]{1,0:T(8,128)(2,1)}, u32[]{:S(2)}) copy-start(bf16[128,512]{1,0:T(8,128)(2,1)} %param.6) | copy-start | bytes 393220
  60.1 7.6 %collective-permute-start.19 = (bf16[128,512]{1,0:T(8,128)(2,1)S(1)}, bf16[128,512]{1,0:T(8,128)(2,1)S(1)}, u32[]{:S(2)}, u32[]{:S(2)}) collective-permute-start(bf16[128,512]{1,0:T(8,128)(2,1)S(1)} %get-tuple-element.125), channel_id=1, source_target_pairs={{0,3},{1,2},{2,1},{3,0},{4,7},{5,6},{6,5},{7,4},{8,11},{9,10},{10,... | collective-permute-start | bytes 393224 | tf_op jit(solution)/shard_map/ppermute | solution.py:17
  61.3 7.9 %collective-permute-start.21 = (bf16[128,512]{1,0:T(8,128)(2,1)S(1)}, bf16[128,512]{1,0:T(8,128)(2,1)S(1)}, u32[]{:S(2)}, u32[]{:S(2)}) collective-permute-start(bf16[128,512]{1,0:T(8,128)(2,1)S(1)} %fusion.13), channel_id=1, source_target_pairs={{0,1},{1,0},{2,3},{3,2},{4,5},{5,4},{6,7},{7,6},{8,9},{9,8},{10,11... | collective-permute-start | bytes 393224 | tf_op jit(solution)/shard_map/ppermute | solution.py:17
  69.9 6.2 %collective-permute-start.24 = (bf16[128,512]{1,0:T(8,128)(2,1)S(1)}, bf16[128,512]{1,0:T(8,128)(2,1)S(1)}, u32[]{:S(2)}, u32[]{:S(2)}) collective-permute-start(bf16[128,512]{1,0:T(8,128)(2,1)S(1)} %get-tuple-element.119), channel_id=1, source_target_pairs={{0,1},{1,0},{2,3},{3,2},{4,5},{5,4},{6,7},{7,6},{8,9},{9,8},{10,11... | collective-permute-start | bytes 393224 | tf_op jit(solution)/shard_map/ppermute | solution.py:17
  71.4 6.9 %collective-permute-start.22 = (bf16[1,128,512]{2,1,0:T(8,128)(2,1)S(1)}, bf16[1,128,512]{2,1,0:T(8,128)(2,1)S(1)}, u32[]{:S(2)}, u32[]{:S(2)}) collective-permute-start(bf16[1,128,512]{2,1,0:T(8,128)(2,1)S(1)} %bitcast.83), channel_id=1, source_target_pairs={{0,16},{4,20},{8,24},{12,28},{16,0},{20,4},{24,8},{28,12},{1,17},{... | collective-permute-start | bytes 393224 | tf_op jit(solution)/shard_map/ppermute | solution.py:36
  71.9 11.3 %collective-permute-start.26 = (bf16[128,512]{1,0:T(8,128)(2,1)S(1)}, bf16[128,512]{1,0:T(8,128)(2,1)S(1)}, u32[]{:S(2)}, u32[]{:S(2)}) collective-permute-start(bf16[128,512]{1,0:T(8,128)(2,1)S(1)} %get-tuple-element.119), channel_id=1, source_target_pairs={{0,2},{1,3},{2,0},{3,1},{4,6},{5,7},{6,4},{7,5},{8,10},{9,11},{10,... | collective-permute-start | bytes 393224 | tf_op jit(solution)/shard_map/ppermute | solution.py:17
  73.6 11.1 %collective-permute-start.27 = (bf16[128,512]{1,0:T(8,128)(2,1)S(1)}, bf16[128,512]{1,0:T(8,128)(2,1)S(1)}, u32[]{:S(2)}, u32[]{:S(2)}) collective-permute-start(bf16[128,512]{1,0:T(8,128)(2,1)S(1)} %get-tuple-element.119), channel_id=1, source_target_pairs={{0,3},{1,2},{2,1},{3,0},{4,7},{5,6},{6,5},{7,4},{8,11},{9,10},{10,... | collective-permute-start | bytes 393224 | tf_op jit(solution)/shard_map/ppermute | solution.py:17
  76.2 8.5 %collective-permute-start.28 = (bf16[1,128,512]{2,1,0:T(8,128)(2,1)S(1)}, bf16[1,128,512]{2,1,0:T(8,128)(2,1)S(1)}, u32[]{:S(2)}, u32[]{:S(2)}) collective-permute-start(bf16[1,128,512]{2,1,0:T(8,128)(2,1)S(1)} %bitcast.87), channel_id=1, source_target_pairs={{0,8},{4,12},{8,0},{12,4},{16,24},{20,28},{24,16},{28,20},{1,9},{5... | collective-permute-start | bytes 393224 | tf_op jit(solution)/shard_map/ppermute | solution.py:23
  76.2 8.7 %collective-permute-start.33 = (bf16[1,128,512]{2,1,0:T(8,128)(2,1)S(1)}, bf16[1,128,512]{2,1,0:T(8,128)(2,1)S(1)}, u32[]{:S(2)}, u32[]{:S(2)}) collective-permute-start(bf16[1,128,512]{2,1,0:T(8,128)(2,1)S(1)} %bitcast.84), channel_id=1, source_target_pairs={{0,8},{4,12},{8,0},{12,4},{16,24},{20,28},{24,16},{28,20},{1,9},{5... | collective-permute-start | bytes 393224 | tf_op jit(solution)/shard_map/ppermute | solution.py:23
  78.2 7.5 %collective-permute-start.23 = (bf16[1,128,512]{2,1,0:T(8,128)(2,1)S(1)}, bf16[1,128,512]{2,1,0:T(8,128)(2,1)S(1)}, u32[]{:S(2)}, u32[]{:S(2)}) collective-permute-start(bf16[1,128,512]{2,1,0:T(8,128)(2,1)S(1)} %collective-permute-done.22.refs_0_), channel_id=1, source_target_pairs={{0,8},{4,12},{8,0},{12,4},{16,24},{20,28},{24,16},{28,20},{1,9},{5... | collective-permute-start | bytes 393224 | tf_op jit(solution)/shard_map/ppermute | solution.py:23
  83.2 5.3 %collective-permute-start.25 = (bf16[1,128,512]{2,1,0:T(8,128)(2,1)S(1)}, bf16[1,128,512]{2,1,0:T(8,128)(2,1)S(1)}, u32[]{:S(2)}, u32[]{:S(2)}) collective-permute-start(bf16[1,128,512]{2,1,0:T(8,128)(2,1)S(1)} %bitcast.88), channel_id=1, source_target_pairs={{0,16},{4,20},{8,24},{12,28},{16,0},{20,4},{24,8},{28,12},{1,17},{... | collective-permute-start | bytes 393224 | tf_op jit(solution)/shard_map/ppermute | solution.py:36
  84.7 5.1 %collective-permute-start.36 = (bf16[2,128,512]{2,1,0:T(8,128)(2,1)S(1)}, bf16[2,128,512]{2,1,0:T(8,128)(2,1)S(1)}, u32[]{:S(2)}, u32[]{:S(2)}) collective-permute-start(bf16[2,128,512]{2,1,0:T(8,128)(2,1)S(1)} %pad_maximum_fusion.2.refs_2_), channel_id=1, source_target_pairs={{0,4},{4,0},{8,12},{12,8},{16,20},{20,16},{24,28},{28,24},{1,5},{5... | collective-permute-start | bytes 786440 | tf_op jit(solution)/shard_map/ppermute | solution.py:23
  84.8 9.2 %collective-permute-start.37 = (bf16[2,128,512]{2,1,0:T(8,128)(2,1)S(1)}, bf16[2,128,512]{2,1,0:T(8,128)(2,1)S(1)}, u32[]{:S(2)}, u32[]{:S(2)}) collective-permute-start(bf16[2,128,512]{2,1,0:T(8,128)(2,1)S(1)} %pad_maximum_fusion.2.refs_2_), channel_id=1, source_target_pairs={{0,8},{4,12},{8,0},{12,4},{16,24},{20,28},{24,16},{28,20},{1,9},{5... | collective-permute-start | bytes 786440 | tf_op jit(solution)/shard_map/ppermute | solution.py:23
  84.9 9.6 %collective-permute-start.29 = (bf16[2,128,512]{2,1,0:T(8,128)(2,1)S(1)}, bf16[2,128,512]{2,1,0:T(8,128)(2,1)S(1)}, u32[]{:S(2)}, u32[]{:S(2)}) collective-permute-start(bf16[2,128,512]{2,1,0:T(8,128)(2,1)S(1)} %pad_maximum_fusion.2.refs_2_), channel_id=1, source_target_pairs={{0,16},{4,20},{8,24},{12,28},{16,0},{20,4},{24,8},{28,12},{1,17},{... | collective-permute-start | bytes 786440 | tf_op jit(solution)/shard_map/ppermute | solution.py:36
  85.7 2.8 %collective-permute-start.35 = (bf16[1,128,512]{2,1,0:T(8,128)(2,1)S(1)}, bf16[1,128,512]{2,1,0:T(8,128)(2,1)S(1)}, u32[]{:S(2)}, u32[]{:S(2)}) collective-permute-start(bf16[1,128,512]{2,1,0:T(8,128)(2,1)S(1)} %bitcast.89), channel_id=1, source_target_pairs={{0,4},{4,0},{8,12},{12,8},{16,20},{20,16},{24,28},{28,24},{1,5},{5... | collective-permute-start | bytes 393224 | tf_op jit(solution)/shard_map/ppermute | solution.py:23
  88.5 1.3 %collective-permute-start.34 = (bf16[1,128,512]{2,1,0:T(8,128)(2,1)S(1)}, bf16[1,128,512]{2,1,0:T(8,128)(2,1)S(1)}, u32[]{:S(2)}, u32[]{:S(2)}) collective-permute-start(bf16[1,128,512]{2,1,0:T(8,128)(2,1)S(1)} %bitcast.85), channel_id=1, source_target_pairs={{0,4},{4,0},{8,12},{12,8},{16,20},{20,16},{24,28},{28,24},{1,5},{5... | collective-permute-start | bytes 393224 | tf_op jit(solution)/shard_map/ppermute | solution.py:23
  88.5 7.8 %collective-permute-start.41 = (bf16[1,128,512]{2,1,0:T(8,128)(2,1)S(1)}, bf16[1,128,512]{2,1,0:T(8,128)(2,1)S(1)}, u32[]{:S(2)}, u32[]{:S(2)}) collective-permute-start(bf16[1,128,512]{2,1,0:T(8,128)(2,1)S(1)} %collective-permute-done.25.refs_1_), channel_id=1, source_target_pairs={{0,8},{4,12},{8,0},{12,4},{16,24},{20,28},{24,16},{28,20},{1,9},{5... | collective-permute-start | bytes 393224 | tf_op jit(solution)/shard_map/ppermute | solution.py:23
  93.9 3.5 %collective-permute-start.40 = (bf16[2,128,512]{2,1,0:T(8,128)(2,1)S(1)}, bf16[2,128,512]{2,1,0:T(8,128)(2,1)S(1)}, u32[]{:S(2)}, u32[]{:S(2)}) collective-permute-start(bf16[2,128,512]{2,1,0:T(8,128)(2,1)S(1)} %collective-permute-done.37.refs_2_), channel_id=1, source_target_pairs={{0,4},{4,0},{8,12},{12,8},{16,20},{20,16},{24,28},{28,24},{1,5},{5... | collective-permute-start | bytes 786440 | tf_op jit(solution)/shard_map/ppermute | solution.py:23
  94.0 2.9 %collective-permute-start.39 = (bf16[1,128,512]{2,1,0:T(8,128)(2,1)S(1)}, bf16[1,128,512]{2,1,0:T(8,128)(2,1)S(1)}, u32[]{:S(2)}, u32[]{:S(2)}) collective-permute-start(bf16[1,128,512]{2,1,0:T(8,128)(2,1)S(1)} %collective-permute-done.28.refs_1_), channel_id=1, source_target_pairs={{0,4},{4,0},{8,12},{12,8},{16,20},{20,16},{24,28},{28,24},{1,5},{5... | collective-permute-start | bytes 393224 | tf_op jit(solution)/shard_map/ppermute | solution.py:23
  94.5 2.4 %collective-permute-start.38 = (bf16[1,128,512]{2,1,0:T(8,128)(2,1)S(1)}, bf16[1,128,512]{2,1,0:T(8,128)(2,1)S(1)}, u32[]{:S(2)}, u32[]{:S(2)}) collective-permute-start(bf16[1,128,512]{2,1,0:T(8,128)(2,1)S(1)} %collective-permute-done.33.refs_0_), channel_id=1, source_target_pairs={{0,4},{4,0},{8,12},{12,8},{16,20},{20,16},{24,28},{28,24},{1,5},{5... | collective-permute-start | bytes 393224 | tf_op jit(solution)/shard_map/ppermute | solution.py:23
  94.5 6.1 %collective-permute-start.32 = (bf16[2,128,512]{2,1,0:T(8,128)(2,1)S(1)}, bf16[2,128,512]{2,1,0:T(8,128)(2,1)S(1)}, u32[]{:S(2)}, u32[]{:S(2)}) collective-permute-start(bf16[2,128,512]{2,1,0:T(8,128)(2,1)S(1)} %collective-permute-done.29.refs_2_), channel_id=1, source_target_pairs={{0,4},{4,0},{8,12},{12,8},{16,20},{20,16},{24,28},{28,24},{1,5},{5... | collective-permute-start | bytes 786440 | tf_op jit(solution)/shard_map/ppermute | solution.py:23
  96.3 7.9 %collective-permute-start.42 = (bf16[2,128,512]{2,1,0:T(8,128)(2,1)S(1)}, bf16[2,128,512]{2,1,0:T(8,128)(2,1)S(1)}, u32[]{:S(2)}, u32[]{:S(2)}) collective-permute-start(bf16[2,128,512]{2,1,0:T(8,128)(2,1)S(1)} %collective-permute-done.37.refs_2_), channel_id=1, source_target_pairs={{0,16},{4,20},{8,24},{12,28},{16,0},{20,4},{24,8},{28,12},{1,17},{... | collective-permute-start | bytes 786440 | tf_op jit(solution)/shard_map/ppermute | solution.py:36
  96.9 3.7 %collective-permute-start.30 = (bf16[1,128,512]{2,1,0:T(8,128)(2,1)S(1)}, bf16[1,128,512]{2,1,0:T(8,128)(2,1)S(1)}, u32[]{:S(2)}, u32[]{:S(2)}) collective-permute-start(bf16[1,128,512]{2,1,0:T(8,128)(2,1)S(1)} %collective-permute-done.22.refs_0_), channel_id=1, source_target_pairs={{0,4},{4,0},{8,12},{12,8},{16,20},{20,16},{24,28},{28,24},{1,5},{5... | collective-permute-start | bytes 393224 | tf_op jit(solution)/shard_map/ppermute | solution.py:23
  96.9 3.7 %collective-permute-start.31 = (bf16[1,128,512]{2,1,0:T(8,128)(2,1)S(1)}, bf16[1,128,512]{2,1,0:T(8,128)(2,1)S(1)}, u32[]{:S(2)}, u32[]{:S(2)}) collective-permute-start(bf16[1,128,512]{2,1,0:T(8,128)(2,1)S(1)} %collective-permute-done.25.refs_1_), channel_id=1, source_target_pairs={{0,4},{4,0},{8,12},{12,8},{16,20},{20,16},{24,28},{28,24},{1,5},{5... | collective-permute-start | bytes 393224 | tf_op jit(solution)/shard_map/ppermute | solution.py:23
  104.2 1.9 %collective-permute-start.45 = (bf16[2,128,512]{2,1,0:T(8,128)(2,1)S(1)}, bf16[2,128,512]{2,1,0:T(8,128)(2,1)S(1)}, u32[]{:S(2)}, u32[]{:S(2)}) collective-permute-start(bf16[2,128,512]{2,1,0:T(8,128)(2,1)S(1)} %collective-permute-done.42.refs_2_), channel_id=1, source_target_pairs={{0,4},{4,0},{8,12},{12,8},{16,20},{20,16},{24,28},{28,24},{1,5},{5... | collective-permute-start | bytes 786440 | tf_op jit(solution)/shard_map/ppermute | solution.py:23
  104.2 1.7 %collective-permute-start.44 = (bf16[1,128,512]{2,1,0:T(8,128)(2,1)S(1)}, bf16[1,128,512]{2,1,0:T(8,128)(2,1)S(1)}, u32[]{:S(2)}, u32[]{:S(2)}) collective-permute-start(bf16[1,128,512]{2,1,0:T(8,128)(2,1)S(1)} %collective-permute-done.41.refs_1_), channel_id=1, source_target_pairs={{0,4},{4,0},{8,12},{12,8},{16,20},{20,16},{24,28},{28,24},{1,5},{5... | collective-permute-start | bytes 393224 | tf_op jit(solution)/shard_map/ppermute | solution.py:23
  104.7 1.4 %collective-permute-start.43 = (bf16[1,128,512]{2,1,0:T(8,128)(2,1)S(1)}, bf16[1,128,512]{2,1,0:T(8,128)(2,1)S(1)}, u32[]{:S(2)}, u32[]{:S(2)}) collective-permute-start(bf16[1,128,512]{2,1,0:T(8,128)(2,1)S(1)} %collective-permute-done.23.refs_0_), channel_id=1, source_target_pairs={{0,4},{4,0},{8,12},{12,8},{16,20},{20,16},{24,28},{28,24},{1,5},{5... | collective-permute-start | bytes 393224 | tf_op jit(solution)/shard_map/ppermute | solution.py:23

commit v9 on v7

--- a/solution.py
+++ b/solution.py
@@ -245,9 +245,8 @@
             grad = jnp.concatenate(
                 [jnp.where(second, sides[1], sides[0]), jnp.where(second, sides[0], sides[1])], 1
             )
-            for copy, start in zip(copies, starts):
-                here = slice(start, start + tile)
-                held[here] = dot(feat_ref[here], grad, (1, 0)).astype(jnp.bfloat16)
+            held[...] = dot(feat_ref[...], grad, (1, 0)).astype(jnp.bfloat16)
+            for copy in copies:
                 copy.start()
             for start in starts:
                 here = slice(start, start + tile)
@@ -287,7 +286,7 @@
         ],
         input_output_aliases={} if first else {len(inputs) + 3: 0, len(inputs) + 4: 1},
         name="backward_pair",
-        **params(tok * cols, tok * cols, 8),
+        **params(tok * cols, tok * cols, 12),
     )(info, *inputs, turned_features, dec_weight, *extra)
 
 
@@ -310,20 +309,21 @@
             preact[:, here] = kept
             bias_ref[:, here] = jnp.sum(kept.astype(jnp.float32), 0, keepdims=True)
         copies = []
-        for piece in range(pieces):
-            held[piece] = dot(
-                token_refs[piece // count][piece % count], preact[...], (1, 0)
-            ).astype(jnp.bfloat16)
-            size = cols // 4
-            for part in range(4):
-                row = (info_ref[0] ^ rels[piece]) * 4 + part
-                copy = pltpu.make_async_copy(
-                    held.at[piece, pl.ds(part * size, size)],
-                    enc_ref.at[span(row, size)],
-                    sems.at[4 * piece + part],
-                )
-                copy.start()
-                copies.append(copy)
+        for first in range(0, pieces, 2):
+            both = [token_refs[piece][0] for piece in range(first, first + 2)]
+            product = dot(jnp.concatenate(both, 0), preact[...], (1, 0)).astype(jnp.bfloat16)
+            for piece in range(first, first + 2):
+                held[piece] = product[(piece - first) * cols : (piece - first + 1) * cols]
+                size = cols // 4
+                for part in range(4):
+                    row = (info_ref[0] ^ rels[piece]) * 4 + part
+                    copy = pltpu.make_async_copy(
+                        held.at[piece, pl.ds(part * size, size)],
+                        enc_ref.at[span(row, size)],
+                        sems.at[4 * piece + part],
+                    )
+                    copy.start()
+                    copies.append(copy)
         for copy in copies:
             copy.wait()
 
@@ -343,7 +343,7 @@
         ],
         name="encoder_grad",
         **params(
-            2 * pieces * tok * cols * width, 2 * pieces * cols * (tok + width) + 6 * tok * width, 10
+            2 * pieces * tok * cols * width, 2 * pieces * cols * (tok + width) + 6 * tok * width, 14
         ),
     )(info, *turned_tokens, features, feature_grad, *squares)
 

time: 114 us -> 116 us (1.018)
  Pallas kernels: 33.6 us -> 35.9 us
    pallas_call x4, Pallas kernels: 12.8 us -> 14.8 us  [backward_pair(): pl.pallas_call(kernel, in_specs=[in_smem] + [in_vmem] * (len(inputs) + 2)...]
where the time goes in v9:
time: 116 us
  starting transfers between devices  43.6 us (38%)
  Pallas kernels  35.9 us (31%)
  waiting for transfers between devices  33.5 us (29%)
  other arithmetic  1.96 us (2%)
    ppermute x9, starting transfers between devices, over_feat(): return lax.ppermute(value, 'feat', pairs)  18.1 us
    ppermute x30, waiting for transfers between devices, over_members(): return lax.ppermute(value, 'layer', pairs)  17.9 us
    ppermute x30, starting transfers between devices, over_members(): return lax.ppermute(value, 'layer', pairs)  15.7 us
    pallas_call x4, Pallas kernels, backward_pair(): pl.pallas_call(kernel, in_specs=[in_smem] + [in_vmem] * (len(inputs) + 2)...  14.8 us
    ppermute x9, waiting for transfers between devices, over_feat(): return lax.ppermute(value, 'feat', pairs)  12.8 us
    pallas_call x2, Pallas kernels, decode(): pl.pallas_call(kernel, in_specs=[in_smem, in_vmem, in_vmem], out_specs=[i...  5.78 us
    pallas_call x1, Pallas kernels, encoder_grad(): pl.pallas_call(kernel, in_specs=[in_smem] + [in_vmem] * (len(turned_token...  5.06 us
    ppermute x4, starting transfers between devices, from_layer(): return lax.ppermute(value, 'layer', pairs)  5.04 us
  transfers between devices with their start and end apart: 46, of which 19 were waited for; matrix products, arithmetic and copies ran while one was open for 1% of the time, Pallas kernels for 19%

profile of v9, /device:TPU:0, one launch (start us, length us, event | category | flops | bytes accessed | tf_op | source)
XLA Modules:
  0.0 116.3 jit_solution(13832512361619249997)
XLA Ops:
  0.7 3.0 %collective-permute-start.1 = (bf16[128,512]{1,0:T(8,128)(2,1)}, bf16[128,512]{1,0:T(8,128)(2,1)S(1)}, u32[]{:S(2)}, u32[]{:S(2)}) collective-permute-start(bf16[128,512]{1,0:T(8,128)(2,1)} %param.5), channel_id=1, source_target_pairs={{0,1},{1,0},{2,3},{3,2},{4,5},{5,4},{6,7},{7,6},{8,9},{9,8},{10,11... | collective-permute-start | bytes 393224 | tf_op jit(solution)/shard_map/ppermute | solution.py:17
  3.8 2.5 %collective-permute-start.3 = (bf16[128,512]{1,0:T(8,128)(2,1)}, bf16[128,512]{1,0:T(8,128)(2,1)S(1)}, u32[]{:S(2)}, u32[]{:S(2)}) collective-permute-start(bf16[128,512]{1,0:T(8,128)(2,1)} %param.5), channel_id=1, source_target_pairs={{0,3},{1,2},{2,1},{3,0},{4,7},{5,6},{6,5},{7,4},{8,11},{9,10},{10,... | collective-permute-start | bytes 393224 | tf_op jit(solution)/shard_map/ppermute | solution.py:17
  6.4 1.5 %collective-permute-start = (bf16[128,512]{1,0:T(8,128)(2,1)}, bf16[128,512]{1,0:T(8,128)(2,1)S(1)}, u32[]{:S(2)}, u32[]{:S(2)}) collective-permute-start(bf16[128,512]{1,0:T(8,128)(2,1)} %param.5), channel_id=1, source_target_pairs={{0,8},{4,12},{8,0},{12,4},{16,24},{20,28},{24,16},{28,20},{1,9},{5... | collective-permute-start | bytes 393224 | tf_op jit(solution)/shard_map/ppermute | solution.py:23
  7.9 4.7 %fetch.1 = (bf16[2048,1024]{1,0:T(8,128)(2,1)S(1)}, bf16[2,1024,2048]{2,1,0:T(8,128)(2,1)S(1)}) custom-call(bf16[2048,1024]{1,0:T(8,128)(2,1)} %refs_0_.1, bf16[2,1024,2048]{2,1,0:T(8,128)(2,1)} %refs_1_), custom_call_target="tpu_custom_call" | custom-call | bytes 12582912 | tf_op jit(solution)/shard_map/fetch/pallas_call | solution.py:88
  12.6 1.1 collective-permute-done.3
  13.7 1.5 %collective-permute-start.5 = (bf16[128,512]{1,0:T(8,128)(2,1)S(1)}, bf16[128,512]{1,0:T(8,128)(2,1)S(1)}, u32[]{:S(2)}, u32[]{:S(2)}) collective-permute-start(bf16[128,512]{1,0:T(8,128)(2,1)S(1)} %collective-permute-done.3), channel_id=1, source_target_pairs={{0,8},{4,12},{8,0},{12,4},{16,24},{20,28},{24,16},{28,20},{1,9},{5... | collective-permute-start | bytes 393224 | tf_op jit(solution)/shard_map/ppermute | solution.py:23
  15.2 0.5 collective-permute-start.4
  15.8 2.5 %collective-permute-done.2 = bf16[128,512]{1,0:T(8,128)(2,1)S(1)} collective-permute-done((bf16[128,512]{1,0:T(8,128)(2,1)}, bf16[128,512]{1,0:T(8,128)(2,1)S(1)}, u32[]{:S(2)}, u32[]{:S(2)}) %collective-permute-start.2) | collective-permute-done | bytes 131104 | tf_op jit(solution)/shard_map/ppermute | solution.py:17
  18.3 0.4 collective-permute-done.5
  18.7 1.5 %collective-permute-done.4 = bf16[128,512]{1,0:T(8,128)(2,1)S(1)} collective-permute-done((bf16[128,512]{1,0:T(8,128)(2,1)S(1)}, bf16[128,512]{1,0:T(8,128)(2,1)S(1)}, u32[]{:S(2)}, u32[]{:S(2)}) %collective-permute-start.4) | collective-permute-done | bytes 131104 | tf_op jit(solution)/shard_map/ppermute | solution.py:23
  20.2 1.4 %collective-permute-start.7 = (bf16[128,512]{1,0:T(8,128)(2,1)S(1)}, bf16[128,512]{1,0:T(8,128)(2,1)S(1)}, u32[]{:S(2)}, u32[]{:S(2)}) collective-permute-start(bf16[128,512]{1,0:T(8,128)(2,1)S(1)} %collective-permute-done.2), channel_id=1, source_target_pairs={{0,8},{4,12},{8,0},{12,4},{16,24},{20,28},{24,16},{28,20},{1,9},{5... | collective-permute-start | bytes 393224 | tf_op jit(solution)/shard_map/ppermute | solution.py:23
  21.6 0.5 collective-permute-done.6.refs_1_
  22.1 1.8 %encode.3.refs_2_ = f32[512,1024]{1,0:T(8,128)S(1)} custom-call(s32[2]{0:T(128)S(1)} %pad_add_fusion.info_ref, bf16[4,128,512]{2,1,0:T(8,128)(2,1)S(1)} %pad_maximum_fusion.refs_0_, bf16[4,128,512]{2,1,0:T(8,128)(2,1)S(1)} %collective-permute-done.6.refs_1_, bf16[2048,1024]{1,0:T(8,128)(2,1)S(1)} %get-tuple-element.63.refs_2_.refs_1_), custom_call_target="tpu_custom_call" | custom-call | flops 1073741824 | bytes 3145728 | tf_op jit(solution)/shard_map/encode/pallas_call | solution.py:128
  23.9 2.2 %collective-permute-done.7 = bf16[128,512]{1,0:T(8,128)(2,1)S(1)} collective-permute-done((bf16[128,512]{1,0:T(8,128)(2,1)S(1)}, bf16[128,512]{1,0:T(8,128)(2,1)S(1)}, u32[]{:S(2)}, u32[]{:S(2)}) %collective-permute-start.7) | collective-permute-done | bytes 131104 | tf_op jit(solution)/shard_map/ppermute | solution.py:23
  26.3 1.3 %encode.4.refs_2_ = f32[512,1024]{1,0:T(8,128)S(1)} custom-call(s32[2]{0:T(128)S(1)} %pad_add_fusion.info_ref, bf16[4,128,512]{2,1,0:T(8,128)(2,1)S(1)} %pad_maximum_fusion.1.refs_0_, bf16[2048,1024]{1,0:T(8,128)(2,1)S(1)} %get-tuple-element.63.refs_2_.refs_1_, f32[512,1024]{1,0:T(8,128)S(1)} %encode.3.refs_2_), custom_call_target="tpu_custom_call" | custom-call | flops 536870912 | bytes 1572864 | tf_op jit(solution)/shard_map/encode/pallas_call | solution.py:128
  27.5 0.6 collective-permute-done.8.refs_0_
  28.2 1.4 %encode.5.feat_ref.in_ref.refs_4_ = bf16[2,512,1024]{2,1,0:T(8,128)(2,1)S(1)} custom-call(s32[2]{0:T(128)S(1)} %pad_add_fusion.info_ref, bf16[4,128,512]{2,1,0:T(8,128)(2,1)S(1)} %collective-permute-done.8.refs_0_, bf16[2048,1024]{1,0:T(8,128)(2,1)S(1)} %get-tuple-element.63.refs_2_.refs_1_, f32[512,1024]{1,0:T(8,128)S(1)} %encode.4.refs_2_, ...), custom_call_target="tpu_custom_call" | custom-call | flops 536870912 | bytes 1572864 | tf_op jit(solution)/shard_map/encode/pallas_call | solution.py:128
  29.6 2.9 %decode.2 = (bf16[2,2,128,512]{3,2,1,0:T(8,128)(2,1)S(1)}, bf16[2,2,128,512]{3,2,1,0:T(8,128)(2,1)S(1)}, bf16[2,2,128,512]{3,2,1,0:T(8,128)(2,1)S(1)}, bf16[2,2,128,512]{3,2,1,0:T(8,128)(2,1)S(1)}) custom-call(s32[2]{0:T(128)S(1)} %pad_add_fusion.info_ref, bf16[2,512,1024]{2,1,0:T(8,128)(2,1)S(1)} %encode.5.feat_ref.in_ref.refs_4_, ...), custom_call_target="tpu_custom_call" | custom-call | flops 2147483648 | bytes 4194304 | tf_op jit(solution)/shard_map/decode/pallas_call | solution.py:167
  32.7 0.4 collective-permute-start.10
  33.1 2.9 %decode.3 = (bf16[2,2,128,512]{3,2,1,0:T(8,128)(2,1)S(1)}, bf16[2,2,128,512]{3,2,1,0:T(8,128)(2,1)S(1)}, bf16[2,2,128,512]{3,2,1,0:T(8,128)(2,1)S(1)}, bf16[2,2,128,512]{3,2,1,0:T(8,128)(2,1)S(1)}) custom-call(s32[2]{0:T(128)S(1)} %pad_add_fusion.info_ref, bf16[2,512,1024]{2,1,0:T(8,128)(2,1)S(1)} %encode.5.feat_ref.in_ref.refs_4_, ...), custom_call_target="tpu_custom_call" | custom-call | flops 2147483648 | bytes 4194304 | tf_op jit(solution)/shard_map/decode/pallas_call | solution.py:167
  36.2 0.4 collective-permute-start.9
  36.7 1.5 %collective-permute-start.13 = (bf16[1,2,128,512]{3,2,1,0:T(8,128)(2,1)S(1)}, bf16[1,2,128,512]{3,2,1,0:T(8,128)(2,1)S(1)}, u32[]{:S(2)}, u32[]{:S(2)}) collective-permute-start(bf16[1,2,128,512]{3,2,1,0:T(8,128)(2,1)S(1)} %slice_bitcast_fusion.5), channel_id=1, source_target_pairs={{0,8},{4,12},{8,0},{12,4},{16,24},{20,28},{24,16},{28,20},{1,9},{5... | collective-permute-start | bytes 786440 | tf_op jit(solution)/shard_map/ppermute | solution.py:23
  38.4 1.6 %collective-permute-start.11 = (bf16[1,2,128,512]{3,2,1,0:T(8,128)(2,1)S(1)}, bf16[1,2,128,512]{3,2,1,0:T(8,128)(2,1)S(1)}, u32[]{:S(2)}, u32[]{:S(2)}) collective-permute-start(bf16[1,2,128,512]{3,2,1,0:T(8,128)(2,1)S(1)} %get-tuple-element.120), channel_id=1, source_target_pairs={{0,16},{4,20},{8,24},{12,28},{16,0},{20,4},{24,8},{28,12},{1,17},{... | collective-permute-start | bytes 786440 | tf_op jit(solution)/shard_map/ppermute | solution.py:29
  40.1 0.7 collective-permute-start.16
  41.0 5.0 %collective-permute-done.13 = bf16[1,2,128,512]{3,2,1,0:T(8,128)(2,1)S(1)} collective-permute-done((bf16[1,2,128,512]{3,2,1,0:T(8,128)(2,1)S(1)}, bf16[1,2,128,512]{3,2,1,0:T(8,128)(2,1)S(1)}, u32[]{:S(2)}, u32[]{:S(2)}) %collective-permute-start.13) | collective-permute-done | bytes 262176 | tf_op jit(solution)/shard_map/ppermute | solution.py:23
  46.0 0.5 collective-permute-done.11
  46.6 1.6 %collective-permute-start.17 = (bf16[1,2,128,512]{3,2,1,0:T(8,128)(2,1)S(1)}, bf16[1,2,128,512]{3,2,1,0:T(8,128)(2,1)S(1)}, u32[]{:S(2)}, u32[]{:S(2)}) collective-permute-start(bf16[1,2,128,512]{3,2,1,0:T(8,128)(2,1)S(1)} %fusion.4), channel_id=1, source_target_pairs={{0,16},{4,20},{8,24},{12,28},{16,0},{20,4},{24,8},{28,12},{1,17},{... | collective-permute-start | bytes 786440 | tf_op jit(solution)/shard_map/ppermute | solution.py:29
  48.2 0.9 collective-permute-start.15
  49.1 2.5 %collective-permute-done.16 = bf16[1,2,128,512]{3,2,1,0:T(8,128)(2,1)S(1)} collective-permute-done((bf16[1,2,128,512]{3,2,1,0:T(8,128)(2,1)S(1)}, bf16[1,2,128,512]{3,2,1,0:T(8,128)(2,1)S(1)}, u32[]{:S(2)}, u32[]{:S(2)}) %collective-permute-start.16) | collective-permute-done | bytes 262176 | tf_op jit(solution)/shard_map/ppermute | solution.py:23
  51.5 2.3 %collective-permute-done.17 = bf16[1,2,128,512]{3,2,1,0:T(8,128)(2,1)S(1)} collective-permute-done((bf16[1,2,128,512]{3,2,1,0:T(8,128)(2,1)S(1)}, bf16[1,2,128,512]{3,2,1,0:T(8,128)(2,1)S(1)}, u32[]{:S(2)}, u32[]{:S(2)}) %collective-permute-start.17) | collective-permute-done | bytes 262176 | tf_op jit(solution)/shard_map/ppermute | solution.py:29
  54.0 1.6 %collective-permute-start.18 = (bf16[1,2,128,512]{3,2,1,0:T(8,128)(2,1)S(1)}, bf16[1,2,128,512]{3,2,1,0:T(8,128)(2,1)S(1)}, u32[]{:S(2)}, u32[]{:S(2)}) collective-permute-start(bf16[1,2,128,512]{3,2,1,0:T(8,128)(2,1)S(1)} %get-tuple-element.86), channel_id=1, source_target_pairs={{0,16},{4,20},{8,24},{12,28},{16,0},{20,4},{24,8},{28,12},{1,17},{... | collective-permute-start | bytes 786440 | tf_op jit(solution)/shard_map/ppermute | solution.py:29
  55.6 4.6 %collective-permute-start.20 = (bf16[128,512]{1,0:T(8,128)(2,1)S(1)}, bf16[128,512]{1,0:T(8,128)(2,1)S(1)}, u32[]{:S(2)}, u32[]{:S(2)}) collective-permute-start(bf16[128,512]{1,0:T(8,128)(2,1)S(1)} %get-tuple-element.122), channel_id=1, source_target_pairs={{0,2},{1,3},{2,0},{3,1},{4,6},{5,7},{6,4},{7,5},{8,10},{9,11},{10,... | collective-permute-start | bytes 393224 | tf_op jit(solution)/shard_map/ppermute | solution.py:17
  60.2 1.0 collective-permute-start.19
  61.3 2.6 %collective-permute-start.21 = (bf16[128,512]{1,0:T(8,128)(2,1)S(1)}, bf16[128,512]{1,0:T(8,128)(2,1)S(1)}, u32[]{:S(2)}, u32[]{:S(2)}) collective-permute-start(bf16[128,512]{1,0:T(8,128)(2,1)S(1)} %fusion.13), channel_id=1, source_target_pairs={{0,1},{1,0},{2,3},{3,2},{4,5},{5,4},{6,7},{7,6},{8,9},{9,8},{10,11... | collective-permute-start | bytes 393224 | tf_op jit(solution)/shard_map/ppermute | solution.py:17
  63.8 0.3 turned.5
  64.9 2.8 %collective-permute-done.19 = bf16[128,512]{1,0:T(8,128)(2,1)S(1)} collective-permute-done((bf16[128,512]{1,0:T(8,128)(2,1)S(1)}, bf16[128,512]{1,0:T(8,128)(2,1)S(1)}, u32[]{:S(2)}, u32[]{:S(2)}) %collective-permute-start.19) | collective-permute-done | bytes 131104 | tf_op jit(solution)/shard_map/ppermute | solution.py:17
  67.8 0.9 collective-permute-done.20
  68.7 0.5 collective-permute-done.21
  69.2 0.8 multiply_convert_fusion
  70.0 0.8 collective-permute-start.22
  70.8 1.2 collective-permute-start.24
  71.9 1.7 %collective-permute-start.26 = (bf16[128,512]{1,0:T(8,128)(2,1)S(1)}, bf16[128,512]{1,0:T(8,128)(2,1)S(1)}, u32[]{:S(2)}, u32[]{:S(2)}) collective-permute-start(bf16[128,512]{1,0:T(8,128)(2,1)S(1)} %get-tuple-element.115), channel_id=1, source_target_pairs={{0,2},{1,3},{2,0},{3,1},{4,6},{5,7},{6,4},{7,5},{8,10},{9,11},{10,... | collective-permute-start | bytes 393224 | tf_op jit(solution)/shard_map/ppermute | solution.py:17
  73.6 1.5 %collective-permute-start.27 = (bf16[128,512]{1,0:T(8,128)(2,1)S(1)}, bf16[128,512]{1,0:T(8,128)(2,1)S(1)}, u32[]{:S(2)}, u32[]{:S(2)}) collective-permute-start(bf16[128,512]{1,0:T(8,128)(2,1)S(1)} %get-tuple-element.115), channel_id=1, source_target_pairs={{0,3},{1,2},{2,1},{3,0},{4,7},{5,6},{6,5},{7,4},{8,11},{9,10},{10,... | collective-permute-start | bytes 393224 | tf_op jit(solution)/shard_map/ppermute | solution.py:17
  75.1 0.6 collective-permute-start.32
  75.8 1.4 %collective-permute-start.23 = (bf16[1,128,512]{2,1,0:T(8,128)(2,1)S(1)}, bf16[1,128,512]{2,1,0:T(8,128)(2,1)S(1)}, u32[]{:S(2)}, u32[]{:S(2)}) collective-permute-start(bf16[1,128,512]{2,1,0:T(8,128)(2,1)S(1)} %collective-permute-done.22.refs_0_), channel_id=1, source_target_pairs={{0,8},{4,12},{8,0},{12,4},{16,24},{20,28},{24,16},{28,20},{1,9},{5... | collective-permute-start | bytes 393224 | tf_op jit(solution)/shard_map/ppermute | solution.py:23
  77.2 1.2 %collective-permute-start.25 = (bf16[1,128,512]{2,1,0:T(8,128)(2,1)S(1)}, bf16[1,128,512]{2,1,0:T(8,128)(2,1)S(1)}, u32[]{:S(2)}, u32[]{:S(2)}) collective-permute-start(bf16[1,128,512]{2,1,0:T(8,128)(2,1)S(1)} %bitcast.87), channel_id=1, source_target_pairs={{0,16},{4,20},{8,24},{12,28},{16,0},{20,4},{24,8},{28,12},{1,17},{... | collective-permute-start | bytes 393224 | tf_op jit(solution)/shard_map/ppermute | solution.py:36
  78.4 4.9 %collective-permute-done.26 = bf16[128,512]{1,0:T(8,128)(2,1)S(1)} collective-permute-done((bf16[128,512]{1,0:T(8,128)(2,1)S(1)}, bf16[128,512]{1,0:T(8,128)(2,1)S(1)}, u32[]{:S(2)}, u32[]{:S(2)}) %collective-permute-start.26) | collective-permute-done | bytes 131104 | tf_op jit(solution)/shard_map/ppermute | solution.py:17
  83.3 0.3 collective-permute-start.33
  83.8 1.8 %collective-permute-start.37 = (bf16[2,128,512]{2,1,0:T(8,128)(2,1)S(1)}, bf16[2,128,512]{2,1,0:T(8,128)(2,1)S(1)}, u32[]{:S(2)}, u32[]{:S(2)}) collective-permute-start(bf16[2,128,512]{2,1,0:T(8,128)(2,1)S(1)} %pad_maximum_fusion.2.refs_2_), channel_id=1, source_target_pairs={{0,8},{4,12},{8,0},{12,4},{16,24},{20,28},{24,16},{28,20},{1,9},{5... | collective-permute-start | bytes 786440 | tf_op jit(solution)/shard_map/ppermute | solution.py:23
  85.6 1.5 %collective-permute-start.28 = (bf16[2,128,512]{2,1,0:T(8,128)(2,1)S(1)}, bf16[2,128,512]{2,1,0:T(8,128)(2,1)S(1)}, u32[]{:S(2)}, u32[]{:S(2)}) collective-permute-start(bf16[2,128,512]{2,1,0:T(8,128)(2,1)S(1)} %pad_maximum_fusion.2.refs_2_), channel_id=1, source_target_pairs={{0,16},{4,20},{8,24},{12,28},{16,0},{20,4},{24,8},{28,12},{1,17},{... | collective-permute-start | bytes 786440 | tf_op jit(solution)/shard_map/ppermute | solution.py:36
  87.1 2.6 %collective-permute-done.33.refs_1_ = bf16[1,128,512]{2,1,0:T(8,128)(2,1)S(1)} collective-permute-done((bf16[1,128,512]{2,1,0:T(8,128)(2,1)S(1)}, bf16[1,128,512]{2,1,0:T(8,128)(2,1)S(1)}, u32[]{:S(2)}, u32[]{:S(2)}) %collective-permute-start.33) | collective-permute-done | bytes 131104 | tf_op jit(solution)/shard_map/ppermute | solution.py:23
  89.7 1.3 %collective-permute-done.34.refs_3_ = bf16[1,128,512]{2,1,0:T(8,128)(2,1)S(1)} collective-permute-done((bf16[1,128,512]{2,1,0:T(8,128)(2,1)S(1)}, bf16[1,128,512]{2,1,0:T(8,128)(2,1)S(1)}, u32[]{:S(2)}, u32[]{:S(2)}) %collective-permute-start.34) | collective-permute-done | bytes 131104 | tf_op jit(solution)/shard_map/ppermute | solution.py:23
  91.1 3.2 %backward_pair.4 = (f32[512,1024]{1,0:T(8,128)S(1)}, bf16[2,1024,2048]{2,1,0:T(8,128)(2,1)}, f32[8,128]{1,0:T(8,128)S(1)}) custom-call(s32[2]{0:T(128)S(1)} %pad_add_fusion.info_ref, bf16[1,128,512]{2,1,0:T(8,128)(2,1)S(1)} %bitcast.86, bf16[1,128,512]{2,1,0:T(8,128)(2,1)S(1)} %bitcast.90, bf16[2,128,512]{2,1,0:T(8,128)(2,1)S(1)} %pad_maximum_fusion.2.refs_2_, ...), custom_call_target="tpu_custom_call" | custom-call | flops 262144 | bytes 262144 | tf_op jit(solution)/shard_map/backward_pair/pallas_call | solution.py:272
  94.3 0.2 collective-permute-start.40
  94.5 0.4 collective-permute-start.39
  95.0 0.4 collective-permute-start.31
  95.4 1.5 %collective-permute-start.42 = (bf16[2,128,512]{2,1,0:T(8,128)(2,1)S(1)}, bf16[2,128,512]{2,1,0:T(8,128)(2,1)S(1)}, u32[]{:S(2)}, u32[]{:S(2)}) collective-permute-start(bf16[2,128,512]{2,1,0:T(8,128)(2,1)S(1)} %collective-permute-done.37.refs_2_), channel_id=1, source_target_pairs={{0,16},{4,20},{8,24},{12,28},{16,0},{20,4},{24,8},{28,12},{1,17},{... | collective-permute-start | bytes 786440 | tf_op jit(solution)/shard_map/ppermute | solution.py:36
  96.9 0.5 collective-permute-start.30
  97.4 3.2 %backward_pair.5 = (f32[512,1024]{1,0:T(8,128)S(1)}, bf16[2,1024,2048]{2,1,0:T(8,128)(2,1)}, f32[8,128]{1,0:T(8,128)S(1)}) custom-call(s32[2]{0:T(128)S(1)} %pad_add_fusion.info_ref, bf16[1,128,512]{2,1,0:T(8,128)(2,1)S(1)} %collective-permute-done.32.refs_0_, ...), custom_call_target="tpu_custom_call", output_to_operand_aliasing={{0}: (9, {}), {1}: (10, {})} | custom-call | flops 262144 | bytes 262144 | tf_op jit(solution)/shard_map/backward_pair/pallas_call | solution.py:272
  100.7 4.2 %backward_pair.6 = (f32[512,1024]{1,0:T(8,128)S(1)}, bf16[2,1024,2048]{2,1,0:T(8,128)(2,1)}, f32[8,128]{1,0:T(8,128)S(1)}) custom-call(s32[2]{0:T(128)S(1)} %pad_add_fusion.info_ref, bf16[1,128,512]{2,1,0:T(8,128)(2,1)S(1)} %collective-permute-done.22.refs_0_, ...), custom_call_target="tpu_custom_call", output_to_operand_aliasing={{0}: (9, {}), {1}: (10, {})} | custom-call | flops 262144 | bytes 262144 | tf_op jit(solution)/shard_map/backward_pair/pallas_call | solution.py:272
  105.0 0.4 collective-permute-start.44
  105.5 1.1 collective-permute-done.44.refs_4_
  106.9 4.2 %backward_pair.7 = (f32[512,1024]{1,0:T(8,128)S(1)}, bf16[2,1024,2048]{2,1,0:T(8,128)(2,1)}, f32[8,128]{1,0:T(8,128)S(1)}) custom-call(s32[2]{0:T(128)S(1)} %pad_add_fusion.info_ref, bf16[1,128,512]{2,1,0:T(8,128)(2,1)S(1)} %collective-permute-done.23.refs_0_, ...), custom_call_target="tpu_custom_call", output_to_operand_aliasing={{0}: (9, {}), {1}: (10, {})} | custom-call | flops 262144 | bytes 262144 | tf_op jit(solution)/shard_map/backward_pair/pallas_call | solution.py:272
  111.0 5.1 %encoder_grad.1 = (bf16[2048,1024]{1,0:T(8,128)(2,1)}, f32[1,1024]{1,0:T(1,128)}, f32[1,1]{1,0:T(1,128)}) custom-call(s32[2]{0:T(128)S(1)} %pad_add_fusion.info_ref, bf16[1,512,512]{2,1,0:T(8,128)(2,1)S(1)} %turned.6.refs_0_, bf16[1,512,512]{2,1,0:T(8,128)(2,1)S(1)} %turned.7.refs_1_, bf16[1,512,512]{2,1,0:T(8,128)(2,1)S(1)} %turned.8.refs_2_, ...), custom_call_target="tpu_custom_call" | custom-call | flops 2147483648 | bytes 9437184 | tf_op jit(solution)/shard_map/encoder_grad/pallas_call | solution.py:330
  (68 shorter events, 3.4 us)
Async XLA Ops:
  0.7 17.5 %copy-start.2 = (bf16[128,512]{1,0:T(8,128)(2,1)S(1)}, bf16[128,512]{1,0:T(8,128)(2,1)}, u32[]{:S(2)}) copy-start(bf16[128,512]{1,0:T(8,128)(2,1)} %param.5) | copy-start | bytes 393220
  0.7 7.1 %collective-permute-start.1 = (bf16[128,512]{1,0:T(8,128)(2,1)}, bf16[128,512]{1,0:T(8,128)(2,1)S(1)}, u32[]{:S(2)}, u32[]{:S(2)}) collective-permute-start(bf16[128,512]{1,0:T(8,128)(2,1)} %param.5), channel_id=1, source_target_pairs={{0,1},{1,0},{2,3},{3,2},{4,5},{5,4},{6,7},{7,6},{8,9},{9,8},{10,11... | collective-permute-start | bytes 393224 | tf_op jit(solution)/shard_map/ppermute | solution.py:17
  3.8 10.0 %collective-permute-start.3 = (bf16[128,512]{1,0:T(8,128)(2,1)}, bf16[128,512]{1,0:T(8,128)(2,1)S(1)}, u32[]{:S(2)}, u32[]{:S(2)}) collective-permute-start(bf16[128,512]{1,0:T(8,128)(2,1)} %param.5), channel_id=1, source_target_pairs={{0,3},{1,2},{2,1},{3,0},{4,7},{5,6},{6,5},{7,4},{8,11},{9,10},{10,... | collective-permute-start | bytes 393224 | tf_op jit(solution)/shard_map/ppermute | solution.py:17
  6.2 12.0 %collective-permute-start.2 = (bf16[128,512]{1,0:T(8,128)(2,1)}, bf16[128,512]{1,0:T(8,128)(2,1)S(1)}, u32[]{:S(2)}, u32[]{:S(2)}) collective-permute-start(bf16[128,512]{1,0:T(8,128)(2,1)} %param.5), channel_id=1, source_target_pairs={{0,2},{1,3},{2,0},{3,1},{4,6},{5,7},{6,4},{7,5},{8,10},{9,11},{10,... | collective-permute-start | bytes 393224 | tf_op jit(solution)/shard_map/ppermute | solution.py:17
  6.4 12.0 %collective-permute-start = (bf16[128,512]{1,0:T(8,128)(2,1)}, bf16[128,512]{1,0:T(8,128)(2,1)S(1)}, u32[]{:S(2)}, u32[]{:S(2)}) collective-permute-start(bf16[128,512]{1,0:T(8,128)(2,1)} %param.5), channel_id=1, source_target_pairs={{0,8},{4,12},{8,0},{12,4},{16,24},{20,28},{24,16},{28,20},{1,9},{5... | collective-permute-start | bytes 393224 | tf_op jit(solution)/shard_map/ppermute | solution.py:23
  13.7 5.0 %collective-permute-start.5 = (bf16[128,512]{1,0:T(8,128)(2,1)S(1)}, bf16[128,512]{1,0:T(8,128)(2,1)S(1)}, u32[]{:S(2)}, u32[]{:S(2)}) collective-permute-start(bf16[128,512]{1,0:T(8,128)(2,1)S(1)} %collective-permute-done.3), channel_id=1, source_target_pairs={{0,8},{4,12},{8,0},{12,4},{16,24},{20,28},{24,16},{28,20},{1,9},{5... | collective-permute-start | bytes 393224 | tf_op jit(solution)/shard_map/ppermute | solution.py:23
  15.2 5.0 %collective-permute-start.4 = (bf16[128,512]{1,0:T(8,128)(2,1)S(1)}, bf16[128,512]{1,0:T(8,128)(2,1)S(1)}, u32[]{:S(2)}, u32[]{:S(2)}) collective-permute-start(bf16[128,512]{1,0:T(8,128)(2,1)S(1)} %collective-permute-done.1), channel_id=1, source_target_pairs={{0,8},{4,12},{8,0},{12,4},{16,24},{20,28},{24,16},{28,20},{1,9},{5... | collective-permute-start | bytes 393224 | tf_op jit(solution)/shard_map/ppermute | solution.py:23
  20.2 1.9 %collective-permute-start.6 = (bf16[4,128,512]{2,1,0:T(8,128)(2,1)S(1)}, bf16[4,128,512]{2,1,0:T(8,128)(2,1)S(1)}, u32[]{:S(2)}, u32[]{:S(2)}) collective-permute-start(bf16[4,128,512]{2,1,0:T(8,128)(2,1)S(1)} %pad_maximum_fusion.refs_0_), channel_id=1, source_target_pairs={{0,4},{4,0},{8,12},{12,8},{16,20},{20,16},{24,28},{28,24},{1,5},{5... | collective-permute-start | bytes 1572872 | tf_op jit(solution)/shard_map/ppermute | solution.py:23
  20.2 5.9 %collective-permute-start.7 = (bf16[128,512]{1,0:T(8,128)(2,1)S(1)}, bf16[128,512]{1,0:T(8,128)(2,1)S(1)}, u32[]{:S(2)}, u32[]{:S(2)}) collective-permute-start(bf16[128,512]{1,0:T(8,128)(2,1)S(1)} %collective-permute-done.2), channel_id=1, source_target_pairs={{0,8},{4,12},{8,0},{12,4},{16,24},{20,28},{24,16},{28,20},{1,9},{5... | collective-permute-start | bytes 393224 | tf_op jit(solution)/shard_map/ppermute | solution.py:23
  26.2 2.0 %copy-start = (f32[1024]{0:T(1024)S(1)}, f32[1024]{0:T(1024)}, u32[]{:S(2)}) copy-start(f32[1024]{0:T(1024)} %param.8) | copy-start | bytes 12292
  26.2 2.0 %collective-permute-start.8 = (bf16[4,128,512]{2,1,0:T(8,128)(2,1)S(1)}, bf16[4,128,512]{2,1,0:T(8,128)(2,1)S(1)}, u32[]{:S(2)}, u32[]{:S(2)}) collective-permute-start(bf16[4,128,512]{2,1,0:T(8,128)(2,1)S(1)} %pad_maximum_fusion.1.refs_0_), channel_id=1, source_target_pairs={{0,4},{4,0},{8,12},{12,8},{16,20},{20,16},{24,28},{28,24},{1,5},{5... | collective-permute-start | bytes 1572872 | tf_op jit(solution)/shard_map/ppermute | solution.py:23
  32.5 4.0 %collective-permute-start.12 = (bf16[2,2,128,512]{3,2,1,0:T(8,128)(2,1)S(1)}, bf16[2,2,128,512]{3,2,1,0:T(8,128)(2,1)S(1)}, u32[]{:S(2)}, u32[]{:S(2)}) collective-permute-start(bf16[2,2,128,512]{3,2,1,0:T(8,128)(2,1)S(1)} %get-tuple-element.79), channel_id=1, source_target_pairs={{0,4},{4,0},{8,12},{12,8},{16,20},{20,16},{24,28},{28,24},{1,5},{5... | collective-permute-start | bytes 1572872 | tf_op jit(solution)/shard_map/ppermute | solution.py:23
  32.7 5.5 %collective-permute-start.10 = (bf16[2,2,128,512]{3,2,1,0:T(8,128)(2,1)S(1)}, bf16[2,2,128,512]{3,2,1,0:T(8,128)(2,1)S(1)}, u32[]{:S(2)}, u32[]{:S(2)}) collective-permute-start(bf16[2,2,128,512]{3,2,1,0:T(8,128)(2,1)S(1)} %get-tuple-element.78), channel_id=1, source_target_pairs={{0,4},{4,0},{8,12},{12,8},{16,20},{20,16},{24,28},{28,24},{1,5},{5... | collective-permute-start | bytes 1572872 | tf_op jit(solution)/shard_map/ppermute | solution.py:23
  36.0 4.0 %collective-permute-start.14 = (bf16[2,2,128,512]{3,2,1,0:T(8,128)(2,1)S(1)}, bf16[2,2,128,512]{3,2,1,0:T(8,128)(2,1)S(1)}, u32[]{:S(2)}, u32[]{:S(2)}) collective-permute-start(bf16[2,2,128,512]{3,2,1,0:T(8,128)(2,1)S(1)} %get-tuple-element.81), channel_id=1, source_target_pairs={{0,4},{4,0},{8,12},{12,8},{16,20},{20,16},{24,28},{28,24},{1,5},{5... | collective-permute-start | bytes 1572872 | tf_op jit(solution)/shard_map/ppermute | solution.py:23
  36.2 4.7 %collective-permute-start.9 = (bf16[2,2,128,512]{3,2,1,0:T(8,128)(2,1)S(1)}, bf16[2,2,128,512]{3,2,1,0:T(8,128)(2,1)S(1)}, u32[]{:S(2)}, u32[]{:S(2)}) collective-permute-start(bf16[2,2,128,512]{3,2,1,0:T(8,128)(2,1)S(1)} %get-tuple-element.75), channel_id=1, source_target_pairs={{0,4},{4,0},{8,12},{12,8},{16,20},{20,16},{24,28},{28,24},{1,5},{5... | collective-permute-start | bytes 1572872 | tf_op jit(solution)/shard_map/ppermute | solution.py:23
  36.7 9.2 %collective-permute-start.13 = (bf16[1,2,128,512]{3,2,1,0:T(8,128)(2,1)S(1)}, bf16[1,2,128,512]{3,2,1,0:T(8,128)(2,1)S(1)}, u32[]{:S(2)}, u32[]{:S(2)}) collective-permute-start(bf16[1,2,128,512]{3,2,1,0:T(8,128)(2,1)S(1)} %slice_bitcast_fusion.5), channel_id=1, source_target_pairs={{0,8},{4,12},{8,0},{12,4},{16,24},{20,28},{24,16},{28,20},{1,9},{5... | collective-permute-start | bytes 786440 | tf_op jit(solution)/shard_map/ppermute | solution.py:23
  38.4 8.1 %collective-permute-start.11 = (bf16[1,2,128,512]{3,2,1,0:T(8,128)(2,1)S(1)}, bf16[1,2,128,512]{3,2,1,0:T(8,128)(2,1)S(1)}, u32[]{:S(2)}, u32[]{:S(2)}) collective-permute-start(bf16[1,2,128,512]{3,2,1,0:T(8,128)(2,1)S(1)} %get-tuple-element.120), channel_id=1, source_target_pairs={{0,16},{4,20},{8,24},{12,28},{16,0},{20,4},{24,8},{28,12},{1,17},{... | collective-permute-start | bytes 786440 | tf_op jit(solution)/shard_map/ppermute | solution.py:29
  40.1 11.4 %collective-permute-start.16 = (bf16[1,2,128,512]{3,2,1,0:T(8,128)(2,1)S(1)}, bf16[1,2,128,512]{3,2,1,0:T(8,128)(2,1)S(1)}, u32[]{:S(2)}, u32[]{:S(2)}) collective-permute-start(bf16[1,2,128,512]{3,2,1,0:T(8,128)(2,1)S(1)} %slice_bitcast_fusion.4), channel_id=1, source_target_pairs={{0,8},{4,12},{8,0},{12,4},{16,24},{20,28},{24,16},{28,20},{1,9},{5... | collective-permute-start | bytes 786440 | tf_op jit(solution)/shard_map/ppermute | solution.py:23
  46.6 7.3 %collective-permute-start.17 = (bf16[1,2,128,512]{3,2,1,0:T(8,128)(2,1)S(1)}, bf16[1,2,128,512]{3,2,1,0:T(8,128)(2,1)S(1)}, u32[]{:S(2)}, u32[]{:S(2)}) collective-permute-start(bf16[1,2,128,512]{3,2,1,0:T(8,128)(2,1)S(1)} %fusion.4), channel_id=1, source_target_pairs={{0,16},{4,20},{8,24},{12,28},{16,0},{20,4},{24,8},{28,12},{1,17},{... | collective-permute-start | bytes 786440 | tf_op jit(solution)/shard_map/ppermute | solution.py:29
  48.2 13.0 %collective-permute-start.15 = (bf16[1,2,128,512]{3,2,1,0:T(8,128)(2,1)S(1)}, bf16[1,2,128,512]{3,2,1,0:T(8,128)(2,1)S(1)}, u32[]{:S(2)}, u32[]{:S(2)}) collective-permute-start(bf16[1,2,128,512]{3,2,1,0:T(8,128)(2,1)S(1)} %fusion.7), channel_id=1, source_target_pairs={{0,8},{4,12},{8,0},{12,4},{16,24},{20,28},{24,16},{28,20},{1,9},{5... | collective-permute-start | bytes 786440 | tf_op jit(solution)/shard_map/ppermute | solution.py:23
  54.0 7.2 %collective-permute-start.18 = (bf16[1,2,128,512]{3,2,1,0:T(8,128)(2,1)S(1)}, bf16[1,2,128,512]{3,2,1,0:T(8,128)(2,1)S(1)}, u32[]{:S(2)}, u32[]{:S(2)}) collective-permute-start(bf16[1,2,128,512]{3,2,1,0:T(8,128)(2,1)S(1)} %get-tuple-element.86), channel_id=1, source_target_pairs={{0,16},{4,20},{8,24},{12,28},{16,0},{20,4},{24,8},{28,12},{1,17},{... | collective-permute-start | bytes 786440 | tf_op jit(solution)/shard_map/ppermute | solution.py:29
  55.6 13.1 %collective-permute-start.20 = (bf16[128,512]{1,0:T(8,128)(2,1)S(1)}, bf16[128,512]{1,0:T(8,128)(2,1)S(1)}, u32[]{:S(2)}, u32[]{:S(2)}) collective-permute-start(bf16[128,512]{1,0:T(8,128)(2,1)S(1)} %get-tuple-element.122), channel_id=1, source_target_pairs={{0,2},{1,3},{2,0},{3,1},{4,6},{5,7},{6,4},{7,5},{8,10},{9,11},{10,... | collective-permute-start | bytes 393224 | tf_op jit(solution)/shard_map/ppermute | solution.py:17
  60.2 9.0 %copy-start.1 = (bf16[128,512]{1,0:T(8,128)(2,1)S(1)}, bf16[128,512]{1,0:T(8,128)(2,1)}, u32[]{:S(2)}) copy-start(bf16[128,512]{1,0:T(8,128)(2,1)} %param.6) | copy-start | bytes 393220
  60.2 7.6 %collective-permute-start.19 = (bf16[128,512]{1,0:T(8,128)(2,1)S(1)}, bf16[128,512]{1,0:T(8,128)(2,1)S(1)}, u32[]{:S(2)}, u32[]{:S(2)}) collective-permute-start(bf16[128,512]{1,0:T(8,128)(2,1)S(1)} %get-tuple-element.121), channel_id=1, source_target_pairs={{0,3},{1,2},{2,1},{3,0},{4,7},{5,6},{6,5},{7,4},{8,11},{9,10},{10,... | collective-permute-start | bytes 393224 | tf_op jit(solution)/shard_map/ppermute | solution.py:17
  61.3 7.9 %collective-permute-start.21 = (bf16[128,512]{1,0:T(8,128)(2,1)S(1)}, bf16[128,512]{1,0:T(8,128)(2,1)S(1)}, u32[]{:S(2)}, u32[]{:S(2)}) collective-permute-start(bf16[128,512]{1,0:T(8,128)(2,1)S(1)} %fusion.13), channel_id=1, source_target_pairs={{0,1},{1,0},{2,3},{3,2},{4,5},{5,4},{6,7},{7,6},{8,9},{9,8},{10,11... | collective-permute-start | bytes 393224 | tf_op jit(solution)/shard_map/ppermute | solution.py:17
  70.0 5.8 %collective-permute-start.22 = (bf16[1,128,512]{2,1,0:T(8,128)(2,1)S(1)}, bf16[1,128,512]{2,1,0:T(8,128)(2,1)S(1)}, u32[]{:S(2)}, u32[]{:S(2)}) collective-permute-start(bf16[1,128,512]{2,1,0:T(8,128)(2,1)S(1)} %bitcast.83), channel_id=1, source_target_pairs={{0,16},{4,20},{8,24},{12,28},{16,0},{20,4},{24,8},{28,12},{1,17},{... | collective-permute-start | bytes 393224 | tf_op jit(solution)/shard_map/ppermute | solution.py:36
  70.8 6.4 %collective-permute-start.24 = (bf16[128,512]{1,0:T(8,128)(2,1)S(1)}, bf16[128,512]{1,0:T(8,128)(2,1)S(1)}, u32[]{:S(2)}, u32[]{:S(2)}) collective-permute-start(bf16[128,512]{1,0:T(8,128)(2,1)S(1)} %get-tuple-element.115), channel_id=1, source_target_pairs={{0,1},{1,0},{2,3},{3,2},{4,5},{5,4},{6,7},{7,6},{8,9},{9,8},{10,11... | collective-permute-start | bytes 393224 | tf_op jit(solution)/shard_map/ppermute | solution.py:17
  71.9 11.4 %collective-permute-start.26 = (bf16[128,512]{1,0:T(8,128)(2,1)S(1)}, bf16[128,512]{1,0:T(8,128)(2,1)S(1)}, u32[]{:S(2)}, u32[]{:S(2)}) collective-permute-start(bf16[128,512]{1,0:T(8,128)(2,1)S(1)} %get-tuple-element.115), channel_id=1, source_target_pairs={{0,2},{1,3},{2,0},{3,1},{4,6},{5,7},{6,4},{7,5},{8,10},{9,11},{10,... | collective-permute-start | bytes 393224 | tf_op jit(solution)/shard_map/ppermute | solution.py:17
  73.6 10.0 %collective-permute-start.27 = (bf16[128,512]{1,0:T(8,128)(2,1)S(1)}, bf16[128,512]{1,0:T(8,128)(2,1)S(1)}, u32[]{:S(2)}, u32[]{:S(2)}) collective-permute-start(bf16[128,512]{1,0:T(8,128)(2,1)S(1)} %get-tuple-element.115), channel_id=1, source_target_pairs={{0,3},{1,2},{2,1},{3,0},{4,7},{5,6},{6,5},{7,4},{8,11},{9,10},{10,... | collective-permute-start | bytes 393224 | tf_op jit(solution)/shard_map/ppermute | solution.py:17
  75.1 8.6 %collective-permute-start.32 = (bf16[1,128,512]{2,1,0:T(8,128)(2,1)S(1)}, bf16[1,128,512]{2,1,0:T(8,128)(2,1)S(1)}, u32[]{:S(2)}, u32[]{:S(2)}) collective-permute-start(bf16[1,128,512]{2,1,0:T(8,128)(2,1)S(1)} %bitcast.84), channel_id=1, source_target_pairs={{0,8},{4,12},{8,0},{12,4},{16,24},{20,28},{24,16},{28,20},{1,9},{5... | collective-permute-start | bytes 393224 | tf_op jit(solution)/shard_map/ppermute | solution.py:23
  75.8 9.8 %collective-permute-start.23 = (bf16[1,128,512]{2,1,0:T(8,128)(2,1)S(1)}, bf16[1,128,512]{2,1,0:T(8,128)(2,1)S(1)}, u32[]{:S(2)}, u32[]{:S(2)}) collective-permute-start(bf16[1,128,512]{2,1,0:T(8,128)(2,1)S(1)} %collective-permute-done.22.refs_0_), channel_id=1, source_target_pairs={{0,8},{4,12},{8,0},{12,4},{16,24},{20,28},{24,16},{28,20},{1,9},{5... | collective-permute-start | bytes 393224 | tf_op jit(solution)/shard_map/ppermute | solution.py:23
  77.2 9.9 %collective-permute-start.25 = (bf16[1,128,512]{2,1,0:T(8,128)(2,1)S(1)}, bf16[1,128,512]{2,1,0:T(8,128)(2,1)S(1)}, u32[]{:S(2)}, u32[]{:S(2)}) collective-permute-start(bf16[1,128,512]{2,1,0:T(8,128)(2,1)S(1)} %bitcast.87), channel_id=1, source_target_pairs={{0,16},{4,20},{8,24},{12,28},{16,0},{20,4},{24,8},{28,12},{1,17},{... | collective-permute-start | bytes 393224 | tf_op jit(solution)/shard_map/ppermute | solution.py:36
  83.3 6.4 %collective-permute-start.33 = (bf16[1,128,512]{2,1,0:T(8,128)(2,1)S(1)}, bf16[1,128,512]{2,1,0:T(8,128)(2,1)S(1)}, u32[]{:S(2)}, u32[]{:S(2)}) collective-permute-start(bf16[1,128,512]{2,1,0:T(8,128)(2,1)S(1)} %bitcast.88), channel_id=1, source_target_pairs={{0,8},{4,12},{8,0},{12,4},{16,24},{20,28},{24,16},{28,20},{1,9},{5... | collective-permute-start | bytes 393224 | tf_op jit(solution)/shard_map/ppermute | solution.py:23
  83.7 6.0 %collective-permute-start.36 = (bf16[2,128,512]{2,1,0:T(8,128)(2,1)S(1)}, bf16[2,128,512]{2,1,0:T(8,128)(2,1)S(1)}, u32[]{:S(2)}, u32[]{:S(2)}) collective-permute-start(bf16[2,128,512]{2,1,0:T(8,128)(2,1)S(1)} %pad_maximum_fusion.2.refs_2_), channel_id=1, source_target_pairs={{0,4},{4,0},{8,12},{12,8},{16,20},{20,16},{24,28},{28,24},{1,5},{5... | collective-permute-start | bytes 786440 | tf_op jit(solution)/shard_map/ppermute | solution.py:23
  83.8 10.5 %collective-permute-start.37 = (bf16[2,128,512]{2,1,0:T(8,128)(2,1)S(1)}, bf16[2,128,512]{2,1,0:T(8,128)(2,1)S(1)}, u32[]{:S(2)}, u32[]{:S(2)}) collective-permute-start(bf16[2,128,512]{2,1,0:T(8,128)(2,1)S(1)} %pad_maximum_fusion.2.refs_2_), channel_id=1, source_target_pairs={{0,8},{4,12},{8,0},{12,4},{16,24},{20,28},{24,16},{28,20},{1,9},{5... | collective-permute-start | bytes 786440 | tf_op jit(solution)/shard_map/ppermute | solution.py:23
  85.6 9.5 %collective-permute-start.28 = (bf16[2,128,512]{2,1,0:T(8,128)(2,1)S(1)}, bf16[2,128,512]{2,1,0:T(8,128)(2,1)S(1)}, u32[]{:S(2)}, u32[]{:S(2)}) collective-permute-start(bf16[2,128,512]{2,1,0:T(8,128)(2,1)S(1)} %pad_maximum_fusion.2.refs_2_), channel_id=1, source_target_pairs={{0,16},{4,20},{8,24},{12,28},{16,0},{20,4},{24,8},{28,12},{1,17},{... | collective-permute-start | bytes 786440 | tf_op jit(solution)/shard_map/ppermute | solution.py:36
  87.1 2.6 %collective-permute-start.35 = (bf16[1,128,512]{2,1,0:T(8,128)(2,1)S(1)}, bf16[1,128,512]{2,1,0:T(8,128)(2,1)S(1)}, u32[]{:S(2)}, u32[]{:S(2)}) collective-permute-start(bf16[1,128,512]{2,1,0:T(8,128)(2,1)S(1)} %bitcast.89), channel_id=1, source_target_pairs={{0,4},{4,0},{8,12},{12,8},{16,20},{20,16},{24,28},{28,24},{1,5},{5... | collective-permute-start | bytes 393224 | tf_op jit(solution)/shard_map/ppermute | solution.py:23
  89.7 1.3 %collective-permute-start.34 = (bf16[1,128,512]{2,1,0:T(8,128)(2,1)S(1)}, bf16[1,128,512]{2,1,0:T(8,128)(2,1)S(1)}, u32[]{:S(2)}, u32[]{:S(2)}) collective-permute-start(bf16[1,128,512]{2,1,0:T(8,128)(2,1)S(1)} %bitcast.85), channel_id=1, source_target_pairs={{0,4},{4,0},{8,12},{12,8},{16,20},{20,16},{24,28},{28,24},{1,5},{5... | collective-permute-start | bytes 393224 | tf_op jit(solution)/shard_map/ppermute | solution.py:23
  94.3 3.1 %collective-permute-start.40 = (bf16[2,128,512]{2,1,0:T(8,128)(2,1)S(1)}, bf16[2,128,512]{2,1,0:T(8,128)(2,1)S(1)}, u32[]{:S(2)}, u32[]{:S(2)}) collective-permute-start(bf16[2,128,512]{2,1,0:T(8,128)(2,1)S(1)} %collective-permute-done.37.refs_2_), channel_id=1, source_target_pairs={{0,4},{4,0},{8,12},{12,8},{16,20},{20,16},{24,28},{28,24},{1,5},{5... | collective-permute-start | bytes 786440 | tf_op jit(solution)/shard_map/ppermute | solution.py:23
  94.5 2.4 %collective-permute-start.39 = (bf16[1,128,512]{2,1,0:T(8,128)(2,1)S(1)}, bf16[1,128,512]{2,1,0:T(8,128)(2,1)S(1)}, u32[]{:S(2)}, u32[]{:S(2)}) collective-permute-start(bf16[1,128,512]{2,1,0:T(8,128)(2,1)S(1)} %collective-permute-done.33.refs_1_), channel_id=1, source_target_pairs={{0,4},{4,0},{8,12},{12,8},{16,20},{20,16},{24,28},{28,24},{1,5},{5... | collective-permute-start | bytes 393224 | tf_op jit(solution)/shard_map/ppermute | solution.py:23
  94.9 2.0 %collective-permute-start.38 = (bf16[1,128,512]{2,1,0:T(8,128)(2,1)S(1)}, bf16[1,128,512]{2,1,0:T(8,128)(2,1)S(1)}, u32[]{:S(2)}, u32[]{:S(2)}) collective-permute-start(bf16[1,128,512]{2,1,0:T(8,128)(2,1)S(1)} %collective-permute-done.32.refs_0_), channel_id=1, source_target_pairs={{0,4},{4,0},{8,12},{12,8},{16,20},{20,16},{24,28},{28,24},{1,5},{5... | collective-permute-start | bytes 393224 | tf_op jit(solution)/shard_map/ppermute | solution.py:23
  95.0 5.6 %collective-permute-start.31 = (bf16[2,128,512]{2,1,0:T(8,128)(2,1)S(1)}, bf16[2,128,512]{2,1,0:T(8,128)(2,1)S(1)}, u32[]{:S(2)}, u32[]{:S(2)}) collective-permute-start(bf16[2,128,512]{2,1,0:T(8,128)(2,1)S(1)} %collective-permute-done.28.refs_2_), channel_id=1, source_target_pairs={{0,4},{4,0},{8,12},{12,8},{16,20},{20,16},{24,28},{28,24},{1,5},{5... | collective-permute-start | bytes 786440 | tf_op jit(solution)/shard_map/ppermute | solution.py:23
  95.4 9.5 %collective-permute-start.42 = (bf16[2,128,512]{2,1,0:T(8,128)(2,1)S(1)}, bf16[2,128,512]{2,1,0:T(8,128)(2,1)S(1)}, u32[]{:S(2)}, u32[]{:S(2)}) collective-permute-start(bf16[2,128,512]{2,1,0:T(8,128)(2,1)S(1)} %collective-permute-done.37.refs_2_), channel_id=1, source_target_pairs={{0,16},{4,20},{8,24},{12,28},{16,0},{20,4},{24,8},{28,12},{1,17},{... | collective-permute-start | bytes 786440 | tf_op jit(solution)/shard_map/ppermute | solution.py:36
  96.9 3.8 %collective-permute-start.29 = (bf16[1,128,512]{2,1,0:T(8,128)(2,1)S(1)}, bf16[1,128,512]{2,1,0:T(8,128)(2,1)S(1)}, u32[]{:S(2)}, u32[]{:S(2)}) collective-permute-start(bf16[1,128,512]{2,1,0:T(8,128)(2,1)S(1)} %collective-permute-done.22.refs_0_), channel_id=1, source_target_pairs={{0,4},{4,0},{8,12},{12,8},{16,20},{20,16},{24,28},{28,24},{1,5},{5... | collective-permute-start | bytes 393224 | tf_op jit(solution)/shard_map/ppermute | solution.py:23
  96.9 3.8 %collective-permute-start.30 = (bf16[1,128,512]{2,1,0:T(8,128)(2,1)S(1)}, bf16[1,128,512]{2,1,0:T(8,128)(2,1)S(1)}, u32[]{:S(2)}, u32[]{:S(2)}) collective-permute-start(bf16[1,128,512]{2,1,0:T(8,128)(2,1)S(1)} %collective-permute-done.25.refs_1_), channel_id=1, source_target_pairs={{0,4},{4,0},{8,12},{12,8},{16,20},{20,16},{24,28},{28,24},{1,5},{5... | collective-permute-start | bytes 393224 | tf_op jit(solution)/shard_map/ppermute | solution.py:23
  97.4 7.6 %collective-permute-start.41 = (bf16[1,128,512]{2,1,0:T(8,128)(2,1)S(1)}, bf16[1,128,512]{2,1,0:T(8,128)(2,1)S(1)}, u32[]{:S(2)}, u32[]{:S(2)}) collective-permute-start(bf16[1,128,512]{2,1,0:T(8,128)(2,1)S(1)} %collective-permute-done.25.refs_1_), channel_id=1, source_target_pairs={{0,8},{4,12},{8,0},{12,4},{16,24},{20,28},{24,16},{28,20},{1,9},{5... | collective-permute-start | bytes 393224 | tf_op jit(solution)/shard_map/ppermute | solution.py:23
  104.9 2.0 %collective-permute-start.45 = (bf16[2,128,512]{2,1,0:T(8,128)(2,1)S(1)}, bf16[2,128,512]{2,1,0:T(8,128)(2,1)S(1)}, u32[]{:S(2)}, u32[]{:S(2)}) collective-permute-start(bf16[2,128,512]{2,1,0:T(8,128)(2,1)S(1)} %collective-permute-done.42.refs_2_), channel_id=1, source_target_pairs={{0,4},{4,0},{8,12},{12,8},{16,20},{20,16},{24,28},{28,24},{1,5},{5... | collective-permute-start | bytes 786440 | tf_op jit(solution)/shard_map/ppermute | solution.py:23
  105.0 1.6 %collective-permute-start.44 = (bf16[1,128,512]{2,1,0:T(8,128)(2,1)S(1)}, bf16[1,128,512]{2,1,0:T(8,128)(2,1)S(1)}, u32[]{:S(2)}, u32[]{:S(2)}) collective-permute-start(bf16[1,128,512]{2,1,0:T(8,128)(2,1)S(1)} %collective-permute-done.41.refs_1_), channel_id=1, source_target_pairs={{0,4},{4,0},{8,12},{12,8},{16,20},{20,16},{24,28},{28,24},{1,5},{5... | collective-permute-start | bytes 393224 | tf_op jit(solution)/shard_map/ppermute | solution.py:23
  105.5 1.4 %collective-permute-start.43 = (bf16[1,128,512]{2,1,0:T(8,128)(2,1)S(1)}, bf16[1,128,512]{2,1,0:T(8,128)(2,1)S(1)}, u32[]{:S(2)}, u32[]{:S(2)}) collective-permute-start(bf16[1,128,512]{2,1,0:T(8,128)(2,1)S(1)} %collective-permute-done.23.refs_0_), channel_id=1, source_target_pairs={{0,4},{4,0},{8,12},{12,8},{16,20},{20,16},{24,28},{28,24},{1,5},{5... | collective-permute-start | bytes 393224 | tf_op jit(solution)/shard_map/ppermute | solution.py:23

commit v10 on v7

--- a/solution.py
+++ b/solution.py
@@ -377,7 +377,9 @@
         known = [0]
         for bit_level in range(bit_count - 1, 0, -1):
             for rel in known:
-                value = after(held[rel][s], dec_held) if s > 1 else held[rel][s]
+                value = held[rel][s]
+                if s > 1:
+                    value = after(value, dec_held, held[rel ^ 2**bit_level][1])
                 held[rel ^ 2**bit_level][s] = over_members(value, bit_level)
             known += [rel ^ 2**bit_level for rel in known]
     early = [

time: 114 us -> 115 us (level)
  starting transfers between devices: 43.7 us -> 46.4 us
  waiting for transfers between devices: 33.5 us -> 31.2 us
    ppermute x9, waiting for transfers between devices: 12.8 us -> 8.28 us  [over_feat(): return lax.ppermute(value, 'feat', pairs)]
    ppermute x9, starting transfers between devices: 18.1 us -> 21.8 us  [over_feat(): return lax.ppermute(value, 'feat', pairs)]
    ppermute x30, waiting for transfers between devices: 17.9 us -> 19.4 us  [over_members(): return lax.ppermute(value, 'layer', pairs)]
where the time goes in v10:
time: 115 us
  starting transfers between devices  46.4 us (40%)
  Pallas kernels  33.6 us (29%)
  waiting for transfers between devices  31.2 us (27%)
  other arithmetic  1.96 us (2%)
  between operations  1.17 us (1%)
    ppermute x9, starting transfers between devices, over_feat(): return lax.ppermute(value, 'feat', pairs)  21.8 us
    ppermute x30, waiting for transfers between devices, over_members(): return lax.ppermute(value, 'layer', pairs)  19.4 us
    ppermute x30, starting transfers between devices, over_members(): return lax.ppermute(value, 'layer', pairs)  15.7 us
    pallas_call x4, Pallas kernels, backward_pair(): pl.pallas_call(kernel, in_specs=[in_smem] + [in_vmem] * (len(inputs) + 2)...  12.8 us
    ppermute x9, waiting for transfers between devices, over_feat(): return lax.ppermute(value, 'feat', pairs)  8.28 us
    pallas_call x2, Pallas kernels, decode(): pl.pallas_call(kernel, in_specs=[in_smem, in_vmem, in_vmem], out_specs=[i...  5.78 us
    pallas_call x1, Pallas kernels, encoder_grad(): pl.pallas_call(kernel, in_specs=[in_smem] + [in_vmem] * (len(turned_token...  4.79 us
    ppermute x3, starting transfers between devices, to_layer(): moved = lax.ppermute(value, 'layer', pairs)  4.77 us
  transfers between devices with their start and end apart: 46, of which 19 were waited for; matrix products, arithmetic and copies ran while one was open for 1% of the time, Pallas kernels for 19%

profile of v10, /device:TPU:0, one launch (start us, length us, event | category | flops | bytes accessed | tf_op | source)
XLA Modules:
  0.0 114.5 jit_solution(13744206657493334977)
XLA Ops:
  0.7 3.0 %collective-permute-start.1 = (bf16[128,512]{1,0:T(8,128)(2,1)}, bf16[128,512]{1,0:T(8,128)(2,1)S(1)}, u32[]{:S(2)}, u32[]{:S(2)}) collective-permute-start(bf16[128,512]{1,0:T(8,128)(2,1)} %param.5), channel_id=1, source_target_pairs={{0,1},{1,0},{2,3},{3,2},{4,5},{5,4},{6,7},{7,6},{8,9},{9,8},{10,11... | collective-permute-start | bytes 393224 | tf_op jit(solution)/shard_map/ppermute | solution.py:17
  3.8 2.5 %collective-permute-start.3 = (bf16[128,512]{1,0:T(8,128)(2,1)}, bf16[128,512]{1,0:T(8,128)(2,1)S(1)}, u32[]{:S(2)}, u32[]{:S(2)}) collective-permute-start(bf16[128,512]{1,0:T(8,128)(2,1)} %param.5), channel_id=1, source_target_pairs={{0,3},{1,2},{2,1},{3,0},{4,7},{5,6},{6,5},{7,4},{8,11},{9,10},{10,... | collective-permute-start | bytes 393224 | tf_op jit(solution)/shard_map/ppermute | solution.py:17
  6.2 1.3 %collective-permute-done.1 = bf16[128,512]{1,0:T(8,128)(2,1)S(1)} collective-permute-done((bf16[128,512]{1,0:T(8,128)(2,1)}, bf16[128,512]{1,0:T(8,128)(2,1)S(1)}, u32[]{:S(2)}, u32[]{:S(2)}) %collective-permute-start.1) | collective-permute-done | bytes 131104 | tf_op jit(solution)/shard_map/ppermute | solution.py:17
  7.5 1.6 %collective-permute-start.4 = (bf16[128,512]{1,0:T(8,128)(2,1)S(1)}, bf16[128,512]{1,0:T(8,128)(2,1)S(1)}, u32[]{:S(2)}, u32[]{:S(2)}) collective-permute-start(bf16[128,512]{1,0:T(8,128)(2,1)S(1)} %collective-permute-done.1), channel_id=1, source_target_pairs={{0,8},{4,12},{8,0},{12,4},{16,24},{20,28},{24,16},{28,20},{1,9},{5... | collective-permute-start | bytes 393224 | tf_op jit(solution)/shard_map/ppermute | solution.py:23
  9.1 3.7 %collective-permute-start.2 = (bf16[128,512]{1,0:T(8,128)(2,1)}, bf16[128,512]{1,0:T(8,128)(2,1)S(1)}, u32[]{:S(2)}, u32[]{:S(2)}) collective-permute-start(bf16[128,512]{1,0:T(8,128)(2,1)} %param.5), channel_id=1, source_target_pairs={{0,2},{1,3},{2,0},{3,1},{4,6},{5,7},{6,4},{7,5},{8,10},{9,11},{10,... | collective-permute-start | bytes 393224 | tf_op jit(solution)/shard_map/ppermute | solution.py:17
  12.9 0.5 collective-permute-start
  13.4 4.7 %fetch.1 = (bf16[2048,1024]{1,0:T(8,128)(2,1)S(1)}, bf16[2,1024,2048]{2,1,0:T(8,128)(2,1)S(1)}) custom-call(bf16[2048,1024]{1,0:T(8,128)(2,1)} %refs_0_.1, bf16[2,1024,2048]{2,1,0:T(8,128)(2,1)} %refs_1_), custom_call_target="tpu_custom_call" | custom-call | bytes 12582912 | tf_op jit(solution)/shard_map/fetch/pallas_call | solution.py:88
  18.2 1.6 %collective-permute-start.5 = (bf16[128,512]{1,0:T(8,128)(2,1)S(1)}, bf16[128,512]{1,0:T(8,128)(2,1)S(1)}, u32[]{:S(2)}, u32[]{:S(2)}) collective-permute-start(bf16[128,512]{1,0:T(8,128)(2,1)S(1)} %collective-permute-done.3), channel_id=1, source_target_pairs={{0,8},{4,12},{8,0},{12,4},{16,24},{20,28},{24,16},{28,20},{1,9},{5... | collective-permute-start | bytes 393224 | tf_op jit(solution)/shard_map/ppermute | solution.py:23
  19.8 3.4 %collective-permute-done.5 = bf16[128,512]{1,0:T(8,128)(2,1)S(1)} collective-permute-done((bf16[128,512]{1,0:T(8,128)(2,1)S(1)}, bf16[128,512]{1,0:T(8,128)(2,1)S(1)}, u32[]{:S(2)}, u32[]{:S(2)}) %collective-permute-start.5) | collective-permute-done | bytes 131104 | tf_op jit(solution)/shard_map/ppermute | solution.py:23
  23.2 1.5 %collective-permute-start.7 = (bf16[128,512]{1,0:T(8,128)(2,1)S(1)}, bf16[128,512]{1,0:T(8,128)(2,1)S(1)}, u32[]{:S(2)}, u32[]{:S(2)}) collective-permute-start(bf16[128,512]{1,0:T(8,128)(2,1)S(1)} %collective-permute-done.2), channel_id=1, source_target_pairs={{0,8},{4,12},{8,0},{12,4},{16,24},{20,28},{24,16},{28,20},{1,9},{5... | collective-permute-start | bytes 393224 | tf_op jit(solution)/shard_map/ppermute | solution.py:23
  24.7 0.4 collective-permute-done.6.refs_1_
  25.1 1.8 %encode.3.refs_2_ = f32[512,1024]{1,0:T(8,128)S(1)} custom-call(s32[2]{0:T(128)S(1)} %pad_add_fusion.info_ref, bf16[4,128,512]{2,1,0:T(8,128)(2,1)S(1)} %pad_maximum_fusion.refs_0_, bf16[4,128,512]{2,1,0:T(8,128)(2,1)S(1)} %collective-permute-done.6.refs_1_, bf16[2048,1024]{1,0:T(8,128)(2,1)S(1)} %get-tuple-element.63.refs_2_.refs_1_), custom_call_target="tpu_custom_call" | custom-call | flops 1073741824 | bytes 3145728 | tf_op jit(solution)/shard_map/encode/pallas_call | solution.py:128
  26.9 2.2 %collective-permute-done.7 = bf16[128,512]{1,0:T(8,128)(2,1)S(1)} collective-permute-done((bf16[128,512]{1,0:T(8,128)(2,1)S(1)}, bf16[128,512]{1,0:T(8,128)(2,1)S(1)}, u32[]{:S(2)}, u32[]{:S(2)}) %collective-permute-start.7) | collective-permute-done | bytes 131104 | tf_op jit(solution)/shard_map/ppermute | solution.py:23
  29.3 1.3 %encode.4.refs_2_ = f32[512,1024]{1,0:T(8,128)S(1)} custom-call(s32[2]{0:T(128)S(1)} %pad_add_fusion.info_ref, bf16[4,128,512]{2,1,0:T(8,128)(2,1)S(1)} %pad_maximum_fusion.1.refs_0_, bf16[2048,1024]{1,0:T(8,128)(2,1)S(1)} %get-tuple-element.63.refs_2_.refs_1_, f32[512,1024]{1,0:T(8,128)S(1)} %encode.3.refs_2_), custom_call_target="tpu_custom_call" | custom-call | flops 536870912 | bytes 1572864 | tf_op jit(solution)/shard_map/encode/pallas_call | solution.py:128
  30.5 0.6 collective-permute-done.8.refs_0_
  31.2 1.4 %encode.5.feat_ref.in_ref.refs_4_ = bf16[2,512,1024]{2,1,0:T(8,128)(2,1)S(1)} custom-call(s32[2]{0:T(128)S(1)} %pad_add_fusion.info_ref, bf16[4,128,512]{2,1,0:T(8,128)(2,1)S(1)} %collective-permute-done.8.refs_0_, bf16[2048,1024]{1,0:T(8,128)(2,1)S(1)} %get-tuple-element.63.refs_2_.refs_1_, f32[512,1024]{1,0:T(8,128)S(1)} %encode.4.refs_2_, ...), custom_call_target="tpu_custom_call" | custom-call | flops 536870912 | bytes 1572864 | tf_op jit(solution)/shard_map/encode/pallas_call | solution.py:128
  32.6 2.9 %decode.2 = (bf16[2,2,128,512]{3,2,1,0:T(8,128)(2,1)S(1)}, bf16[2,2,128,512]{3,2,1,0:T(8,128)(2,1)S(1)}, bf16[2,2,128,512]{3,2,1,0:T(8,128)(2,1)S(1)}, bf16[2,2,128,512]{3,2,1,0:T(8,128)(2,1)S(1)}) custom-call(s32[2]{0:T(128)S(1)} %pad_add_fusion.info_ref, bf16[2,512,1024]{2,1,0:T(8,128)(2,1)S(1)} %encode.5.feat_ref.in_ref.refs_4_, ...), custom_call_target="tpu_custom_call" | custom-call | flops 2147483648 | bytes 4194304 | tf_op jit(solution)/shard_map/decode/pallas_call | solution.py:167
  35.7 0.4 collective-permute-start.10
  36.1 2.9 %decode.3 = (bf16[2,2,128,512]{3,2,1,0:T(8,128)(2,1)S(1)}, bf16[2,2,128,512]{3,2,1,0:T(8,128)(2,1)S(1)}, bf16[2,2,128,512]{3,2,1,0:T(8,128)(2,1)S(1)}, bf16[2,2,128,512]{3,2,1,0:T(8,128)(2,1)S(1)}) custom-call(s32[2]{0:T(128)S(1)} %pad_add_fusion.info_ref, bf16[2,512,1024]{2,1,0:T(8,128)(2,1)S(1)} %encode.5.feat_ref.in_ref.refs_4_, ...), custom_call_target="tpu_custom_call" | custom-call | flops 2147483648 | bytes 4194304 | tf_op jit(solution)/shard_map/decode/pallas_call | solution.py:167
  39.2 0.4 collective-permute-start.9
  39.7 1.6 %collective-permute-start.13 = (bf16[1,2,128,512]{3,2,1,0:T(8,128)(2,1)S(1)}, bf16[1,2,128,512]{3,2,1,0:T(8,128)(2,1)S(1)}, u32[]{:S(2)}, u32[]{:S(2)}) collective-permute-start(bf16[1,2,128,512]{3,2,1,0:T(8,128)(2,1)S(1)} %slice_bitcast_fusion.5), channel_id=1, source_target_pairs={{0,8},{4,12},{8,0},{12,4},{16,24},{20,28},{24,16},{28,20},{1,9},{5... | collective-permute-start | bytes 786440 | tf_op jit(solution)/shard_map/ppermute | solution.py:23
  41.5 1.6 %collective-permute-start.11 = (bf16[1,2,128,512]{3,2,1,0:T(8,128)(2,1)S(1)}, bf16[1,2,128,512]{3,2,1,0:T(8,128)(2,1)S(1)}, u32[]{:S(2)}, u32[]{:S(2)}) collective-permute-start(bf16[1,2,128,512]{3,2,1,0:T(8,128)(2,1)S(1)} %get-tuple-element.120), channel_id=1, source_target_pairs={{0,16},{4,20},{8,24},{12,28},{16,0},{20,4},{24,8},{28,12},{1,17},{... | collective-permute-start | bytes 786440 | tf_op jit(solution)/shard_map/ppermute | solution.py:29
  43.2 0.6 collective-permute-start.16
  44.0 4.9 %collective-permute-done.13 = bf16[1,2,128,512]{3,2,1,0:T(8,128)(2,1)S(1)} collective-permute-done((bf16[1,2,128,512]{3,2,1,0:T(8,128)(2,1)S(1)}, bf16[1,2,128,512]{3,2,1,0:T(8,128)(2,1)S(1)}, u32[]{:S(2)}, u32[]{:S(2)}) %collective-permute-start.13) | collective-permute-done | bytes 262176 | tf_op jit(solution)/shard_map/ppermute | solution.py:23
  49.0 0.6 collective-permute-done.11
  49.7 1.6 %collective-permute-start.17 = (bf16[1,2,128,512]{3,2,1,0:T(8,128)(2,1)S(1)}, bf16[1,2,128,512]{3,2,1,0:T(8,128)(2,1)S(1)}, u32[]{:S(2)}, u32[]{:S(2)}) collective-permute-start(bf16[1,2,128,512]{3,2,1,0:T(8,128)(2,1)S(1)} %fusion.4), channel_id=1, source_target_pairs={{0,16},{4,20},{8,24},{12,28},{16,0},{20,4},{24,8},{28,12},{1,17},{... | collective-permute-start | bytes 786440 | tf_op jit(solution)/shard_map/ppermute | solution.py:29
  51.3 0.9 collective-permute-start.15
  52.2 2.4 %collective-permute-done.16 = bf16[1,2,128,512]{3,2,1,0:T(8,128)(2,1)S(1)} collective-permute-done((bf16[1,2,128,512]{3,2,1,0:T(8,128)(2,1)S(1)}, bf16[1,2,128,512]{3,2,1,0:T(8,128)(2,1)S(1)}, u32[]{:S(2)}, u32[]{:S(2)}) %collective-permute-start.16) | collective-permute-done | bytes 262176 | tf_op jit(solution)/shard_map/ppermute | solution.py:23
  54.6 2.4 %collective-permute-done.17 = bf16[1,2,128,512]{3,2,1,0:T(8,128)(2,1)S(1)} collective-permute-done((bf16[1,2,128,512]{3,2,1,0:T(8,128)(2,1)S(1)}, bf16[1,2,128,512]{3,2,1,0:T(8,128)(2,1)S(1)}, u32[]{:S(2)}, u32[]{:S(2)}) %collective-permute-start.17) | collective-permute-done | bytes 262176 | tf_op jit(solution)/shard_map/ppermute | solution.py:29
  57.1 1.6 %collective-permute-start.18 = (bf16[1,2,128,512]{3,2,1,0:T(8,128)(2,1)S(1)}, bf16[1,2,128,512]{3,2,1,0:T(8,128)(2,1)S(1)}, u32[]{:S(2)}, u32[]{:S(2)}) collective-permute-start(bf16[1,2,128,512]{3,2,1,0:T(8,128)(2,1)S(1)} %get-tuple-element.86), channel_id=1, source_target_pairs={{0,16},{4,20},{8,24},{12,28},{16,0},{20,4},{24,8},{28,12},{1,17},{... | collective-permute-start | bytes 786440 | tf_op jit(solution)/shard_map/ppermute | solution.py:29
  58.8 5.5 %collective-permute-start.19 = (bf16[128,512]{1,0:T(8,128)(2,1)S(1)}, bf16[128,512]{1,0:T(8,128)(2,1)S(1)}, u32[]{:S(2)}, u32[]{:S(2)}) collective-permute-start(bf16[128,512]{1,0:T(8,128)(2,1)S(1)} %get-tuple-element.121), channel_id=1, source_target_pairs={{0,3},{1,2},{2,1},{3,0},{4,7},{5,6},{6,5},{7,4},{8,11},{9,10},{10,... | collective-permute-start | bytes 393224 | tf_op jit(solution)/shard_map/ppermute | solution.py:17
  64.4 2.5 %collective-permute-start.21 = (bf16[128,512]{1,0:T(8,128)(2,1)S(1)}, bf16[128,512]{1,0:T(8,128)(2,1)S(1)}, u32[]{:S(2)}, u32[]{:S(2)}) collective-permute-start(bf16[128,512]{1,0:T(8,128)(2,1)S(1)} %fusion.13), channel_id=1, source_target_pairs={{0,1},{1,0},{2,3},{3,2},{4,5},{5,4},{6,7},{7,6},{8,9},{9,8},{10,11... | collective-permute-start | bytes 393224 | tf_op jit(solution)/shard_map/ppermute | solution.py:17
  67.0 0.3 turned.5
  68.1 1.7 %collective-permute-done.19 = bf16[128,512]{1,0:T(8,128)(2,1)S(1)} collective-permute-done((bf16[128,512]{1,0:T(8,128)(2,1)S(1)}, bf16[128,512]{1,0:T(8,128)(2,1)S(1)}, u32[]{:S(2)}, u32[]{:S(2)}) %collective-permute-start.19) | collective-permute-done | bytes 131104 | tf_op jit(solution)/shard_map/ppermute | solution.py:17
  69.8 0.5 collective-permute-done.20
  70.2 1.3 %collective-permute-done.21 = bf16[128,512]{1,0:T(8,128)(2,1)S(1)} collective-permute-done((bf16[128,512]{1,0:T(8,128)(2,1)S(1)}, bf16[128,512]{1,0:T(8,128)(2,1)S(1)}, u32[]{:S(2)}, u32[]{:S(2)}) %collective-permute-start.21) | collective-permute-done | bytes 131104 | tf_op jit(solution)/shard_map/ppermute | solution.py:17
  71.6 0.8 multiply_convert_fusion
  72.4 0.5 collective-permute-start.22
  72.9 1.4 %collective-permute-start.24 = (bf16[128,512]{1,0:T(8,128)(2,1)S(1)}, bf16[128,512]{1,0:T(8,128)(2,1)S(1)}, u32[]{:S(2)}, u32[]{:S(2)}) collective-permute-start(bf16[128,512]{1,0:T(8,128)(2,1)S(1)} %get-tuple-element.115), channel_id=1, source_target_pairs={{0,1},{1,0},{2,3},{3,2},{4,5},{5,4},{6,7},{7,6},{8,9},{9,8},{10,11... | collective-permute-start | bytes 393224 | tf_op jit(solution)/shard_map/ppermute | solution.py:17
  74.3 0.7 collective-permute-start.26
  75.0 2.3 %collective-permute-start.27 = (bf16[128,512]{1,0:T(8,128)(2,1)S(1)}, bf16[128,512]{1,0:T(8,128)(2,1)S(1)}, u32[]{:S(2)}, u32[]{:S(2)}) collective-permute-start(bf16[128,512]{1,0:T(8,128)(2,1)S(1)} %get-tuple-element.115), channel_id=1, source_target_pairs={{0,3},{1,2},{2,1},{3,0},{4,7},{5,6},{6,5},{7,4},{8,11},{9,10},{10,... | collective-permute-start | bytes 393224 | tf_op jit(solution)/shard_map/ppermute | solution.py:17
  77.4 0.5 collective-permute-done.22.refs_0_
  77.9 1.4 %collective-permute-start.23 = (bf16[1,128,512]{2,1,0:T(8,128)(2,1)S(1)}, bf16[1,128,512]{2,1,0:T(8,128)(2,1)S(1)}, u32[]{:S(2)}, u32[]{:S(2)}) collective-permute-start(bf16[1,128,512]{2,1,0:T(8,128)(2,1)S(1)} %collective-permute-done.22.refs_0_), channel_id=1, source_target_pairs={{0,8},{4,12},{8,0},{12,4},{16,24},{20,28},{24,16},{28,20},{1,9},{5... | collective-permute-start | bytes 393224 | tf_op jit(solution)/shard_map/ppermute | solution.py:23
  79.3 0.4 collective-permute-done.24
  79.7 1.1 collective-permute-start.25
  80.8 3.1 %collective-permute-done.26 = bf16[128,512]{1,0:T(8,128)(2,1)S(1)} collective-permute-done((bf16[128,512]{1,0:T(8,128)(2,1)S(1)}, bf16[128,512]{1,0:T(8,128)(2,1)S(1)}, u32[]{:S(2)}, u32[]{:S(2)}) %collective-permute-start.26) | collective-permute-done | bytes 131104 | tf_op jit(solution)/shard_map/ppermute | solution.py:17
  83.9 0.4 collective-permute-start.33
  84.5 1.7 %collective-permute-start.37 = (bf16[2,128,512]{2,1,0:T(8,128)(2,1)S(1)}, bf16[2,128,512]{2,1,0:T(8,128)(2,1)S(1)}, u32[]{:S(2)}, u32[]{:S(2)}) collective-permute-start(bf16[2,128,512]{2,1,0:T(8,128)(2,1)S(1)} %pad_maximum_fusion.2.refs_2_), channel_id=1, source_target_pairs={{0,8},{4,12},{8,0},{12,4},{16,24},{20,28},{24,16},{28,20},{1,9},{5... | collective-permute-start | bytes 786440 | tf_op jit(solution)/shard_map/ppermute | solution.py:23
  86.1 1.3 %collective-permute-start.28 = (bf16[2,128,512]{2,1,0:T(8,128)(2,1)S(1)}, bf16[2,128,512]{2,1,0:T(8,128)(2,1)S(1)}, u32[]{:S(2)}, u32[]{:S(2)}) collective-permute-start(bf16[2,128,512]{2,1,0:T(8,128)(2,1)S(1)} %pad_maximum_fusion.2.refs_2_), channel_id=1, source_target_pairs={{0,16},{4,20},{8,24},{12,28},{16,0},{20,4},{24,8},{28,12},{1,17},{... | collective-permute-start | bytes 786440 | tf_op jit(solution)/shard_map/ppermute | solution.py:36
  87.5 2.7 %collective-permute-done.33.refs_1_ = bf16[1,128,512]{2,1,0:T(8,128)(2,1)S(1)} collective-permute-done((bf16[1,128,512]{2,1,0:T(8,128)(2,1)S(1)}, bf16[1,128,512]{2,1,0:T(8,128)(2,1)S(1)}, u32[]{:S(2)}, u32[]{:S(2)}) %collective-permute-start.33) | collective-permute-done | bytes 131104 | tf_op jit(solution)/shard_map/ppermute | solution.py:23
  90.2 1.3 %collective-permute-done.34.refs_3_ = bf16[1,128,512]{2,1,0:T(8,128)(2,1)S(1)} collective-permute-done((bf16[1,128,512]{2,1,0:T(8,128)(2,1)S(1)}, bf16[1,128,512]{2,1,0:T(8,128)(2,1)S(1)}, u32[]{:S(2)}, u32[]{:S(2)}) %collective-permute-start.34) | collective-permute-done | bytes 131104 | tf_op jit(solution)/shard_map/ppermute | solution.py:23
  91.6 3.2 %backward_pair.4 = (f32[512,1024]{1,0:T(8,128)S(1)}, bf16[2,1024,2048]{2,1,0:T(8,128)(2,1)}, f32[8,128]{1,0:T(8,128)S(1)}) custom-call(s32[2]{0:T(128)S(1)} %pad_add_fusion.info_ref, bf16[1,128,512]{2,1,0:T(8,128)(2,1)S(1)} %bitcast.86, bf16[1,128,512]{2,1,0:T(8,128)(2,1)S(1)} %bitcast.90, bf16[2,128,512]{2,1,0:T(8,128)(2,1)S(1)} %pad_maximum_fusion.2.refs_2_, ...), custom_call_target="tpu_custom_call" | custom-call | flops 262144 | bytes 262144 | tf_op jit(solution)/shard_map/backward_pair/pallas_call | solution.py:273
  94.8 0.2 collective-permute-start.40
  95.0 0.4 collective-permute-start.39
  95.5 0.4 collective-permute-start.31
  95.9 1.2 %collective-permute-start.42 = (bf16[2,128,512]{2,1,0:T(8,128)(2,1)S(1)}, bf16[2,128,512]{2,1,0:T(8,128)(2,1)S(1)}, u32[]{:S(2)}, u32[]{:S(2)}) collective-permute-start(bf16[2,128,512]{2,1,0:T(8,128)(2,1)S(1)} %collective-permute-done.37.refs_2_), channel_id=1, source_target_pairs={{0,16},{4,20},{8,24},{12,28},{16,0},{20,4},{24,8},{28,12},{1,17},{... | collective-permute-start | bytes 786440 | tf_op jit(solution)/shard_map/ppermute | solution.py:36
  97.1 0.5 collective-permute-start.30
  97.6 0.3 collective-permute-start.41
  97.9 3.1 %backward_pair.5 = (f32[512,1024]{1,0:T(8,128)S(1)}, bf16[2,1024,2048]{2,1,0:T(8,128)(2,1)}, f32[8,128]{1,0:T(8,128)S(1)}) custom-call(s32[2]{0:T(128)S(1)} %pad_add_fusion.info_ref, bf16[1,128,512]{2,1,0:T(8,128)(2,1)S(1)} %collective-permute-done.32.refs_0_, ...), custom_call_target="tpu_custom_call", output_to_operand_aliasing={{0}: (9, {}), {1}: (10, {})} | custom-call | flops 262144 | bytes 262144 | tf_op jit(solution)/shard_map/backward_pair/pallas_call | solution.py:273
  101.1 3.2 %backward_pair.6 = (f32[512,1024]{1,0:T(8,128)S(1)}, bf16[2,1024,2048]{2,1,0:T(8,128)(2,1)}, f32[8,128]{1,0:T(8,128)S(1)}) custom-call(s32[2]{0:T(128)S(1)} %pad_add_fusion.info_ref, bf16[1,128,512]{2,1,0:T(8,128)(2,1)S(1)} %collective-permute-done.22.refs_0_, ...), custom_call_target="tpu_custom_call", output_to_operand_aliasing={{0}: (9, {}), {1}: (10, {})} | custom-call | flops 262144 | bytes 262144 | tf_op jit(solution)/shard_map/backward_pair/pallas_call | solution.py:273
  104.4 0.5 collective-permute-start.44
  105.0 1.1 collective-permute-done.44.refs_4_
  106.3 3.2 %backward_pair.7 = (f32[512,1024]{1,0:T(8,128)S(1)}, bf16[2,1024,2048]{2,1,0:T(8,128)(2,1)}, f32[8,128]{1,0:T(8,128)S(1)}) custom-call(s32[2]{0:T(128)S(1)} %pad_add_fusion.info_ref, bf16[1,128,512]{2,1,0:T(8,128)(2,1)S(1)} %collective-permute-done.23.refs_0_, ...), custom_call_target="tpu_custom_call", output_to_operand_aliasing={{0}: (9, {}), {1}: (10, {})} | custom-call | flops 262144 | bytes 262144 | tf_op jit(solution)/shard_map/backward_pair/pallas_call | solution.py:273
  109.6 4.8 %encoder_grad.1 = (bf16[2048,1024]{1,0:T(8,128)(2,1)}, f32[1,1024]{1,0:T(1,128)}, f32[1,1]{1,0:T(1,128)}) custom-call(s32[2]{0:T(128)S(1)} %pad_add_fusion.info_ref, bf16[1,512,512]{2,1,0:T(8,128)(2,1)S(1)} %turned.6.refs_0_, bf16[1,512,512]{2,1,0:T(8,128)(2,1)S(1)} %turned.7.refs_1_, bf16[1,512,512]{2,1,0:T(8,128)(2,1)S(1)} %turned.8.refs_2_, ...), custom_call_target="tpu_custom_call" | custom-call | flops 2147483648 | bytes 9437184 | tf_op jit(solution)/shard_map/encoder_grad/pallas_call | solution.py:330
  (68 shorter events, 3.4 us)
Async XLA Ops:
  0.7 19.0 %copy-start.2 = (bf16[128,512]{1,0:T(8,128)(2,1)S(1)}, bf16[128,512]{1,0:T(8,128)(2,1)}, u32[]{:S(2)}) copy-start(bf16[128,512]{1,0:T(8,128)(2,1)} %param.5) | copy-start | bytes 393220
  0.7 6.8 %collective-permute-start.1 = (bf16[128,512]{1,0:T(8,128)(2,1)}, bf16[128,512]{1,0:T(8,128)(2,1)S(1)}, u32[]{:S(2)}, u32[]{:S(2)}) collective-permute-start(bf16[128,512]{1,0:T(8,128)(2,1)} %param.5), channel_id=1, source_target_pairs={{0,1},{1,0},{2,3},{3,2},{4,5},{5,4},{6,7},{7,6},{8,9},{9,8},{10,11... | collective-permute-start | bytes 393224 | tf_op jit(solution)/shard_map/ppermute | solution.py:17
  3.8 14.4 %collective-permute-start.3 = (bf16[128,512]{1,0:T(8,128)(2,1)}, bf16[128,512]{1,0:T(8,128)(2,1)S(1)}, u32[]{:S(2)}, u32[]{:S(2)}) collective-permute-start(bf16[128,512]{1,0:T(8,128)(2,1)} %param.5), channel_id=1, source_target_pairs={{0,3},{1,2},{2,1},{3,0},{4,7},{5,6},{6,5},{7,4},{8,11},{9,10},{10,... | collective-permute-start | bytes 393224 | tf_op jit(solution)/shard_map/ppermute | solution.py:17
  7.5 10.6 %collective-permute-start.4 = (bf16[128,512]{1,0:T(8,128)(2,1)S(1)}, bf16[128,512]{1,0:T(8,128)(2,1)S(1)}, u32[]{:S(2)}, u32[]{:S(2)}) collective-permute-start(bf16[128,512]{1,0:T(8,128)(2,1)S(1)} %collective-permute-done.1), channel_id=1, source_target_pairs={{0,8},{4,12},{8,0},{12,4},{16,24},{20,28},{24,16},{28,20},{1,9},{5... | collective-permute-start | bytes 393224 | tf_op jit(solution)/shard_map/ppermute | solution.py:23
  9.1 10.6 %collective-permute-start.2 = (bf16[128,512]{1,0:T(8,128)(2,1)}, bf16[128,512]{1,0:T(8,128)(2,1)S(1)}, u32[]{:S(2)}, u32[]{:S(2)}) collective-permute-start(bf16[128,512]{1,0:T(8,128)(2,1)} %param.5), channel_id=1, source_target_pairs={{0,2},{1,3},{2,0},{3,1},{4,6},{5,7},{6,4},{7,5},{8,10},{9,11},{10,... | collective-permute-start | bytes 393224 | tf_op jit(solution)/shard_map/ppermute | solution.py:17
  12.9 6.9 %collective-permute-start = (bf16[128,512]{1,0:T(8,128)(2,1)}, bf16[128,512]{1,0:T(8,128)(2,1)S(1)}, u32[]{:S(2)}, u32[]{:S(2)}) collective-permute-start(bf16[128,512]{1,0:T(8,128)(2,1)} %param.5), channel_id=1, source_target_pairs={{0,8},{4,12},{8,0},{12,4},{16,24},{20,28},{24,16},{28,20},{1,9},{5... | collective-permute-start | bytes 393224 | tf_op jit(solution)/shard_map/ppermute | solution.py:23
  18.2 5.0 %collective-permute-start.5 = (bf16[128,512]{1,0:T(8,128)(2,1)S(1)}, bf16[128,512]{1,0:T(8,128)(2,1)S(1)}, u32[]{:S(2)}, u32[]{:S(2)}) collective-permute-start(bf16[128,512]{1,0:T(8,128)(2,1)S(1)} %collective-permute-done.3), channel_id=1, source_target_pairs={{0,8},{4,12},{8,0},{12,4},{16,24},{20,28},{24,16},{28,20},{1,9},{5... | collective-permute-start | bytes 393224 | tf_op jit(solution)/shard_map/ppermute | solution.py:23
  23.2 1.9 %collective-permute-start.6 = (bf16[4,128,512]{2,1,0:T(8,128)(2,1)S(1)}, bf16[4,128,512]{2,1,0:T(8,128)(2,1)S(1)}, u32[]{:S(2)}, u32[]{:S(2)}) collective-permute-start(bf16[4,128,512]{2,1,0:T(8,128)(2,1)S(1)} %pad_maximum_fusion.refs_0_), channel_id=1, source_target_pairs={{0,4},{4,0},{8,12},{12,8},{16,20},{20,16},{24,28},{28,24},{1,5},{5... | collective-permute-start | bytes 1572872 | tf_op jit(solution)/shard_map/ppermute | solution.py:23
  23.2 5.9 %collective-permute-start.7 = (bf16[128,512]{1,0:T(8,128)(2,1)S(1)}, bf16[128,512]{1,0:T(8,128)(2,1)S(1)}, u32[]{:S(2)}, u32[]{:S(2)}) collective-permute-start(bf16[128,512]{1,0:T(8,128)(2,1)S(1)} %collective-permute-done.2), channel_id=1, source_target_pairs={{0,8},{4,12},{8,0},{12,4},{16,24},{20,28},{24,16},{28,20},{1,9},{5... | collective-permute-start | bytes 393224 | tf_op jit(solution)/shard_map/ppermute | solution.py:23
  29.2 2.0 %copy-start = (f32[1024]{0:T(1024)S(1)}, f32[1024]{0:T(1024)}, u32[]{:S(2)}) copy-start(f32[1024]{0:T(1024)} %param.8) | copy-start | bytes 12292
  29.2 2.0 %collective-permute-start.8 = (bf16[4,128,512]{2,1,0:T(8,128)(2,1)S(1)}, bf16[4,128,512]{2,1,0:T(8,128)(2,1)S(1)}, u32[]{:S(2)}, u32[]{:S(2)}) collective-permute-start(bf16[4,128,512]{2,1,0:T(8,128)(2,1)S(1)} %pad_maximum_fusion.1.refs_0_), channel_id=1, source_target_pairs={{0,4},{4,0},{8,12},{12,8},{16,20},{20,16},{24,28},{28,24},{1,5},{5... | collective-permute-start | bytes 1572872 | tf_op jit(solution)/shard_map/ppermute | solution.py:23
  35.5 4.0 %collective-permute-start.12 = (bf16[2,2,128,512]{3,2,1,0:T(8,128)(2,1)S(1)}, bf16[2,2,128,512]{3,2,1,0:T(8,128)(2,1)S(1)}, u32[]{:S(2)}, u32[]{:S(2)}) collective-permute-start(bf16[2,2,128,512]{3,2,1,0:T(8,128)(2,1)S(1)} %get-tuple-element.79), channel_id=1, source_target_pairs={{0,4},{4,0},{8,12},{12,8},{16,20},{20,16},{24,28},{28,24},{1,5},{5... | collective-permute-start | bytes 1572872 | tf_op jit(solution)/shard_map/ppermute | solution.py:23
  35.7 5.6 %collective-permute-start.10 = (bf16[2,2,128,512]{3,2,1,0:T(8,128)(2,1)S(1)}, bf16[2,2,128,512]{3,2,1,0:T(8,128)(2,1)S(1)}, u32[]{:S(2)}, u32[]{:S(2)}) collective-permute-start(bf16[2,2,128,512]{3,2,1,0:T(8,128)(2,1)S(1)} %get-tuple-element.78), channel_id=1, source_target_pairs={{0,4},{4,0},{8,12},{12,8},{16,20},{20,16},{24,28},{28,24},{1,5},{5... | collective-permute-start | bytes 1572872 | tf_op jit(solution)/shard_map/ppermute | solution.py:23
  39.0 4.1 %collective-permute-start.14 = (bf16[2,2,128,512]{3,2,1,0:T(8,128)(2,1)S(1)}, bf16[2,2,128,512]{3,2,1,0:T(8,128)(2,1)S(1)}, u32[]{:S(2)}, u32[]{:S(2)}) collective-permute-start(bf16[2,2,128,512]{3,2,1,0:T(8,128)(2,1)S(1)} %get-tuple-element.81), channel_id=1, source_target_pairs={{0,4},{4,0},{8,12},{12,8},{16,20},{20,16},{24,28},{28,24},{1,5},{5... | collective-permute-start | bytes 1572872 | tf_op jit(solution)/shard_map/ppermute | solution.py:23
  39.2 4.7 %collective-permute-start.9 = (bf16[2,2,128,512]{3,2,1,0:T(8,128)(2,1)S(1)}, bf16[2,2,128,512]{3,2,1,0:T(8,128)(2,1)S(1)}, u32[]{:S(2)}, u32[]{:S(2)}) collective-permute-start(bf16[2,2,128,512]{3,2,1,0:T(8,128)(2,1)S(1)} %get-tuple-element.75), channel_id=1, source_target_pairs={{0,4},{4,0},{8,12},{12,8},{16,20},{20,16},{24,28},{28,24},{1,5},{5... | collective-permute-start | bytes 1572872 | tf_op jit(solution)/shard_map/ppermute | solution.py:23
  39.7 9.2 %collective-permute-start.13 = (bf16[1,2,128,512]{3,2,1,0:T(8,128)(2,1)S(1)}, bf16[1,2,128,512]{3,2,1,0:T(8,128)(2,1)S(1)}, u32[]{:S(2)}, u32[]{:S(2)}) collective-permute-start(bf16[1,2,128,512]{3,2,1,0:T(8,128)(2,1)S(1)} %slice_bitcast_fusion.5), channel_id=1, source_target_pairs={{0,8},{4,12},{8,0},{12,4},{16,24},{20,28},{24,16},{28,20},{1,9},{5... | collective-permute-start | bytes 786440 | tf_op jit(solution)/shard_map/ppermute | solution.py:23
  41.5 8.1 %collective-permute-start.11 = (bf16[1,2,128,512]{3,2,1,0:T(8,128)(2,1)S(1)}, bf16[1,2,128,512]{3,2,1,0:T(8,128)(2,1)S(1)}, u32[]{:S(2)}, u32[]{:S(2)}) collective-permute-start(bf16[1,2,128,512]{3,2,1,0:T(8,128)(2,1)S(1)} %get-tuple-element.120), channel_id=1, source_target_pairs={{0,16},{4,20},{8,24},{12,28},{16,0},{20,4},{24,8},{28,12},{1,17},{... | collective-permute-start | bytes 786440 | tf_op jit(solution)/shard_map/ppermute | solution.py:29
  43.2 11.3 %collective-permute-start.16 = (bf16[1,2,128,512]{3,2,1,0:T(8,128)(2,1)S(1)}, bf16[1,2,128,512]{3,2,1,0:T(8,128)(2,1)S(1)}, u32[]{:S(2)}, u32[]{:S(2)}) collective-permute-start(bf16[1,2,128,512]{3,2,1,0:T(8,128)(2,1)S(1)} %slice_bitcast_fusion.4), channel_id=1, source_target_pairs={{0,8},{4,12},{8,0},{12,4},{16,24},{20,28},{24,16},{28,20},{1,9},{5... | collective-permute-start | bytes 786440 | tf_op jit(solution)/shard_map/ppermute | solution.py:23
  49.7 7.3 %collective-permute-start.17 = (bf16[1,2,128,512]{3,2,1,0:T(8,128)(2,1)S(1)}, bf16[1,2,128,512]{3,2,1,0:T(8,128)(2,1)S(1)}, u32[]{:S(2)}, u32[]{:S(2)}) collective-permute-start(bf16[1,2,128,512]{3,2,1,0:T(8,128)(2,1)S(1)} %fusion.4), channel_id=1, source_target_pairs={{0,16},{4,20},{8,24},{12,28},{16,0},{20,4},{24,8},{28,12},{1,17},{... | collective-permute-start | bytes 786440 | tf_op jit(solution)/shard_map/ppermute | solution.py:29
  51.3 13.0 %collective-permute-start.15 = (bf16[1,2,128,512]{3,2,1,0:T(8,128)(2,1)S(1)}, bf16[1,2,128,512]{3,2,1,0:T(8,128)(2,1)S(1)}, u32[]{:S(2)}, u32[]{:S(2)}) collective-permute-start(bf16[1,2,128,512]{3,2,1,0:T(8,128)(2,1)S(1)} %fusion.7), channel_id=1, source_target_pairs={{0,8},{4,12},{8,0},{12,4},{16,24},{20,28},{24,16},{28,20},{1,9},{5... | collective-permute-start | bytes 786440 | tf_op jit(solution)/shard_map/ppermute | solution.py:23
  57.1 7.2 %collective-permute-start.18 = (bf16[1,2,128,512]{3,2,1,0:T(8,128)(2,1)S(1)}, bf16[1,2,128,512]{3,2,1,0:T(8,128)(2,1)S(1)}, u32[]{:S(2)}, u32[]{:S(2)}) collective-permute-start(bf16[1,2,128,512]{3,2,1,0:T(8,128)(2,1)S(1)} %get-tuple-element.86), channel_id=1, source_target_pairs={{0,16},{4,20},{8,24},{12,28},{16,0},{20,4},{24,8},{28,12},{1,17},{... | collective-permute-start | bytes 786440 | tf_op jit(solution)/shard_map/ppermute | solution.py:29
  58.7 11.5 %collective-permute-start.20 = (bf16[128,512]{1,0:T(8,128)(2,1)S(1)}, bf16[128,512]{1,0:T(8,128)(2,1)S(1)}, u32[]{:S(2)}, u32[]{:S(2)}) collective-permute-start(bf16[128,512]{1,0:T(8,128)(2,1)S(1)} %get-tuple-element.122), channel_id=1, source_target_pairs={{0,2},{1,3},{2,0},{3,1},{4,6},{5,7},{6,4},{7,5},{8,10},{9,11},{10,... | collective-permute-start | bytes 393224 | tf_op jit(solution)/shard_map/ppermute | solution.py:17
  58.8 12.8 %copy-start.1 = (bf16[128,512]{1,0:T(8,128)(2,1)S(1)}, bf16[128,512]{1,0:T(8,128)(2,1)}, u32[]{:S(2)}) copy-start(bf16[128,512]{1,0:T(8,128)(2,1)} %param.6) | copy-start | bytes 393220
  58.8 11.0 %collective-permute-start.19 = (bf16[128,512]{1,0:T(8,128)(2,1)S(1)}, bf16[128,512]{1,0:T(8,128)(2,1)S(1)}, u32[]{:S(2)}, u32[]{:S(2)}) collective-permute-start(bf16[128,512]{1,0:T(8,128)(2,1)S(1)} %get-tuple-element.121), channel_id=1, source_target_pairs={{0,3},{1,2},{2,1},{3,0},{4,7},{5,6},{6,5},{7,4},{8,11},{9,10},{10,... | collective-permute-start | bytes 393224 | tf_op jit(solution)/shard_map/ppermute | solution.py:17
  64.4 7.1 %collective-permute-start.21 = (bf16[128,512]{1,0:T(8,128)(2,1)S(1)}, bf16[128,512]{1,0:T(8,128)(2,1)S(1)}, u32[]{:S(2)}, u32[]{:S(2)}) collective-permute-start(bf16[128,512]{1,0:T(8,128)(2,1)S(1)} %fusion.13), channel_id=1, source_target_pairs={{0,1},{1,0},{2,3},{3,2},{4,5},{5,4},{6,7},{7,6},{8,9},{9,8},{10,11... | collective-permute-start | bytes 393224 | tf_op jit(solution)/shard_map/ppermute | solution.py:17
  72.4 5.5 %collective-permute-start.22 = (bf16[1,128,512]{2,1,0:T(8,128)(2,1)S(1)}, bf16[1,128,512]{2,1,0:T(8,128)(2,1)S(1)}, u32[]{:S(2)}, u32[]{:S(2)}) collective-permute-start(bf16[1,128,512]{2,1,0:T(8,128)(2,1)S(1)} %bitcast.83), channel_id=1, source_target_pairs={{0,16},{4,20},{8,24},{12,28},{16,0},{20,4},{24,8},{28,12},{1,17},{... | collective-permute-start | bytes 393224 | tf_op jit(solution)/shard_map/ppermute | solution.py:36
  72.9 6.8 %collective-permute-start.24 = (bf16[128,512]{1,0:T(8,128)(2,1)S(1)}, bf16[128,512]{1,0:T(8,128)(2,1)S(1)}, u32[]{:S(2)}, u32[]{:S(2)}) collective-permute-start(bf16[128,512]{1,0:T(8,128)(2,1)S(1)} %get-tuple-element.115), channel_id=1, source_target_pairs={{0,1},{1,0},{2,3},{3,2},{4,5},{5,4},{6,7},{7,6},{8,9},{9,8},{10,11... | collective-permute-start | bytes 393224 | tf_op jit(solution)/shard_map/ppermute | solution.py:17
  74.3 9.7 %collective-permute-start.26 = (bf16[128,512]{1,0:T(8,128)(2,1)S(1)}, bf16[128,512]{1,0:T(8,128)(2,1)S(1)}, u32[]{:S(2)}, u32[]{:S(2)}) collective-permute-start(bf16[128,512]{1,0:T(8,128)(2,1)S(1)} %get-tuple-element.115), channel_id=1, source_target_pairs={{0,2},{1,3},{2,0},{3,1},{4,6},{5,7},{6,4},{7,5},{8,10},{9,11},{10,... | collective-permute-start | bytes 393224 | tf_op jit(solution)/shard_map/ppermute | solution.py:17
  75.0 9.4 %collective-permute-start.27 = (bf16[128,512]{1,0:T(8,128)(2,1)S(1)}, bf16[128,512]{1,0:T(8,128)(2,1)S(1)}, u32[]{:S(2)}, u32[]{:S(2)}) collective-permute-start(bf16[128,512]{1,0:T(8,128)(2,1)S(1)} %get-tuple-element.115), channel_id=1, source_target_pairs={{0,3},{1,2},{2,1},{3,0},{4,7},{5,6},{6,5},{7,4},{8,11},{9,10},{10,... | collective-permute-start | bytes 393224 | tf_op jit(solution)/shard_map/ppermute | solution.py:17
  77.3 7.2 %collective-permute-start.32 = (bf16[1,128,512]{2,1,0:T(8,128)(2,1)S(1)}, bf16[1,128,512]{2,1,0:T(8,128)(2,1)S(1)}, u32[]{:S(2)}, u32[]{:S(2)}) collective-permute-start(bf16[1,128,512]{2,1,0:T(8,128)(2,1)S(1)} %bitcast.84), channel_id=1, source_target_pairs={{0,8},{4,12},{8,0},{12,4},{16,24},{20,28},{24,16},{28,20},{1,9},{5... | collective-permute-start | bytes 393224 | tf_op jit(solution)/shard_map/ppermute | solution.py:23
  77.9 8.2 %collective-permute-start.23 = (bf16[1,128,512]{2,1,0:T(8,128)(2,1)S(1)}, bf16[1,128,512]{2,1,0:T(8,128)(2,1)S(1)}, u32[]{:S(2)}, u32[]{:S(2)}) collective-permute-start(bf16[1,128,512]{2,1,0:T(8,128)(2,1)S(1)} %collective-permute-done.22.refs_0_), channel_id=1, source_target_pairs={{0,8},{4,12},{8,0},{12,4},{16,24},{20,28},{24,16},{28,20},{1,9},{5... | collective-permute-start | bytes 393224 | tf_op jit(solution)/shard_map/ppermute | solution.py:23
  79.7 7.8 %collective-permute-start.25 = (bf16[1,128,512]{2,1,0:T(8,128)(2,1)S(1)}, bf16[1,128,512]{2,1,0:T(8,128)(2,1)S(1)}, u32[]{:S(2)}, u32[]{:S(2)}) collective-permute-start(bf16[1,128,512]{2,1,0:T(8,128)(2,1)S(1)} %bitcast.87), channel_id=1, source_target_pairs={{0,16},{4,20},{8,24},{12,28},{16,0},{20,4},{24,8},{28,12},{1,17},{... | collective-permute-start | bytes 393224 | tf_op jit(solution)/shard_map/ppermute | solution.py:36
  83.9 6.3 %collective-permute-start.33 = (bf16[1,128,512]{2,1,0:T(8,128)(2,1)S(1)}, bf16[1,128,512]{2,1,0:T(8,128)(2,1)S(1)}, u32[]{:S(2)}, u32[]{:S(2)}) collective-permute-start(bf16[1,128,512]{2,1,0:T(8,128)(2,1)S(1)} %bitcast.88), channel_id=1, source_target_pairs={{0,8},{4,12},{8,0},{12,4},{16,24},{20,28},{24,16},{28,20},{1,9},{5... | collective-permute-start | bytes 393224 | tf_op jit(solution)/shard_map/ppermute | solution.py:23
  84.4 7.2 %collective-permute-start.36 = (bf16[2,128,512]{2,1,0:T(8,128)(2,1)S(1)}, bf16[2,128,512]{2,1,0:T(8,128)(2,1)S(1)}, u32[]{:S(2)}, u32[]{:S(2)}) collective-permute-start(bf16[2,128,512]{2,1,0:T(8,128)(2,1)S(1)} %pad_maximum_fusion.2.refs_2_), channel_id=1, source_target_pairs={{0,4},{4,0},{8,12},{12,8},{16,20},{20,16},{24,28},{28,24},{1,5},{5... | collective-permute-start | bytes 786440 | tf_op jit(solution)/shard_map/ppermute | solution.py:23
  84.5 10.3 %collective-permute-start.37 = (bf16[2,128,512]{2,1,0:T(8,128)(2,1)S(1)}, bf16[2,128,512]{2,1,0:T(8,128)(2,1)S(1)}, u32[]{:S(2)}, u32[]{:S(2)}) collective-permute-start(bf16[2,128,512]{2,1,0:T(8,128)(2,1)S(1)} %pad_maximum_fusion.2.refs_2_), channel_id=1, source_target_pairs={{0,8},{4,12},{8,0},{12,4},{16,24},{20,28},{24,16},{28,20},{1,9},{5... | collective-permute-start | bytes 786440 | tf_op jit(solution)/shard_map/ppermute | solution.py:23
  86.1 9.4 %collective-permute-start.28 = (bf16[2,128,512]{2,1,0:T(8,128)(2,1)S(1)}, bf16[2,128,512]{2,1,0:T(8,128)(2,1)S(1)}, u32[]{:S(2)}, u32[]{:S(2)}) collective-permute-start(bf16[2,128,512]{2,1,0:T(8,128)(2,1)S(1)} %pad_maximum_fusion.2.refs_2_), channel_id=1, source_target_pairs={{0,16},{4,20},{8,24},{12,28},{16,0},{20,4},{24,8},{28,12},{1,17},{... | collective-permute-start | bytes 786440 | tf_op jit(solution)/shard_map/ppermute | solution.py:36
  87.5 2.8 %collective-permute-start.35 = (bf16[1,128,512]{2,1,0:T(8,128)(2,1)S(1)}, bf16[1,128,512]{2,1,0:T(8,128)(2,1)S(1)}, u32[]{:S(2)}, u32[]{:S(2)}) collective-permute-start(bf16[1,128,512]{2,1,0:T(8,128)(2,1)S(1)} %bitcast.89), channel_id=1, source_target_pairs={{0,4},{4,0},{8,12},{12,8},{16,20},{20,16},{24,28},{28,24},{1,5},{5... | collective-permute-start | bytes 393224 | tf_op jit(solution)/shard_map/ppermute | solution.py:23
  90.2 1.3 %collective-permute-start.34 = (bf16[1,128,512]{2,1,0:T(8,128)(2,1)S(1)}, bf16[1,128,512]{2,1,0:T(8,128)(2,1)S(1)}, u32[]{:S(2)}, u32[]{:S(2)}) collective-permute-start(bf16[1,128,512]{2,1,0:T(8,128)(2,1)S(1)} %bitcast.85), channel_id=1, source_target_pairs={{0,4},{4,0},{8,12},{12,8},{16,20},{20,16},{24,28},{28,24},{1,5},{5... | collective-permute-start | bytes 393224 | tf_op jit(solution)/shard_map/ppermute | solution.py:23
  94.8 2.8 %collective-permute-start.40 = (bf16[2,128,512]{2,1,0:T(8,128)(2,1)S(1)}, bf16[2,128,512]{2,1,0:T(8,128)(2,1)S(1)}, u32[]{:S(2)}, u32[]{:S(2)}) collective-permute-start(bf16[2,128,512]{2,1,0:T(8,128)(2,1)S(1)} %collective-permute-done.37.refs_2_), channel_id=1, source_target_pairs={{0,4},{4,0},{8,12},{12,8},{16,20},{20,16},{24,28},{28,24},{1,5},{5... | collective-permute-start | bytes 786440 | tf_op jit(solution)/shard_map/ppermute | solution.py:23
  95.0 2.1 %collective-permute-start.39 = (bf16[1,128,512]{2,1,0:T(8,128)(2,1)S(1)}, bf16[1,128,512]{2,1,0:T(8,128)(2,1)S(1)}, u32[]{:S(2)}, u32[]{:S(2)}) collective-permute-start(bf16[1,128,512]{2,1,0:T(8,128)(2,1)S(1)} %collective-permute-done.33.refs_1_), channel_id=1, source_target_pairs={{0,4},{4,0},{8,12},{12,8},{16,20},{20,16},{24,28},{28,24},{1,5},{5... | collective-permute-start | bytes 393224 | tf_op jit(solution)/shard_map/ppermute | solution.py:23
  95.4 1.7 %collective-permute-start.38 = (bf16[1,128,512]{2,1,0:T(8,128)(2,1)S(1)}, bf16[1,128,512]{2,1,0:T(8,128)(2,1)S(1)}, u32[]{:S(2)}, u32[]{:S(2)}) collective-permute-start(bf16[1,128,512]{2,1,0:T(8,128)(2,1)S(1)} %collective-permute-done.32.refs_0_), channel_id=1, source_target_pairs={{0,4},{4,0},{8,12},{12,8},{16,20},{20,16},{24,28},{28,24},{1,5},{5... | collective-permute-start | bytes 393224 | tf_op jit(solution)/shard_map/ppermute | solution.py:23
  95.5 5.6 %collective-permute-start.31 = (bf16[2,128,512]{2,1,0:T(8,128)(2,1)S(1)}, bf16[2,128,512]{2,1,0:T(8,128)(2,1)S(1)}, u32[]{:S(2)}, u32[]{:S(2)}) collective-permute-start(bf16[2,128,512]{2,1,0:T(8,128)(2,1)S(1)} %collective-permute-done.28.refs_2_), channel_id=1, source_target_pairs={{0,4},{4,0},{8,12},{12,8},{16,20},{20,16},{24,28},{28,24},{1,5},{5... | collective-permute-start | bytes 786440 | tf_op jit(solution)/shard_map/ppermute | solution.py:23
  95.9 8.5 %collective-permute-start.42 = (bf16[2,128,512]{2,1,0:T(8,128)(2,1)S(1)}, bf16[2,128,512]{2,1,0:T(8,128)(2,1)S(1)}, u32[]{:S(2)}, u32[]{:S(2)}) collective-permute-start(bf16[2,128,512]{2,1,0:T(8,128)(2,1)S(1)} %collective-permute-done.37.refs_2_), channel_id=1, source_target_pairs={{0,16},{4,20},{8,24},{12,28},{16,0},{20,4},{24,8},{28,12},{1,17},{... | collective-permute-start | bytes 786440 | tf_op jit(solution)/shard_map/ppermute | solution.py:36
  97.1 4.0 %collective-permute-start.29 = (bf16[1,128,512]{2,1,0:T(8,128)(2,1)S(1)}, bf16[1,128,512]{2,1,0:T(8,128)(2,1)S(1)}, u32[]{:S(2)}, u32[]{:S(2)}) collective-permute-start(bf16[1,128,512]{2,1,0:T(8,128)(2,1)S(1)} %collective-permute-done.22.refs_0_), channel_id=1, source_target_pairs={{0,4},{4,0},{8,12},{12,8},{16,20},{20,16},{24,28},{28,24},{1,5},{5... | collective-permute-start | bytes 393224 | tf_op jit(solution)/shard_map/ppermute | solution.py:23
  97.1 4.0 %collective-permute-start.30 = (bf16[1,128,512]{2,1,0:T(8,128)(2,1)S(1)}, bf16[1,128,512]{2,1,0:T(8,128)(2,1)S(1)}, u32[]{:S(2)}, u32[]{:S(2)}) collective-permute-start(bf16[1,128,512]{2,1,0:T(8,128)(2,1)S(1)} %collective-permute-done.25.refs_1_), channel_id=1, source_target_pairs={{0,4},{4,0},{8,12},{12,8},{16,20},{20,16},{24,28},{28,24},{1,5},{5... | collective-permute-start | bytes 393224 | tf_op jit(solution)/shard_map/ppermute | solution.py:23
  97.6 6.8 %collective-permute-start.41 = (bf16[1,128,512]{2,1,0:T(8,128)(2,1)S(1)}, bf16[1,128,512]{2,1,0:T(8,128)(2,1)S(1)}, u32[]{:S(2)}, u32[]{:S(2)}) collective-permute-start(bf16[1,128,512]{2,1,0:T(8,128)(2,1)S(1)} %collective-permute-done.25.refs_1_), channel_id=1, source_target_pairs={{0,8},{4,12},{8,0},{12,4},{16,24},{20,28},{24,16},{28,20},{1,9},{5... | collective-permute-start | bytes 393224 | tf_op jit(solution)/shard_map/ppermute | solution.py:23
  104.3 2.0 %collective-permute-start.45 = (bf16[2,128,512]{2,1,0:T(8,128)(2,1)S(1)}, bf16[2,128,512]{2,1,0:T(8,128)(2,1)S(1)}, u32[]{:S(2)}, u32[]{:S(2)}) collective-permute-start(bf16[2,128,512]{2,1,0:T(8,128)(2,1)S(1)} %collective-permute-done.42.refs_2_), channel_id=1, source_target_pairs={{0,4},{4,0},{8,12},{12,8},{16,20},{20,16},{24,28},{28,24},{1,5},{5... | collective-permute-start | bytes 786440 | tf_op jit(solution)/shard_map/ppermute | solution.py:23
  104.4 1.7 %collective-permute-start.44 = (bf16[1,128,512]{2,1,0:T(8,128)(2,1)S(1)}, bf16[1,128,512]{2,1,0:T(8,128)(2,1)S(1)}, u32[]{:S(2)}, u32[]{:S(2)}) collective-permute-start(bf16[1,128,512]{2,1,0:T(8,128)(2,1)S(1)} %collective-permute-done.41.refs_1_), channel_id=1, source_target_pairs={{0,4},{4,0},{8,12},{12,8},{16,20},{20,16},{24,28},{28,24},{1,5},{5... | collective-permute-start | bytes 393224 | tf_op jit(solution)/shard_map/ppermute | solution.py:23
  104.9 1.4 %collective-permute-start.43 = (bf16[1,128,512]{2,1,0:T(8,128)(2,1)S(1)}, bf16[1,128,512]{2,1,0:T(8,128)(2,1)S(1)}, u32[]{:S(2)}, u32[]{:S(2)}) collective-permute-start(bf16[1,128,512]{2,1,0:T(8,128)(2,1)S(1)} %collective-permute-done.23.refs_0_), channel_id=1, source_target_pairs={{0,4},{4,0},{8,12},{12,8},{16,20},{20,16},{24,28},{28,24},{1,5},{5... | collective-permute-start | bytes 393224 | tf_op jit(solution)/shard_map/ppermute | solution.py:23
